TPU v7x, 256 devices: a whole 4x4x8 slice. The times are simulated.
256 devices in a mesh: px: 16 (over y_lo, x, core), py: 16 (over z, y_hi).
Axes of the slice: x: 4, y: 4 (y_hi: 2, y_lo: 2; y = y_hi * 2 + y_lo), z: 8, core: 2. Of those that a mesh axis runs over, the one named last changes fastest.
Arguments:
- electric: float32 [3, 256, 256, 128], P(None, 'px', 'py'), may hold values from -4 to 4
- magnetic: float32 [3, 256, 256, 128], P(None, 'px', 'py'), may hold values from -4 to 4
- material: int32 [256, 256, 128], P('px', 'py'), may hold values from 0 to 7
- permittivity: float32 [8], replicated, may hold values from 1 to 4.5
- conductivity: float32 [8], replicated, may hold values from 0.002 to 0.05
Outputs:
- electric_next: float32 [3, 256, 256, 128], P(None, 'px', 'py')
- magnetic_next: float32 [3, 256, 256, 128], P(None, 'px', 'py')
All inputs are finite; a program needn't handle non-finite values.
Results may differ from a plain program's by a relative error of at most 0.005.
Values sent between devices are 32-bit elements; how exact they have to be, the bound alone decides.
No kernel may reach another device: no remote copies, remote signals or barrier semaphores. Data moves between devices by JAX's collectives and lax.ppermute only.
A program may use at most 64 MiB of HBM per device.

v0:
```python
import jax
import jax.numpy as jnp
from jax import lax
from jax.sharding import PartitionSpec as P

half_step = 32.0


def padded_2(cells, sides, width):
    for axis, dim in sides:
        count = lax.axis_size(axis)
        ends = count - 1
        head = lax.slice_in_dim(cells, 0, width, axis=dim)
        tail = lax.slice_in_dim(cells, cells.shape[dim] - width, cells.shape[dim], axis=dim)
        cells = jnp.concatenate(
            [
                lax.ppermute(tail, axis, [(i, (i + 1) % count) for i in range(ends)]),
                cells,
                lax.ppermute(head, axis, [((i + 1) % count, i) for i in range(ends)]),
            ],
            axis=dim,
        )
    return cells


def from_before(values, stride, direction, filler):
    length = values.shape[direction]
    widths = [(0, 0)] * values.ndim
    widths[direction] = (stride, 0)
    padded = jnp.pad(values, widths, constant_values=filler)
    return lax.slice_in_dim(padded, 0, length, axis=direction)


def from_after(values, stride, direction, filler):
    length = values.shape[direction]
    widths = [(0, 0)] * values.ndim
    widths[direction] = (0, stride)
    padded = jnp.pad(values, widths, constant_values=filler)
    return lax.slice_in_dim(padded, stride, stride + length, axis=direction)


def reduce_lines(lower_band, middle, upper_band, sources, direction):
    length = middle.shape[direction]
    stride = 1
    while stride < length:
        left_ratio = lower_band / from_before(middle, stride, direction, 1.0)
        right_ratio = upper_band / from_after(middle, stride, direction, 1.0)
        new_middle = (
            middle
            - from_before(upper_band, stride, direction, 0.0) * left_ratio
            - from_after(lower_band, stride, direction, 0.0) * right_ratio
        )
        lower_band = -from_before(lower_band, stride, direction, 0.0) * left_ratio
        upper_band = -from_after(upper_band, stride, direction, 0.0) * right_ratio
        sources = tuple(
            (
                column
                - from_before(column, stride, direction, 0.0) * left_ratio
                - from_after(column, stride, direction, 0.0) * right_ratio
                for column in sources
            )
        )
        middle = new_middle
        stride = stride * 2
    return tuple((column / middle for column in sources))


def line_system(line_rate, first_row, final_row):
    zero_band = jnp.zeros_like(line_rate)
    lower_band = jnp.where(first_row, zero_band, -line_rate)
    upper_band = jnp.where(final_row, zero_band, -line_rate)
    middle = 1.0 + 2.0 * line_rate - jnp.where(first_row, line_rate, zero_band)
    return (lower_band, middle, upper_band)


def solve_whole(line_rate, source, direction):
    length = line_rate.shape[direction]
    dims_shape = [1] * line_rate.ndim
    dims_shape[direction] = length
    position = lax.broadcasted_iota(jnp.int32, tuple(dims_shape), direction)
    lower_band, middle, upper_band = line_system(line_rate, position == 0, position == length - 1)
    return reduce_lines(lower_band, middle, upper_band, (source,), direction)[0]


def ahead_last(values):
    return from_after(values, 1, 2, 0.0) - values


def behind_last(values):
    return values - from_before(values, 1, 2, 0.0)


def material_table(material, entries):
    entry_count = entries.shape[0]
    labels = lax.broadcasted_iota(jnp.int32, (entry_count, 1, 1, 1), 0)
    return jnp.sum(jnp.where(material[None] == labels, entries[:, None, None, None], 0.0), axis=0)


def with_rims(stacked):
    return padded_2(stacked, (("px", 1), ("py", 2)), 1)


def x_lines_moved(source, rate_moved):
    moved = lax.all_to_all(source, "px", split_axis=1, concat_axis=0, tiled=True)
    solved = solve_whole(rate_moved, moved, 0)
    return lax.all_to_all(solved, "px", split_axis=0, concat_axis=1, tiled=True)


def y_lines_moved(source, rate_moved):
    moved = lax.all_to_all(source, "py", split_axis=0, concat_axis=1, tiled=True)
    solved = solve_whole(rate_moved, moved, 1)
    return lax.all_to_all(solved, "py", split_axis=1, concat_axis=0, tiled=True)


def x_lines(source, rate_moved):
    return x_lines_moved(source, rate_moved)


def y_lines(source, rate_moved):
    return y_lines_moved(source, rate_moved)


def local(electric, magnetic, material, permittivity, conductivity):
    perm_cell = material_table(material, permittivity)
    cond_cell = material_table(material, conductivity)
    denominator = perm_cell / half_step + 0.5 * cond_cell
    retain = (perm_cell / half_step - 0.5 * cond_cell) / denominator
    driving = 1.0 / denominator
    line_rate = half_step * driving
    rate_x = lax.all_to_all(line_rate, "px", split_axis=1, concat_axis=0, tiled=True)
    rate_y = lax.all_to_all(line_rate, "py", split_axis=0, concat_axis=1, tiled=True)
    rows = electric.shape[1]
    columns = electric.shape[2]
    elec_x, elec_y, elec_z = (electric[0], electric[1], electric[2])
    magn_x, magn_y, magn_z = (magnetic[0], magnetic[1], magnetic[2])
    grown = with_rims(jnp.concatenate([electric, magnetic], axis=0))
    rim_ex, rim_ey, rim_ez = (grown[0], grown[1], grown[2])
    rim_hx, rim_hy, rim_hz = (grown[3], grown[4], grown[5])
    rise_x_ey = rim_ey[2:, :-1] - rim_ey[1:-1, :-1]
    source_x = (
        retain * elec_x
        + driving * (rim_hz[1:-1, 1:-1] - rim_hz[1:-1, :-2] - behind_last(magn_y))
        - line_rate * (rise_x_ey[:, 1:] - rise_x_ey[:, :-1])
    )
    rise_y_ez = rim_ez[1:-1, 2:] - rim_ez[1:-1, 1:-1]
    source_y = (
        retain * elec_y
        + driving * (behind_last(magn_x) - (rim_hz[1:-1, 1:-1] - rim_hz[:-2, 1:-1]))
        - line_rate * behind_last(rise_y_ez)
    )
    rise_z_ex = ahead_last(rim_ex[:-1, 1:-1])
    source_z = (
        retain * elec_z
        + driving
        * (rim_hy[1:-1, 1:-1] - rim_hy[:-2, 1:-1] - (rim_hx[1:-1, 1:-1] - rim_hx[1:-1, :-2]))
        - line_rate * (rise_z_ex[1:] - rise_z_ex[:-1])
    )
    half_x = y_lines(source_x, rate_y)
    half_y = solve_whole(line_rate, source_y, 2)
    half_z = x_lines(source_z, rate_x)
    grown_half = with_rims(jnp.stack([half_x, half_y, half_z], axis=0))
    rim_fx, rim_fy, rim_fz = (grown_half[0], grown_half[1], grown_half[2])
    px_first = lax.axis_index("px") == 0
    py_first = lax.axis_index("py") == 0
    ext_rows = lax.broadcasted_iota(jnp.int32, (rows + 1, 1, 1), 0) == 0
    ext_cols = lax.broadcasted_iota(jnp.int32, (1, columns + 1, 1), 1) == 0
    inside = jnp.where(ext_rows & px_first | ext_cols & py_first, 0.0, 1.0)
    rise_z_fy = ahead_last(rim_fy[:-1, :-1])
    rise_x_fz = rim_fz[1:, :-1] - rim_fz[:-1, :-1]
    rise_y_fx = rim_fx[:-1, 1:] - rim_fx[:-1, :-1]
    mid_x = (
        rim_hx[:-1, :-1] - half_step * (rim_ez[:-1, 1:] - rim_ez[:-1, :-1]) + half_step * rise_z_fy
    ) * inside
    mid_y = (
        rim_hy[:-1, :-1] - half_step * ahead_last(rim_ex[:-1, :-1]) + half_step * rise_x_fz
    ) * inside
    mid_z = (
        rim_hz[:-1, :-1] - half_step * (rim_ey[1:, :-1] - rim_ey[:-1, :-1]) + half_step * rise_y_fx
    ) * inside
    hold_x, hold_y, hold_z = (mid_x[1:, 1:], mid_y[1:, 1:], mid_z[1:, 1:])
    rise_x_inner = rise_x_fz[1:, 1:]
    source_x2 = (
        retain * half_x
        + driving * (mid_z[1:, 1:] - mid_z[1:, :-1] - behind_last(hold_y))
        - line_rate * behind_last(rise_x_inner)
    )
    source_y2 = (
        retain * half_y
        + driving * (behind_last(hold_x) - (mid_z[1:, 1:] - mid_z[:-1, 1:]))
        - line_rate * (rise_y_fx[1:, 1:] - rise_y_fx[:-1, 1:])
    )
    source_z2 = (
        retain * half_z
        + driving * (mid_y[1:, 1:] - mid_y[:-1, 1:] - (mid_x[1:, 1:] - mid_x[1:, :-1]))
        - line_rate * (rise_z_fy[1:, 1:] - rise_z_fy[1:, :-1])
    )
    full_x = solve_whole(line_rate, source_x2, 2)
    full_y = x_lines(source_y2, rate_x)
    full_z = y_lines(source_z2, rate_y)
    grown_full = with_rims(jnp.stack([full_y, full_z], axis=0))
    rim_gy, rim_gz = (grown_full[0], grown_full[1])
    new_x = (
        hold_x - half_step * (rim_gz[1:-1, 2:] - rim_gz[1:-1, 1:-1]) + half_step * rise_z_fy[1:, 1:]
    )
    new_y = hold_y - half_step * ahead_last(full_x) + half_step * rise_x_inner
    new_z = (
        hold_z - half_step * (rim_gy[2:, 1:-1] - rim_gy[1:-1, 1:-1]) + half_step * rise_y_fx[1:, 1:]
    )
    return (jnp.stack([full_x, full_y, full_z], axis=0), jnp.stack([new_x, new_y, new_z], axis=0))


def solution(mesh):
    placed = (P(None, "px", "py", None), P(None, "px", "py", None), P("px", "py", None), P(), P())
    return jax.shard_map(
        local,
        mesh=mesh,
        in_specs=placed,
        out_specs=(P(None, "px", "py", None), P(None, "px", "py", None)),
        check_vma=False,
    )
```

profile of v0, /device:TPU:1, one launch (start us, length us, event | category | flops | bytes accessed | tf_op | source)
XLA Modules:
  0.0 209.9 jit_solution(12773030655780745653)
XLA Ops:
  2.8 4.5 %collective-permute-start = (f32[6,1,16,128]{3,2,1,0:T(8,128)S(1)}, f32[6,1,16,128]{3,2,1,0:T(8,128)S(1)}, u32[]{:S(2)}, u32[]{:S(2)}) collective-permute-start(f32[6,1,16,128]{3,2,1,0:T(8,128)S(1)} %get-tuple-element.103), channel_id=1, source_target_pairs={{0,16},{16,32},{32,48},{48,64},{64,80},{80,96},{96,112},{112,128},... | collective-permute-start | bytes 147464 | tf_op jit(solution)/shard_map/ppermute | solution.py:17
  12.8 4.8 %collective-permute-start.2 = (f32[6,18,1,128]{3,2,1,0:T(1,128)S(1)}, f32[6,18,1,128]{3,2,1,0:T(1,128)S(1)}, u32[]{:S(2)}, u32[]{:S(2)}) collective-permute-start(f32[6,18,1,128]{3,2,1,0:T(1,128)S(1)} %get-tuple-element.101), channel_id=1, source_target_pairs={{0,1},{1,2},{2,3},{3,4},{4,5},{5,6},{6,7},{7,8},{8,9},{9,10},{10,1... | collective-permute-start | bytes 165896 | tf_op jit(solution)/shard_map/ppermute | solution.py:17
  19.0 5.1 %collective-permute-done.3 = f32[6,18,1,128]{3,2,1,0:T(1,128)S(1)} collective-permute-done((f32[6,18,1,128]{3,2,1,0:T(1,128)S(1)}, f32[6,18,1,128]{3,2,1,0:T(1,128)S(1)}, u32[]{:S(2)}, u32[]{:S(2)}) %collective-permute-start.3) | collective-permute-done | bytes 55328 | tf_op jit(solution)/shard_map/ppermute | solution.py:19
  29.3 6.0 %all-to-all-start.4 = ((f32[16,16,128]{2,0,1:T(8,128)}), f32[16,16,128]{2,0,1:T(8,128)S(1)}, u32[]{:S(2)}, u32[]{:S(2)}) async-start(f32[16,16,128]{2,0,1:T(8,128)} %copy.32), calls=%async_computation.4 | async-start | bytes 262144 | tf_op jit(solution)/shard_map/all_to_all | solution.py:130
  41.3 3.9 %all-to-all-start.3 = ((f32[16,16,128]{2,0,1:T(8,128)}), f32[16,16,128]{2,0,1:T(8,128)S(1)}, u32[]{:S(2)}, u32[]{:S(2)}) async-start(f32[16,16,128]{2,0,1:T(8,128)} %copy.31), calls=%async_computation.3 | async-start | bytes 262144 | tf_op jit(solution)/shard_map/all_to_all | solution.py:104
  45.5 5.8 %all-to-all-done.3 = f32[16,16,128]{2,0,1:T(8,128)S(1)} async-done(((f32[16,16,128]{2,0,1:T(8,128)}), f32[16,16,128]{2,0,1:T(8,128)S(1)}, u32[]{:S(2)}, u32[]{:S(2)}) %all-to-all-start.3) | async-done | bytes 131104 | tf_op jit(solution)/shard_map/all_to_all | solution.py:104
  51.3 11.0 %all-to-all-start.1 = ((f32[16,16,128]{2,1,0:T(8,128)}), f32[16,16,128]{2,1,0:T(8,128)}, u32[]{:S(2)}, u32[]{:S(2)}) async-start(f32[16,16,128]{2,1,0:T(8,128)} %get-tuple-element.162), calls=%async_computation.1 | async-start | bytes 262144 | tf_op jit(solution)/shard_map/all_to_all | solution.py:131
  66.4 6.0 %all-to-all-done.1 = f32[16,16,128]{2,1,0:T(8,128)} async-done(((f32[16,16,128]{2,1,0:T(8,128)}), f32[16,16,128]{2,1,0:T(8,128)}, u32[]{:S(2)}, u32[]{:S(2)}) %all-to-all-start.1) | async-done | bytes 131104 | tf_op jit(solution)/shard_map/all_to_all | solution.py:131
  72.3 4.2 %all-to-all-start = ((f32[16,16,128]{2,1,0:T(8,128)}), f32[16,16,128]{2,1,0:T(8,128)}, u32[]{:S(2)}, u32[]{:S(2)}) async-start(f32[16,16,128]{2,1,0:T(8,128)} %get-tuple-element.40), calls=%async_computation | async-start | bytes 262144 | tf_op jit(solution)/shard_map/all_to_all | solution.py:110
  79.0 7.6 %all-to-all-done = f32[16,16,128]{2,1,0:T(8,128)} async-done(((f32[16,16,128]{2,1,0:T(8,128)}), f32[16,16,128]{2,1,0:T(8,128)}, u32[]{:S(2)}, u32[]{:S(2)}) %all-to-all-start) | async-done | bytes 131104 | tf_op jit(solution)/shard_map/all_to_all | solution.py:110
  86.6 7.1 %all-to-all-start.5 = ((f32[256,1,128]{2,1,0:T(1,128)}), f32[256,1,128]{2,1,0:T(1,128)}, u32[]{:S(2)}, u32[]{:S(2)}) async-start(f32[256,1,128]{2,1,0:T(1,128)} %bitcast.135), calls=%async_computation.5 | async-start | bytes 262144 | tf_op jit(solution)/shard_map/all_to_all | solution.py:106
  100.3 3.5 %all-to-all-start.2 = ((f32[1,256,128]{2,0,1:T(1,128)}), f32[1,256,128]{2,0,1:T(1,128)S(1)}, u32[]{:S(2)}, u32[]{:S(2)}) async-start(f32[1,256,128]{2,0,1:T(1,128)} %bitcast.136), calls=%async_computation.2 | async-start | bytes 262144 | tf_op jit(solution)/shard_map/all_to_all | solution.py:112
  107.5 6.6 %all-to-all-done.2 = f32[1,256,128]{2,0,1:T(1,128)S(1)} async-done(((f32[1,256,128]{2,0,1:T(1,128)}), f32[1,256,128]{2,0,1:T(1,128)S(1)}, u32[]{:S(2)}, u32[]{:S(2)}) %all-to-all-start.2) | async-done | bytes 131104 | tf_op jit(solution)/shard_map/all_to_all | solution.py:112
  114.1 5.0 %collective-permute-start.4 = (f32[3,1,16,128]{3,2,1,0:T(8,128)S(1)}, f32[3,1,16,128]{3,2,1,0:T(8,128)S(1)}, u32[]{:S(2)}, u32[]{:S(2)}) collective-permute-start(f32[3,1,16,128]{3,2,1,0:T(8,128)S(1)} %get-tuple-element.116), channel_id=1, source_target_pairs={{0,16},{16,32},{32,48},{48,64},{64,80},{80,96},{96,112},{112,128},... | collective-permute-start | bytes 73736 | tf_op jit(solution)/shard_map/ppermute | solution.py:17
  127.9 4.7 %collective-permute-done.7 = f32[3,18,1,128]{3,2,1,0:T(1,128)S(1)} collective-permute-done((f32[3,18,1,128]{3,2,1,0:T(1,128)S(1)}, f32[3,18,1,128]{3,2,1,0:T(1,128)S(1)}, u32[]{:S(2)}, u32[]{:S(2)}) %collective-permute-start.7) | collective-permute-done | bytes 27680 | tf_op jit(solution)/shard_map/ppermute | solution.py:19
  137.0 7.0 %all-to-all-start.6 = ((f32[16,16,128]{2,0,1:T(8,128)}), f32[16,16,128]{2,0,1:T(8,128)S(1)}, u32[]{:S(2)}, u32[]{:S(2)}) async-start(f32[16,16,128]{2,0,1:T(8,128)} %copy.35), calls=%async_computation.6 | async-start | bytes 262144 | tf_op jit(solution)/shard_map/all_to_all | solution.py:104
  145.8 4.2 %all-to-all-done.6 = f32[16,16,128]{2,0,1:T(8,128)S(1)} async-done(((f32[16,16,128]{2,0,1:T(8,128)}), f32[16,16,128]{2,0,1:T(8,128)S(1)}, u32[]{:S(2)}, u32[]{:S(2)}) %all-to-all-start.6) | async-done | bytes 131104 | tf_op jit(solution)/shard_map/all_to_all | solution.py:104
  150.1 6.0 %all-to-all-start.8 = ((f32[16,16,128]{2,1,0:T(8,128)}), f32[16,16,128]{2,1,0:T(8,128)}, u32[]{:S(2)}, u32[]{:S(2)}) async-start(f32[16,16,128]{2,1,0:T(8,128)} %get-tuple-element.125), calls=%async_computation.8 | async-start | bytes 262144 | tf_op jit(solution)/shard_map/all_to_all | solution.py:110
  158.1 8.0 %all-to-all-done.8 = f32[16,16,128]{2,1,0:T(8,128)} async-done(((f32[16,16,128]{2,1,0:T(8,128)}), f32[16,16,128]{2,1,0:T(8,128)}, u32[]{:S(2)}, u32[]{:S(2)}) %all-to-all-start.8) | async-done | bytes 131104 | tf_op jit(solution)/shard_map/all_to_all | solution.py:110
  166.1 5.4 %all-to-all-start.7 = ((f32[256,1,128]{2,1,0:T(1,128)}), f32[256,1,128]{2,1,0:T(1,128)S(1)}, u32[]{:S(2)}, u32[]{:S(2)}) async-start(f32[256,1,128]{2,1,0:T(1,128)} %bitcast.40), calls=%async_computation.7 | async-start | bytes 262144 | tf_op jit(solution)/shard_map/all_to_all | solution.py:106
  177.6 3.5 %all-to-all-start.9 = ((f32[1,256,128]{2,0,1:T(1,128)}), f32[1,256,128]{2,0,1:T(1,128)S(1)}, u32[]{:S(2)}, u32[]{:S(2)}) async-start(f32[1,256,128]{2,0,1:T(1,128)} %bitcast.46), calls=%async_computation.9 | async-start | bytes 262144 | tf_op jit(solution)/shard_map/all_to_all | solution.py:112
  181.2 10.1 %all-to-all-done.9 = f32[1,256,128]{2,0,1:T(1,128)S(1)} async-done(((f32[1,256,128]{2,0,1:T(1,128)}), f32[1,256,128]{2,0,1:T(1,128)S(1)}, u32[]{:S(2)}, u32[]{:S(2)}) %all-to-all-start.9) | async-done | bytes 131104 | tf_op jit(solution)/shard_map/all_to_all | solution.py:112
  191.3 4.1 %collective-permute-start.8 = (f32[2,1,16,128]{3,2,1,0:T(8,128)S(1)}, f32[2,1,16,128]{3,2,1,0:T(8,128)S(1)}, u32[]{:S(2)}, u32[]{:S(2)}) collective-permute-start(f32[2,1,16,128]{3,2,1,0:T(8,128)S(1)} %get-tuple-element.122), channel_id=1, source_target_pairs={{0,16},{16,32},{32,48},{48,64},{64,80},{80,96},{96,112},{112,128},... | collective-permute-start | bytes 49160 | tf_op jit(solution)/shard_map/ppermute | solution.py:17
  204.9 3.9 %collective-permute-done.11 = f32[2,18,1,128]{3,2,1,0:T(1,128)S(1)} collective-permute-done((f32[2,18,1,128]{3,2,1,0:T(1,128)S(1)}, f32[2,18,1,128]{3,2,1,0:T(1,128)S(1)}, u32[]{:S(2)}, u32[]{:S(2)}) %collective-permute-start.11) | collective-permute-done | bytes 18464 | tf_op jit(solution)/shard_map/ppermute | solution.py:19
  (337 shorter events, 69.6 us)
Async XLA Ops:
  2.8 6.8 %collective-permute-start = (f32[6,1,16,128]{3,2,1,0:T(8,128)S(1)}, f32[6,1,16,128]{3,2,1,0:T(8,128)S(1)}, u32[]{:S(2)}, u32[]{:S(2)}) collective-permute-start(f32[6,1,16,128]{3,2,1,0:T(8,128)S(1)} %get-tuple-element.103), channel_id=1, source_target_pairs={{0,16},{16,32},{32,48},{48,64},{64,80},{80,96},{96,112},{112,128},... | collective-permute-start | bytes 147464 | tf_op jit(solution)/shard_map/ppermute | solution.py:17
  7.3 5.4 %collective-permute-start.1 = (f32[6,1,16,128]{3,2,1,0:T(8,128)S(1)}, f32[6,1,16,128]{3,2,1,0:T(8,128)S(1)}, u32[]{:S(2)}, u32[]{:S(2)}) collective-permute-start(f32[6,1,16,128]{3,2,1,0:T(8,128)S(1)} %get-tuple-element.104), channel_id=1, source_target_pairs={{16,0},{32,16},{48,32},{64,48},{80,64},{96,80},{112,96},{128,112},... | collective-permute-start | bytes 147464 | tf_op jit(solution)/shard_map/ppermute | solution.py:19
  12.8 6.2 %collective-permute-start.2 = (f32[6,18,1,128]{3,2,1,0:T(1,128)S(1)}, f32[6,18,1,128]{3,2,1,0:T(1,128)S(1)}, u32[]{:S(2)}, u32[]{:S(2)}) collective-permute-start(f32[6,18,1,128]{3,2,1,0:T(1,128)S(1)} %get-tuple-element.101), channel_id=1, source_target_pairs={{0,1},{1,2},{2,3},{3,4},{4,5},{5,6},{6,7},{7,8},{8,9},{9,10},{10,1... | collective-permute-start | bytes 165896 | tf_op jit(solution)/shard_map/ppermute | solution.py:17
  17.6 6.4 %collective-permute-start.3 = (f32[6,18,1,128]{3,2,1,0:T(1,128)S(1)}, f32[6,18,1,128]{3,2,1,0:T(1,128)S(1)}, u32[]{:S(2)}, u32[]{:S(2)}) collective-permute-start(f32[6,18,1,128]{3,2,1,0:T(1,128)S(1)} %get-tuple-element.102), channel_id=1, source_target_pairs={{1,0},{2,1},{3,2},{4,3},{5,4},{6,5},{7,6},{8,7},{9,8},{10,9},{11,1... | collective-permute-start | bytes 165896 | tf_op jit(solution)/shard_map/ppermute | solution.py:19
  29.3 12.1 %all-to-all-start.4 = ((f32[16,16,128]{2,0,1:T(8,128)}), f32[16,16,128]{2,0,1:T(8,128)S(1)}, u32[]{:S(2)}, u32[]{:S(2)}) async-start(f32[16,16,128]{2,0,1:T(8,128)} %copy.32), calls=%async_computation.4 | async-start | bytes 262144 | tf_op jit(solution)/shard_map/all_to_all | solution.py:130
  38.6 66.5 %copy-start.24 = (f32[16,16,128]{2,1,0:T(8,128)}, f32[16,16,128]{2,1,0:T(8,128)S(1)}, u32[]{:S(2)}) copy-start(f32[16,16,128]{2,1,0:T(8,128)S(1)} %get-tuple-element.43) | copy-start | bytes 393220
  41.3 10.0 %all-to-all-start.3 = ((f32[16,16,128]{2,0,1:T(8,128)}), f32[16,16,128]{2,0,1:T(8,128)S(1)}, u32[]{:S(2)}, u32[]{:S(2)}) async-start(f32[16,16,128]{2,0,1:T(8,128)} %copy.31), calls=%async_computation.3 | async-start | bytes 262144 | tf_op jit(solution)/shard_map/all_to_all | solution.py:104
  51.3 21.0 %all-to-all-start.1 = ((f32[16,16,128]{2,1,0:T(8,128)}), f32[16,16,128]{2,1,0:T(8,128)}, u32[]{:S(2)}, u32[]{:S(2)}) async-start(f32[16,16,128]{2,1,0:T(8,128)} %get-tuple-element.162), calls=%async_computation.1 | async-start | bytes 262144 | tf_op jit(solution)/shard_map/all_to_all | solution.py:131
  72.3 14.2 %all-to-all-start = ((f32[16,16,128]{2,1,0:T(8,128)}), f32[16,16,128]{2,1,0:T(8,128)}, u32[]{:S(2)}, u32[]{:S(2)}) async-start(f32[16,16,128]{2,1,0:T(8,128)} %get-tuple-element.40), calls=%async_computation | async-start | bytes 262144 | tf_op jit(solution)/shard_map/all_to_all | solution.py:110
  86.6 13.7 %all-to-all-start.5 = ((f32[256,1,128]{2,1,0:T(1,128)}), f32[256,1,128]{2,1,0:T(1,128)}, u32[]{:S(2)}, u32[]{:S(2)}) async-start(f32[256,1,128]{2,1,0:T(1,128)} %bitcast.135), calls=%async_computation.5 | async-start | bytes 262144 | tf_op jit(solution)/shard_map/all_to_all | solution.py:106
  100.3 13.8 %all-to-all-start.2 = ((f32[1,256,128]{2,0,1:T(1,128)}), f32[1,256,128]{2,0,1:T(1,128)S(1)}, u32[]{:S(2)}, u32[]{:S(2)}) async-start(f32[1,256,128]{2,0,1:T(1,128)} %bitcast.136), calls=%async_computation.2 | async-start | bytes 262144 | tf_op jit(solution)/shard_map/all_to_all | solution.py:112
  114.1 7.0 %collective-permute-start.4 = (f32[3,1,16,128]{3,2,1,0:T(8,128)S(1)}, f32[3,1,16,128]{3,2,1,0:T(8,128)S(1)}, u32[]{:S(2)}, u32[]{:S(2)}) collective-permute-start(f32[3,1,16,128]{3,2,1,0:T(8,128)S(1)} %get-tuple-element.116), channel_id=1, source_target_pairs={{0,16},{16,32},{32,48},{48,64},{64,80},{80,96},{96,112},{112,128},... | collective-permute-start | bytes 73736 | tf_op jit(solution)/shard_map/ppermute | solution.py:17
  119.1 5.1 %collective-permute-start.5 = (f32[3,1,16,128]{3,2,1,0:T(8,128)S(1)}, f32[3,1,16,128]{3,2,1,0:T(8,128)S(1)}, u32[]{:S(2)}, u32[]{:S(2)}) collective-permute-start(f32[3,1,16,128]{3,2,1,0:T(8,128)S(1)} %get-tuple-element.117), channel_id=1, source_target_pairs={{16,0},{32,16},{48,32},{64,48},{80,64},{96,80},{112,96},{128,112},... | collective-permute-start | bytes 73736 | tf_op jit(solution)/shard_map/ppermute | solution.py:19
  124.3 3.6 %collective-permute-start.6 = (f32[3,18,1,128]{3,2,1,0:T(1,128)S(1)}, f32[3,18,1,128]{3,2,1,0:T(1,128)S(1)}, u32[]{:S(2)}, u32[]{:S(2)}) collective-permute-start(f32[3,18,1,128]{3,2,1,0:T(1,128)S(1)} %get-tuple-element.114), channel_id=1, source_target_pairs={{0,1},{1,2},{2,3},{3,4},{4,5},{5,6},{6,7},{7,8},{8,9},{9,10},{10,1... | collective-permute-start | bytes 82952 | tf_op jit(solution)/shard_map/ppermute | solution.py:17
  126.5 6.1 %collective-permute-start.7 = (f32[3,18,1,128]{3,2,1,0:T(1,128)S(1)}, f32[3,18,1,128]{3,2,1,0:T(1,128)S(1)}, u32[]{:S(2)}, u32[]{:S(2)}) collective-permute-start(f32[3,18,1,128]{3,2,1,0:T(1,128)S(1)} %get-tuple-element.115), channel_id=1, source_target_pairs={{1,0},{2,1},{3,2},{4,3},{5,4},{6,5},{7,6},{8,7},{9,8},{10,9},{11,1... | collective-permute-start | bytes 82952 | tf_op jit(solution)/shard_map/ppermute | solution.py:19
  137.0 13.0 %all-to-all-start.6 = ((f32[16,16,128]{2,0,1:T(8,128)}), f32[16,16,128]{2,0,1:T(8,128)S(1)}, u32[]{:S(2)}, u32[]{:S(2)}) async-start(f32[16,16,128]{2,0,1:T(8,128)} %copy.35), calls=%async_computation.6 | async-start | bytes 262144 | tf_op jit(solution)/shard_map/all_to_all | solution.py:104
  150.1 16.0 %all-to-all-start.8 = ((f32[16,16,128]{2,1,0:T(8,128)}), f32[16,16,128]{2,1,0:T(8,128)}, u32[]{:S(2)}, u32[]{:S(2)}) async-start(f32[16,16,128]{2,1,0:T(8,128)} %get-tuple-element.125), calls=%async_computation.8 | async-start | bytes 262144 | tf_op jit(solution)/shard_map/all_to_all | solution.py:110
  166.1 11.5 %all-to-all-start.7 = ((f32[256,1,128]{2,1,0:T(1,128)}), f32[256,1,128]{2,1,0:T(1,128)S(1)}, u32[]{:S(2)}, u32[]{:S(2)}) async-start(f32[256,1,128]{2,1,0:T(1,128)} %bitcast.40), calls=%async_computation.7 | async-start | bytes 262144 | tf_op jit(solution)/shard_map/all_to_all | solution.py:106
  173.0 31.2 %copy-start.82 = (f32[16,16,128]{2,1,0:T(8,128)S(1)}, f32[16,16,128]{2,1,0:T(8,128)}, u32[]{:S(2)}) copy-start(f32[16,16,128]{2,1,0:T(8,128)} %copy-done.81) | copy-start | bytes 393220
  177.6 13.7 %all-to-all-start.9 = ((f32[1,256,128]{2,0,1:T(1,128)}), f32[1,256,128]{2,0,1:T(1,128)S(1)}, u32[]{:S(2)}, u32[]{:S(2)}) async-start(f32[1,256,128]{2,0,1:T(1,128)} %bitcast.46), calls=%async_computation.9 | async-start | bytes 262144 | tf_op jit(solution)/shard_map/all_to_all | solution.py:112
  191.3 6.1 %collective-permute-start.8 = (f32[2,1,16,128]{3,2,1,0:T(8,128)S(1)}, f32[2,1,16,128]{3,2,1,0:T(8,128)S(1)}, u32[]{:S(2)}, u32[]{:S(2)}) collective-permute-start(f32[2,1,16,128]{3,2,1,0:T(8,128)S(1)} %get-tuple-element.122), channel_id=1, source_target_pairs={{0,16},{16,32},{32,48},{48,64},{64,80},{80,96},{96,112},{112,128},... | collective-permute-start | bytes 49160 | tf_op jit(solution)/shard_map/ppermute | solution.py:17
  195.4 5.2 %collective-permute-start.9 = (f32[2,1,16,128]{3,2,1,0:T(8,128)S(1)}, f32[2,1,16,128]{3,2,1,0:T(8,128)S(1)}, u32[]{:S(2)}, u32[]{:S(2)}) collective-permute-start(f32[2,1,16,128]{3,2,1,0:T(8,128)S(1)} %get-tuple-element.123), channel_id=1, source_target_pairs={{16,0},{32,16},{48,32},{64,48},{80,64},{96,80},{112,96},{128,112},... | collective-permute-start | bytes 49160 | tf_op jit(solution)/shard_map/ppermute | solution.py:19
  200.6 4.3 %collective-permute-start.10 = (f32[2,18,1,128]{3,2,1,0:T(1,128)S(1)}, f32[2,18,1,128]{3,2,1,0:T(1,128)S(1)}, u32[]{:S(2)}, u32[]{:S(2)}) collective-permute-start(f32[2,18,1,128]{3,2,1,0:T(1,128)S(1)} %get-tuple-element.120), channel_id=1, source_target_pairs={{0,1},{1,2},{2,3},{3,4},{4,5},{5,6},{6,7},{7,8},{8,9},{9,10},{10,1... | collective-permute-start | bytes 55304 | tf_op jit(solution)/shard_map/ppermute | solution.py:17
  202.8 6.0 %collective-permute-start.11 = (f32[2,18,1,128]{3,2,1,0:T(1,128)S(1)}, f32[2,18,1,128]{3,2,1,0:T(1,128)S(1)}, u32[]{:S(2)}, u32[]{:S(2)}) collective-permute-start(f32[2,18,1,128]{3,2,1,0:T(1,128)S(1)} %get-tuple-element.121), channel_id=1, source_target_pairs={{1,0},{2,1},{3,2},{4,3},{5,4},{6,5},{7,6},{8,7},{9,8},{10,9},{11,1... | collective-permute-start | bytes 55304 | tf_op jit(solution)/shard_map/ppermute | solution.py:19
  (91 other events, 470.8 us)
where the time goes:
time: 214 us; the launch traced here: 210 us
  starting transfers between devices  90 us (42%)
  waiting for transfers between devices  76.4 us (36%)
  other arithmetic  26.1 us (12%)
  local copies, waits for them, and re-layouts  15 us (7%)
  between operations  2.35 us (1%)
    ppermute x6, waiting for transfers between devices, padded_2(): lax.ppermute(head, axis, [((i + 1) % count, i) for i in range(ends)])  23.1 us
    ppermute x6, starting transfers between devices, padded_2(): lax.ppermute(tail, axis, [(i, (i + 1) % count) for i in range(ends)])  22.8 us
    all_to_all x2, waiting for transfers between devices, y_lines_moved(): return lax.all_to_all(solved, 'py', split_axis=1, concat_axis=0, tiled=True)  16.8 us
    all_to_all x2, waiting for transfers between devices, y_lines_moved(): lax.all_to_all(source, 'py', split_axis=0, concat_axis=1, tiled=True)  15.6 us
    all_to_all x2, starting transfers between devices, x_lines_moved(): return lax.all_to_all(solved, 'px', split_axis=0, concat_axis=1, tiled=True)  12.5 us
    all_to_all x1, starting transfers between devices, local(): lax.all_to_all(line_rate, 'py', split_axis=0, concat_axis=1, tiled=True)  11 us
    all_to_all x2, starting transfers between devices, x_lines_moved(): lax.all_to_all(source, 'px', split_axis=1, concat_axis=0, tiled=True)  10.9 us
    all_to_all x2, starting transfers between devices, y_lines_moved(): lax.all_to_all(source, 'py', split_axis=0, concat_axis=1, tiled=True)  10.1 us
  transfers between devices with their start and end apart: 22, of which 15 were waited for; matrix products, arithmetic and copies ran while one was open for 10% of the time, Pallas kernels for 0%

commit v1 on v0

v1 whole, which is shorter than its diff:
```python
import functools

import jax
import jax.numpy as jnp
from jax import lax
from jax.experimental import pallas as pl
from jax.experimental.pallas import tpu as pltpu
from jax.sharding import PartitionSpec as P

h = 32.0
B = 16
F32 = jnp.float32


def plane(i):
    return pl.ds(i * B, B)


def strided(j):
    return pl.ds(j, B, stride=B)


def lanes(v):
    return lax.broadcasted_iota(jnp.int32, v.shape, 1)


def behind_z(v):
    return v - jnp.where(lanes(v) == 0, 0.0, pltpu.roll(v, 1, 1))


def ahead_z(v):
    n = v.shape[1]
    return jnp.where(lanes(v) == n - 1, 0.0, pltpu.roll(v, n - 1, 1)) - v


def factor(w_of, first_block, p, u, v):
    d = None
    y = []
    for j in range(B):
        w = w_of(j)
        e = w + (jnp.where(first_block, 0.0, 1.0) if j == 0 else d)
        inv = 1.0 / (1.0 + e)
        d = e * inv
        p[plane(j)] = inv
        y.append(jnp.ones_like(inv) if j == 0 else y[-1] * last)
        last = inv
    uj = y[B - 1] * last
    vj = last
    u[plane(B - 1)] = uj
    v[plane(B - 1)] = vj
    for j in range(B - 2, -1, -1):
        inv = p[plane(j)]
        uj = inv * (y[j] + uj)
        vj = inv * vj
        u[plane(j)] = uj
        v[plane(j)] = vj


def eliminate(source_of, p, g):
    y = source_of(0)
    ys = [y]
    for j in range(1, B):
        y = source_of(j) + p[plane(j - 1)] * y
        ys.append(y)
    x = y * p[plane(B - 1)]
    end = x
    g[plane(B - 1)] = x
    for j in range(B - 2, -1, -1):
        x = p[plane(j)] * (ys[j] + x)
        g[plane(j)] = x
    return x, end


def boundary(me, n, rows_of, coef_of):
    zero = jnp.zeros_like(coef_of(0)[0])
    alpha, beta, gamma, delta = zero, zero, zero, zero
    for s in range(n - 1):
        gf, dl = rows_of(s)
        ff, fl, ll = coef_of(s)
        t = fl / (1.0 - ff * beta)
        on = s < me
        alpha, beta = (
            jnp.where(on, dl + t * (alpha + beta * gf), alpha),
            jnp.where(on, ll + t * beta * fl, beta),
        )
        m = n - 1 - s
        gf, dl = rows_of(m)
        ff, fl, ll = coef_of(m)
        t = fl / (1.0 - ll * delta)
        on = m > me
        gamma, delta = (
            jnp.where(on, gf + t * (gamma + delta * dl), gamma),
            jnp.where(on, ff + t * delta * fl, delta),
        )
    gf, dl = rows_of(me)
    ff, fl, ll = coef_of(me)
    t = fl / (1.0 - ll * delta)
    gamma_here = gf + t * (gamma + delta * dl)
    delta_here = ff + t * delta * fl
    before = (alpha + beta * gamma_here) / (1.0 - beta * delta_here)
    after = (gamma + delta * (dl + fl * before)) / (1.0 - delta * ll)
    return before, after


def solve_z(r, w):
    n = r.shape[1]
    lane = lanes(r)
    e = jnp.where(lane == n - 1, 0.0, 1.0)
    l = jnp.where(lane == 0, 0.0, 1.0)
    s = w + jnp.where(lane == n - 1, 1.0, 0.0)
    step = 1
    while step < n:
        inv = 1.0 / (s + (l + e))
        kl = l * pltpu.roll(inv, step, 1)
        kr = e * pltpu.roll(inv, n - step, 1)
        r = r + (kl * pltpu.roll(r, step, 1) + kr * pltpu.roll(r, n - step, 1))
        s = s + (kl * pltpu.roll(s, step, 1) + kr * pltpu.roll(s, n - step, 1))
        l = kl * pltpu.roll(l, step, 1)
        e = kr * pltpu.roll(e, n - step, 1)
        step *= 2
    return r / s


def tables_kernel(me, eps, sig, material, w, c, p, u, v):
    ws = [eps[m] * (1.0 / (h * h)) + sig[m] * (0.5 / h) for m in range(eps.shape[0])]
    cs = [eps[m] * (1.0 / (h * h)) - sig[m] * (0.5 / h) for m in range(eps.shape[0])]
    for i in range(B):
        ids = material[plane(i)]
        wi = jnp.full(ids.shape, ws[0], F32)
        ci = jnp.full(ids.shape, cs[0], F32)
        for m in range(1, len(ws)):
            wi = jnp.where(ids == m, ws[m], wi)
            ci = jnp.where(ids == m, cs[m], ci)
        w[plane(i)] = wi
        c[plane(i)] = ci
    factor(lambda j: w[strided(j)], me[1] == 0, p, u, v)


def first_y_kernel(n, elec, magn, ey_next, c, p, u, v, flux, g, msg):
    for i in range(B):
        ahead = elec[1, plane(i + 1)] if i < B - 1 else ey_next[...]
        flux[plane(i)] = magn[2, plane(i)] * (1.0 / h) - (ahead - elec[1, plane(i)])

    def source(j):
        f = flux[strided(j)]
        if j > 0:
            f = f - flux[strided(j - 1)]
        own = c[strided(j)] * elec.at[0][strided(j)]
        return own + (f - behind_z(magn.at[1][strided(j)]) * (1.0 / h))

    first, last = eliminate(source, p, g)
    last = last - flux[strided(B - 1)]
    for m in range(n):
        msg[m, plane(0)] = first
        msg[m, plane(1)] = last
        msg[m, plane(2)] = u[plane(0)]
        msg[m, plane(3)] = v[plane(0)]
        msg[m, plane(4)] = v[plane(B - 1)]


def first_x_kernel(me, elec, magn, hx_prev, w, c, p, u, v, flux, g, ends):
    factor(lambda i: w[plane(i)], me[0] == 0, p, u, v)
    row = lax.broadcasted_iota(jnp.int32, (B, w.shape[1]), 0)

    def source(i):
        q = magn[1, plane(i)] * (1.0 / h) - ahead_z(elec[0, plane(i)])
        flux[plane(i)] = q
        if i > 0:
            q = q - flux[plane(i - 1)]
        hx = magn[0, plane(i)]
        before = jnp.where(row == 0, hx_prev[pl.ds(i, 1)], pltpu.roll(hx, 1, 0))
        return c[plane(i)] * elec[2, plane(i)] + (q - (hx - before) * (1.0 / h))

    first, last = eliminate(source, p, g)
    ends[plane(0)] = first
    ends[plane(1)] = last - flux[plane(B - 1)]


def first_z_kernel(elec, magn, ez_next, hz_prev, w, c, fy, curl, flux):
    row = lax.broadcasted_iota(jnp.int32, (B, w.shape[1]), 0)
    for i in range(B):
        ez = elec[2, plane(i)]
        after = jnp.where(row == B - 1, ez_next[pl.ds(i, 1)], pltpu.roll(ez, B - 1, 0))
        r = magn[0, plane(i)] * (1.0 / h) - (after - ez)
        hz = magn[2, plane(i)]
        before = magn[2, plane(i - 1)] if i > 0 else hz_prev[...]
        ci = c[plane(i)]
        v = solve_z(ci * elec[1, plane(i)] + (behind_z(r) - (hz - before) * (1.0 / h)), w[plane(i)])
        rise = ahead_z(v)
        mx = r + rise
        fy[plane(i)] = v
        curl[plane(i)] = ci * v + behind_z(mx)
        flux[plane(i)] = -(mx + rise)


def second_x_kernel(n, me, got, g, u, v, flux, c, curl, p_x, u_x, v_x, ends, part, flux2, g2, msg, fx):
    my = me[1]
    before, after = boundary(
        my,
        n[1],
        lambda m: (got[m, plane(0)], got[m, plane(1)]),
        lambda m: (got[m, plane(2)], got[m, plane(3)], got[m, plane(4)]),
    )
    for j in range(B):
        fx[plane(j)] = g[plane(j)] + (u[plane(j)] * before + v[plane(j)] * after)
    mz_before = jnp.where(my == 0, 0.0, fx[plane(0)] - before)
    for j in range(B):
        here = fx[plane(j)]
        rise = (fx[plane(j + 1)] if j < B - 1 else after) - here
        mz = flux[strided(j)] + rise
        part[strided(j)] = c[strided(j)] * here + (mz - mz_before)
        flux2[strided(j)] = -(mz + rise)
        mz_before = mz

    def source(i):
        f = flux2[plane(i)]
        if i > 0:
            f = f - flux2[plane(i - 1)]
        return curl[plane(i)] + f

    first, last = eliminate(source, p_x, g2)
    last = last - flux2[plane(B - 1)]
    for m in range(n[0]):
        msg[m, plane(0)] = first
        msg[m, plane(1)] = last
        msg[m, plane(2)] = ends[plane(0)]
        msg[m, plane(3)] = ends[plane(1)]
        msg[m, plane(4)] = u_x[plane(0)]
        msg[m, plane(5)] = v_x[plane(0)]
        msg[m, plane(6)] = v_x[plane(B - 1)]


def second_y_kernel(
    n, me, got, g, g2, u, v, flux, flux2, c, flux_y, p_y, full_y, new_z, rise_y, part, g3, msg, fz
):
    mx = me[0]
    coef = lambda m: (got[m, plane(4)], got[m, plane(5)], got[m, plane(6)])
    before, after = boundary(mx, n[0], lambda m: (got[m, plane(0)], got[m, plane(1)]), coef)
    for i in range(B):
        full_y[plane(i)] = g2[plane(i)] + (u[plane(i)] * before + v[plane(i)] * after)
    for i in range(B):
        rise = (full_y[plane(i + 1)] if i < B - 1 else after) - full_y[plane(i)]
        new_z[plane(i)] = -h * (flux2[plane(i)] + rise)
    before, after = boundary(mx, n[0], lambda m: (got[m, plane(2)], got[m, plane(3)]), coef)
    for i in range(B):
        fz[plane(i)] = g[plane(i)] + (u[plane(i)] * before + v[plane(i)] * after)
    my_before = jnp.where(mx == 0, 0.0, fz[plane(0)] - before)
    for i in range(B):
        here = fz[plane(i)]
        rise = (fz[plane(i + 1)] if i < B - 1 else after) - here
        my = flux[plane(i)] + rise
        rise_y[plane(i)] = my + rise
        part[plane(i)] = c[plane(i)] * here + (my - my_before)
        my_before = my

    def source(j):
        f = flux_y[strided(j)]
        if j > 0:
            f = f - flux_y[strided(j - 1)]
        return part[strided(j)] + f

    first, last = eliminate(source, p_y, g3)
    last = last - flux_y[strided(B - 1)]
    for m in range(n[1]):
        msg[m, plane(0)] = first
        msg[m, plane(1)] = last


def second_z_kernel(part, rise_y, w, full_x, new_y):
    for i in range(B):
        a = rise_y[plane(i)]
        v = solve_z(part[plane(i)] - behind_z(a), w[plane(i)])
        full_x[plane(i)] = v
        new_y[plane(i)] = h * (a - ahead_z(v))


def last_kernel(n, me, coefs, got, g, u, v, flux_y, full_x, full_y, new_y, new_z, elec, magn):
    before, after = boundary(
        me[1],
        n[1],
        lambda m: (got[m, plane(0)], got[m, plane(1)]),
        lambda m: (coefs[m, plane(2)], coefs[m, plane(3)], coefs[m, plane(4)]),
    )
    elec[0] = full_x[...]
    elec[1] = full_y[...]
    magn[1] = new_y[...]
    magn[2] = new_z[...]
    ez, hx = elec.at[2], magn.at[0]
    here = None
    for j in range(B):
        ahead = g[plane(j)] + (u[plane(j)] * before + v[plane(j)] * after)
        ez[strided(j)] = ahead
        if j > 0:
            hx[strided(j - 1)] = -h * (flux_y[strided(j - 1)] + (ahead - here))
        here = ahead
    hx[strided(B - 1)] = -h * (flux_y[strided(B - 1)] + (after - here))


VMEM = pl.BlockSpec(memory_space=pltpu.VMEM)
SMEM = pl.BlockSpec(memory_space=pltpu.SMEM)


def call(kernel, ins, outs, scalars=0, scratch=(), flops=2_000_000):
    shapes = [jax.ShapeDtypeStruct(s, F32) for s in outs]
    size = sum(4 * x.size for x in ins) + sum(4 * s.size for s in shapes)
    return pl.pallas_call(
        kernel,
        out_shape=shapes,
        in_specs=[SMEM] * scalars + [VMEM] * (len(ins) - scalars),
        out_specs=[VMEM] * len(outs),
        scratch_shapes=[pltpu.VMEM(s, F32) for s in scratch],
        compiler_params=pltpu.CompilerParams(vmem_limit_bytes=40 * 1024 * 1024),
        cost_estimate=pl.CostEstimate(flops=flops, bytes_accessed=size, transcendentals=0),
    )(*ins)


def local(electric, magnetic, material, permittivity, conductivity):
    nx, ny = lax.axis_size("px"), lax.axis_size("py")
    nz = material.shape[2]
    cells, edge = (B * B, nz), (B, nz)
    me = jnp.stack([lax.axis_index("px"), lax.axis_index("py")]).astype(jnp.int32)
    elec = electric.reshape(3, *cells)
    magn = magnetic.reshape(3, *cells)
    ids = material.reshape(cells)

    down = lambda n: [(i + 1, i) for i in range(n - 1)]
    up = lambda n: [(i, i + 1) for i in range(n - 1)]
    ey_next = lax.ppermute(electric[1, 0], "px", down(nx))
    hx_prev = lax.ppermute(magnetic[0, :, B - 1], "py", up(ny))
    ez_next = lax.ppermute(electric[2, :, 0], "py", down(ny))
    hz_prev = lax.ppermute(magnetic[2, B - 1], "px", up(nx))

    w, c, p_y, u_y, v_y = call(
        tables_kernel, [me, permittivity, conductivity, ids], [cells] * 5, scalars=3
    )
    flux_a, g_a, msg = call(
        functools.partial(first_y_kernel, ny),
        [elec, magn, ey_next, c, p_y, u_y, v_y],
        [cells, cells, (ny, 5 * B, nz)],
    )
    got_y = lax.all_to_all(msg, "py", 0, 0, tiled=True)
    p_x, u_x, v_x, flux_b, g_b, ends_b = call(
        first_x_kernel, [me, elec, magn, hx_prev, w, c], [cells] * 5 + [(2 * B, nz)], scalars=1
    )
    fy, curl, flux_y = call(
        first_z_kernel, [elec, magn, ez_next, hz_prev, w, c], [cells] * 3, flops=8_000_000
    )
    part_x, flux2, g_a2, msg = call(
        functools.partial(second_x_kernel, (nx, ny)),
        [me, got_y, g_a, u_y, v_y, flux_a, c, curl, p_x, u_x, v_x, ends_b],
        [cells] * 3 + [(nx, 7 * B, nz)],
        scalars=1,
        scratch=[cells],
    )
    got_x = lax.all_to_all(msg, "px", 0, 0, tiled=True)
    full_y, new_z, rise_y, part_z, g_b2, msg = call(
        functools.partial(second_y_kernel, (nx, ny)),
        [me, got_x, g_b, g_a2, u_x, v_x, flux_b, flux2, c, flux_y, p_y],
        [cells] * 5 + [(ny, 2 * B, nz)],
        scalars=1,
        scratch=[cells],
    )
    got = lax.all_to_all(msg, "py", 0, 0, tiled=True)
    full_x, new_y = call(second_z_kernel, [part_x, rise_y, w], [cells] * 2, flops=8_000_000)
    out = call(
        functools.partial(last_kernel, (nx, ny)),
        [me, got_y, got, g_b2, u_y, v_y, flux_y, full_x, full_y, new_y, new_z],
        [(3, *cells)] * 2,
        scalars=1,
    )
    return tuple(a.reshape(3, B, B, nz) for a in out)


def solution(mesh):
    placed = (P(None, "px", "py", None), P(None, "px", "py", None), P("px", "py", None), P(), P())
    return jax.shard_map(
        local,
        mesh=mesh,
        in_specs=placed,
        out_specs=(P(None, "px", "py", None), P(None, "px", "py", None)),
        check_vma=False,
    )
```

time: 214 us -> 91.8 us (0.43); the launches traced: 210 us -> 90.2 us
  waiting for transfers between devices: 76.4 us -> 9.11 us
  starting transfers between devices: 90 us -> 34.7 us
  other arithmetic: 26.1 us -> 0.08 us
  Pallas kernels: 0 us -> 22.7 us
  blocking collectives: 0 us -> 18.5 us
  local copies, waits for them, and re-layouts: 15 us -> 4.29 us
    all_to_all x10 -> x2, waiting for transfers between devices: 53.3 us -> 4.17 us  [the longest x1 4.17 us: local(): got = lax.all_to_all(msg, 'py', 0, 0, tiled=True)]
    all_to_all x10 -> x2, starting transfers between devices: 57.5 us -> 19.6 us  [the longest x1 10.3 us: local(): got = lax.all_to_all(msg, 'py', 0, 0, tiled=True)]
    pallas_call x0 -> x8, Pallas kernels: none -> 22.7 us  [call(): pl.pallas_call(kernel, out_shape=shapes, in_specs=[SMEM] * scalars + [VME...]
    all_to_all x0 -> x1, blocking collectives: none -> 18.5 us  [local(): got_x = lax.all_to_all(msg, 'px', 0, 0, tiled=True)]
    ppermute x12 -> x4, waiting for transfers between devices: 23.1 us -> 4.94 us  [the longest x1 4.93 us: local(): ez_next = lax.ppermute(electric[2, :, 0], 'py', down(ny))]
    ppermute x12 -> x4, starting transfers between devices: 32.6 us -> 15.1 us  [the longest x1 5.14 us: local(): ey_next = lax.ppermute(electric[1, 0], 'px', down(nx))]
    mul x41 -> x0, other arithmetic: 8.63 us -> none  [the longest x20 4.69 us: reduce_lines(): lower_band = -from_before(lower_band, stride, direction, 0.0) * left_ratio]
    sub x45 -> x0, other arithmetic: 6.68 us -> none  [the longest x20 3.12 us: reduce_lines(): middle - from_before(upper_band, stride, direction, 0.0) * left_ratio]
  transfers between devices with their start and end apart: 22 -> 6, of which waited for: 15 -> 2; matrix products, arithmetic and copies ran while one was open for 10% -> 0% of each run, Pallas kernels for 0% -> 19%
where the time goes in v1:
time: 91.8 us; the launch traced here: 90.2 us
  starting transfers between devices  34.7 us (38%)
  Pallas kernels  22.7 us (25%)
  blocking collectives  18.5 us (20%)
  waiting for transfers between devices  9.11 us (10%)
  local copies, waits for them, and re-layouts  4.29 us (5%)
    pallas_call x8, Pallas kernels, call(): pl.pallas_call(kernel, out_shape=shapes, in_specs=[SMEM] * scalars + [VME...  22.7 us
    all_to_all x1, blocking collectives, local(): got_x = lax.all_to_all(msg, 'px', 0, 0, tiled=True)  18.5 us
    all_to_all x1, starting transfers between devices, local(): got = lax.all_to_all(msg, 'py', 0, 0, tiled=True)  10.3 us
    all_to_all x1, starting transfers between devices, local(): got_y = lax.all_to_all(msg, 'py', 0, 0, tiled=True)  9.32 us
    ppermute x1, starting transfers between devices, local(): ey_next = lax.ppermute(electric[1, 0], 'px', down(nx))  5.14 us
    ppermute x1, waiting for transfers between devices, local(): ez_next = lax.ppermute(electric[2, :, 0], 'py', down(ny))  4.93 us
    ppermute x1, starting transfers between devices, local(): hx_prev = lax.ppermute(magnetic[0, :, B - 1], 'py', up(ny))  4.77 us
    all_to_all x1, waiting for transfers between devices, local(): got = lax.all_to_all(msg, 'py', 0, 0, tiled=True)  4.17 us
  transfers between devices with their start and end apart: 6, of which 2 were waited for; matrix products, arithmetic and copies ran while one was open for 0% of the time, Pallas kernels for 19%

profile of v1, /device:TPU:1, one launch (start us, length us, event | category | flops | bytes accessed | tf_op | source)
XLA Modules:
  0.0 90.2 jit_solution(7501641385458220774)
XLA Ops:
  0.6 0.7 slice_bitcast_fusion.1
  1.3 5.1 %collective-permute-start = (f32[16,128]{1,0:T(8,128)S(1)}, f32[16,128]{1,0:T(8,128)S(1)}, u32[]{:S(2)}, u32[]{:S(2)}) collective-permute-start(f32[16,128]{1,0:T(8,128)S(1)} %slice_bitcast_fusion.1), channel_id=1, source_target_pairs={{16,0},{32,16},{48,32},{64,48},{80,64},{96,80},{112,96},{128,112},... | collective-permute-start | bytes 24584 | tf_op jit(solution)/shard_map/ppermute | solution.py:328
  6.5 0.1 pad_add_fusion.me
  6.6 0.7 copy-done.5
  7.2 0.0 copy-done.6
  7.2 0.9 %copy-done.4 = s32[16,16,128]{2,1,0:T(8,128)S(1)} copy-done((s32[16,16,128]{2,1,0:T(8,128)S(1)}, s32[16,16,128]{2,1,0:T(8,128)}, u32[]{:S(2)}) %copy-start.4) | copy-done | bytes 131096
  8.1 0.8 shard_map.68
  9.0 1.0 %copy-done = f32[3,16,16,128]{3,2,1,0:T(8,128)S(1)} copy-done((f32[3,16,16,128]{3,2,1,0:T(8,128)S(1)}, f32[3,16,16,128]{3,2,1,0:T(8,128)}, u32[]{:S(2)}) %copy-start) | copy-done | bytes 393240
  10.0 1.0 %copy-done.2 = f32[3,16,16,128]{3,2,1,0:T(8,128)S(1)} copy-done((f32[3,16,16,128]{3,2,1,0:T(8,128)S(1)}, f32[3,16,16,128]{3,2,1,0:T(8,128)}, u32[]{:S(2)}) %copy-start.2) | copy-done | bytes 393240
  11.0 1.1 %shard_map.69 = (f32[256,128]{1,0:T(8,128)S(1)}, f32[256,128]{1,0:T(8,128)S(1)}, f32[16,80,128]{2,1,0:T(8,128)}) custom-call(f32[3,256,128]{2,1,0:T(8,128)S(1)} %bitcast.17, f32[3,256,128]{2,1,0:T(8,128)S(1)} %bitcast.20, f32[16,128]{1,0:T(8,128)S(1)} %collective-permute-done.ey_next, f32[256,128]{1,0:T(8,128)S(1)} %get-tuple-element.31.c, ...), custom_call_target="tpu_custom_call" | custom-call | flops 2000000 | bytes 2236416 | tf_op jit(solution)/shard_map/pallas_call | solution.py:306
  12.1 9.3 %all-to-all-start = ((f32[16,80,128]{2,1,0:T(8,128)}), f32[16,80,128]{2,1,0:T(8,128)S(1)}, u32[]{:S(2)}, u32[]{:S(2)}) async-start(f32[16,80,128]{2,1,0:T(8,128)} %get-tuple-element.35), calls=%async_computation | async-start | bytes 1310720 | tf_op jit(solution)/shard_map/all_to_all | solution.py:341
  21.4 4.8 %collective-permute-start.3 = (f32[16,128]{1,0:T(8,128)S(1)}, f32[16,128]{1,0:T(8,128)S(1)}, u32[]{:S(2)}, u32[]{:S(2)}) collective-permute-start(f32[16,128]{1,0:T(8,128)S(1)} %bitcast.25), channel_id=1, source_target_pairs={{0,1},{1,2},{2,3},{3,4},{4,5},{5,6},{6,7},{7,8},{8,9},{9,10},{10,1... | collective-permute-start | bytes 24584 | tf_op jit(solution)/shard_map/ppermute | solution.py:329
  26.2 3.9 %collective-permute-start.2 = (f32[16,128]{1,0:T(8,128)S(1)}, f32[16,128]{1,0:T(8,128)S(1)}, u32[]{:S(2)}, u32[]{:S(2)}) collective-permute-start(f32[16,128]{1,0:T(8,128)S(1)} %slice_bitcast_fusion), channel_id=1, source_target_pairs={{0,16},{16,32},{32,48},{48,64},{64,80},{80,96},{96,112},{112,128},... | collective-permute-start | bytes 24584 | tf_op jit(solution)/shard_map/ppermute | solution.py:331
  30.1 1.3 %collective-permute-start.1 = (f32[16,128]{1,0:T(8,128)S(1)}, f32[16,128]{1,0:T(8,128)S(1)}, u32[]{:S(2)}, u32[]{:S(2)}) collective-permute-start(f32[16,128]{1,0:T(8,128)S(1)} %bitcast.24), channel_id=1, source_target_pairs={{1,0},{2,1},{3,2},{4,3},{5,4},{6,5},{7,6},{8,7},{9,8},{10,9},{11,1... | collective-permute-start | bytes 24584 | tf_op jit(solution)/shard_map/ppermute | solution.py:330
  31.4 0.7 shard_map.71
  32.2 4.9 %collective-permute-done.1.ez_next = f32[16,128]{1,0:T(8,128)S(1)} collective-permute-done((f32[16,128]{1,0:T(8,128)S(1)}, f32[16,128]{1,0:T(8,128)S(1)}, u32[]{:S(2)}, u32[]{:S(2)}) %collective-permute-start.1) | collective-permute-done | bytes 8224 | tf_op jit(solution)/shard_map/ppermute | solution.py:330
  37.1 8.2 %shard_map.70 = (f32[256,128]{1,0:T(8,128)}, f32[256,128]{1,0:T(8,128)S(1)}, f32[256,128]{1,0:T(8,128)S(1)}) custom-call(f32[3,256,128]{2,1,0:T(8,128)S(1)} %bitcast.19, f32[3,256,128]{2,1,0:T(8,128)S(1)} %bitcast.22, f32[16,128]{1,0:T(8,128)S(1)} %collective-permute-done.1.ez_next, f32[16,128]{1,0:T(8,128)S(1)} %collective-permute-done.2.hz_prev, ...), custom_call_target="tpu_custom_call" | custom-call | flops 8000000 | bytes 1458176 | tf_op jit(solution)/shard_map/pallas_call | solution.py:306
  45.3 1.0 %shard_map.72 = (f32[256,128]{1,0:T(8,128)S(1)}, f32[256,128]{1,0:T(8,128)S(1)}, f32[256,128]{1,0:T(8,128)S(1)}, f32[16,112,128]{2,1,0:T(8,128)S(1)}) custom-call(s32[2]{0:T(128)S(1)} %pad_add_fusion.me, f32[16,80,128]{2,1,0:T(8,128)S(1)} %all-to-all-done.got.coefs, f32[256,128]{1,0:T(8,128)S(1)} %get-tuple-element.36.g, ...), custom_call_target="tpu_custom_call" | custom-call | flops 2000000 | bytes 3162120 | tf_op jit(solution)/shard_map/pallas_call | solution.py:306
  46.4 18.5 %all_to_all.15.got = f32[16,112,128]{2,1,0:T(8,128)S(1)} all-to-all(f32[16,112,128]{2,1,0:T(8,128)S(1)} %get-tuple-element.44), channel_id=1, replica_groups=mesh['px'=16,'py'=16] {'px'}, dimensions={0} | all-to-all | bytes 1835008 | tf_op jit(solution)/shard_map/all_to_all | solution.py:355
  64.9 1.8 %shard_map.73 = (f32[256,128]{1,0:T(8,128)S(1)}, f32[256,128]{1,0:T(8,128)S(1)}, f32[256,128]{1,0:T(8,128)S(1)}, f32[256,128]{1,0:T(8,128)}, f32[256,128]{1,0:T(8,128)S(1)}, /*index=5*/f32[16,32,128]{2,1,0:T(8,128)}) custom-call(s32[2]{0:T(128)S(1)} %pad_add_fusion.me, f32[16,112,128]{2,1,0:T(8,128)S(1)} %all_to_all.15.got, ...), custom_call_target="tpu_custom_call" | custom-call | flops 2000000 | bytes 3014664 | tf_op jit(solution)/shard_map/pallas_call | solution.py:306
  66.6 10.3 %all-to-all-start.2 = ((f32[16,32,128]{2,1,0:T(8,128)}), f32[16,32,128]{2,1,0:T(8,128)S(1)}, u32[]{:S(2)}, u32[]{:S(2)}) async-start(f32[16,32,128]{2,1,0:T(8,128)} %get-tuple-element.50), calls=%async_computation.2 | async-start | bytes 524288 | tf_op jit(solution)/shard_map/all_to_all | solution.py:363
  77.0 7.3 %shard_map.74 = (f32[256,128]{1,0:T(8,128)S(1)}, f32[256,128]{1,0:T(8,128)S(1)}) custom-call(f32[256,128]{1,0:T(8,128)S(1)} %get-tuple-element.52.part, f32[256,128]{1,0:T(8,128)S(1)} %get-tuple-element.53.rise_y, f32[256,128]{1,0:T(8,128)S(1)} %get-tuple-element.38.w), custom_call_target="tpu_custom_call" | custom-call | flops 8000000 | bytes 655360 | tf_op jit(solution)/shard_map/pallas_call | solution.py:306
  84.3 4.2 %all-to-all-done.2.got = f32[16,32,128]{2,1,0:T(8,128)S(1)} async-done(((f32[16,32,128]{2,1,0:T(8,128)}), f32[16,32,128]{2,1,0:T(8,128)S(1)}, u32[]{:S(2)}, u32[]{:S(2)}) %all-to-all-start.2) | async-done | bytes 262176 | tf_op jit(solution)/shard_map/all_to_all | solution.py:363
  88.4 1.8 %shard_map.75 = (f32[3,256,128]{2,1,0:T(8,128)}, f32[3,256,128]{2,1,0:T(8,128)}) custom-call(s32[2]{0:T(128)S(1)} %pad_add_fusion.me, f32[16,80,128]{2,1,0:T(8,128)S(1)} %all-to-all-done.got.coefs, f32[16,32,128]{2,1,0:T(8,128)S(1)} %all-to-all-done.2.got, f32[256,128]{1,0:T(8,128)S(1)} %get-tuple-element.51.g, f32[256,128]{1,0:T(8,128)S(1)} %get-tuple-element.33.u, ...), custom_call_target="tpu_custom_call" | custom-call | flops 2000000 | bytes 2752520 | tf_op jit(solution)/shard_map/pallas_call | solution.py:306
  (16 shorter events, 0.0 us)
Async XLA Ops:
  1.3 7.6 %collective-permute-start = (f32[16,128]{1,0:T(8,128)S(1)}, f32[16,128]{1,0:T(8,128)S(1)}, u32[]{:S(2)}, u32[]{:S(2)}) collective-permute-start(f32[16,128]{1,0:T(8,128)S(1)} %slice_bitcast_fusion.1), channel_id=1, source_target_pairs={{16,0},{32,16},{48,32},{64,48},{80,64},{96,80},{112,96},{128,112},... | collective-permute-start | bytes 24584 | tf_op jit(solution)/shard_map/ppermute | solution.py:328
  6.6 0.7 copy-start.5
  6.6 0.7 copy-start.6
  7.2 0.9 %copy-start.4 = (s32[16,16,128]{2,1,0:T(8,128)S(1)}, s32[16,16,128]{2,1,0:T(8,128)}, u32[]{:S(2)}) copy-start(s32[16,16,128]{2,1,0:T(8,128)} %param.7) | copy-start | bytes 393220
  9.0 1.0 %copy-start = (f32[3,16,16,128]{3,2,1,0:T(8,128)S(1)}, f32[3,16,16,128]{3,2,1,0:T(8,128)}, u32[]{:S(2)}) copy-start(f32[3,16,16,128]{3,2,1,0:T(8,128)} %param.5) | copy-start | bytes 1179652
  10.0 1.0 %copy-start.2 = (f32[3,16,16,128]{3,2,1,0:T(8,128)S(1)}, f32[3,16,16,128]{3,2,1,0:T(8,128)}, u32[]{:S(2)}) copy-start(f32[3,16,16,128]{3,2,1,0:T(8,128)} %param.6) | copy-start | bytes 1179652
  12.1 9.3 %copy-start.3 = (f32[3,16,16,128]{3,2,1,0:T(8,128)S(1)}, f32[3,16,16,128]{3,2,1,0:T(8,128)}, u32[]{:S(2)}) copy-start(f32[3,16,16,128]{3,2,1,0:T(8,128)} %param.6) | copy-start | bytes 1179652
  12.1 18.0 %copy-start.1 = (f32[3,16,16,128]{3,2,1,0:T(8,128)S(1)}, f32[3,16,16,128]{3,2,1,0:T(8,128)}, u32[]{:S(2)}) copy-start(f32[3,16,16,128]{3,2,1,0:T(8,128)} %param.5) | copy-start | bytes 1179652
  12.1 33.3 %all-to-all-start = ((f32[16,80,128]{2,1,0:T(8,128)}), f32[16,80,128]{2,1,0:T(8,128)S(1)}, u32[]{:S(2)}, u32[]{:S(2)}) async-start(f32[16,80,128]{2,1,0:T(8,128)} %get-tuple-element.35), calls=%async_computation | async-start | bytes 1310720 | tf_op jit(solution)/shard_map/all_to_all | solution.py:341
  21.4 10.0 %collective-permute-start.3 = (f32[16,128]{1,0:T(8,128)S(1)}, f32[16,128]{1,0:T(8,128)S(1)}, u32[]{:S(2)}, u32[]{:S(2)}) collective-permute-start(f32[16,128]{1,0:T(8,128)S(1)} %bitcast.25), channel_id=1, source_target_pairs={{0,1},{1,2},{2,3},{3,4},{4,5},{5,6},{6,7},{7,8},{8,9},{9,10},{10,1... | collective-permute-start | bytes 24584 | tf_op jit(solution)/shard_map/ppermute | solution.py:329
  26.2 5.9 %collective-permute-start.2 = (f32[16,128]{1,0:T(8,128)S(1)}, f32[16,128]{1,0:T(8,128)S(1)}, u32[]{:S(2)}, u32[]{:S(2)}) collective-permute-start(f32[16,128]{1,0:T(8,128)S(1)} %slice_bitcast_fusion), channel_id=1, source_target_pairs={{0,16},{16,32},{32,48},{48,64},{64,80},{80,96},{96,112},{112,128},... | collective-permute-start | bytes 24584 | tf_op jit(solution)/shard_map/ppermute | solution.py:331
  30.1 7.0 %collective-permute-start.1 = (f32[16,128]{1,0:T(8,128)S(1)}, f32[16,128]{1,0:T(8,128)S(1)}, u32[]{:S(2)}, u32[]{:S(2)}) collective-permute-start(f32[16,128]{1,0:T(8,128)S(1)} %bitcast.24), channel_id=1, source_target_pairs={{1,0},{2,1},{3,2},{4,3},{5,4},{6,5},{7,6},{8,7},{9,8},{10,9},{11,1... | collective-permute-start | bytes 24584 | tf_op jit(solution)/shard_map/ppermute | solution.py:330
  66.6 21.8 %all-to-all-start.2 = ((f32[16,32,128]{2,1,0:T(8,128)}), f32[16,32,128]{2,1,0:T(8,128)S(1)}, u32[]{:S(2)}, u32[]{:S(2)}) async-start(f32[16,32,128]{2,1,0:T(8,128)} %get-tuple-element.50), calls=%async_computation.2 | async-start | bytes 524288 | tf_op jit(solution)/shard_map/all_to_all | solution.py:363

commit v2 on v1

v2 whole, which is shorter than its diff:
```python
import functools

import jax
import jax.numpy as jnp
from jax import lax
from jax.experimental import pallas as pl
from jax.experimental.pallas import tpu as pltpu
from jax.sharding import PartitionSpec as P

h = 32.0
B = 16
F32 = jnp.float32


def plane(i):
    return pl.ds(i * B, B)


def strided(j):
    return pl.ds(j, B, stride=B)


def lanes(v):
    return lax.broadcasted_iota(jnp.int32, v.shape, 1)


def behind_z(v):
    return v - jnp.where(lanes(v) == 0, 0.0, pltpu.roll(v, 1, 1))


def ahead_z(v):
    n = v.shape[1]
    return jnp.where(lanes(v) == n - 1, 0.0, pltpu.roll(v, n - 1, 1)) - v


def factor(w_of, first_block, p, u, v):
    d = None
    y = []
    for j in range(B):
        w = w_of(j)
        e = w + (jnp.where(first_block, 0.0, 1.0) if j == 0 else d)
        inv = 1.0 / (1.0 + e)
        d = e * inv
        p[plane(j)] = inv
        y.append(jnp.ones_like(inv) if j == 0 else y[-1] * last)
        last = inv
    uj = y[B - 1] * last
    vj = last
    u[plane(B - 1)] = uj
    v[plane(B - 1)] = vj
    for j in range(B - 2, -1, -1):
        inv = p[plane(j)]
        uj = inv * (y[j] + uj)
        vj = inv * vj
        u[plane(j)] = uj
        v[plane(j)] = vj


def eliminate(source_of, p, g):
    y = source_of(0)
    ys = [y]
    for j in range(1, B):
        y = source_of(j) + p[plane(j - 1)] * y
        ys.append(y)
    x = y * p[plane(B - 1)]
    end = x
    g[plane(B - 1)] = x
    for j in range(B - 2, -1, -1):
        x = p[plane(j)] * (ys[j] + x)
        g[plane(j)] = x
    return x, end


def boundary(me, n, rows_of, coef_of, outer):
    left = [a for a, _ in outer]
    right = [b for _, b in outer]
    beta = delta = jnp.zeros_like(left[0])
    for s in range(n - 1):
        ff, fl, ll = coef_of(s)
        t = fl / (1.0 - ff * beta)
        on = s < me
        left = [
            jnp.where(on, dl + t * (a + beta * gf), a) for a, (gf, dl) in zip(left, rows_of(s))
        ]
        beta = jnp.where(on, ll + t * beta * fl, beta)
        m = n - 1 - s
        ff, fl, ll = coef_of(m)
        t = fl / (1.0 - ll * delta)
        on = m > me
        right = [
            jnp.where(on, gf + t * (b + delta * dl), b) for b, (gf, dl) in zip(right, rows_of(m))
        ]
        delta = jnp.where(on, ff + t * delta * fl, delta)
    ff, fl, ll = coef_of(me)
    after_scale = 1.0 / (1.0 - delta * ll)
    t = fl * after_scale
    before_scale = 1.0 / (1.0 - beta * (ff + t * delta * fl))
    ends = []
    for a, b, (gf, dl) in zip(left, right, rows_of(me)):
        before = (a + beta * (gf + t * (b + delta * dl))) * before_scale
        ends.append((before, (b + delta * (dl + fl * before)) * after_scale))
    return ends


def merge(one, two):
    (ff1, fl1, ll1), rows1 = one
    (ff2, fl2, ll2), rows2 = two
    d = 1.0 / (1.0 - ll1 * ff2)
    t1, t2 = fl1 * d, fl2 * d
    rows = [
        (gf1 + t1 * (gf2 + ff2 * dl1), dl2 + t2 * (dl1 + ll1 * gf2))
        for (gf1, dl1), (gf2, dl2) in zip(rows1, rows2)
    ]
    return (ff1 + t1 * fl1 * ff2, t1 * fl2, ll2 + t2 * fl2 * ll1), rows


def solve_z(r, w):
    n = r.shape[1]
    lane = lanes(r)
    e = jnp.where(lane == n - 1, 0.0, 1.0)
    l = jnp.where(lane == 0, 0.0, 1.0)
    s = w + jnp.where(lane == n - 1, 1.0, 0.0)
    step = 1
    while step < n:
        inv = 1.0 / (s + (l + e))
        kl = l * pltpu.roll(inv, step, 1)
        kr = e * pltpu.roll(inv, n - step, 1)
        r = r + (kl * pltpu.roll(r, step, 1) + kr * pltpu.roll(r, n - step, 1))
        s = s + (kl * pltpu.roll(s, step, 1) + kr * pltpu.roll(s, n - step, 1))
        l = kl * pltpu.roll(l, step, 1)
        e = kr * pltpu.roll(e, n - step, 1)
        step *= 2
    return r / s


def tables_kernel(
    me, eps, sig, material, elec, magn, w, c, p, u, v, flux, part, ids, ex, ez, hx, hy, sems
):
    loads = [(material, ids), (elec.at[0], ex), (magn.at[1], hy), (elec.at[2], ez), (magn.at[0], hx)]
    loads = [pltpu.make_async_copy(a, b, sems.at[k]) for k, (a, b) in enumerate(loads)]
    for load in loads:
        load.start()
    ws = [eps[m] * (1.0 / (h * h)) + sig[m] * (0.5 / h) for m in range(eps.shape[0])]
    cs = [eps[m] * (1.0 / (h * h)) - sig[m] * (0.5 / h) for m in range(eps.shape[0])]
    loads[0].wait()
    for i in range(B):
        cell = ids[plane(i)]
        wi = jnp.full(cell.shape, ws[0], F32)
        ci = jnp.full(cell.shape, cs[0], F32)
        for m in range(1, len(ws)):
            wi = jnp.where(cell == m, ws[m], wi)
            ci = jnp.where(cell == m, cs[m], ci)
        w[plane(i)] = wi
        c[plane(i)] = ci
    factor(lambda i: w[plane(i)], me[0] == 0, p, u, v)
    for load in loads[1:]:
        load.wait()
    row = lax.broadcasted_iota(jnp.int32, (B, w.shape[1]), 0)
    for i in range(B):
        q = hy[plane(i)] * (1.0 / h) - ahead_z(ex[plane(i)])
        flux[plane(i)] = q
        if i > 0:
            q = q - flux[plane(i - 1)]
        here = hx[plane(i)]
        before = jnp.where(row == 0, 0.0, pltpu.roll(here, 1, 0))
        part[plane(i)] = c[plane(i)] * ez[plane(i)] + (q - (here - before) * (1.0 / h))


def first_x_kernel(n, part, hx_prev, ey_first, hz_last, flux, p, u, v, g, msg):
    row = lax.broadcasted_iota(jnp.int32, hx_prev.shape, 0)

    def source(i):
        return part[plane(i)] + jnp.where(row == 0, hx_prev[pl.ds(i, 1)] * (1.0 / h), 0.0)

    first, last = eliminate(source, p, g)
    last = last - flux[plane(B - 1)]
    sent = [first, last, u[plane(0)], v[plane(0)], v[plane(B - 1)], ey_first[...], hz_last[...]]
    for m in range(n):
        for k, value in enumerate(sent):
            msg[m, plane(k)] = value


def first_z_kernel(me, elec, magn, ez_next, w, c, p, u, v, r, curl, flux_y, flux_a, part_a, fy):
    factor(lambda j: w[strided(j)], me[1] == 0, p, u, v)
    row = lax.broadcasted_iota(jnp.int32, (B, w.shape[1]), 0)
    for i in range(B):
        ez = elec[2, plane(i)]
        after = jnp.where(row == B - 1, ez_next[pl.ds(i, 1)], pltpu.roll(ez, B - 1, 0))
        ri = magn[0, plane(i)] * (1.0 / h) - (after - ez)
        r[plane(i)] = ri
        if i > 0:
            gain = (magn[2, plane(i)] - magn[2, plane(i - 1)]) * (1.0 / h)
            fy[plane(i)] = c[plane(i)] * elec[1, plane(i)] + (behind_z(ri) - gain)
        here = c[plane(i)] * elec[0, plane(i)]
        part_a[plane(i)] = here - behind_z(magn[1, plane(i)]) * (1.0 / h)
        if i < B - 1:
            rise = elec[1, plane(i + 1)] - elec[1, plane(i)]
            flux_a[plane(i)] = magn[2, plane(i)] * (1.0 / h) - rise
    flux_a[plane(B - 1)] = magn[2, plane(B - 1)] * (1.0 / h) + elec[1, plane(B - 1)]
    fy[plane(0)] = jnp.zeros((B, w.shape[1]), F32)

    def solve(k, carry):
        rows = pl.ds(k * (4 * B), 4 * B)
        x = solve_z(fy[rows], w[rows])
        rise = ahead_z(x)
        mx = r[rows] + rise
        curl[rows] = c[rows] * x + behind_z(mx)
        flux_y[rows] = -(mx + rise)
        return carry

    lax.fori_loop(0, B // 4, solve, 0)


def both_y_kernel(
    n, near, me, got, elec, magn, g_b, u_x, v_x, flux_b, w, c, r, curl_in, flux_y_in, flux_a_in, part_a,
    p_y, u_y, v_y, rise_y, curl, flux_y, flux_a, g_a, g_c, msg, part, fz
):
    me_x = me[0]
    top, bottom = plane(0), plane(B - 1)
    ahead = jnp.where(me_x == n - 1, 0.0, got[jnp.minimum(me_x + 1, n - 1), plane(5)])
    before = jnp.where(me_x == 0, 0.0, got[jnp.maximum(me_x - 1, 0), plane(6)])
    flux_a[...] = flux_a_in[...]
    flux_a[bottom] = flux_a_in[bottom] - ahead
    curl[...] = curl_in[...]
    flux_y[...] = flux_y_in[...]
    hz = (magn[2, top] - before) * (1.0 / h)
    x = solve_z(c[top] * elec[1, top] + (behind_z(r[top]) - hz), w[top])
    rise = ahead_z(x)
    mx = r[top] + rise
    curl[top] = c[top] * x + behind_z(mx)
    flux_y[top] = -(mx + rise)

    def source_a(j):
        f = flux_a[strided(j)]
        if j > 0:
            f = f - flux_a[strided(j - 1)]
        return part_a[strided(j)] + f

    first_a, last_a = eliminate(source_a, p_y, g_a)
    last_a = last_a - flux_a[strided(B - 1)]

    zero = jnp.zeros_like(ahead)
    ((before, after),) = boundary(
        me_x,
        n,
        lambda m: [(got[m, plane(0)], got[m, plane(1)])],
        lambda m: (got[m, plane(2)], got[m, plane(3)], got[m, plane(4)]),
        [(zero, zero)],
    )
    for i in range(B):
        fz[plane(i)] = g_b[plane(i)] + (u_x[plane(i)] * before + v_x[plane(i)] * after)
    my_before = jnp.where(me_x == 0, 0.0, fz[top] - before)
    for i in range(B):
        here = fz[plane(i)]
        rise = (fz[plane(i + 1)] if i < B - 1 else after) - here
        my = flux_b[plane(i)] + rise
        rise_y[plane(i)] = my + rise
        part[plane(i)] = c[plane(i)] * here + (my - my_before)
        my_before = my

    def source_c(j):
        f = flux_y[strided(j)]
        if j > 0:
            f = f - flux_y[strided(j - 1)]
        return part[strided(j)] + f

    first_c, last_c = eliminate(source_c, p_y, g_c)
    last_c = last_c - flux_y[strided(B - 1)]
    sent = [first_a, last_a, first_c, last_c, u_y[plane(0)], v_y[plane(0)], v_y[plane(B - 1)]]
    for m in range(near):
        for k, value in enumerate(sent):
            msg[m, plane(k)] = value


def y_rows(got):
    return lambda m: [(got[m, plane(0)], got[m, plane(1)]), (got[m, plane(2)], got[m, plane(3)])]


def y_coefs(got):
    return lambda m: (got[m, plane(4)], got[m, plane(5)], got[m, plane(6)])


def merge_kernel(near, far, got, msg):
    blocks = [(y_coefs(got)(m), y_rows(got)(m)) for m in range(near)]
    while len(blocks) > 1:
        blocks = [merge(a, b) for a, b in zip(blocks[::2], blocks[1::2])]
    coefs, rows = blocks[0]
    sent = [value for pair in rows for value in pair] + list(coefs)
    for m in range(far):
        for k, value in enumerate(sent):
            msg[m, plane(k)] = value


def second_x_kernel(
    n, near, far, me, got_near, got_far, g_a, g_c, u, v, flux_a, flux_y, c, curl, p_x, part, flux2, g2, full_z, new_x,
    msg, fx
):
    my = me[1]
    zero = jnp.zeros((B, c.shape[1]), F32)
    outer = boundary(lax.div(my, near), far, y_rows(got_far), y_coefs(got_far), [(zero, zero)] * 2)
    (before, after), (before_c, after_c) = boundary(
        lax.rem(my, near), near, y_rows(got_near), y_coefs(got_near), outer
    )
    for j in range(B):
        fx[plane(j)] = g_a[plane(j)] + (u[plane(j)] * before + v[plane(j)] * after)
    mz_before = jnp.where(my == 0, 0.0, fx[plane(0)] - before)
    for j in range(B):
        here = fx[plane(j)]
        rise = (fx[plane(j + 1)] if j < B - 1 else after) - here
        mz = flux_a[strided(j)] + rise
        part[strided(j)] = c[strided(j)] * here + (mz - mz_before)
        flux2[strided(j)] = -(mz + rise)
        mz_before = mz

    def source(i):
        f = flux2[plane(i)]
        if i > 0:
            f = f - flux2[plane(i - 1)]
        return curl[plane(i)] + f

    first, last = eliminate(source, p_x, g2)
    last = last - flux2[plane(B - 1)]
    for m in range(n):
        msg[m, plane(0)] = first
        msg[m, plane(1)] = last
    here = None
    for j in range(B):
        ahead = g_c[plane(j)] + (u[plane(j)] * before_c + v[plane(j)] * after_c)
        full_z[strided(j)] = ahead
        if j > 0:
            new_x[strided(j - 1)] = -h * (flux_y[strided(j - 1)] + (ahead - here))
        here = ahead
    new_x[strided(B - 1)] = -h * (flux_y[strided(B - 1)] + (after_c - here))


def second_z_kernel(part, rise_y, w, full_x, new_y):
    def solve(k, carry):
        rows = pl.ds(k * (4 * B), 4 * B)
        a = rise_y[rows]
        x = solve_z(part[rows] - behind_z(a), w[rows])
        full_x[rows] = x
        new_y[rows] = h * (a - ahead_z(x))
        return carry

    lax.fori_loop(0, B // 4, solve, 0)


def last_kernel(n, me, coefs, got, g, u, v, flux2, full_x, full_z, new_x, new_y, elec, magn):
    elec[0] = full_x[...]
    elec[2] = full_z[...]
    magn[0] = new_x[...]
    magn[1] = new_y[...]
    zero = jnp.zeros_like(got[0, plane(0)])
    ((before, after),) = boundary(
        me[0],
        n,
        lambda m: [(got[m, plane(0)], got[m, plane(1)])],
        lambda m: (coefs[m, plane(2)], coefs[m, plane(3)], coefs[m, plane(4)]),
        [(zero, zero)],
    )
    here = None
    for i in range(B):
        ahead = g[plane(i)] + (u[plane(i)] * before + v[plane(i)] * after)
        elec[1, plane(i)] = ahead
        if i > 0:
            magn[2, plane(i - 1)] = -h * (flux2[plane(i - 1)] + (ahead - here))
        here = ahead
    magn[2, plane(B - 1)] = -h * (flux2[plane(B - 1)] + (after - here))


VMEM = pl.BlockSpec(memory_space=pltpu.VMEM)
SMEM = pl.BlockSpec(memory_space=pltpu.SMEM)
HBM = pl.BlockSpec(memory_space=pltpu.HBM)


def call(kernel, ins, outs, scalars=0, specs=None, scratch=(), flops=2_000_000):
    shapes = [jax.ShapeDtypeStruct(s, F32) for s in outs]
    size = sum(4 * x.size for x in ins) + sum(4 * s.size for s in shapes)
    return pl.pallas_call(
        kernel,
        out_shape=shapes,
        in_specs=specs or [SMEM] * scalars + [VMEM] * (len(ins) - scalars),
        out_specs=[VMEM] * len(outs),
        scratch_shapes=[s if not isinstance(s, tuple) else pltpu.VMEM(s, F32) for s in scratch],
        compiler_params=pltpu.CompilerParams(vmem_limit_bytes=32 * 1024 * 1024),
        cost_estimate=pl.CostEstimate(flops=flops, bytes_accessed=size, transcendentals=0),
    )(*ins)


def local(electric, magnetic, material, permittivity, conductivity):
    nx, ny = lax.axis_size("px"), lax.axis_size("py")
    near = 1 << (ny.bit_length() // 2)
    far = ny // near
    nz = material.shape[2]
    cells = (B * B, nz)
    me = jnp.stack([lax.axis_index("px"), lax.axis_index("py")]).astype(jnp.int32)
    elec = electric.reshape(3, *cells)
    magn = magnetic.reshape(3, *cells)
    ids = material.reshape(cells)

    hx_prev = lax.ppermute(magnetic[0, :, B - 1], "py", [(i, i + 1) for i in range(ny - 1)])
    w, c, p_x, u_x, v_x, flux_b, part_b = call(
        tables_kernel,
        [me, permittivity, conductivity, ids, elec, magn],
        [cells] * 7,
        specs=[SMEM] * 3 + [HBM] * 3,
        scratch=[pltpu.VMEM(cells, jnp.int32)] + [cells] * 4 + [pltpu.SemaphoreType.DMA((5,))],
    )
    g_b, msg = call(
        functools.partial(first_x_kernel, nx),
        [part_b, hx_prev, electric[1, 0], magnetic[2, B - 1], flux_b, p_x, u_x, v_x],
        [cells, (nx, 7 * B, nz)],
    )
    got_x = lax.all_to_all(msg, "px", 0, 0, tiled=True)
    ez_next = lax.ppermute(electric[2, :, 0], "py", [(i + 1, i) for i in range(ny - 1)])
    p_y, u_y, v_y, r, curl, flux_y, flux_a, part_a = call(
        first_z_kernel,
        [me, elec, magn, ez_next, w, c],
        [cells] * 8,
        scalars=1,
        scratch=[cells],
        flops=8_000_000,
    )
    rise_y, curl, flux_y, flux_a, g_a, g_c, msg = call(
        functools.partial(both_y_kernel, nx, near),
        [me, got_x, elec, magn, g_b, u_x, v_x, flux_b, w, c, r, curl, flux_y, flux_a, part_a, p_y, u_y, v_y],
        [cells] * 6 + [(near, 7 * B, nz)],
        scalars=1,
        scratch=[cells] * 2,
    )
    groups = [[q * near + k for k in range(near)] for q in range(far)]
    got_near = lax.all_to_all(msg, "py", 0, 0, axis_index_groups=groups, tiled=True)
    (msg,) = call(functools.partial(merge_kernel, near, far), [got_near], [(far, 7 * B, nz)])
    groups = [[q * near + k for q in range(far)] for k in range(near)]
    got_far = lax.all_to_all(msg, "py", 0, 0, axis_index_groups=groups, tiled=True)
    part_x, flux2, g2, full_z, new_x, msg = call(
        functools.partial(second_x_kernel, nx, near, far),
        [me, got_near, got_far, g_a, g_c, u_y, v_y, flux_a, flux_y, c, curl, p_x],
        [cells] * 5 + [(nx, 2 * B, nz)],
        scalars=1,
        scratch=[cells],
    )
    got = lax.all_to_all(msg, "px", 0, 0, tiled=True)
    full_x, new_y = call(second_z_kernel, [part_x, rise_y, w], [cells] * 2, flops=8_000_000)
    out = call(
        functools.partial(last_kernel, nx),
        [me, got_x, got, g2, u_x, v_x, flux2, full_x, full_z, new_x, new_y],
        [(3, *cells)] * 2,
        scalars=1,
    )
    return tuple(a.reshape(3, B, B, nz) for a in out)


def solution(mesh):
    placed = (P(None, "px", "py", None), P(None, "px", "py", None), P("px", "py", None), P(), P())
    return jax.shard_map(
        local,
        mesh=mesh,
        in_specs=placed,
        out_specs=(P(None, "px", "py", None), P(None, "px", "py", None)),
        check_vma=False,
    )
```

time: 91.8 us -> 86.9 us (0.947); the launches traced: 90.2 us -> 86.2 us
  starting transfers between devices: 34.7 us -> 24 us
  Pallas kernels: 22.7 us -> 15.4 us
  blocking collectives: 18.5 us -> 24.9 us
  local copies, waits for them, and re-layouts: 4.29 us -> 8.94 us
  waiting for transfers between devices: 9.11 us -> 12.1 us
    ppermute x4 -> x2, starting transfers between devices: 15.1 us -> 6.93 us  [the longest x1 5.64 us: local(): lax.ppermute(magnetic[0, :, B - 1], 'py', [(i, i + 1) for i in range(ny -...]
    pallas_call x8, Pallas kernels: 22.7 us -> 15.4 us  [call(): pl.pallas_call(kernel, out_shape=shapes, in_specs=specs or [SMEM] * scala...]
    all_to_all x1 -> x2, blocking collectives: 18.5 us -> 24.9 us  [local(): lax.all_to_all(msg, 'py', 0, 0, axis_index_groups=groups, tiled=True)]
    ppermute x4 -> x2, waiting for transfers between devices: 4.94 us -> 8.14 us  [the longest x1 8.14 us: local(): lax.ppermute(electric[2, :, 0], 'py', [(i + 1, i) for i in range(ny - 1)])]
    unnamed x14 -> x22, local copies, waits for them, and re-layouts: 3.57 us -> 6.68 us
    all_to_all x2, starting transfers between devices: 19.6 us -> 17.1 us  [the longest x1 11.6 us: local(): got = lax.all_to_all(msg, 'px', 0, 0, tiled=True)]
  transfers between devices with their start and end apart: 6 -> 4, of which waited for: 2 -> 2; matrix products, arithmetic and copies ran while one was open for 0% -> 2% of each run, Pallas kernels for 19% -> 11%
where the time goes in v2:
time: 86.9 us; the launch traced here: 86.2 us
  blocking collectives  24.9 us (29%)
  starting transfers between devices  24 us (28%)
  Pallas kernels  15.4 us (18%)
  waiting for transfers between devices  12.1 us (14%)
  local copies, waits for them, and re-layouts  8.94 us (10%)
    all_to_all x2, blocking collectives, local(): lax.all_to_all(msg, 'py', 0, 0, axis_index_groups=groups, tiled=True)  24.9 us
    pallas_call x8, Pallas kernels, call(): pl.pallas_call(kernel, out_shape=shapes, in_specs=specs or [SMEM] * scala...  15.4 us
    all_to_all x1, starting transfers between devices, local(): got = lax.all_to_all(msg, 'px', 0, 0, tiled=True)  11.6 us
    ppermute x1, waiting for transfers between devices, local(): lax.ppermute(electric[2, :, 0], 'py', [(i + 1, i) for i in range(ny - 1)])  8.14 us
    unnamed x22, local copies, waits for them, and re-layouts  6.68 us
    ppermute x1, starting transfers between devices, local(): lax.ppermute(magnetic[0, :, B - 1], 'py', [(i, i + 1) for i in range(ny -...  5.64 us
    all_to_all x1, starting transfers between devices, local(): got_x = lax.all_to_all(msg, 'px', 0, 0, tiled=True)  5.51 us
    all_to_all x1, waiting for transfers between devices, local(): got = lax.all_to_all(msg, 'px', 0, 0, tiled=True)  3.97 us
  transfers between devices with their start and end apart: 4, of which 2 were waited for; matrix products, arithmetic and copies ran while one was open for 2% of the time, Pallas kernels for 11%

profile of v2, /device:TPU:1, one launch (start us, length us, event | category | flops | bytes accessed | tf_op | source)
XLA Modules:
  0.0 86.2 jit_solution(1534820800407098287)
XLA Ops:
  0.6 0.9 slice.12
  1.5 5.6 %collective-permute-start = (f32[16,128]{1,0:T(8,128)S(1)}, f32[16,128]{1,0:T(8,128)S(1)}, u32[]{:S(2)}, u32[]{:S(2)}) collective-permute-start(f32[16,128]{1,0:T(8,128)S(1)} %bitcast.24), channel_id=1, source_target_pairs={{0,1},{1,2},{2,3},{3,4},{4,5},{5,6},{6,7},{7,8},{8,9},{9,10},{10,1... | collective-permute-start | bytes 24584 | tf_op jit(solution)/shard_map/ppermute | solution.py:401
  7.1 0.7 slice_bitcast_fusion.hz_last
  7.8 0.7 slice_bitcast_fusion.1.ey_first
  9.3 1.0 %copy-done = f32[3,16,16,128]{3,2,1,0:T(8,128)S(1)} copy-done((f32[3,16,16,128]{3,2,1,0:T(8,128)S(1)}, f32[3,16,16,128]{3,2,1,0:T(8,128)}, u32[]{:S(2)}) %copy-start) | copy-done | bytes 393240
  10.3 1.0 %copy-done.2 = f32[3,16,16,128]{3,2,1,0:T(8,128)S(1)} copy-done((f32[3,16,16,128]{3,2,1,0:T(8,128)S(1)}, f32[3,16,16,128]{3,2,1,0:T(8,128)}, u32[]{:S(2)}) %copy-start.2) | copy-done | bytes 393240
  11.3 0.9 %copy-done.4 = s32[16,16,128]{2,1,0:T(8,128)S(1)} copy-done((s32[16,16,128]{2,1,0:T(8,128)S(1)}, s32[16,16,128]{2,1,0:T(8,128)}, u32[]{:S(2)}) %copy-start.4) | copy-done | bytes 131096
  12.2 1.8 %shard_map.68 = (f32[256,128]{1,0:T(8,128)S(1)}, f32[256,128]{1,0:T(8,128)S(1)}, f32[256,128]{1,0:T(8,128)S(1)}, f32[256,128]{1,0:T(8,128)S(1)}, f32[256,128]{1,...) custom-call(s32[2]{0:T(128)S(1)} %pad_add_fusion.me, f32[8]{0:T(128)S(1)} %copy-done.9, f32[8]{0:T(128)S(1)} %copy-done.10, ...), custom_call_target="tpu_custom_call" | custom-call | flops 2000000 | bytes 1835080 | tf_op jit(solution)/shard_map/pallas_call | solution.py:379
  14.0 1.1 %shard_map.69 = (f32[256,128]{1,0:T(8,128)S(1)}, f32[16,112,128]{2,1,0:T(8,128)}) custom-call(f32[256,128]{1,0:T(8,128)S(1)} %get-tuple-element.36.part, f32[16,128]{1,0:T(8,128)S(1)} %collective-permute-done.hx_prev, f32[16,128]{1,0:T(8,128)S(1)} %slice_bitcast_fusion.1.ey_first, f32[16,128]{1,0:T(8,128)S(1)} %slice_bitcast_fusion.hz_last, ...), custom_call_target="tpu_custom_call" | custom-call | flops 2000000 | bytes 1728512 | tf_op jit(solution)/shard_map/pallas_call | solution.py:379
  15.1 5.5 %all-to-all-start = ((f32[16,112,128]{2,1,0:T(8,128)}), f32[16,112,128]{2,1,0:T(8,128)S(1)}, u32[]{:S(2)}, u32[]{:S(2)}) async-start(f32[16,112,128]{2,1,0:T(8,128)} %get-tuple-element.41), calls=%async_computation | async-start | bytes 1835008 | tf_op jit(solution)/shard_map/all_to_all | solution.py:414
  20.6 1.3 %collective-permute-start.1 = (f32[16,128]{1,0:T(8,128)S(1)}, f32[16,128]{1,0:T(8,128)S(1)}, u32[]{:S(2)}, u32[]{:S(2)}) collective-permute-start(f32[16,128]{1,0:T(8,128)S(1)} %bitcast.25), channel_id=1, source_target_pairs={{1,0},{2,1},{3,2},{4,3},{5,4},{6,5},{7,6},{8,7},{9,8},{10,9},{11,1... | collective-permute-start | bytes 24584 | tf_op jit(solution)/shard_map/ppermute | solution.py:415
  21.9 8.1 %collective-permute-done.1.ez_next = f32[16,128]{1,0:T(8,128)S(1)} collective-permute-done((f32[16,128]{1,0:T(8,128)S(1)}, f32[16,128]{1,0:T(8,128)S(1)}, u32[]{:S(2)}, u32[]{:S(2)}) %collective-permute-start.1) | collective-permute-done | bytes 8224 | tf_op jit(solution)/shard_map/ppermute | solution.py:415
  30.1 4.4 %shard_map.70 = (f32[256,128]{1,0:T(8,128)S(1)}, f32[256,128]{1,0:T(8,128)S(1)}, f32[256,128]{1,0:T(8,128)S(1)}, f32[256,128]{1,0:T(8,128)S(1)}, f32[256,128]{1,...) custom-call(s32[2]{0:T(128)S(1)} %pad_add_fusion.me, ...), custom_call_target="tpu_custom_call" | custom-call | flops 8000000 | bytes 2105352 | tf_op jit(solution)/shard_map/pallas_call | solution.py:379
  35.2 0.7 copy-done.7
  35.8 0.9 %copy-done.6 = f32[256,128]{1,0:T(8,128)S(1)} copy-done((f32[256,128]{1,0:T(8,128)S(1)}, f32[256,128]{1,0:T(8,128)}, u32[]{:S(2)}) %copy-start.6) | copy-done | bytes 131096
  36.7 0.9 %copy-done.8 = f32[256,128]{1,0:T(8,128)S(1)} copy-done((f32[256,128]{1,0:T(8,128)S(1)}, f32[256,128]{1,0:T(8,128)}, u32[]{:S(2)}) %copy-start.8) | copy-done | bytes 131096
  37.6 1.4 %shard_map.71 = (f32[256,128]{1,0:T(8,128)S(1)}, f32[256,128]{1,0:T(8,128)S(1)}, f32[256,128]{1,0:T(8,128)S(1)}, f32[256,128]{1,0:T(8,128)S(1)}, f32[256,128]{1,...) custom-call(s32[2]{0:T(128)S(1)} %pad_add_fusion.me, f32[16,112,128]{2,1,0:T(8,128)S(1)} %all-to-all-done.got.coefs, ...), custom_call_target="tpu_custom_call" | custom-call | flops 2000000 | bytes 4554760 | tf_op jit(solution)/shard_map/pallas_call | solution.py:379
  39.0 10.7 %all_to_all.20.got.got_near = f32[4,112,128]{2,1,0:T(8,128)S(1)} all-to-all(f32[4,112,128]{2,1,0:T(8,128)S(1)} %get-tuple-element.53), channel_id=1, replica_groups={{0,1,2,3},{4,5,6,7},{8,9,10,11},{12,13,14,15},{16,17,18,19},{20,21,22,2..., dimensions={0} | all-to-all | bytes 458752 | tf_op jit(solution)/shard_map/all_to_all | solution.py:432
  49.7 14.3 %all_to_all.21.got_far = f32[4,112,128]{2,1,0:T(8,128)S(1)} all-to-all(f32[4,112,128]{2,1,0:T(8,128)S(1)} %shard_map.72), channel_id=1, replica_groups={{0,4,8,12},{1,5,9,13},{2,6,10,14},{3,7,11,15},{16,20,24,28},{17,21,25,2..., dimensions={0} | all-to-all | bytes 458752 | tf_op jit(solution)/shard_map/all_to_all | solution.py:435
  64.0 1.7 %shard_map.73 = (f32[256,128]{1,0:T(8,128)S(1)}, f32[256,128]{1,0:T(8,128)S(1)}, f32[256,128]{1,0:T(8,128)S(1)}, f32[256,128]{1,0:T(8,128)S(1)}, f32[256,128]{1,0:T(8,128)S(1)}, /*index=5*/f32[16,32,128]{2,1,0:T(8,128)}) custom-call(s32[2]{0:T(128)S(1)} %pad_add_fusion.me, f32[4,112,128]{2,1,0:T(8,128)S(1)} %all_to_all.20.got.got_near, ...), custom_call_target="tpu_custom_call" | custom-call | flops 2000000 | bytes 2555912 | tf_op jit(solution)/shard_map/pallas_call | solution.py:379
  65.8 11.6 %all-to-all-start.3 = ((f32[16,32,128]{2,1,0:T(8,128)}), f32[16,32,128]{2,1,0:T(8,128)S(1)}, u32[]{:S(2)}, u32[]{:S(2)}) async-start(f32[16,32,128]{2,1,0:T(8,128)} %get-tuple-element.59), calls=%async_computation.3 | async-start | bytes 524288 | tf_op jit(solution)/shard_map/all_to_all | solution.py:443
  77.4 3.2 %shard_map.74 = (f32[256,128]{1,0:T(8,128)S(1)}, f32[256,128]{1,0:T(8,128)S(1)}) custom-call(f32[256,128]{1,0:T(8,128)S(1)} %get-tuple-element.62.part, f32[256,128]{1,0:T(8,128)S(1)} %get-tuple-element.63.rise_y, f32[256,128]{1,0:T(8,128)S(1)} %get-tuple-element.43.w), custom_call_target="tpu_custom_call" | custom-call | flops 8000000 | bytes 655360 | tf_op jit(solution)/shard_map/pallas_call | solution.py:379
  80.6 4.0 %all-to-all-done.3.got = f32[16,32,128]{2,1,0:T(8,128)S(1)} async-done(((f32[16,32,128]{2,1,0:T(8,128)}), f32[16,32,128]{2,1,0:T(8,128)S(1)}, u32[]{:S(2)}, u32[]{:S(2)}) %all-to-all-start.3) | async-done | bytes 262176 | tf_op jit(solution)/shard_map/all_to_all | solution.py:443
  84.5 1.7 %shard_map.75 = (f32[3,256,128]{2,1,0:T(8,128)}, f32[3,256,128]{2,1,0:T(8,128)}) custom-call(s32[2]{0:T(128)S(1)} %pad_add_fusion.me, f32[16,112,128]{2,1,0:T(8,128)S(1)} %all-to-all-done.got.coefs, f32[16,32,128]{2,1,0:T(8,128)S(1)} %all-to-all-done.3.got, f32[256,128]{1,0:T(8,128)S(1)} %get-tuple-element.60.g, f32[256,128]{1,0:T(8,128)S(1)} %get-tuple-element.39.u.u_x, ...), custom_call_target="tpu_custom_call" | custom-call | flops 2000000 | bytes 3014664 | tf_op jit(solution)/shard_map/pallas_call | solution.py:379
  (21 shorter events, 1.5 us)
Async XLA Ops:
  1.5 12.5 %collective-permute-start = (f32[16,128]{1,0:T(8,128)S(1)}, f32[16,128]{1,0:T(8,128)S(1)}, u32[]{:S(2)}, u32[]{:S(2)}) collective-permute-start(f32[16,128]{1,0:T(8,128)S(1)} %bitcast.24), channel_id=1, source_target_pairs={{0,1},{1,2},{2,3},{3,4},{4,5},{5,6},{6,7},{7,8},{8,9},{9,10},{10,1... | collective-permute-start | bytes 24584 | tf_op jit(solution)/shard_map/ppermute | solution.py:401
  8.6 0.7 copy-start.9
  8.6 0.7 copy-start.10
  9.3 1.0 %copy-start = (f32[3,16,16,128]{3,2,1,0:T(8,128)S(1)}, f32[3,16,16,128]{3,2,1,0:T(8,128)}, u32[]{:S(2)}) copy-start(f32[3,16,16,128]{3,2,1,0:T(8,128)} %param.5) | copy-start | bytes 1179652
  10.3 1.0 %copy-start.2 = (f32[3,16,16,128]{3,2,1,0:T(8,128)S(1)}, f32[3,16,16,128]{3,2,1,0:T(8,128)}, u32[]{:S(2)}) copy-start(f32[3,16,16,128]{3,2,1,0:T(8,128)} %param.6) | copy-start | bytes 1179652
  11.3 0.9 %copy-start.4 = (s32[16,16,128]{2,1,0:T(8,128)S(1)}, s32[16,16,128]{2,1,0:T(8,128)}, u32[]{:S(2)}) copy-start(s32[16,16,128]{2,1,0:T(8,128)} %param.7) | copy-start | bytes 393220
  15.1 5.5 %copy-start.1 = (f32[3,16,16,128]{3,2,1,0:T(8,128)S(1)}, f32[3,16,16,128]{3,2,1,0:T(8,128)}, u32[]{:S(2)}) copy-start(f32[3,16,16,128]{3,2,1,0:T(8,128)} %param.5) | copy-start | bytes 1179652
  15.1 15.0 %copy-start.3 = (f32[3,16,16,128]{3,2,1,0:T(8,128)S(1)}, f32[3,16,16,128]{3,2,1,0:T(8,128)}, u32[]{:S(2)}) copy-start(f32[3,16,16,128]{3,2,1,0:T(8,128)} %param.6) | copy-start | bytes 1179652
  15.1 20.7 %all-to-all-start = ((f32[16,112,128]{2,1,0:T(8,128)}), f32[16,112,128]{2,1,0:T(8,128)S(1)}, u32[]{:S(2)}, u32[]{:S(2)}) async-start(f32[16,112,128]{2,1,0:T(8,128)} %get-tuple-element.41), calls=%async_computation | async-start | bytes 1835008 | tf_op jit(solution)/shard_map/all_to_all | solution.py:414
  20.6 9.4 %collective-permute-start.1 = (f32[16,128]{1,0:T(8,128)S(1)}, f32[16,128]{1,0:T(8,128)S(1)}, u32[]{:S(2)}, u32[]{:S(2)}) collective-permute-start(f32[16,128]{1,0:T(8,128)S(1)} %bitcast.25), channel_id=1, source_target_pairs={{1,0},{2,1},{3,2},{4,3},{5,4},{6,5},{7,6},{8,7},{9,8},{10,9},{11,1... | collective-permute-start | bytes 24584 | tf_op jit(solution)/shard_map/ppermute | solution.py:415
  34.5 0.7 copy-start.5
  35.2 0.7 copy-start.7
  35.8 0.9 %copy-start.6 = (f32[256,128]{1,0:T(8,128)S(1)}, f32[256,128]{1,0:T(8,128)}, u32[]{:S(2)}) copy-start(f32[256,128]{1,0:T(8,128)} %copy-done.5) | copy-start | bytes 393220
  36.7 0.9 %copy-start.8 = (f32[256,128]{1,0:T(8,128)S(1)}, f32[256,128]{1,0:T(8,128)}, u32[]{:S(2)}) copy-start(f32[256,128]{1,0:T(8,128)} %copy-done.7) | copy-start | bytes 393220
  65.8 18.8 %all-to-all-start.3 = ((f32[16,32,128]{2,1,0:T(8,128)}), f32[16,32,128]{2,1,0:T(8,128)S(1)}, u32[]{:S(2)}, u32[]{:S(2)}) async-start(f32[16,32,128]{2,1,0:T(8,128)} %get-tuple-element.59), calls=%async_computation.3 | async-start | bytes 524288 | tf_op jit(solution)/shard_map/all_to_all | solution.py:443

commit v3 on v2

v3 whole, which is shorter than its diff:
```python
import functools

import jax
import jax.numpy as jnp
from jax import lax
from jax.experimental import pallas as pl
from jax.experimental.pallas import tpu as pltpu
from jax.sharding import PartitionSpec as P

h = 32.0
B = 16
F32 = jnp.float32


def plane(i):
    return pl.ds(i * B, B)


def strided(j):
    return pl.ds(j, B, stride=B)


def lanes(v):
    return lax.broadcasted_iota(jnp.int32, v.shape, 1)


def behind_z(v):
    return v - jnp.where(lanes(v) == 0, 0.0, pltpu.roll(v, 1, 1))


def ahead_z(v):
    n = v.shape[1]
    return jnp.where(lanes(v) == n - 1, 0.0, pltpu.roll(v, n - 1, 1)) - v


def factor(w_of, first_block, p, u, v):
    d = None
    y = []
    for j in range(B):
        w = w_of(j)
        e = w + (jnp.where(first_block, 0.0, 1.0) if j == 0 else d)
        inv = 1.0 / (1.0 + e)
        d = e * inv
        p[plane(j)] = inv
        y.append(jnp.ones_like(inv) if j == 0 else y[-1] * last)
        last = inv
    uj = y[B - 1] * last
    vj = last
    u[plane(B - 1)] = uj
    v[plane(B - 1)] = vj
    for j in range(B - 2, -1, -1):
        inv = p[plane(j)]
        uj = inv * (y[j] + uj)
        vj = inv * vj
        u[plane(j)] = uj
        v[plane(j)] = vj


def eliminate(source_of, p, g):
    y = source_of(0)
    ys = [y]
    for j in range(1, B):
        y = source_of(j) + p[plane(j - 1)] * y
        ys.append(y)
    x = y * p[plane(B - 1)]
    end = x
    g[plane(B - 1)] = x
    for j in range(B - 2, -1, -1):
        x = p[plane(j)] * (ys[j] + x)
        g[plane(j)] = x
    return x, end


def boundary(me, n, rows_of, coef_of, outer):
    left = [a for a, _ in outer]
    right = [b for _, b in outer]
    beta = delta = jnp.zeros_like(left[0])
    for s in range(n - 1):
        ff, fl, ll = coef_of(s)
        t = fl / (1.0 - ff * beta)
        on = s < me
        left = [
            jnp.where(on, dl + t * (a + beta * gf), a) for a, (gf, dl) in zip(left, rows_of(s))
        ]
        beta = jnp.where(on, ll + t * beta * fl, beta)
        m = n - 1 - s
        ff, fl, ll = coef_of(m)
        t = fl / (1.0 - ll * delta)
        on = m > me
        right = [
            jnp.where(on, gf + t * (b + delta * dl), b) for b, (gf, dl) in zip(right, rows_of(m))
        ]
        delta = jnp.where(on, ff + t * delta * fl, delta)
    ff, fl, ll = coef_of(me)
    after_scale = 1.0 / (1.0 - delta * ll)
    t = fl * after_scale
    before_scale = 1.0 / (1.0 - beta * (ff + t * delta * fl))
    ends = []
    for a, b, (gf, dl) in zip(left, right, rows_of(me)):
        before = (a + beta * (gf + t * (b + delta * dl))) * before_scale
        ends.append((before, (b + delta * (dl + fl * before)) * after_scale))
    return ends


def merge(one, two):
    (ff1, fl1, ll1), rows1 = one
    (ff2, fl2, ll2), rows2 = two
    d = 1.0 / (1.0 - ll1 * ff2)
    t1, t2 = fl1 * d, fl2 * d
    rows = [
        (gf1 + t1 * (gf2 + ff2 * dl1), dl2 + t2 * (dl1 + ll1 * gf2))
        for (gf1, dl1), (gf2, dl2) in zip(rows1, rows2)
    ]
    return (ff1 + t1 * fl1 * ff2, t1 * fl2, ll2 + t2 * fl2 * ll1), rows


def solve_z(r, w):
    n = r.shape[1]
    lane = lanes(r)
    e = jnp.where(lane == n - 1, 0.0, 1.0)
    l = jnp.where(lane == 0, 0.0, 1.0)
    s = w + jnp.where(lane == n - 1, 1.0, 0.0)
    step = 1
    while step < n:
        inv = 1.0 / (s + (l + e))
        kl = l * pltpu.roll(inv, step, 1)
        kr = e * pltpu.roll(inv, n - step, 1)
        r = r + (kl * pltpu.roll(r, step, 1) + kr * pltpu.roll(r, n - step, 1))
        s = s + (kl * pltpu.roll(s, step, 1) + kr * pltpu.roll(s, n - step, 1))
        l = kl * pltpu.roll(l, step, 1)
        e = kr * pltpu.roll(e, n - step, 1)
        step *= 2
    return r / s


def collect(r, own, others, got):
    got[r] = own[...]
    for s, other in enumerate(others, 1):
        got[lax.bitwise_xor(r, s)] = other[...]


def rows_in(got, sources):
    return lambda m: [(got[m, plane(2 * k)], got[m, plane(2 * k + 1)]) for k in range(sources)]


def coefs_in(got, at):
    return lambda m: tuple(got[m, plane(at + k)] for k in range(3))


def tables_kernel(
    me, eps, sig, material, elec, magn, w, c, p, u, v, flux, part, ids, ex, ez, hx, hy, sems
):
    loads = [(material, ids), (elec.at[0], ex), (magn.at[1], hy), (elec.at[2], ez), (magn.at[0], hx)]
    loads = [pltpu.make_async_copy(a, b, sems.at[k]) for k, (a, b) in enumerate(loads)]
    for load in loads:
        load.start()
    ws = [eps[m] * (1.0 / (h * h)) + sig[m] * (0.5 / h) for m in range(eps.shape[0])]
    cs = [eps[m] * (1.0 / (h * h)) - sig[m] * (0.5 / h) for m in range(eps.shape[0])]
    loads[0].wait()
    for i in range(B):
        cell = ids[plane(i)]
        wi = jnp.full(cell.shape, ws[0], F32)
        ci = jnp.full(cell.shape, cs[0], F32)
        for m in range(1, len(ws)):
            wi = jnp.where(cell == m, ws[m], wi)
            ci = jnp.where(cell == m, cs[m], ci)
        w[plane(i)] = wi
        c[plane(i)] = ci
    factor(lambda i: w[plane(i)], me[0] == 0, p, u, v)
    for load in loads[1:]:
        load.wait()
    row = lax.broadcasted_iota(jnp.int32, (B, w.shape[1]), 0)
    for i in range(B):
        q = hy[plane(i)] * (1.0 / h) - ahead_z(ex[plane(i)])
        flux[plane(i)] = q
        if i > 0:
            q = q - flux[plane(i - 1)]
        here = hx[plane(i)]
        before = jnp.where(row == 0, 0.0, pltpu.roll(here, 1, 0))
        part[plane(i)] = c[plane(i)] * ez[plane(i)] + (q - (here - before) * (1.0 / h))


def first_x_kernel(part, hx_prev, flux, p, u, v, g, msg):
    row = lax.broadcasted_iota(jnp.int32, hx_prev.shape, 0)

    def source(i):
        return part[plane(i)] + jnp.where(row == 0, hx_prev[pl.ds(i, 1)] * (1.0 / h), 0.0)

    first, last = eliminate(source, p, g)
    msg[plane(0)] = first
    msg[plane(1)] = last - flux[plane(B - 1)]
    msg[plane(2)] = u[plane(0)]
    msg[plane(3)] = v[plane(0)]
    msg[plane(4)] = v[plane(B - 1)]


def merge_kernel(axis, near, sources, me, *refs):
    got, msg = refs[-2:]
    collect(lax.rem(me[axis], near), refs[0], refs[1:near], got)
    rows_of, coef_of = rows_in(got, sources), coefs_in(got, 2 * sources)
    blocks = [(coef_of(m), rows_of(m)) for m in range(near)]
    while len(blocks) > 1:
        blocks = [merge(a, b) for a, b in zip(blocks[::2], blocks[1::2])]
    coefs, rows = blocks[0]
    for k, value in enumerate([v for pair in rows for v in pair] + list(coefs)):
        msg[plane(k)] = value


def merge_rows_kernel(axis, near, me, coefs, *refs):
    got, msg = refs[-2:]
    collect(lax.rem(me[axis], near), refs[0], refs[1:near], got)
    rows_of, coef_of = rows_in(got, 1), coefs_in(coefs, 2)
    blocks = [(coef_of(m), rows_of(m)) for m in range(near)]
    while len(blocks) > 1:
        blocks = [merge(a, b) for a, b in zip(blocks[::2], blocks[1::2])]
    msg[plane(0)], msg[plane(1)] = blocks[0][1][0]


def solved_ends(here, near, far, sources, got_near, got_far, coefs_near, coefs_far):
    zero = jnp.zeros_like(got_near[0, plane(0)])
    outer = boundary(
        lax.div(here, near), far, rows_in(got_far, sources), coefs_far, [(zero, zero)] * sources
    )
    return boundary(lax.rem(here, near), near, rows_in(got_near, sources), coefs_near, outer)


def first_z_kernel(me, elec, magn, w, c, p, u, v, r2, src2, curl, flux_y, flux_a, part_a, src, r, ef, mf, sems):
    loads = [pltpu.make_async_copy(elec, ef, sems.at[0]), pltpu.make_async_copy(magn, mf, sems.at[1])]
    for load in loads:
        load.start()
    factor(lambda j: w[strided(j)], me[1] == 0, p, u, v)
    for load in loads:
        load.wait()
    row = lax.broadcasted_iota(jnp.int32, (B, w.shape[1]), 0)
    for i in range(B):
        ez = ef[2, plane(i)]
        after = jnp.where(row == B - 1, 0.0, pltpu.roll(ez, B - 1, 0))
        ri = mf[0, plane(i)] * (1.0 / h) - (after - ez)
        r[plane(i)] = ri
        gain = mf[2, plane(i)]
        if i > 0:
            gain = gain - mf[2, plane(i - 1)]
        src[plane(i)] = c[plane(i)] * ef[1, plane(i)] + (behind_z(ri) - gain * (1.0 / h))
        part_a[plane(i)] = c[plane(i)] * ef[0, plane(i)] - behind_z(mf[1, plane(i)]) * (1.0 / h)
        if i < B - 1:
            rise = ef[1, plane(i + 1)] - ef[1, plane(i)]
            flux_a[plane(i)] = mf[2, plane(i)] * (1.0 / h) - rise
    flux_a[plane(B - 1)] = mf[2, plane(B - 1)] * (1.0 / h) + ef[1, plane(B - 1)]
    for two, of in ((r2, r), (src2, src)):
        two[plane(0)] = of[plane(0)]
        two[plane(1)] = of[strided(B - 1)]

    def solve(k, carry):
        rows = pl.ds(k * (4 * B), 4 * B)
        x = solve_z(src[rows], w[rows])
        rise = ahead_z(x)
        mx = r[rows] + rise
        curl[rows] = c[rows] * x + behind_z(mx)
        flux_y[rows] = -(mx + rise)
        return carry

    lax.fori_loop(0, B // 4, solve, 0)


def both_y_kernel(near, far, me, got_near, *refs):
    others, refs = refs[:far], refs[far:]
    (ey_next, ez_next, hz_prev, g_b, u_x, v_x, flux_b, w, c, r2, src2, curl_in, flux_y_in, flux_a_in, part_a, p_y, u_y, v_y) = refs[:18]
    got_far, rise_y, curl, flux_y, flux_a, g_a, g_c, msg, part, fz = refs[18:]
    me_x = me[0]
    top, corner = plane(0), strided(B - 1)
    collect(lax.div(me_x, near), others[0], others[1:], got_far)

    curl[...] = curl_in[...]
    flux_y[...] = flux_y_in[...]
    flux_a[...] = flux_a_in[...]

    last = lax.broadcasted_iota(jnp.int32, ez_next.shape, 0) == B - 1
    ez = ez_next[...]
    ez_top = jnp.where(last, ez[0:1], 0.0)
    rr = jnp.concatenate([r2[plane(0)] - ez_top, r2[plane(1)] - ez])
    ss = jnp.concatenate(
        [src2[plane(0)] + (hz_prev[...] * (1.0 / h) - behind_z(ez_top)), src2[plane(1)] - behind_z(ez)]
    )
    x = solve_z(ss, jnp.concatenate([w[top], w[corner]]))
    rise = ahead_z(x)
    mx = rr + rise
    cc = jnp.concatenate([c[top], c[corner]]) * x + behind_z(mx)
    ff = -(mx + rise)
    curl[corner] = cc[B:]
    flux_y[corner] = ff[B:]
    curl[top] = cc[:B]
    flux_y[top] = ff[:B]

    flux_a[plane(B - 1)] = flux_a[plane(B - 1)] - ey_next[...]

    def source_a(j):
        f = flux_a[strided(j)]
        if j > 0:
            f = f - flux_a[strided(j - 1)]
        return part_a[strided(j)] + f

    first_a, last_a = eliminate(source_a, p_y, g_a)
    last_a = last_a - flux_a[strided(B - 1)]

    ((before, after),) = solved_ends(
        me_x, near, far, 1, got_near, got_far, coefs_in(got_near, 2), coefs_in(got_far, 2)
    )
    for i in range(B):
        fz[plane(i)] = g_b[plane(i)] + (u_x[plane(i)] * before + v_x[plane(i)] * after)
    my_before = jnp.where(me_x == 0, 0.0, fz[top] - before)
    for i in range(B):
        here = fz[plane(i)]
        rise = (fz[plane(i + 1)] if i < B - 1 else after) - here
        my = flux_b[plane(i)] + rise
        rise_y[plane(i)] = my + rise
        part[plane(i)] = c[plane(i)] * here + (my - my_before)
        my_before = my

    def source_c(j):
        f = flux_y[strided(j)]
        if j > 0:
            f = f - flux_y[strided(j - 1)]
        return part[strided(j)] + f

    first_c, last_c = eliminate(source_c, p_y, g_c)
    last_c = last_c - flux_y[strided(B - 1)]
    sent = [first_a, last_a, first_c, last_c, u_y[plane(0)], v_y[plane(0)], v_y[plane(B - 1)]]
    for k, value in enumerate(sent):
        msg[plane(k)] = value


def second_x_kernel(near, far, me, got_near, *refs):
    others, refs = refs[:far], refs[far:]
    g_a, u, v, flux_a, c, curl, p_x, part, flux2, g2, ends_c, msg, got_far, fx = refs
    my = me[1]
    collect(lax.div(my, near), others[0], others[1:], got_far)
    (before, after), (before_c, after_c) = solved_ends(
        my, near, far, 2, got_near, got_far, coefs_in(got_near, 4), coefs_in(got_far, 4)
    )
    ends_c[plane(0)] = before_c
    ends_c[plane(1)] = after_c
    for j in range(B):
        fx[plane(j)] = g_a[plane(j)] + (u[plane(j)] * before + v[plane(j)] * after)
    mz_before = jnp.where(my == 0, 0.0, fx[plane(0)] - before)
    for j in range(B):
        here = fx[plane(j)]
        rise = (fx[plane(j + 1)] if j < B - 1 else after) - here
        mz = flux_a[strided(j)] + rise
        part[strided(j)] = c[strided(j)] * here + (mz - mz_before)
        flux2[strided(j)] = -(mz + rise)
        mz_before = mz

    def source(i):
        f = flux2[plane(i)]
        if i > 0:
            f = f - flux2[plane(i - 1)]
        return curl[plane(i)] + f

    first, last = eliminate(source, p_x, g2)
    msg[plane(0)] = first
    msg[plane(1)] = last - flux2[plane(B - 1)]


def second_z_kernel(
    part, rise_y, w, ends_c, g_c, u, v, flux_y, elec, magn, full_x, full_z, new_x, new_y, sems
):
    before, after = ends_c[plane(0)], ends_c[plane(1)]
    here = None
    for j in range(B):
        ahead = g_c[plane(j)] + (u[plane(j)] * before + v[plane(j)] * after)
        full_z[strided(j)] = ahead
        if j > 0:
            new_x[strided(j - 1)] = -h * (flux_y[strided(j - 1)] + (ahead - here))
        here = ahead
    new_x[strided(B - 1)] = -h * (flux_y[strided(B - 1)] + (after - here))
    stores = [(full_z, elec.at[2]), (new_x, magn.at[0]), (full_x, elec.at[0]), (new_y, magn.at[1])]
    stores = [pltpu.make_async_copy(a, b, sems.at[k]) for k, (a, b) in enumerate(stores)]
    stores[0].start()
    stores[1].start()

    def solve(k, carry):
        rows = pl.ds(k * (4 * B), 4 * B)
        a = rise_y[rows]
        x = solve_z(part[rows] - behind_z(a), w[rows])
        full_x[rows] = x
        new_y[rows] = h * (a - ahead_z(x))
        return carry

    lax.fori_loop(0, B // 4, solve, 0)
    stores[2].start()
    stores[3].start()
    for store in stores:
        store.wait()


def last_kernel(near, far, me, coefs_near, coefs_far, got_near, *refs):
    others, refs = refs[:far], refs[far:]
    g, u, v, flux2, _, _, elec, magn, got_far, full_y, new_z, sems = refs
    collect(lax.div(me[0], near), others[0], others[1:], got_far)
    ((before, after),) = solved_ends(
        me[0], near, far, 1, got_near, got_far, coefs_in(coefs_near, 2), coefs_in(coefs_far, 2)
    )
    here = None
    for i in range(B):
        ahead = g[plane(i)] + (u[plane(i)] * before + v[plane(i)] * after)
        full_y[plane(i)] = ahead
        if i > 0:
            new_z[plane(i - 1)] = -h * (flux2[plane(i - 1)] + (ahead - here))
        here = ahead
    new_z[plane(B - 1)] = -h * (flux2[plane(B - 1)] + (after - here))
    stores = [(full_y, elec.at[1]), (new_z, magn.at[2])]
    stores = [pltpu.make_async_copy(a, b, sems.at[k]) for k, (a, b) in enumerate(stores)]
    for store in stores:
        store.start()
    for store in stores:
        store.wait()


VMEM = pl.BlockSpec(memory_space=pltpu.VMEM)
SMEM = pl.BlockSpec(memory_space=pltpu.SMEM)
HBM = pl.BlockSpec(memory_space=pltpu.HBM)


def call(kernel, ins, outs, specs=None, out_specs=None, scratch=(), aliases=None, flops=1_000_000):
    shapes = [pltpu.HBM(s, F32) if out_specs else jax.ShapeDtypeStruct(s, F32) for s in outs]
    return pl.pallas_call(
        kernel,
        out_shape=shapes,
        in_specs=specs or [SMEM] + [VMEM] * (len(ins) - 1),
        out_specs=out_specs or [VMEM] * len(outs),
        scratch_shapes=[pltpu.VMEM(s, F32) if isinstance(s, tuple) else s for s in scratch],
        input_output_aliases=aliases or {},
        compiler_params=pltpu.CompilerParams(vmem_limit_bytes=24 * 1024 * 1024),
        cost_estimate=pl.CostEstimate(flops=flops, bytes_accessed=1_000_000, transcendentals=0),
    )(*ins)


def shared(value, axis, n, step, count):
    others = [
        lax.ppermute(value, axis, [(i, i ^ (step * s)) for i in range(n)]) for s in range(1, count)
    ]
    return [value] + others


def split(n):
    near = 1 << (n.bit_length() // 2)
    return near, n // near


def local(electric, magnetic, material, permittivity, conductivity):
    nx, ny = lax.axis_size("px"), lax.axis_size("py")
    near_x, far_x = split(nx)
    near_y, far_y = split(ny)
    nz = material.shape[2]
    cells = (B * B, nz)
    me = jnp.stack([lax.axis_index("px"), lax.axis_index("py")]).astype(jnp.int32)
    in_hbm = lambda a: pltpu.with_memory_space_constraint(a, pltpu.HBM)
    elec = in_hbm(electric.reshape(3, *cells))
    magn = in_hbm(magnetic.reshape(3, *cells))
    ids = in_hbm(material.reshape(cells))
    dma = pltpu.SemaphoreType.DMA
    down = lambda n: [(i + 1, i) for i in range(n - 1)]
    up = lambda n: [(i, i + 1) for i in range(n - 1)]

    hx_prev = lax.ppermute(magnetic[0, :, B - 1], "py", up(ny))
    w, c, p_x, u_x, v_x, flux_b, part_b = call(
        tables_kernel,
        [me, permittivity, conductivity, ids, elec, magn],
        [cells] * 7,
        specs=[SMEM] * 3 + [HBM] * 3,
        scratch=[pltpu.VMEM(cells, jnp.int32)] + [cells] * 4 + [dma((5,))],
    )
    g_b, msg = call(
        first_x_kernel, [part_b, hx_prev, flux_b, p_x, u_x, v_x], [cells, (5 * B, nz)], specs=[VMEM] * 6
    )
    ins = shared(msg, "px", nx, 1, near_x)
    ey_next = lax.ppermute(electric[1, 0], "px", down(nx))
    hz_prev = lax.ppermute(magnetic[2, B - 1], "px", up(nx))
    ez_next = lax.ppermute(electric[2, :, 0], "py", down(ny))
    near_b, msg = call(
        functools.partial(merge_kernel, 0, near_x, 1), [me] + ins, [(near_x, 5 * B, nz), (5 * B, nz)]
    )
    ins = shared(msg, "px", nx, near_x, far_x)
    p_y, u_y, v_y, r2, src2, curl, flux_y, flux_a, part_a = call(
        first_z_kernel,
        [me, elec, magn, w, c],
        [cells] * 3 + [(2 * B, nz)] * 2 + [cells] * 4,
        specs=[SMEM, HBM, HBM, VMEM, VMEM],
        scratch=[cells] * 2 + [(3, *cells)] * 2 + [dma((2,))],
        flops=8_000_000,
    )
    ins = [me, near_b] + ins + [ey_next, ez_next, hz_prev, g_b, u_x, v_x, flux_b, w, c, r2, src2]
    far_b, rise_y, curl, flux_y, flux_a, g_a, g_c, msg = call(
        functools.partial(both_y_kernel, near_x, far_x),
        ins + [curl, flux_y, flux_a, part_a, p_y, u_y, v_y],
        [(far_x, 5 * B, nz)] + [cells] * 6 + [(7 * B, nz)],
        scratch=[cells] * 2,
    )
    ins = shared(msg, "py", ny, 1, near_y)
    near_ac, msg = call(
        functools.partial(merge_kernel, 1, near_y, 2), [me] + ins, [(near_y, 7 * B, nz), (7 * B, nz)]
    )
    ins = shared(msg, "py", ny, near_y, far_y)
    part_x, flux2, g2, ends_c, msg = call(
        functools.partial(second_x_kernel, near_y, far_y),
        [me, near_ac] + ins + [g_a, u_y, v_y, flux_a, c, curl, p_x],
        [cells] * 3 + [(2 * B, nz)] * 2,
        scratch=[(far_y, 7 * B, nz), cells],
    )
    ins = shared(msg, "px", nx, 1, near_x)
    near_a, msg = call(
        functools.partial(merge_rows_kernel, 0, near_x),
        [me, near_b] + ins,
        [(near_x, 2 * B, nz), (2 * B, nz)],
    )
    ins = shared(msg, "px", nx, near_x, far_x)
    elec, magn = call(
        second_z_kernel,
        [part_x, rise_y, w, ends_c, g_c, u_y, v_y, flux_y],
        [(3, *cells)] * 2,
        specs=[VMEM] * 8,
        out_specs=[HBM] * 2,
        scratch=[cells] * 4 + [dma((4,))],
        flops=8_000_000,
    )
    ins = [me, near_b, far_b, near_a] + ins + [g2, u_x, v_x, flux2]
    at = len(ins)
    out = call(
        functools.partial(last_kernel, near_x, far_x),
        ins + [elec, magn],
        [(3, *cells)] * 2,
        specs=[SMEM] + [VMEM] * (at - 1) + [HBM] * 2,
        out_specs=[HBM] * 2,
        scratch=[(far_x, 2 * B, nz), cells, cells, dma((2,))],
        aliases={at: 0, at + 1: 1},
    )
    return tuple(a.reshape(3, B, B, nz) for a in out)


def solution(mesh):
    placed = (P(None, "px", "py", None), P(None, "px", "py", None), P("px", "py", None), P(), P())
    return jax.shard_map(
        local,
        mesh=mesh,
        in_specs=placed,
        out_specs=(P(None, "px", "py", None), P(None, "px", "py", None)),
        check_vma=False,
    )
```

time: 86.9 us -> 78 us (0.90)
  blocking collectives: 24.9 us -> 0 us
  starting transfers between devices: 24 us -> 44.6 us
  local copies, waits for them, and re-layouts: 8.94 us -> 3.76 us
  Pallas kernels: 15.4 us -> 17.1 us
  waiting for transfers between devices: 12.1 us -> 10.7 us
    ppermute x2 -> x22, starting transfers between devices: 6.93 us -> 44.6 us  [the longest x18 32.2 us: shared(): lax.ppermute(value, axis, [(i, i ^ step * s) for i in range(n)])]
    all_to_all x2 -> x0, blocking collectives: 24.9 us -> none  [local(): lax.all_to_all(msg, 'py', 0, 0, axis_index_groups=groups, tiled=True)]
    all_to_all x2 -> x0, starting transfers between devices: 17.1 us -> none  [the longest x1 11.6 us: local(): got = lax.all_to_all(msg, 'px', 0, 0, tiled=True)]
    unnamed x22 -> x4, local copies, waits for them, and re-layouts: 6.68 us -> 0.67 us
    all_to_all x2 -> x0, waiting for transfers between devices: 3.98 us -> none  [the longest x1 3.97 us: local(): got = lax.all_to_all(msg, 'px', 0, 0, tiled=True)]
    ppermute x2 -> x22, waiting for transfers between devices: 8.14 us -> 10.7 us  [the longest x18 10.7 us: shared(): lax.ppermute(value, axis, [(i, i ^ step * s) for i in range(n)])]
    pallas_call x8 -> x10, Pallas kernels: 15.4 us -> 17.1 us  [call(): pl.pallas_call(kernel, out_shape=shapes, in_specs=specs or [SMEM] + [VMEM...]
  transfers between devices with their start and end apart: 4 -> 22, of which waited for: 2 -> 6; matrix products, arithmetic and copies ran while one was open for 2% -> 3% of each run, Pallas kernels for 11% -> 16%
where the time goes in v3:
time: 78 us; the launch traced here: 77 us
  starting transfers between devices  44.6 us (57%)
  Pallas kernels  17.1 us (22%)
  waiting for transfers between devices  10.7 us (14%)
  local copies, waits for them, and re-layouts  3.76 us (5%)
  between operations  0.82 us (1%)
    ppermute x18, starting transfers between devices, shared(): lax.ppermute(value, axis, [(i, i ^ step * s) for i in range(n)])  32.2 us
    pallas_call x10, Pallas kernels, call(): pl.pallas_call(kernel, out_shape=shapes, in_specs=specs or [SMEM] + [VMEM...  17.1 us
    ppermute x18, waiting for transfers between devices, shared(): lax.ppermute(value, axis, [(i, i ^ step * s) for i in range(n)])  10.7 us
    ppermute x1, starting transfers between devices, local(): hx_prev = lax.ppermute(magnetic[0, :, B - 1], 'py', up(ny))  5.64 us
    ppermute x1, starting transfers between devices, local(): hz_prev = lax.ppermute(magnetic[2, B - 1], 'px', up(nx))  3.26 us
    ppermute x1, starting transfers between devices, local(): ey_next = lax.ppermute(electric[1, 0], 'px', down(nx))  2.22 us
  transfers between devices with their start and end apart: 22, of which 6 were waited for; matrix products, arithmetic and copies ran while one was open for 3% of the time, Pallas kernels for 16%

profile of v3, /device:TPU:1, one launch (start us, length us, event | category | flops | bytes accessed | tf_op | source)
XLA Modules:
  0.0 77.0 jit_solution(15275577793425319588)
XLA Ops:
  1.5 5.6 %collective-permute-start = (f32[16,128]{1,0:T(8,128)S(1)}, f32[16,128]{1,0:T(8,128)S(1)}, u32[]{:S(2)}, u32[]{:S(2)}) collective-permute-start(f32[16,128]{1,0:T(8,128)S(1)} %bitcast.24), channel_id=1, source_target_pairs={{0,1},{1,2},{2,3},{3,4},{4,5},{5,6},{6,7},{7,8},{8,9},{9,10},{10,1... | collective-permute-start | bytes 24584 | tf_op jit(solution)/shard_map/ppermute | solution.py:465
  7.9 1.9 %shard_map.68 = (f32[256,128]{1,0:T(8,128)S(1)}, f32[256,128]{1,0:T(8,128)S(1)}, f32[256,128]{1,0:T(8,128)S(1)}, f32[256,128]{1,0:T(8,128)S(1)}, f32[256,128]{1,...) custom-call(s32[2]{0:T(128)S(1)} %pad_add_fusion.me, f32[8]{0:T(128)S(1)} %copy-done, f32[8]{0:T(128)S(1)} %copy-done.1, ...), custom_call_target="tpu_custom_call" | custom-call | flops 1000000 | bytes 1000000 | tf_op jit(solution)/shard_map/pallas_call | solution.py:426
  9.9 2.1 %collective-permute-start.3 = (f32[80,128]{1,0:T(8,128)S(1)}, f32[80,128]{1,0:T(8,128)S(1)}, u32[]{:S(2)}, u32[]{:S(2)}) collective-permute-start(f32[80,128]{1,0:T(8,128)S(1)} %get-tuple-element.48.refs_0_), channel_id=1, source_target_pairs={{0,48},{16,32},{32,16},{48,0},{64,112},{80,96},{96,80},{112,64},{1... | collective-permute-start | bytes 122888 | tf_op jit(solution)/shard_map/ppermute | solution.py:440
  13.2 3.3 %collective-permute-start.9 = (f32[16,128]{1,0:T(8,128)S(1)}, f32[16,128]{1,0:T(8,128)S(1)}, u32[]{:S(2)}, u32[]{:S(2)}) collective-permute-start(f32[16,128]{1,0:T(8,128)S(1)} %slice_bitcast_fusion), channel_id=1, source_target_pairs={{0,16},{16,32},{32,48},{48,64},{64,80},{80,96},{96,112},{112,128},... | collective-permute-start | bytes 24584 | tf_op jit(solution)/shard_map/ppermute | solution.py:478
  17.1 2.7 %collective-permute-start.6 = (f32[80,128]{1,0:T(8,128)S(1)}, f32[80,128]{1,0:T(8,128)S(1)}, u32[]{:S(2)}, u32[]{:S(2)}) collective-permute-start(f32[80,128]{1,0:T(8,128)S(1)} %get-tuple-element.50.refs_0_), channel_id=1, source_target_pairs={{0,192},{16,208},{32,224},{48,240},{64,128},{80,144},{96,160},{112... | collective-permute-start | bytes 122888 | tf_op jit(solution)/shard_map/ppermute | solution.py:440
  19.7 1.1 %collective-permute-start.5 = (f32[80,128]{1,0:T(8,128)S(1)}, f32[80,128]{1,0:T(8,128)S(1)}, u32[]{:S(2)}, u32[]{:S(2)}) collective-permute-start(f32[80,128]{1,0:T(8,128)S(1)} %get-tuple-element.50.refs_0_), channel_id=1, source_target_pairs={{0,128},{16,144},{32,160},{48,176},{64,192},{80,208},{96,224},{112... | collective-permute-start | bytes 122888 | tf_op jit(solution)/shard_map/ppermute | solution.py:440
  22.0 2.2 %collective-permute-start.7 = (f32[16,128]{1,0:T(8,128)S(1)}, f32[16,128]{1,0:T(8,128)S(1)}, u32[]{:S(2)}, u32[]{:S(2)}) collective-permute-start(f32[16,128]{1,0:T(8,128)S(1)} %slice_bitcast_fusion.1), channel_id=1, source_target_pairs={{16,0},{32,16},{48,32},{64,48},{80,64},{96,80},{112,96},{128,112},... | collective-permute-start | bytes 24584 | tf_op jit(solution)/shard_map/ppermute | solution.py:477
  25.1 1.3 %collective-permute-start.8 = (f32[16,128]{1,0:T(8,128)S(1)}, f32[16,128]{1,0:T(8,128)S(1)}, u32[]{:S(2)}, u32[]{:S(2)}) collective-permute-start(f32[16,128]{1,0:T(8,128)S(1)} %bitcast.25), channel_id=1, source_target_pairs={{1,0},{2,1},{3,2},{4,3},{5,4},{6,5},{7,6},{8,7},{9,8},{10,9},{11,1... | collective-permute-start | bytes 24584 | tf_op jit(solution)/shard_map/ppermute | solution.py:479
  26.4 5.5 %shard_map.71 = (f32[256,128]{1,0:T(8,128)S(1)}, f32[256,128]{1,0:T(8,128)S(1)}, f32[256,128]{1,0:T(8,128)S(1)}, f32[32,128]{1,0:T(8,128)S(1)}, f32[32,128]{1,0:...) custom-call(s32[2]{0:T(128)S(1)} %pad_add_fusion.me, ...), custom_call_target="tpu_custom_call" | custom-call | flops 8000000 | bytes 1000000 | tf_op jit(solution)/shard_map/pallas_call | solution.py:426
  32.0 1.5 %shard_map.72 = (f32[4,80,128]{2,1,0:T(8,128)S(1)}, f32[256,128]{1,0:T(8,128)S(1)}, f32[256,128]{1,0:T(8,128)S(1)}, f32[256,128]{1,0:T(8,128)S(1)}, f32[256,128]...) custom-call(s32[2]{0:T(128)S(1)} %pad_add_fusion.me, ...), custom_call_target="tpu_custom_call" | custom-call | flops 1000000 | bytes 1000000 | tf_op jit(solution)/shard_map/pallas_call | solution.py:426
  33.5 4.9 %collective-permute-start.12 = (f32[112,128]{1,0:T(8,128)S(1)}, f32[112,128]{1,0:T(8,128)S(1)}, u32[]{:S(2)}, u32[]{:S(2)}) collective-permute-start(f32[112,128]{1,0:T(8,128)S(1)} %get-tuple-element.64.refs_0_), channel_id=1, source_target_pairs={{0,3},{1,2},{2,1},{3,0},{4,7},{5,6},{6,5},{7,4},{8,11},{9,10},{10,... | collective-permute-start | bytes 172040 | tf_op jit(solution)/shard_map/ppermute | solution.py:440
  38.4 1.6 %collective-permute-start.10 = (f32[112,128]{1,0:T(8,128)S(1)}, f32[112,128]{1,0:T(8,128)S(1)}, u32[]{:S(2)}, u32[]{:S(2)}) collective-permute-start(f32[112,128]{1,0:T(8,128)S(1)} %get-tuple-element.64.refs_0_), channel_id=1, source_target_pairs={{0,1},{1,0},{2,3},{3,2},{4,5},{5,4},{6,7},{7,6},{8,9},{9,8},{10,11... | collective-permute-start | bytes 172040 | tf_op jit(solution)/shard_map/ppermute | solution.py:440
  40.5 1.5 %collective-permute-done.11.refs_2_ = f32[112,128]{1,0:T(8,128)S(1)} collective-permute-done((f32[112,128]{1,0:T(8,128)S(1)}, f32[112,128]{1,0:T(8,128)S(1)}, u32[]{:S(2)}, u32[]{:S(2)}) %collective-permute-start.11) | collective-permute-done | bytes 57376 | tf_op jit(solution)/shard_map/ppermute | solution.py:440
  43.5 7.1 %collective-permute-start.15 = (f32[112,128]{1,0:T(8,128)S(1)}, f32[112,128]{1,0:T(8,128)S(1)}, u32[]{:S(2)}, u32[]{:S(2)}) collective-permute-start(f32[112,128]{1,0:T(8,128)S(1)} %get-tuple-element.66.refs_0_), channel_id=1, source_target_pairs={{0,12},{1,13},{2,14},{3,15},{4,8},{5,9},{6,10},{7,11},{8,4},{9,5},... | collective-permute-start | bytes 172040 | tf_op jit(solution)/shard_map/ppermute | solution.py:440
  50.5 1.1 %collective-permute-start.14 = (f32[112,128]{1,0:T(8,128)S(1)}, f32[112,128]{1,0:T(8,128)S(1)}, u32[]{:S(2)}, u32[]{:S(2)}) collective-permute-start(f32[112,128]{1,0:T(8,128)S(1)} %get-tuple-element.66.refs_0_), channel_id=1, source_target_pairs={{0,8},{1,9},{2,10},{3,11},{4,12},{5,13},{6,14},{7,15},{8,0},{9,1},... | collective-permute-start | bytes 172040 | tf_op jit(solution)/shard_map/ppermute | solution.py:440
  51.6 1.1 %collective-permute-start.13 = (f32[112,128]{1,0:T(8,128)S(1)}, f32[112,128]{1,0:T(8,128)S(1)}, u32[]{:S(2)}, u32[]{:S(2)}) collective-permute-start(f32[112,128]{1,0:T(8,128)S(1)} %get-tuple-element.66.refs_0_), channel_id=1, source_target_pairs={{0,4},{1,5},{2,6},{3,7},{4,0},{5,1},{6,2},{7,3},{8,12},{9,13},{10,... | collective-permute-start | bytes 172040 | tf_op jit(solution)/shard_map/ppermute | solution.py:440
  52.7 5.6 %collective-permute-done.14.refs_2_ = f32[112,128]{1,0:T(8,128)S(1)} collective-permute-done((f32[112,128]{1,0:T(8,128)S(1)}, f32[112,128]{1,0:T(8,128)S(1)}, u32[]{:S(2)}, u32[]{:S(2)}) %collective-permute-start.14) | collective-permute-done | bytes 57376 | tf_op jit(solution)/shard_map/ppermute | solution.py:440
  59.2 3.9 %collective-permute-start.18 = (f32[32,128]{1,0:T(8,128)S(1)}, f32[32,128]{1,0:T(8,128)S(1)}, u32[]{:S(2)}, u32[]{:S(2)}) collective-permute-start(f32[32,128]{1,0:T(8,128)S(1)} %get-tuple-element.70.refs_0_), channel_id=1, source_target_pairs={{0,48},{16,32},{32,16},{48,0},{64,112},{80,96},{96,80},{112,64},{1... | collective-permute-start | bytes 49160 | tf_op jit(solution)/shard_map/ppermute | solution.py:440
  63.7 1.0 %collective-permute-done.18.refs_3_ = f32[32,128]{1,0:T(8,128)S(1)} collective-permute-done((f32[32,128]{1,0:T(8,128)S(1)}, f32[32,128]{1,0:T(8,128)S(1)}, u32[]{:S(2)}, u32[]{:S(2)}) %collective-permute-start.18) | collective-permute-done | bytes 16416 | tf_op jit(solution)/shard_map/ppermute | solution.py:440
  64.6 1.1 %collective-permute-done.17.refs_2_ = f32[32,128]{1,0:T(8,128)S(1)} collective-permute-done((f32[32,128]{1,0:T(8,128)S(1)}, f32[32,128]{1,0:T(8,128)S(1)}, u32[]{:S(2)}, u32[]{:S(2)}) %collective-permute-start.17) | collective-permute-done | bytes 16416 | tf_op jit(solution)/shard_map/ppermute | solution.py:440
  66.3 3.6 %collective-permute-start.21 = (f32[32,128]{1,0:T(8,128)S(1)}, f32[32,128]{1,0:T(8,128)S(1)}, u32[]{:S(2)}, u32[]{:S(2)}) collective-permute-start(f32[32,128]{1,0:T(8,128)S(1)} %get-tuple-element.72.refs_0_), channel_id=1, source_target_pairs={{0,192},{16,208},{32,224},{48,240},{64,128},{80,144},{96,160},{112... | collective-permute-start | bytes 49160 | tf_op jit(solution)/shard_map/ppermute | solution.py:440
  70.1 1.5 %collective-permute-start.19 = (f32[32,128]{1,0:T(8,128)S(1)}, f32[32,128]{1,0:T(8,128)S(1)}, u32[]{:S(2)}, u32[]{:S(2)}) collective-permute-start(f32[32,128]{1,0:T(8,128)S(1)} %get-tuple-element.72.refs_0_), channel_id=1, source_target_pairs={{0,64},{16,80},{32,96},{48,112},{64,0},{80,16},{96,32},{112,48},{1... | collective-permute-start | bytes 49160 | tf_op jit(solution)/shard_map/ppermute | solution.py:440
  71.6 4.0 %shard_map.76 = (f32[3,256,128]{2,1,0:T(8,128)}, f32[3,256,128]{2,1,0:T(8,128)}) custom-call(f32[256,128]{1,0:T(8,128)S(1)} %get-tuple-element.75.part, f32[256,128]{1,0:T(8,128)S(1)} %get-tuple-element.76.rise_y, f32[256,128]{1,0:T(8,128)S(1)} %get-tuple-element.52.w.refs_11_, f32[32,128]{1,0:T(8,128)S(1)} %get-tuple-element.77.ends_c, ...), custom_call_target="tpu_custom_call" | custom-call | flops 8000000 | bytes 1000000 | tf_op jit(solution)/shard_map/pallas_call | solution.py:426
  75.7 1.4 %shard_map.77 = (f32[3,256,128]{2,1,0:T(8,128)}, f32[3,256,128]{2,1,0:T(8,128)}) custom-call(s32[2]{0:T(128)S(1)} %pad_add_fusion.me, f32[4,80,128]{2,1,0:T(8,128)S(1)} %get-tuple-element.49.got_near.coefs.coefs_near, f32[4,80,128]{2,1,0:T(8,128)S(1)} %get-tuple-element.63.coefs_far, ...), custom_call_target="tpu_custom_call", output_to_operand_aliasing={{0}: (12, {}), {1}: (13, {})} | custom-call | flops 1000000 | bytes 1000000 | tf_op jit(solution)/shard_map/pallas_call | solution.py:426
  (39 shorter events, 9.8 us)
Async XLA Ops:
  1.5 8.3 %collective-permute-start = (f32[16,128]{1,0:T(8,128)S(1)}, f32[16,128]{1,0:T(8,128)S(1)}, u32[]{:S(2)}, u32[]{:S(2)}) collective-permute-start(f32[16,128]{1,0:T(8,128)S(1)} %bitcast.24), channel_id=1, source_target_pairs={{0,1},{1,2},{2,3},{3,4},{4,5},{5,6},{6,7},{7,8},{8,9},{9,10},{10,1... | collective-permute-start | bytes 24584 | tf_op jit(solution)/shard_map/ppermute | solution.py:465
  7.2 0.7 copy-start
  7.2 0.7 copy-start.1
  9.9 6.6 %collective-permute-start.3 = (f32[80,128]{1,0:T(8,128)S(1)}, f32[80,128]{1,0:T(8,128)S(1)}, u32[]{:S(2)}, u32[]{:S(2)}) collective-permute-start(f32[80,128]{1,0:T(8,128)S(1)} %get-tuple-element.48.refs_0_), channel_id=1, source_target_pairs={{0,48},{16,32},{32,16},{48,0},{64,112},{80,96},{96,80},{112,64},{1... | collective-permute-start | bytes 122888 | tf_op jit(solution)/shard_map/ppermute | solution.py:440
  12.0 4.5 %collective-permute-start.2 = (f32[80,128]{1,0:T(8,128)S(1)}, f32[80,128]{1,0:T(8,128)S(1)}, u32[]{:S(2)}, u32[]{:S(2)}) collective-permute-start(f32[80,128]{1,0:T(8,128)S(1)} %get-tuple-element.48.refs_0_), channel_id=1, source_target_pairs={{0,32},{16,48},{32,0},{48,16},{64,96},{80,112},{96,64},{112,80},{1... | collective-permute-start | bytes 122888 | tf_op jit(solution)/shard_map/ppermute | solution.py:440
  12.2 4.2 %collective-permute-start.1 = (f32[80,128]{1,0:T(8,128)S(1)}, f32[80,128]{1,0:T(8,128)S(1)}, u32[]{:S(2)}, u32[]{:S(2)}) collective-permute-start(f32[80,128]{1,0:T(8,128)S(1)} %get-tuple-element.48.refs_0_), channel_id=1, source_target_pairs={{0,16},{16,0},{32,48},{48,32},{64,80},{80,64},{96,112},{112,96},{1... | collective-permute-start | bytes 122888 | tf_op jit(solution)/shard_map/ppermute | solution.py:440
  13.2 11.9 %collective-permute-start.9 = (f32[16,128]{1,0:T(8,128)S(1)}, f32[16,128]{1,0:T(8,128)S(1)}, u32[]{:S(2)}, u32[]{:S(2)}) collective-permute-start(f32[16,128]{1,0:T(8,128)S(1)} %slice_bitcast_fusion), channel_id=1, source_target_pairs={{0,16},{16,32},{32,48},{48,64},{64,80},{80,96},{96,112},{112,128},... | collective-permute-start | bytes 24584 | tf_op jit(solution)/shard_map/ppermute | solution.py:478
  17.1 14.9 %collective-permute-start.6 = (f32[80,128]{1,0:T(8,128)S(1)}, f32[80,128]{1,0:T(8,128)S(1)}, u32[]{:S(2)}, u32[]{:S(2)}) collective-permute-start(f32[80,128]{1,0:T(8,128)S(1)} %get-tuple-element.50.refs_0_), channel_id=1, source_target_pairs={{0,192},{16,208},{32,224},{48,240},{64,128},{80,144},{96,160},{112... | collective-permute-start | bytes 122888 | tf_op jit(solution)/shard_map/ppermute | solution.py:440
  19.7 12.2 %collective-permute-start.5 = (f32[80,128]{1,0:T(8,128)S(1)}, f32[80,128]{1,0:T(8,128)S(1)}, u32[]{:S(2)}, u32[]{:S(2)}) collective-permute-start(f32[80,128]{1,0:T(8,128)S(1)} %get-tuple-element.50.refs_0_), channel_id=1, source_target_pairs={{0,128},{16,144},{32,160},{48,176},{64,192},{80,208},{96,224},{112... | collective-permute-start | bytes 122888 | tf_op jit(solution)/shard_map/ppermute | solution.py:440
  20.8 11.2 %collective-permute-start.4 = (f32[80,128]{1,0:T(8,128)S(1)}, f32[80,128]{1,0:T(8,128)S(1)}, u32[]{:S(2)}, u32[]{:S(2)}) collective-permute-start(f32[80,128]{1,0:T(8,128)S(1)} %get-tuple-element.50.refs_0_), channel_id=1, source_target_pairs={{0,64},{16,80},{32,96},{48,112},{64,0},{80,16},{96,32},{112,48},{1... | collective-permute-start | bytes 122888 | tf_op jit(solution)/shard_map/ppermute | solution.py:440
  22.0 9.9 %collective-permute-start.7 = (f32[16,128]{1,0:T(8,128)S(1)}, f32[16,128]{1,0:T(8,128)S(1)}, u32[]{:S(2)}, u32[]{:S(2)}) collective-permute-start(f32[16,128]{1,0:T(8,128)S(1)} %slice_bitcast_fusion.1), channel_id=1, source_target_pairs={{16,0},{32,16},{48,32},{64,48},{80,64},{96,80},{112,96},{128,112},... | collective-permute-start | bytes 24584 | tf_op jit(solution)/shard_map/ppermute | solution.py:477
  25.1 6.8 %collective-permute-start.8 = (f32[16,128]{1,0:T(8,128)S(1)}, f32[16,128]{1,0:T(8,128)S(1)}, u32[]{:S(2)}, u32[]{:S(2)}) collective-permute-start(f32[16,128]{1,0:T(8,128)S(1)} %bitcast.25), channel_id=1, source_target_pairs={{1,0},{2,1},{3,2},{4,3},{5,4},{6,5},{7,6},{8,7},{9,8},{10,9},{11,1... | collective-permute-start | bytes 24584 | tf_op jit(solution)/shard_map/ppermute | solution.py:479
  33.5 7.0 %collective-permute-start.12 = (f32[112,128]{1,0:T(8,128)S(1)}, f32[112,128]{1,0:T(8,128)S(1)}, u32[]{:S(2)}, u32[]{:S(2)}) collective-permute-start(f32[112,128]{1,0:T(8,128)S(1)} %get-tuple-element.64.refs_0_), channel_id=1, source_target_pairs={{0,3},{1,2},{2,1},{3,0},{4,7},{5,6},{6,5},{7,4},{8,11},{9,10},{10,... | collective-permute-start | bytes 172040 | tf_op jit(solution)/shard_map/ppermute | solution.py:440
  38.4 3.6 %collective-permute-start.11 = (f32[112,128]{1,0:T(8,128)S(1)}, f32[112,128]{1,0:T(8,128)S(1)}, u32[]{:S(2)}, u32[]{:S(2)}) collective-permute-start(f32[112,128]{1,0:T(8,128)S(1)} %get-tuple-element.64.refs_0_), channel_id=1, source_target_pairs={{0,2},{1,3},{2,0},{3,1},{4,6},{5,7},{6,4},{7,5},{8,10},{9,11},{10,... | collective-permute-start | bytes 172040 | tf_op jit(solution)/shard_map/ppermute | solution.py:440
  38.4 4.5 %collective-permute-start.10 = (f32[112,128]{1,0:T(8,128)S(1)}, f32[112,128]{1,0:T(8,128)S(1)}, u32[]{:S(2)}, u32[]{:S(2)}) collective-permute-start(f32[112,128]{1,0:T(8,128)S(1)} %get-tuple-element.64.refs_0_), channel_id=1, source_target_pairs={{0,1},{1,0},{2,3},{3,2},{4,5},{5,4},{6,7},{7,6},{8,9},{9,8},{10,11... | collective-permute-start | bytes 172040 | tf_op jit(solution)/shard_map/ppermute | solution.py:440
  43.5 9.2 %collective-permute-start.15 = (f32[112,128]{1,0:T(8,128)S(1)}, f32[112,128]{1,0:T(8,128)S(1)}, u32[]{:S(2)}, u32[]{:S(2)}) collective-permute-start(f32[112,128]{1,0:T(8,128)S(1)} %get-tuple-element.66.refs_0_), channel_id=1, source_target_pairs={{0,12},{1,13},{2,14},{3,15},{4,8},{5,9},{6,10},{7,11},{8,4},{9,5},... | collective-permute-start | bytes 172040 | tf_op jit(solution)/shard_map/ppermute | solution.py:440
  50.5 7.7 %collective-permute-start.14 = (f32[112,128]{1,0:T(8,128)S(1)}, f32[112,128]{1,0:T(8,128)S(1)}, u32[]{:S(2)}, u32[]{:S(2)}) collective-permute-start(f32[112,128]{1,0:T(8,128)S(1)} %get-tuple-element.66.refs_0_), channel_id=1, source_target_pairs={{0,8},{1,9},{2,10},{3,11},{4,12},{5,13},{6,14},{7,15},{8,0},{9,1},... | collective-permute-start | bytes 172040 | tf_op jit(solution)/shard_map/ppermute | solution.py:440
  51.6 6.7 %collective-permute-start.13 = (f32[112,128]{1,0:T(8,128)S(1)}, f32[112,128]{1,0:T(8,128)S(1)}, u32[]{:S(2)}, u32[]{:S(2)}) collective-permute-start(f32[112,128]{1,0:T(8,128)S(1)} %get-tuple-element.66.refs_0_), channel_id=1, source_target_pairs={{0,4},{1,5},{2,6},{3,7},{4,0},{5,1},{6,2},{7,3},{8,12},{9,13},{10,... | collective-permute-start | bytes 172040 | tf_op jit(solution)/shard_map/ppermute | solution.py:440
  59.2 5.4 %collective-permute-start.18 = (f32[32,128]{1,0:T(8,128)S(1)}, f32[32,128]{1,0:T(8,128)S(1)}, u32[]{:S(2)}, u32[]{:S(2)}) collective-permute-start(f32[32,128]{1,0:T(8,128)S(1)} %get-tuple-element.70.refs_0_), channel_id=1, source_target_pairs={{0,48},{16,32},{32,16},{48,0},{64,112},{80,96},{96,80},{112,64},{1... | collective-permute-start | bytes 49160 | tf_op jit(solution)/shard_map/ppermute | solution.py:440
  63.2 2.6 %collective-permute-start.17 = (f32[32,128]{1,0:T(8,128)S(1)}, f32[32,128]{1,0:T(8,128)S(1)}, u32[]{:S(2)}, u32[]{:S(2)}) collective-permute-start(f32[32,128]{1,0:T(8,128)S(1)} %get-tuple-element.70.refs_0_), channel_id=1, source_target_pairs={{0,32},{16,48},{32,0},{48,16},{64,96},{80,112},{96,64},{112,80},{1... | collective-permute-start | bytes 49160 | tf_op jit(solution)/shard_map/ppermute | solution.py:440
  63.2 2.5 %collective-permute-start.16 = (f32[32,128]{1,0:T(8,128)S(1)}, f32[32,128]{1,0:T(8,128)S(1)}, u32[]{:S(2)}, u32[]{:S(2)}) collective-permute-start(f32[32,128]{1,0:T(8,128)S(1)} %get-tuple-element.70.refs_0_), channel_id=1, source_target_pairs={{0,16},{16,0},{32,48},{48,32},{64,80},{80,64},{96,112},{112,96},{1... | collective-permute-start | bytes 49160 | tf_op jit(solution)/shard_map/ppermute | solution.py:440
  66.3 9.3 %collective-permute-start.21 = (f32[32,128]{1,0:T(8,128)S(1)}, f32[32,128]{1,0:T(8,128)S(1)}, u32[]{:S(2)}, u32[]{:S(2)}) collective-permute-start(f32[32,128]{1,0:T(8,128)S(1)} %get-tuple-element.72.refs_0_), channel_id=1, source_target_pairs={{0,192},{16,208},{32,224},{48,240},{64,128},{80,144},{96,160},{112... | collective-permute-start | bytes 49160 | tf_op jit(solution)/shard_map/ppermute | solution.py:440
  69.9 5.7 %collective-permute-start.20 = (f32[32,128]{1,0:T(8,128)S(1)}, f32[32,128]{1,0:T(8,128)S(1)}, u32[]{:S(2)}, u32[]{:S(2)}) collective-permute-start(f32[32,128]{1,0:T(8,128)S(1)} %get-tuple-element.72.refs_0_), channel_id=1, source_target_pairs={{0,128},{16,144},{32,160},{48,176},{64,192},{80,208},{96,224},{112... | collective-permute-start | bytes 49160 | tf_op jit(solution)/shard_map/ppermute | solution.py:440
  70.1 5.6 %collective-permute-start.19 = (f32[32,128]{1,0:T(8,128)S(1)}, f32[32,128]{1,0:T(8,128)S(1)}, u32[]{:S(2)}, u32[]{:S(2)}) collective-permute-start(f32[32,128]{1,0:T(8,128)S(1)} %get-tuple-element.72.refs_0_), channel_id=1, source_target_pairs={{0,64},{16,80},{32,96},{48,112},{64,0},{80,16},{96,32},{112,48},{1... | collective-permute-start | bytes 49160 | tf_op jit(solution)/shard_map/ppermute | solution.py:440

commit v4 on v3

--- a/solution.py
+++ b/solution.py
@@ -123,12 +123,12 @@
     step = 1
     while step < n:
         inv = 1.0 / (s + (l + e))
-        kl = l * pltpu.roll(inv, step, 1)
-        kr = e * pltpu.roll(inv, n - step, 1)
-        r = r + (kl * pltpu.roll(r, step, 1) + kr * pltpu.roll(r, n - step, 1))
-        s = s + (kl * pltpu.roll(s, step, 1) + kr * pltpu.roll(s, n - step, 1))
-        l = kl * pltpu.roll(l, step, 1)
-        e = kr * pltpu.roll(e, n - step, 1)
+        a, b = e * inv, l * inv
+        r = r + (pltpu.roll(a * r, step, 1) + pltpu.roll(b * r, n - step, 1))
+        s = s + (pltpu.roll(a * s, step, 1) + pltpu.roll(b * s, n - step, 1))
+        g = a * l
+        if 2 * step < n:
+            e, l = pltpu.roll(g, n - step, 1), pltpu.roll(g, step, 1)
         step *= 2
     return r / s
 
@@ -148,15 +148,19 @@
 
 
 def tables_kernel(
-    me, eps, sig, material, elec, magn, w, c, p, u, v, flux, part, ids, ex, ez, hx, hy, sems
+    me, eps_in, sig_in, material, elec_in, magn_in, w, c, p, u, v, flux, part, elec, magn, ez_first, ids, eps, sig, sems
 ):
-    loads = [(material, ids), (elec.at[0], ex), (magn.at[1], hy), (elec.at[2], ez), (magn.at[0], hx)]
+    loads = [(eps_in, eps), (sig_in, sig), (material, ids)]
+    for field, to, k in ((elec_in, elec, 0), (magn_in, magn, 1), (elec_in, elec, 2), (magn_in, magn, 0)):
+        loads.append((field.at[k], to.at[k]))
+    loads += [(elec_in.at[1], elec.at[1]), (magn_in.at[2], magn.at[2])]
     loads = [pltpu.make_async_copy(a, b, sems.at[k]) for k, (a, b) in enumerate(loads)]
     for load in loads:
         load.start()
+    for load in loads[:3]:
+        load.wait()
     ws = [eps[m] * (1.0 / (h * h)) + sig[m] * (0.5 / h) for m in range(eps.shape[0])]
     cs = [eps[m] * (1.0 / (h * h)) - sig[m] * (0.5 / h) for m in range(eps.shape[0])]
-    loads[0].wait()
     for i in range(B):
         cell = ids[plane(i)]
         wi = jnp.full(cell.shape, ws[0], F32)
@@ -167,20 +171,23 @@
         w[plane(i)] = wi
         c[plane(i)] = ci
     factor(lambda i: w[plane(i)], me[0] == 0, p, u, v)
-    for load in loads[1:]:
+    for load in loads[3:7]:
         load.wait()
     row = lax.broadcasted_iota(jnp.int32, (B, w.shape[1]), 0)
     for i in range(B):
-        q = hy[plane(i)] * (1.0 / h) - ahead_z(ex[plane(i)])
+        q = magn[1, plane(i)] * (1.0 / h) - ahead_z(elec[0, plane(i)])
         flux[plane(i)] = q
         if i > 0:
             q = q - flux[plane(i - 1)]
-        here = hx[plane(i)]
+        here = magn[0, plane(i)]
         before = jnp.where(row == 0, 0.0, pltpu.roll(here, 1, 0))
-        part[plane(i)] = c[plane(i)] * ez[plane(i)] + (q - (here - before) * (1.0 / h))
-
-
-def first_x_kernel(part, hx_prev, flux, p, u, v, g, msg):
+        part[plane(i)] = c[plane(i)] * elec[2, plane(i)] + (q - (here - before) * (1.0 / h))
+    ez_first[...] = elec.at[2][strided(0)]
+    for load in loads[7:]:
+        load.wait()
+
+
+def first_x_kernel(part, hx_prev, flux, p, u, v, elec, magn, g, msg):
     row = lax.broadcasted_iota(jnp.int32, hx_prev.shape, 0)
 
     def source(i):
@@ -192,9 +199,11 @@
     msg[plane(2)] = u[plane(0)]
     msg[plane(3)] = v[plane(0)]
     msg[plane(4)] = v[plane(B - 1)]
-
-
-def merge_kernel(axis, near, sources, me, *refs):
+    msg[plane(5)] = elec[1, plane(0)]
+    msg[plane(6)] = magn[2, plane(B - 1)]
+
+
+def merge_kernel(axis, near, sources, halos, me, *refs):
     got, msg = refs[-2:]
     collect(lax.rem(me[axis], near), refs[0], refs[1:near], got)
     rows_of, coef_of = rows_in(got, sources), coefs_in(got, 2 * sources)
@@ -204,6 +213,9 @@
     coefs, rows = blocks[0]
     for k, value in enumerate([v for pair in rows for v in pair] + list(coefs)):
         msg[plane(k)] = value
+    if halos:
+        msg[plane(5)] = got[0, plane(5)]
+        msg[plane(6)] = got[near - 1, plane(6)]
 
 
 def merge_rows_kernel(axis, near, me, coefs, *refs):
@@ -224,13 +236,8 @@
     return boundary(lax.rem(here, near), near, rows_in(got_near, sources), coefs_near, outer)
 
 
-def first_z_kernel(me, elec, magn, w, c, p, u, v, r2, src2, curl, flux_y, flux_a, part_a, src, r, ef, mf, sems):
-    loads = [pltpu.make_async_copy(elec, ef, sems.at[0]), pltpu.make_async_copy(magn, mf, sems.at[1])]
-    for load in loads:
-        load.start()
+def first_z_kernel(me, ef, mf, w, c, p, u, v, r2, src2, curl, flux_y, flux_a, part_a, src, r):
     factor(lambda j: w[strided(j)], me[1] == 0, p, u, v)
-    for load in loads:
-        load.wait()
     row = lax.broadcasted_iota(jnp.int32, (B, w.shape[1]), 0)
     for i in range(B):
         ez = ef[2, plane(i)]
@@ -250,26 +257,31 @@
         two[plane(0)] = of[plane(0)]
         two[plane(1)] = of[strided(B - 1)]
 
-    def solve(k, carry):
-        rows = pl.ds(k * (4 * B), 4 * B)
-        x = solve_z(src[rows], w[rows])
-        rise = ahead_z(x)
-        mx = r[rows] + rise
-        curl[rows] = c[rows] * x + behind_z(mx)
-        flux_y[rows] = -(mx + rise)
-        return carry
-
-    lax.fori_loop(0, B // 4, solve, 0)
+    x = solve_z(src[...], w[...])
+    rise = ahead_z(x)
+    mx = r[...] + rise
+    curl[...] = c[...] * x + behind_z(mx)
+    flux_y[...] = -(mx + rise)
 
 
 def both_y_kernel(near, far, me, got_near, *refs):
     others, refs = refs[:far], refs[far:]
-    (ey_next, ez_next, hz_prev, g_b, u_x, v_x, flux_b, w, c, r2, src2, curl_in, flux_y_in, flux_a_in, part_a, p_y, u_y, v_y) = refs[:18]
-    got_far, rise_y, curl, flux_y, flux_a, g_a, g_c, msg, part, fz = refs[18:]
+    (ez_next, g_b, u_x, v_x, flux_b, w, c, r2, src2, curl_in, flux_y_in, flux_a_in, part_a, p_y, u_y, v_y) = refs[:16]
+    got_far, rise_y, curl, flux_y, flux_a, g_a, g_c, msg, part, fz = refs[16:]
     me_x = me[0]
     top, corner = plane(0), strided(B - 1)
-    collect(lax.div(me_x, near), others[0], others[1:], got_far)
-
+    q, r = lax.div(me_x, near), lax.rem(me_x, near)
+    collect(q, others[0], others[1:], got_far)
+    ey_next = jnp.where(
+        r < near - 1,
+        got_near[jnp.minimum(r + 1, near - 1), plane(5)],
+        jnp.where(q < far - 1, got_far[jnp.minimum(q + 1, far - 1), plane(5)], 0.0),
+    )
+    hz_prev = jnp.where(
+        r > 0,
+        got_near[jnp.maximum(r - 1, 0), plane(6)],
+        jnp.where(q > 0, got_far[jnp.maximum(q - 1, 0), plane(6)], 0.0),
+    )
     curl[...] = curl_in[...]
     flux_y[...] = flux_y_in[...]
     flux_a[...] = flux_a_in[...]
@@ -279,7 +291,7 @@
     ez_top = jnp.where(last, ez[0:1], 0.0)
     rr = jnp.concatenate([r2[plane(0)] - ez_top, r2[plane(1)] - ez])
     ss = jnp.concatenate(
-        [src2[plane(0)] + (hz_prev[...] * (1.0 / h) - behind_z(ez_top)), src2[plane(1)] - behind_z(ez)]
+        [src2[plane(0)] + (hz_prev * (1.0 / h) - behind_z(ez_top)), src2[plane(1)] - behind_z(ez)]
     )
     x = solve_z(ss, jnp.concatenate([w[top], w[corner]]))
     rise = ahead_z(x)
@@ -291,7 +303,7 @@
     curl[top] = cc[:B]
     flux_y[top] = ff[:B]
 
-    flux_a[plane(B - 1)] = flux_a[plane(B - 1)] - ey_next[...]
+    flux_a[plane(B - 1)] = flux_a[plane(B - 1)] - ey_next
 
     def source_a(j):
         f = flux_a[strided(j)]
@@ -378,15 +390,10 @@
     stores[0].start()
     stores[1].start()
 
-    def solve(k, carry):
-        rows = pl.ds(k * (4 * B), 4 * B)
-        a = rise_y[rows]
-        x = solve_z(part[rows] - behind_z(a), w[rows])
-        full_x[rows] = x
-        new_y[rows] = h * (a - ahead_z(x))
-        return carry
-
-    lax.fori_loop(0, B // 4, solve, 0)
+    a = rise_y[...]
+    x = solve_z(part[...] - behind_z(a), w[...])
+    full_x[...] = x
+    new_y[...] = h * (a - ahead_z(x))
     stores[2].start()
     stores[3].start()
     for store in stores:
@@ -400,18 +407,15 @@
     ((before, after),) = solved_ends(
         me[0], near, far, 1, got_near, got_far, coefs_in(coefs_near, 2), coefs_in(coefs_far, 2)
     )
-    here = None
-    for i in range(B):
-        ahead = g[plane(i)] + (u[plane(i)] * before + v[plane(i)] * after)
-        full_y[plane(i)] = ahead
-        if i > 0:
-            new_z[plane(i - 1)] = -h * (flux2[plane(i - 1)] + (ahead - here))
-        here = ahead
-    new_z[plane(B - 1)] = -h * (flux2[plane(B - 1)] + (after - here))
     stores = [(full_y, elec.at[1]), (new_z, magn.at[2])]
     stores = [pltpu.make_async_copy(a, b, sems.at[k]) for k, (a, b) in enumerate(stores)]
-    for store in stores:
-        store.start()
+    for i in range(B):
+        full_y[plane(i)] = g[plane(i)] + (u[plane(i)] * before + v[plane(i)] * after)
+    stores[0].start()
+    for i in range(B):
+        rise = (full_y[plane(i + 1)] if i < B - 1 else after) - full_y[plane(i)]
+        new_z[plane(i)] = -h * (flux2[plane(i)] + rise)
+    stores[1].start()
     for store in stores:
         store.wait()
 
@@ -435,11 +439,11 @@
     )(*ins)
 
 
-def shared(value, axis, n, step, count):
-    others = [
-        lax.ppermute(value, axis, [(i, i ^ (step * s)) for i in range(n)]) for s in range(1, count)
-    ]
-    return [value] + others
+def shared(value, axis, n, step, count, order):
+    got = {
+        s: lax.ppermute(value, axis, [(i, i ^ (step * s)) for i in range(n)]) for s in order if s < count
+    }
+    return [value] + [got[s] for s in range(1, count)]
 
 
 def split(n):
@@ -459,61 +463,62 @@
     magn = in_hbm(magnetic.reshape(3, *cells))
     ids = in_hbm(material.reshape(cells))
     dma = pltpu.SemaphoreType.DMA
-    down = lambda n: [(i + 1, i) for i in range(n - 1)]
-    up = lambda n: [(i, i + 1) for i in range(n - 1)]
-
-    hx_prev = lax.ppermute(magnetic[0, :, B - 1], "py", up(ny))
-    w, c, p_x, u_x, v_x, flux_b, part_b = call(
+    px_near, px_far, py_near, py_far = (1, 2, 3), (2, 1, 3), (2, 3, 1), (1, 3, 2)
+
+    hx_prev = lax.ppermute(magnetic[0, :, B - 1], "py", [(i, i + 1) for i in range(ny - 1)])
+    w, c, p_x, u_x, v_x, flux_b, part_b, ef, mf, ez_first = call(
         tables_kernel,
-        [me, permittivity, conductivity, ids, elec, magn],
-        [cells] * 7,
-        specs=[SMEM] * 3 + [HBM] * 3,
-        scratch=[pltpu.VMEM(cells, jnp.int32)] + [cells] * 4 + [dma((5,))],
+        [me, in_hbm(permittivity), in_hbm(conductivity), ids, elec, magn],
+        [cells] * 7 + [(3, *cells)] * 2 + [(B, nz)],
+        specs=[SMEM] + [HBM] * 5,
+        scratch=[pltpu.VMEM(cells, jnp.int32)] + [pltpu.SMEM(permittivity.shape, F32)] * 2 + [dma((9,))],
     )
     g_b, msg = call(
-        first_x_kernel, [part_b, hx_prev, flux_b, p_x, u_x, v_x], [cells, (5 * B, nz)], specs=[VMEM] * 6
-    )
-    ins = shared(msg, "px", nx, 1, near_x)
-    ey_next = lax.ppermute(electric[1, 0], "px", down(nx))
-    hz_prev = lax.ppermute(magnetic[2, B - 1], "px", up(nx))
-    ez_next = lax.ppermute(electric[2, :, 0], "py", down(ny))
+        first_x_kernel,
+        [part_b, hx_prev, flux_b, p_x, u_x, v_x, ef, mf],
+        [cells, (7 * B, nz)],
+        specs=[VMEM] * 8,
+    )
+    ins = shared(msg, "px", nx, 1, near_x, px_near)
+    ez_next = lax.ppermute(ez_first, "py", [(i + 1, i) for i in range(ny - 1)])
     near_b, msg = call(
-        functools.partial(merge_kernel, 0, near_x, 1), [me] + ins, [(near_x, 5 * B, nz), (5 * B, nz)]
-    )
-    ins = shared(msg, "px", nx, near_x, far_x)
+        functools.partial(merge_kernel, 0, near_x, 1, True),
+        [me] + ins,
+        [(near_x, 7 * B, nz), (7 * B, nz)],
+    )
+    ins = shared(msg, "px", nx, near_x, far_x, px_far)
     p_y, u_y, v_y, r2, src2, curl, flux_y, flux_a, part_a = call(
         first_z_kernel,
-        [me, elec, magn, w, c],
+        [me, ef, mf, w, c],
         [cells] * 3 + [(2 * B, nz)] * 2 + [cells] * 4,
-        specs=[SMEM, HBM, HBM, VMEM, VMEM],
-        scratch=[cells] * 2 + [(3, *cells)] * 2 + [dma((2,))],
+        scratch=[cells] * 2,
         flops=8_000_000,
     )
-    ins = [me, near_b] + ins + [ey_next, ez_next, hz_prev, g_b, u_x, v_x, flux_b, w, c, r2, src2]
+    ins = [me, near_b] + ins + [ez_next, g_b, u_x, v_x, flux_b, w, c, r2, src2]
     far_b, rise_y, curl, flux_y, flux_a, g_a, g_c, msg = call(
         functools.partial(both_y_kernel, near_x, far_x),
         ins + [curl, flux_y, flux_a, part_a, p_y, u_y, v_y],
-        [(far_x, 5 * B, nz)] + [cells] * 6 + [(7 * B, nz)],
+        [(far_x, 7 * B, nz)] + [cells] * 6 + [(7 * B, nz)],
         scratch=[cells] * 2,
     )
-    ins = shared(msg, "py", ny, 1, near_y)
+    ins = shared(msg, "py", ny, 1, near_y, py_near)
     near_ac, msg = call(
-        functools.partial(merge_kernel, 1, near_y, 2), [me] + ins, [(near_y, 7 * B, nz), (7 * B, nz)]
-    )
-    ins = shared(msg, "py", ny, near_y, far_y)
+        functools.partial(merge_kernel, 1, near_y, 2, False), [me] + ins, [(near_y, 7 * B, nz), (7 * B, nz)]
+    )
+    ins = shared(msg, "py", ny, near_y, far_y, py_far)
     part_x, flux2, g2, ends_c, msg = call(
         functools.partial(second_x_kernel, near_y, far_y),
         [me, near_ac] + ins + [g_a, u_y, v_y, flux_a, c, curl, p_x],
         [cells] * 3 + [(2 * B, nz)] * 2,
         scratch=[(far_y, 7 * B, nz), cells],
     )
-    ins = shared(msg, "px", nx, 1, near_x)
+    ins = shared(msg, "px", nx, 1, near_x, px_near)
     near_a, msg = call(
         functools.partial(merge_rows_kernel, 0, near_x),
         [me, near_b] + ins,
         [(near_x, 2 * B, nz), (2 * B, nz)],
     )
-    ins = shared(msg, "px", nx, near_x, far_x)
+    ins = shared(msg, "px", nx, near_x, far_x, px_far)
     elec, magn = call(
         second_z_kernel,
         [part_x, rise_y, w, ends_c, g_c, u_y, v_y, flux_y],

time: 78 us -> 71 us (0.910)
  waiting for transfers between devices: 10.7 us -> 17.8 us
  starting transfers between devices: 44.6 us -> 38.3 us
  Pallas kernels: 17.1 us -> 12.8 us
  local copies, waits for them, and re-layouts: 3.76 us -> 0.85 us
    ppermute x4 -> x2, starting transfers between devices: 12.4 us -> 6.92 us  [the longest x1 5.64 us: local(): lax.ppermute(magnetic[0, :, B - 1], 'py', [(i, i + 1) for i in range(ny -...]
    ppermute x18, waiting for transfers between devices: 10.7 us -> 15.8 us  [shared(): lax.ppermute(value, axis, [(i, i ^ step * s) for i in range(n)])]
    pallas_call x10, Pallas kernels: 17.1 us -> 12.8 us  [call(): pl.pallas_call(kernel, out_shape=shapes, in_specs=specs or [SMEM] + [VMEM...]
    ppermute x4 -> x2, waiting for transfers between devices: 0.01 us -> 2.05 us  [the longest x1 2.05 us: local(): ez_next = lax.ppermute(ez_first, 'py', [(i + 1, i) for i in range(ny - 1)])]
    squeeze x2 -> x0, local copies, waits for them, and re-layouts: 1.39 us -> none  [the longest x1 0.7 us: local(): hz_prev = lax.ppermute(magnetic[2, B - 1], 'px', up(nx))]
    slice x2 -> x1, local copies, waits for them, and re-layouts: 1.7 us -> 0.85 us  [local(): magnetic[0, :, B - 1]]
    ppermute x18, starting transfers between devices: 32.2 us -> 31.4 us  [shared(): lax.ppermute(value, axis, [(i, i ^ step * s) for i in range(n)])]
  transfers between devices with their start and end apart: 22 -> 20, of which waited for: 6 -> 10; matrix products, arithmetic and copies ran while one was open for 3% -> 0% of each run, Pallas kernels for 16% -> 10%
where the time goes in v4:
time: 71 us; the launch traced here: 70.7 us
  starting transfers between devices  38.3 us (54%)
  waiting for transfers between devices  17.8 us (25%)
  Pallas kernels  12.8 us (18%)
  between operations  0.9 us (1%)
  local copies, waits for them, and re-layouts  0.85 us (1%)
    ppermute x18, starting transfers between devices, shared(): lax.ppermute(value, axis, [(i, i ^ step * s) for i in range(n)])  31.4 us
    ppermute x18, waiting for transfers between devices, shared(): lax.ppermute(value, axis, [(i, i ^ step * s) for i in range(n)])  15.8 us
    pallas_call x10, Pallas kernels, call(): pl.pallas_call(kernel, out_shape=shapes, in_specs=specs or [SMEM] + [VMEM...  12.8 us
    ppermute x1, starting transfers between devices, local(): lax.ppermute(magnetic[0, :, B - 1], 'py', [(i, i + 1) for i in range(ny -...  5.64 us
    ppermute x1, waiting for transfers between devices, local(): ez_next = lax.ppermute(ez_first, 'py', [(i + 1, i) for i in range(ny - 1)])  2.05 us
  transfers between devices with their start and end apart: 20, of which 10 were waited for; matrix products, arithmetic and copies ran while one was open for 0% of the time, Pallas kernels for 10%

profile of v4, /device:TPU:1, one launch (start us, length us, event | category | flops | bytes accessed | tf_op | source)
XLA Modules:
  0.0 70.7 jit_solution(466910915092693533)
XLA Ops:
  1.5 5.6 %collective-permute-start = (f32[16,128]{1,0:T(8,128)S(1)}, f32[16,128]{1,0:T(8,128)S(1)}, u32[]{:S(2)}, u32[]{:S(2)}) collective-permute-start(f32[16,128]{1,0:T(8,128)S(1)} %bitcast.15), channel_id=1, source_target_pairs={{0,1},{1,2},{2,3},{3,4},{4,5},{5,6},{6,7},{7,8},{8,9},{9,10},{10,1... | collective-permute-start | bytes 24584 | tf_op jit(solution)/shard_map/ppermute | solution.py:468
  7.2 1.9 %shard_map.68 = (f32[256,128]{1,0:T(8,128)S(1)}, f32[256,128]{1,0:T(8,128)S(1)}, f32[256,128]{1,0:T(8,128)S(1)}, f32[256,128]{1,0:T(8,128)S(1)}, f32[256,128]{1,...) custom-call(s32[2]{0:T(128)S(1)} %pad_add_fusion.me, ...), custom_call_target="tpu_custom_call" | custom-call | flops 1000000 | bytes 1000000 | tf_op jit(solution)/shard_map/pallas_call | solution.py:430
  9.2 2.1 %collective-permute-start.3 = (f32[112,128]{1,0:T(8,128)S(1)}, f32[112,128]{1,0:T(8,128)S(1)}, u32[]{:S(2)}, u32[]{:S(2)}) collective-permute-start(f32[112,128]{1,0:T(8,128)S(1)} %get-tuple-element.53.refs_0_), channel_id=1, source_target_pairs={{0,48},{16,32},{32,16},{48,0},{64,112},{80,96},{96,80},{112,64},{1... | collective-permute-start | bytes 172040 | tf_op jit(solution)/shard_map/ppermute | solution.py:444
  11.9 2.2 %collective-permute-done.3.refs_3_ = f32[112,128]{1,0:T(8,128)S(1)} collective-permute-done((f32[112,128]{1,0:T(8,128)S(1)}, f32[112,128]{1,0:T(8,128)S(1)}, u32[]{:S(2)}, u32[]{:S(2)}) %collective-permute-start.3) | collective-permute-done | bytes 57376 | tf_op jit(solution)/shard_map/ppermute | solution.py:444
  14.0 1.3 %collective-permute-done.2.refs_2_ = f32[112,128]{1,0:T(8,128)S(1)} collective-permute-done((f32[112,128]{1,0:T(8,128)S(1)}, f32[112,128]{1,0:T(8,128)S(1)}, u32[]{:S(2)}, u32[]{:S(2)}) %collective-permute-start.2) | collective-permute-done | bytes 57376 | tf_op jit(solution)/shard_map/ppermute | solution.py:444
  15.9 2.6 %collective-permute-start.6 = (f32[112,128]{1,0:T(8,128)S(1)}, f32[112,128]{1,0:T(8,128)S(1)}, u32[]{:S(2)}, u32[]{:S(2)}) collective-permute-start(f32[112,128]{1,0:T(8,128)S(1)} %get-tuple-element.55.refs_0_), channel_id=1, source_target_pairs={{0,192},{16,208},{32,224},{48,240},{64,128},{80,144},{96,160},{112... | collective-permute-start | bytes 172040 | tf_op jit(solution)/shard_map/ppermute | solution.py:444
  18.6 1.1 %collective-permute-start.5 = (f32[112,128]{1,0:T(8,128)S(1)}, f32[112,128]{1,0:T(8,128)S(1)}, u32[]{:S(2)}, u32[]{:S(2)}) collective-permute-start(f32[112,128]{1,0:T(8,128)S(1)} %get-tuple-element.55.refs_0_), channel_id=1, source_target_pairs={{0,128},{16,144},{32,160},{48,176},{64,192},{80,208},{96,224},{112... | collective-permute-start | bytes 172040 | tf_op jit(solution)/shard_map/ppermute | solution.py:444
  20.2 1.3 %collective-permute-start.7 = (f32[16,128]{1,0:T(8,128)S(1)}, f32[16,128]{1,0:T(8,128)S(1)}, u32[]{:S(2)}, u32[]{:S(2)}) collective-permute-start(f32[16,128]{1,0:T(8,128)S(1)} %get-tuple-element.56), channel_id=1, source_target_pairs={{1,0},{2,1},{3,2},{4,3},{5,4},{6,5},{7,6},{8,7},{9,8},{10,9},{11,1... | collective-permute-start | bytes 24584 | tf_op jit(solution)/shard_map/ppermute | solution.py:483
  21.4 2.5 %shard_map.71 = (f32[256,128]{1,0:T(8,128)S(1)}, f32[256,128]{1,0:T(8,128)S(1)}, f32[256,128]{1,0:T(8,128)S(1)}, f32[32,128]{1,0:T(8,128)S(1)}, f32[32,128]{1,0:...) custom-call(s32[2]{0:T(128)S(1)} %pad_add_fusion.me, ...), custom_call_target="tpu_custom_call" | custom-call | flops 8000000 | bytes 1000000 | tf_op jit(solution)/shard_map/pallas_call | solution.py:430
  24.0 2.1 %collective-permute-done.7.refs_4_ = f32[16,128]{1,0:T(8,128)S(1)} collective-permute-done((f32[16,128]{1,0:T(8,128)S(1)}, f32[16,128]{1,0:T(8,128)S(1)}, u32[]{:S(2)}, u32[]{:S(2)}) %collective-permute-start.7) | collective-permute-done | bytes 8224 | tf_op jit(solution)/shard_map/ppermute | solution.py:483
  26.1 1.4 %shard_map.72 = (f32[4,112,128]{2,1,0:T(8,128)S(1)}, f32[256,128]{1,0:T(8,128)S(1)}, f32[256,128]{1,0:T(8,128)S(1)}, f32[256,128]{1,0:T(8,128)S(1)}, f32[256,128...) custom-call(s32[2]{0:T(128)S(1)} %pad_add_fusion.me, ...), custom_call_target="tpu_custom_call" | custom-call | flops 1000000 | bytes 1000000 | tf_op jit(solution)/shard_map/pallas_call | solution.py:430
  27.5 5.2 %collective-permute-start.10 = (f32[112,128]{1,0:T(8,128)S(1)}, f32[112,128]{1,0:T(8,128)S(1)}, u32[]{:S(2)}, u32[]{:S(2)}) collective-permute-start(f32[112,128]{1,0:T(8,128)S(1)} %get-tuple-element.70.refs_0_), channel_id=1, source_target_pairs={{0,3},{1,2},{2,1},{3,0},{4,7},{5,6},{6,5},{7,4},{8,11},{9,10},{10,... | collective-permute-start | bytes 172040 | tf_op jit(solution)/shard_map/ppermute | solution.py:444
  33.0 1.2 %collective-permute-done.10.refs_3_ = f32[112,128]{1,0:T(8,128)S(1)} collective-permute-done((f32[112,128]{1,0:T(8,128)S(1)}, f32[112,128]{1,0:T(8,128)S(1)}, u32[]{:S(2)}, u32[]{:S(2)}) %collective-permute-start.10) | collective-permute-done | bytes 57376 | tf_op jit(solution)/shard_map/ppermute | solution.py:444
  34.2 1.8 %collective-permute-done.9.refs_2_ = f32[112,128]{1,0:T(8,128)S(1)} collective-permute-done((f32[112,128]{1,0:T(8,128)S(1)}, f32[112,128]{1,0:T(8,128)S(1)}, u32[]{:S(2)}, u32[]{:S(2)}) %collective-permute-start.9) | collective-permute-done | bytes 57376 | tf_op jit(solution)/shard_map/ppermute | solution.py:444
  36.0 1.4 %collective-permute-done.8.refs_1_ = f32[112,128]{1,0:T(8,128)S(1)} collective-permute-done((f32[112,128]{1,0:T(8,128)S(1)}, f32[112,128]{1,0:T(8,128)S(1)}, u32[]{:S(2)}, u32[]{:S(2)}) %collective-permute-start.8) | collective-permute-done | bytes 57376 | tf_op jit(solution)/shard_map/ppermute | solution.py:444
  38.0 6.2 %collective-permute-start.13 = (f32[112,128]{1,0:T(8,128)S(1)}, f32[112,128]{1,0:T(8,128)S(1)}, u32[]{:S(2)}, u32[]{:S(2)}) collective-permute-start(f32[112,128]{1,0:T(8,128)S(1)} %get-tuple-element.72.refs_0_), channel_id=1, source_target_pairs={{0,12},{1,13},{2,14},{3,15},{4,8},{5,9},{6,10},{7,11},{8,4},{9,5},... | collective-permute-start | bytes 172040 | tf_op jit(solution)/shard_map/ppermute | solution.py:444
  44.2 1.4 %collective-permute-start.12 = (f32[112,128]{1,0:T(8,128)S(1)}, f32[112,128]{1,0:T(8,128)S(1)}, u32[]{:S(2)}, u32[]{:S(2)}) collective-permute-start(f32[112,128]{1,0:T(8,128)S(1)} %get-tuple-element.72.refs_0_), channel_id=1, source_target_pairs={{0,8},{1,9},{2,10},{3,11},{4,12},{5,13},{6,14},{7,15},{8,0},{9,1},... | collective-permute-start | bytes 172040 | tf_op jit(solution)/shard_map/ppermute | solution.py:444
  46.4 5.2 %collective-permute-done.12.refs_2_ = f32[112,128]{1,0:T(8,128)S(1)} collective-permute-done((f32[112,128]{1,0:T(8,128)S(1)}, f32[112,128]{1,0:T(8,128)S(1)}, u32[]{:S(2)}, u32[]{:S(2)}) %collective-permute-start.12) | collective-permute-done | bytes 57376 | tf_op jit(solution)/shard_map/ppermute | solution.py:444
  51.6 0.9 %shard_map.74 = (f32[256,128]{1,0:T(8,128)S(1)}, f32[256,128]{1,0:T(8,128)S(1)}, f32[256,128]{1,0:T(8,128)S(1)}, f32[32,128]{1,0:T(8,128)S(1)}, f32[32,128]{1,0:T(8,128)S(1)}) custom-call(s32[2]{0:T(128)S(1)} %pad_add_fusion.me, f32[4,112,128]{2,1,0:T(8,128)S(1)} %get-tuple-element.71.got_near, f32[112,128]{1,0:T(8,128)S(1)} %get-tuple-element.72.refs_0_, ...), custom_call_target="tpu_custom_call" | custom-call | flops 1000000 | bytes 1000000 | tf_op jit(solution)/shard_map/pallas_call | solution.py:430
  52.5 5.3 %collective-permute-start.16 = (f32[32,128]{1,0:T(8,128)S(1)}, f32[32,128]{1,0:T(8,128)S(1)}, u32[]{:S(2)}, u32[]{:S(2)}) collective-permute-start(f32[32,128]{1,0:T(8,128)S(1)} %get-tuple-element.76.refs_0_), channel_id=1, source_target_pairs={{0,48},{16,32},{32,16},{48,0},{64,112},{80,96},{96,80},{112,64},{1... | collective-permute-start | bytes 49160 | tf_op jit(solution)/shard_map/ppermute | solution.py:444
  59.3 1.6 %collective-permute-done.15.refs_2_ = f32[32,128]{1,0:T(8,128)S(1)} collective-permute-done((f32[32,128]{1,0:T(8,128)S(1)}, f32[32,128]{1,0:T(8,128)S(1)}, u32[]{:S(2)}, u32[]{:S(2)}) %collective-permute-start.15) | collective-permute-done | bytes 16416 | tf_op jit(solution)/shard_map/ppermute | solution.py:444
  61.4 3.0 %collective-permute-start.19 = (f32[32,128]{1,0:T(8,128)S(1)}, f32[32,128]{1,0:T(8,128)S(1)}, u32[]{:S(2)}, u32[]{:S(2)}) collective-permute-start(f32[32,128]{1,0:T(8,128)S(1)} %get-tuple-element.78.refs_0_), channel_id=1, source_target_pairs={{0,192},{16,208},{32,224},{48,240},{64,128},{80,144},{96,160},{112... | collective-permute-start | bytes 49160 | tf_op jit(solution)/shard_map/ppermute | solution.py:444
  65.8 2.7 %shard_map.76 = (f32[3,256,128]{2,1,0:T(8,128)}, f32[3,256,128]{2,1,0:T(8,128)}) custom-call(f32[256,128]{1,0:T(8,128)S(1)} %get-tuple-element.81.part, f32[256,128]{1,0:T(8,128)S(1)} %get-tuple-element.82.rise_y, f32[256,128]{1,0:T(8,128)S(1)} %get-tuple-element.58.w.refs_9_, f32[32,128]{1,0:T(8,128)S(1)} %get-tuple-element.83.ends_c, ...), custom_call_target="tpu_custom_call" | custom-call | flops 8000000 | bytes 1000000 | tf_op jit(solution)/shard_map/pallas_call | solution.py:430
  69.2 1.4 %shard_map.77 = (f32[3,256,128]{2,1,0:T(8,128)}, f32[3,256,128]{2,1,0:T(8,128)}) custom-call(s32[2]{0:T(128)S(1)} %pad_add_fusion.me, f32[4,112,128]{2,1,0:T(8,128)S(1)} %get-tuple-element.54.got_near.coefs.coefs_near, f32[4,112,128]{2,1,0:T(8,128)S(1)} %get-tuple-element.69.coefs_far, ...), custom_call_target="tpu_custom_call", output_to_operand_aliasing={{0}: (12, {}), {1}: (13, {})} | custom-call | flops 1000000 | bytes 1000000 | tf_op jit(solution)/shard_map/pallas_call | solution.py:430
  (28 shorter events, 8.4 us)
Async XLA Ops:
  1.5 7.7 %collective-permute-start = (f32[16,128]{1,0:T(8,128)S(1)}, f32[16,128]{1,0:T(8,128)S(1)}, u32[]{:S(2)}, u32[]{:S(2)}) collective-permute-start(f32[16,128]{1,0:T(8,128)S(1)} %bitcast.15), channel_id=1, source_target_pairs={{0,1},{1,2},{2,3},{3,4},{4,5},{5,6},{6,7},{7,8},{8,9},{9,10},{10,1... | collective-permute-start | bytes 24584 | tf_op jit(solution)/shard_map/ppermute | solution.py:468
  9.2 4.8 %collective-permute-start.3 = (f32[112,128]{1,0:T(8,128)S(1)}, f32[112,128]{1,0:T(8,128)S(1)}, u32[]{:S(2)}, u32[]{:S(2)}) collective-permute-start(f32[112,128]{1,0:T(8,128)S(1)} %get-tuple-element.53.refs_0_), channel_id=1, source_target_pairs={{0,48},{16,32},{32,16},{48,0},{64,112},{80,96},{96,80},{112,64},{1... | collective-permute-start | bytes 172040 | tf_op jit(solution)/shard_map/ppermute | solution.py:444
  11.4 3.9 %collective-permute-start.2 = (f32[112,128]{1,0:T(8,128)S(1)}, f32[112,128]{1,0:T(8,128)S(1)}, u32[]{:S(2)}, u32[]{:S(2)}) collective-permute-start(f32[112,128]{1,0:T(8,128)S(1)} %get-tuple-element.53.refs_0_), channel_id=1, source_target_pairs={{0,32},{16,48},{32,0},{48,16},{64,96},{80,112},{96,64},{112,80},{1... | collective-permute-start | bytes 172040 | tf_op jit(solution)/shard_map/ppermute | solution.py:444
  11.6 3.7 %collective-permute-start.1 = (f32[112,128]{1,0:T(8,128)S(1)}, f32[112,128]{1,0:T(8,128)S(1)}, u32[]{:S(2)}, u32[]{:S(2)}) collective-permute-start(f32[112,128]{1,0:T(8,128)S(1)} %get-tuple-element.53.refs_0_), channel_id=1, source_target_pairs={{0,16},{16,0},{32,48},{48,32},{64,80},{80,64},{96,112},{112,96},{1... | collective-permute-start | bytes 172040 | tf_op jit(solution)/shard_map/ppermute | solution.py:444
  15.9 10.1 %collective-permute-start.6 = (f32[112,128]{1,0:T(8,128)S(1)}, f32[112,128]{1,0:T(8,128)S(1)}, u32[]{:S(2)}, u32[]{:S(2)}) collective-permute-start(f32[112,128]{1,0:T(8,128)S(1)} %get-tuple-element.55.refs_0_), channel_id=1, source_target_pairs={{0,192},{16,208},{32,224},{48,240},{64,128},{80,144},{96,160},{112... | collective-permute-start | bytes 172040 | tf_op jit(solution)/shard_map/ppermute | solution.py:444
  18.6 7.5 %collective-permute-start.5 = (f32[112,128]{1,0:T(8,128)S(1)}, f32[112,128]{1,0:T(8,128)S(1)}, u32[]{:S(2)}, u32[]{:S(2)}) collective-permute-start(f32[112,128]{1,0:T(8,128)S(1)} %get-tuple-element.55.refs_0_), channel_id=1, source_target_pairs={{0,128},{16,144},{32,160},{48,176},{64,192},{80,208},{96,224},{112... | collective-permute-start | bytes 172040 | tf_op jit(solution)/shard_map/ppermute | solution.py:444
  19.6 6.4 %collective-permute-start.4 = (f32[112,128]{1,0:T(8,128)S(1)}, f32[112,128]{1,0:T(8,128)S(1)}, u32[]{:S(2)}, u32[]{:S(2)}) collective-permute-start(f32[112,128]{1,0:T(8,128)S(1)} %get-tuple-element.55.refs_0_), channel_id=1, source_target_pairs={{0,64},{16,80},{32,96},{48,112},{64,0},{80,16},{96,32},{112,48},{1... | collective-permute-start | bytes 172040 | tf_op jit(solution)/shard_map/ppermute | solution.py:444
  20.2 5.9 %collective-permute-start.7 = (f32[16,128]{1,0:T(8,128)S(1)}, f32[16,128]{1,0:T(8,128)S(1)}, u32[]{:S(2)}, u32[]{:S(2)}) collective-permute-start(f32[16,128]{1,0:T(8,128)S(1)} %get-tuple-element.56), channel_id=1, source_target_pairs={{1,0},{2,1},{3,2},{4,3},{5,4},{6,5},{7,6},{8,7},{9,8},{10,9},{11,1... | collective-permute-start | bytes 24584 | tf_op jit(solution)/shard_map/ppermute | solution.py:483
  27.5 6.7 %collective-permute-start.10 = (f32[112,128]{1,0:T(8,128)S(1)}, f32[112,128]{1,0:T(8,128)S(1)}, u32[]{:S(2)}, u32[]{:S(2)}) collective-permute-start(f32[112,128]{1,0:T(8,128)S(1)} %get-tuple-element.70.refs_0_), channel_id=1, source_target_pairs={{0,3},{1,2},{2,1},{3,0},{4,7},{5,6},{6,5},{7,4},{8,11},{9,10},{10,... | collective-permute-start | bytes 172040 | tf_op jit(solution)/shard_map/ppermute | solution.py:444
  32.7 3.3 %collective-permute-start.9 = (f32[112,128]{1,0:T(8,128)S(1)}, f32[112,128]{1,0:T(8,128)S(1)}, u32[]{:S(2)}, u32[]{:S(2)}) collective-permute-start(f32[112,128]{1,0:T(8,128)S(1)} %get-tuple-element.70.refs_0_), channel_id=1, source_target_pairs={{0,2},{1,3},{2,0},{3,1},{4,6},{5,7},{6,4},{7,5},{8,10},{9,11},{10,... | collective-permute-start | bytes 172040 | tf_op jit(solution)/shard_map/ppermute | solution.py:444
  32.7 4.7 %collective-permute-start.8 = (f32[112,128]{1,0:T(8,128)S(1)}, f32[112,128]{1,0:T(8,128)S(1)}, u32[]{:S(2)}, u32[]{:S(2)}) collective-permute-start(f32[112,128]{1,0:T(8,128)S(1)} %get-tuple-element.70.refs_0_), channel_id=1, source_target_pairs={{0,1},{1,0},{2,3},{3,2},{4,5},{5,4},{6,7},{7,6},{8,9},{9,8},{10,11... | collective-permute-start | bytes 172040 | tf_op jit(solution)/shard_map/ppermute | solution.py:444
  38.0 8.4 %collective-permute-start.13 = (f32[112,128]{1,0:T(8,128)S(1)}, f32[112,128]{1,0:T(8,128)S(1)}, u32[]{:S(2)}, u32[]{:S(2)}) collective-permute-start(f32[112,128]{1,0:T(8,128)S(1)} %get-tuple-element.72.refs_0_), channel_id=1, source_target_pairs={{0,12},{1,13},{2,14},{3,15},{4,8},{5,9},{6,10},{7,11},{8,4},{9,5},... | collective-permute-start | bytes 172040 | tf_op jit(solution)/shard_map/ppermute | solution.py:444
  44.2 7.4 %collective-permute-start.12 = (f32[112,128]{1,0:T(8,128)S(1)}, f32[112,128]{1,0:T(8,128)S(1)}, u32[]{:S(2)}, u32[]{:S(2)}) collective-permute-start(f32[112,128]{1,0:T(8,128)S(1)} %get-tuple-element.72.refs_0_), channel_id=1, source_target_pairs={{0,8},{1,9},{2,10},{3,11},{4,12},{5,13},{6,14},{7,15},{8,0},{9,1},... | collective-permute-start | bytes 172040 | tf_op jit(solution)/shard_map/ppermute | solution.py:444
  45.6 6.0 %collective-permute-start.11 = (f32[112,128]{1,0:T(8,128)S(1)}, f32[112,128]{1,0:T(8,128)S(1)}, u32[]{:S(2)}, u32[]{:S(2)}) collective-permute-start(f32[112,128]{1,0:T(8,128)S(1)} %get-tuple-element.72.refs_0_), channel_id=1, source_target_pairs={{0,4},{1,5},{2,6},{3,7},{4,0},{5,1},{6,2},{7,3},{8,12},{9,13},{10,... | collective-permute-start | bytes 172040 | tf_op jit(solution)/shard_map/ppermute | solution.py:444
  52.5 6.8 %collective-permute-start.16 = (f32[32,128]{1,0:T(8,128)S(1)}, f32[32,128]{1,0:T(8,128)S(1)}, u32[]{:S(2)}, u32[]{:S(2)}) collective-permute-start(f32[32,128]{1,0:T(8,128)S(1)} %get-tuple-element.76.refs_0_), channel_id=1, source_target_pairs={{0,48},{16,32},{32,16},{48,0},{64,112},{80,96},{96,80},{112,64},{1... | collective-permute-start | bytes 49160 | tf_op jit(solution)/shard_map/ppermute | solution.py:444
  57.9 3.0 %collective-permute-start.15 = (f32[32,128]{1,0:T(8,128)S(1)}, f32[32,128]{1,0:T(8,128)S(1)}, u32[]{:S(2)}, u32[]{:S(2)}) collective-permute-start(f32[32,128]{1,0:T(8,128)S(1)} %get-tuple-element.76.refs_0_), channel_id=1, source_target_pairs={{0,32},{16,48},{32,0},{48,16},{64,96},{80,112},{96,64},{112,80},{1... | collective-permute-start | bytes 49160 | tf_op jit(solution)/shard_map/ppermute | solution.py:444
  58.7 2.1 %collective-permute-start.14 = (f32[32,128]{1,0:T(8,128)S(1)}, f32[32,128]{1,0:T(8,128)S(1)}, u32[]{:S(2)}, u32[]{:S(2)}) collective-permute-start(f32[32,128]{1,0:T(8,128)S(1)} %get-tuple-element.76.refs_0_), channel_id=1, source_target_pairs={{0,16},{16,0},{32,48},{48,32},{64,80},{80,64},{96,112},{112,96},{1... | collective-permute-start | bytes 49160 | tf_op jit(solution)/shard_map/ppermute | solution.py:444
  61.4 7.2 %collective-permute-start.19 = (f32[32,128]{1,0:T(8,128)S(1)}, f32[32,128]{1,0:T(8,128)S(1)}, u32[]{:S(2)}, u32[]{:S(2)}) collective-permute-start(f32[32,128]{1,0:T(8,128)S(1)} %get-tuple-element.78.refs_0_), channel_id=1, source_target_pairs={{0,192},{16,208},{32,224},{48,240},{64,128},{80,144},{96,160},{112... | collective-permute-start | bytes 49160 | tf_op jit(solution)/shard_map/ppermute | solution.py:444
  64.4 4.2 %collective-permute-start.18 = (f32[32,128]{1,0:T(8,128)S(1)}, f32[32,128]{1,0:T(8,128)S(1)}, u32[]{:S(2)}, u32[]{:S(2)}) collective-permute-start(f32[32,128]{1,0:T(8,128)S(1)} %get-tuple-element.78.refs_0_), channel_id=1, source_target_pairs={{0,128},{16,144},{32,160},{48,176},{64,192},{80,208},{96,224},{112... | collective-permute-start | bytes 49160 | tf_op jit(solution)/shard_map/ppermute | solution.py:444
  65.1 4.1 %collective-permute-start.17 = (f32[32,128]{1,0:T(8,128)S(1)}, f32[32,128]{1,0:T(8,128)S(1)}, u32[]{:S(2)}, u32[]{:S(2)}) collective-permute-start(f32[32,128]{1,0:T(8,128)S(1)} %get-tuple-element.78.refs_0_), channel_id=1, source_target_pairs={{0,64},{16,80},{32,96},{48,112},{64,0},{80,16},{96,32},{112,48},{1... | collective-permute-start | bytes 49160 | tf_op jit(solution)/shard_map/ppermute | solution.py:444

commit v5 on v4

--- a/solution.py
+++ b/solution.py
@@ -133,9 +133,9 @@
     return r / s
 
 
-def collect(r, own, others, got):
+def collect(r, order, own, others, got):
     got[r] = own[...]
-    for s, other in enumerate(others, 1):
+    for s, other in zip(order, others):
         got[lax.bitwise_xor(r, s)] = other[...]
 
 
@@ -203,9 +203,9 @@
     msg[plane(6)] = magn[2, plane(B - 1)]
 
 
-def merge_kernel(axis, near, sources, halos, me, *refs):
+def merge_kernel(axis, near, order, sources, halos, me, *refs):
     got, msg = refs[-2:]
-    collect(lax.rem(me[axis], near), refs[0], refs[1:near], got)
+    collect(lax.rem(me[axis], near), order, refs[0], refs[1:near], got)
     rows_of, coef_of = rows_in(got, sources), coefs_in(got, 2 * sources)
     blocks = [(coef_of(m), rows_of(m)) for m in range(near)]
     while len(blocks) > 1:
@@ -218,9 +218,9 @@
         msg[plane(6)] = got[near - 1, plane(6)]
 
 
-def merge_rows_kernel(axis, near, me, coefs, *refs):
+def merge_rows_kernel(axis, near, order, me, coefs, *refs):
     got, msg = refs[-2:]
-    collect(lax.rem(me[axis], near), refs[0], refs[1:near], got)
+    collect(lax.rem(me[axis], near), order, refs[0], refs[1:near], got)
     rows_of, coef_of = rows_in(got, 1), coefs_in(coefs, 2)
     blocks = [(coef_of(m), rows_of(m)) for m in range(near)]
     while len(blocks) > 1:
@@ -264,14 +264,14 @@
     flux_y[...] = -(mx + rise)
 
 
-def both_y_kernel(near, far, me, got_near, *refs):
+def both_y_kernel(near, far, order, me, got_near, *refs):
     others, refs = refs[:far], refs[far:]
     (ez_next, g_b, u_x, v_x, flux_b, w, c, r2, src2, curl_in, flux_y_in, flux_a_in, part_a, p_y, u_y, v_y) = refs[:16]
     got_far, rise_y, curl, flux_y, flux_a, g_a, g_c, msg, part, fz = refs[16:]
     me_x = me[0]
     top, corner = plane(0), strided(B - 1)
     q, r = lax.div(me_x, near), lax.rem(me_x, near)
-    collect(q, others[0], others[1:], got_far)
+    collect(q, order, others[0], others[1:], got_far)
     ey_next = jnp.where(
         r < near - 1,
         got_near[jnp.minimum(r + 1, near - 1), plane(5)],
@@ -341,11 +341,11 @@
         msg[plane(k)] = value
 
 
-def second_x_kernel(near, far, me, got_near, *refs):
+def second_x_kernel(near, far, order, me, got_near, *refs):
     others, refs = refs[:far], refs[far:]
     g_a, u, v, flux_a, c, curl, p_x, part, flux2, g2, ends_c, msg, got_far, fx = refs
     my = me[1]
-    collect(lax.div(my, near), others[0], others[1:], got_far)
+    collect(lax.div(my, near), order, others[0], others[1:], got_far)
     (before, after), (before_c, after_c) = solved_ends(
         my, near, far, 2, got_near, got_far, coefs_in(got_near, 4), coefs_in(got_far, 4)
     )
@@ -373,9 +373,9 @@
     msg[plane(1)] = last - flux2[plane(B - 1)]
 
 
-def second_z_kernel(
-    part, rise_y, w, ends_c, g_c, u, v, flux_y, elec, magn, full_x, full_z, new_x, new_y, sems
-):
+def second_y_kernel(ends_c, g_c, u, v, flux_y, elec, magn, full_z, new_x, sems):
+    stores = [(full_z, elec.at[2]), (new_x, magn.at[0])]
+    stores = [pltpu.make_async_copy(a, b, sems.at[k]) for k, (a, b) in enumerate(stores)]
     before, after = ends_c[plane(0)], ends_c[plane(1)]
     here = None
     for j in range(B):
@@ -385,25 +385,29 @@
             new_x[strided(j - 1)] = -h * (flux_y[strided(j - 1)] + (ahead - here))
         here = ahead
     new_x[strided(B - 1)] = -h * (flux_y[strided(B - 1)] + (after - here))
-    stores = [(full_z, elec.at[2]), (new_x, magn.at[0]), (full_x, elec.at[0]), (new_y, magn.at[1])]
+    for store in stores:
+        store.start()
+    for store in stores:
+        store.wait()
+
+
+def second_z_kernel(part, rise_y, w, _, __, elec, magn, full_x, new_y, sems):
+    stores = [(full_x, elec.at[0]), (new_y, magn.at[1])]
     stores = [pltpu.make_async_copy(a, b, sems.at[k]) for k, (a, b) in enumerate(stores)]
-    stores[0].start()
-    stores[1].start()
-
     a = rise_y[...]
     x = solve_z(part[...] - behind_z(a), w[...])
     full_x[...] = x
+    stores[0].start()
     new_y[...] = h * (a - ahead_z(x))
-    stores[2].start()
-    stores[3].start()
+    stores[1].start()
     for store in stores:
         store.wait()
 
 
-def last_kernel(near, far, me, coefs_near, coefs_far, got_near, *refs):
+def last_kernel(near, far, order, me, coefs_near, coefs_far, got_near, *refs):
     others, refs = refs[:far], refs[far:]
     g, u, v, flux2, _, _, elec, magn, got_far, full_y, new_z, sems = refs
-    collect(lax.div(me[0], near), others[0], others[1:], got_far)
+    collect(lax.div(me[0], near), order, others[0], others[1:], got_far)
     ((before, after),) = solved_ends(
         me[0], near, far, 1, got_near, got_far, coefs_in(coefs_near, 2), coefs_in(coefs_far, 2)
     )
@@ -439,11 +443,8 @@
     )(*ins)
 
 
-def shared(value, axis, n, step, count, order):
-    got = {
-        s: lax.ppermute(value, axis, [(i, i ^ (step * s)) for i in range(n)]) for s in order if s < count
-    }
-    return [value] + [got[s] for s in range(1, count)]
+def shared(value, axis, n, step, order):
+    return [value] + [lax.ppermute(value, axis, [(i, i ^ (step * s)) for i in range(n)]) for s in order]
 
 
 def split(n):
@@ -463,7 +464,11 @@
     magn = in_hbm(magnetic.reshape(3, *cells))
     ids = in_hbm(material.reshape(cells))
     dma = pltpu.SemaphoreType.DMA
-    px_near, px_far, py_near, py_far = (1, 2, 3), (2, 1, 3), (2, 3, 1), (1, 3, 2)
+    orders = [(1, 2, 3), (2, 1, 3), (2, 3, 1), (1, 3, 2)]
+    counts = (near_x, far_x, near_y, far_y)
+    px_near, px_far, py_near, py_far = [
+        tuple(s for s in order if s < count) for order, count in zip(orders, counts)
+    ]
 
     hx_prev = lax.ppermute(magnetic[0, :, B - 1], "py", [(i, i + 1) for i in range(ny - 1)])
     w, c, p_x, u_x, v_x, flux_b, part_b, ef, mf, ez_first = call(
@@ -479,14 +484,15 @@
         [cells, (7 * B, nz)],
         specs=[VMEM] * 8,
     )
-    ins = shared(msg, "px", nx, 1, near_x, px_near)
+    ins = shared(msg, "px", nx, 1, px_near)
     ez_next = lax.ppermute(ez_first, "py", [(i + 1, i) for i in range(ny - 1)])
     near_b, msg = call(
-        functools.partial(merge_kernel, 0, near_x, 1, True),
+        functools.partial(merge_kernel, 0, near_x, px_near, 1, True),
         [me] + ins,
         [(near_x, 7 * B, nz), (7 * B, nz)],
     )
-    ins = shared(msg, "px", nx, near_x, far_x, px_far)
+    msg, ez_next = lax.optimization_barrier((msg, ez_next))
+    ins = shared(msg, "px", nx, near_x, px_far)
     p_y, u_y, v_y, r2, src2, curl, flux_y, flux_a, part_a = call(
         first_z_kernel,
         [me, ef, mf, w, c],
@@ -496,42 +502,52 @@
     )
     ins = [me, near_b] + ins + [ez_next, g_b, u_x, v_x, flux_b, w, c, r2, src2]
     far_b, rise_y, curl, flux_y, flux_a, g_a, g_c, msg = call(
-        functools.partial(both_y_kernel, near_x, far_x),
+        functools.partial(both_y_kernel, near_x, far_x, px_far),
         ins + [curl, flux_y, flux_a, part_a, p_y, u_y, v_y],
         [(far_x, 7 * B, nz)] + [cells] * 6 + [(7 * B, nz)],
         scratch=[cells] * 2,
     )
-    ins = shared(msg, "py", ny, 1, near_y, py_near)
+    ins = shared(msg, "py", ny, 1, py_near)
     near_ac, msg = call(
-        functools.partial(merge_kernel, 1, near_y, 2, False), [me] + ins, [(near_y, 7 * B, nz), (7 * B, nz)]
-    )
-    ins = shared(msg, "py", ny, near_y, far_y, py_far)
+        functools.partial(merge_kernel, 1, near_y, py_near, 2, False), [me] + ins, [(near_y, 7 * B, nz), (7 * B, nz)]
+    )
+    ins = shared(msg, "py", ny, near_y, py_far)
     part_x, flux2, g2, ends_c, msg = call(
-        functools.partial(second_x_kernel, near_y, far_y),
+        functools.partial(second_x_kernel, near_y, far_y, py_far),
         [me, near_ac] + ins + [g_a, u_y, v_y, flux_a, c, curl, p_x],
         [cells] * 3 + [(2 * B, nz)] * 2,
         scratch=[(far_y, 7 * B, nz), cells],
     )
-    ins = shared(msg, "px", nx, 1, near_x, px_near)
+    ins = shared(msg, "px", nx, 1, px_near)
+    elec, magn = call(
+        second_y_kernel,
+        [ends_c, g_c, u_y, v_y, flux_y],
+        [(3, *cells)] * 2,
+        specs=[VMEM] * 5,
+        out_specs=[HBM] * 2,
+        scratch=[cells] * 2 + [dma((2,))],
+    )
     near_a, msg = call(
-        functools.partial(merge_rows_kernel, 0, near_x),
+        functools.partial(merge_rows_kernel, 0, near_x, px_near),
         [me, near_b] + ins,
         [(near_x, 2 * B, nz), (2 * B, nz)],
     )
-    ins = shared(msg, "px", nx, near_x, far_x, px_far)
+    msg, elec = lax.optimization_barrier((msg, elec))
+    ins = shared(msg, "px", nx, near_x, px_far)
     elec, magn = call(
         second_z_kernel,
-        [part_x, rise_y, w, ends_c, g_c, u_y, v_y, flux_y],
+        [part_x, rise_y, w, elec, magn],
         [(3, *cells)] * 2,
-        specs=[VMEM] * 8,
+        specs=[VMEM] * 3 + [HBM] * 2,
         out_specs=[HBM] * 2,
-        scratch=[cells] * 4 + [dma((4,))],
+        scratch=[cells] * 2 + [dma((2,))],
+        aliases={3: 0, 4: 1},
         flops=8_000_000,
     )
     ins = [me, near_b, far_b, near_a] + ins + [g2, u_x, v_x, flux2]
     at = len(ins)
     out = call(
-        functools.partial(last_kernel, near_x, far_x),
+        functools.partial(last_kernel, near_x, far_x, px_far),
         ins + [elec, magn],
         [(3, *cells)] * 2,
         specs=[SMEM] + [VMEM] * (at - 1) + [HBM] * 2,

time: 71 us -> 68.8 us (0.969)
  waiting for transfers between devices: 17.8 us -> 13.1 us
  starting transfers between devices: 38.3 us -> 40 us
    ppermute x18, waiting for transfers between devices: 15.8 us -> 11.2 us  [shared(): lax.ppermute(value, axis, [(i, i ^ step * s) for i in range(n)])]
    ppermute x18, starting transfers between devices: 31.4 us -> 33.1 us  [shared(): lax.ppermute(value, axis, [(i, i ^ step * s) for i in range(n)])]
    pallas_call x10 -> x11, Pallas kernels: 12.8 us -> 13.3 us  [call(): pl.pallas_call(kernel, out_shape=shapes, in_specs=specs or [SMEM] + [VMEM...]
  transfers between devices with their start and end apart: 20 -> 20, of which waited for: 10 -> 8; matrix products, arithmetic and copies ran while one was open for 0% -> 0% of each run, Pallas kernels for 10% -> 12%
where the time goes in v5:
time: 68.8 us; the launch traced here: 68.2 us
  starting transfers between devices  40 us (58%)
  Pallas kernels  13.3 us (19%)
  waiting for transfers between devices  13.1 us (19%)
  between operations  0.92 us (1%)
  local copies, waits for them, and re-layouts  0.85 us (1%)
    ppermute x18, starting transfers between devices, shared(): lax.ppermute(value, axis, [(i, i ^ step * s) for i in range(n)])  33.1 us
    pallas_call x11, Pallas kernels, call(): pl.pallas_call(kernel, out_shape=shapes, in_specs=specs or [SMEM] + [VMEM...  13.3 us
    ppermute x18, waiting for transfers between devices, shared(): lax.ppermute(value, axis, [(i, i ^ step * s) for i in range(n)])  11.2 us
    ppermute x1, starting transfers between devices, local(): lax.ppermute(magnetic[0, :, B - 1], 'py', [(i, i + 1) for i in range(ny -...  5.64 us
    ppermute x1, waiting for transfers between devices, local(): ez_next = lax.ppermute(ez_first, 'py', [(i + 1, i) for i in range(ny - 1)])  1.83 us
  transfers between devices with their start and end apart: 20, of which 8 were waited for; matrix products, arithmetic and copies ran while one was open for 0% of the time, Pallas kernels for 12%

profile of v5, /device:TPU:1, one launch (start us, length us, event | category | flops | bytes accessed | tf_op | source)
XLA Modules:
  0.0 68.2 jit_solution(3869993039296995999)
XLA Ops:
  1.5 5.6 %collective-permute-start = (f32[16,128]{1,0:T(8,128)S(1)}, f32[16,128]{1,0:T(8,128)S(1)}, u32[]{:S(2)}, u32[]{:S(2)}) collective-permute-start(f32[16,128]{1,0:T(8,128)S(1)} %bitcast.15), channel_id=1, source_target_pairs={{0,1},{1,2},{2,3},{3,4},{4,5},{5,6},{6,7},{7,8},{8,9},{9,10},{10,1... | collective-permute-start | bytes 24584 | tf_op jit(solution)/shard_map/ppermute | solution.py:473
  7.2 1.9 %shard_map.68 = (f32[256,128]{1,0:T(8,128)S(1)}, f32[256,128]{1,0:T(8,128)S(1)}, f32[256,128]{1,0:T(8,128)S(1)}, f32[256,128]{1,0:T(8,128)S(1)}, f32[256,128]{1,...) custom-call(s32[2]{0:T(128)S(1)} %pad_add_fusion.me, ...), custom_call_target="tpu_custom_call" | custom-call | flops 1000000 | bytes 1000000 | tf_op jit(solution)/shard_map/pallas_call | solution.py:434
  9.2 2.1 %collective-permute-start.3 = (f32[112,128]{1,0:T(8,128)S(1)}, f32[112,128]{1,0:T(8,128)S(1)}, u32[]{:S(2)}, u32[]{:S(2)}) collective-permute-start(f32[112,128]{1,0:T(8,128)S(1)} %get-tuple-element.59.refs_0_), channel_id=1, source_target_pairs={{0,48},{16,32},{32,16},{48,0},{64,112},{80,96},{96,80},{112,64},{1... | collective-permute-start | bytes 172040 | tf_op jit(solution)/shard_map/ppermute | solution.py:447
  11.9 1.3 %collective-permute-start.4 = (f32[16,128]{1,0:T(8,128)S(1)}, f32[16,128]{1,0:T(8,128)S(1)}, u32[]{:S(2)}, u32[]{:S(2)}) collective-permute-start(f32[16,128]{1,0:T(8,128)S(1)} %get-tuple-element.62), channel_id=1, source_target_pairs={{1,0},{2,1},{3,2},{4,3},{5,4},{6,5},{7,6},{8,7},{9,8},{10,9},{11,1... | collective-permute-start | bytes 24584 | tf_op jit(solution)/shard_map/ppermute | solution.py:488
  13.1 0.9 %collective-permute-done.3.refs_3_ = f32[112,128]{1,0:T(8,128)S(1)} collective-permute-done((f32[112,128]{1,0:T(8,128)S(1)}, f32[112,128]{1,0:T(8,128)S(1)}, u32[]{:S(2)}, u32[]{:S(2)}) %collective-permute-start.3) | collective-permute-done | bytes 57376 | tf_op jit(solution)/shard_map/ppermute | solution.py:447
  14.0 1.3 %collective-permute-done.2.refs_2_ = f32[112,128]{1,0:T(8,128)S(1)} collective-permute-done((f32[112,128]{1,0:T(8,128)S(1)}, f32[112,128]{1,0:T(8,128)S(1)}, u32[]{:S(2)}, u32[]{:S(2)}) %collective-permute-start.2) | collective-permute-done | bytes 57376 | tf_op jit(solution)/shard_map/ppermute | solution.py:447
  15.9 1.8 %collective-permute-done.4.refs_4_ = f32[16,128]{1,0:T(8,128)S(1)} collective-permute-done((f32[16,128]{1,0:T(8,128)S(1)}, f32[16,128]{1,0:T(8,128)S(1)}, u32[]{:S(2)}, u32[]{:S(2)}) %collective-permute-start.4) | collective-permute-done | bytes 8224 | tf_op jit(solution)/shard_map/ppermute | solution.py:488
  17.7 2.6 %collective-permute-start.7 = (f32[112,128]{1,0:T(8,128)S(1)}, f32[112,128]{1,0:T(8,128)S(1)}, u32[]{:S(2)}, u32[]{:S(2)}) collective-permute-start(f32[112,128]{1,0:T(8,128)S(1)} %get-tuple-element.63.refs_0_), channel_id=1, source_target_pairs={{0,192},{16,208},{32,224},{48,240},{64,128},{80,144},{96,160},{112... | collective-permute-start | bytes 172040 | tf_op jit(solution)/shard_map/ppermute | solution.py:447
  20.8 1.1 %collective-permute-start.5 = (f32[112,128]{1,0:T(8,128)S(1)}, f32[112,128]{1,0:T(8,128)S(1)}, u32[]{:S(2)}, u32[]{:S(2)}) collective-permute-start(f32[112,128]{1,0:T(8,128)S(1)} %get-tuple-element.63.refs_0_), channel_id=1, source_target_pairs={{0,128},{16,144},{32,160},{48,176},{64,192},{80,208},{96,224},{112... | collective-permute-start | bytes 172040 | tf_op jit(solution)/shard_map/ppermute | solution.py:447
  21.9 2.5 %shard_map.71 = (f32[256,128]{1,0:T(8,128)S(1)}, f32[256,128]{1,0:T(8,128)S(1)}, f32[256,128]{1,0:T(8,128)S(1)}, f32[32,128]{1,0:T(8,128)S(1)}, f32[32,128]{1,0:...) custom-call(s32[2]{0:T(128)S(1)} %pad_add_fusion.me, ...), custom_call_target="tpu_custom_call" | custom-call | flops 8000000 | bytes 1000000 | tf_op jit(solution)/shard_map/pallas_call | solution.py:434
  25.2 1.4 %shard_map.72 = (f32[4,112,128]{2,1,0:T(8,128)S(1)}, f32[256,128]{1,0:T(8,128)S(1)}, f32[256,128]{1,0:T(8,128)S(1)}, f32[256,128]{1,0:T(8,128)S(1)}, f32[256,128...) custom-call(s32[2]{0:T(128)S(1)} %pad_add_fusion.me, ...), custom_call_target="tpu_custom_call" | custom-call | flops 1000000 | bytes 1000000 | tf_op jit(solution)/shard_map/pallas_call | solution.py:434
  26.6 4.1 %collective-permute-start.10 = (f32[112,128]{1,0:T(8,128)S(1)}, f32[112,128]{1,0:T(8,128)S(1)}, u32[]{:S(2)}, u32[]{:S(2)}) collective-permute-start(f32[112,128]{1,0:T(8,128)S(1)} %get-tuple-element.78.refs_0_), channel_id=1, source_target_pairs={{0,1},{1,0},{2,3},{3,2},{4,5},{5,4},{6,7},{7,6},{8,9},{9,8},{10,11... | collective-permute-start | bytes 172040 | tf_op jit(solution)/shard_map/ppermute | solution.py:447
  30.7 1.7 %collective-permute-start.9 = (f32[112,128]{1,0:T(8,128)S(1)}, f32[112,128]{1,0:T(8,128)S(1)}, u32[]{:S(2)}, u32[]{:S(2)}) collective-permute-start(f32[112,128]{1,0:T(8,128)S(1)} %get-tuple-element.78.refs_0_), channel_id=1, source_target_pairs={{0,3},{1,2},{2,1},{3,0},{4,7},{5,6},{6,5},{7,4},{8,11},{9,10},{10,... | collective-permute-start | bytes 172040 | tf_op jit(solution)/shard_map/ppermute | solution.py:447
  32.4 3.7 %collective-permute-done.9.refs_2_ = f32[112,128]{1,0:T(8,128)S(1)} collective-permute-done((f32[112,128]{1,0:T(8,128)S(1)}, f32[112,128]{1,0:T(8,128)S(1)}, u32[]{:S(2)}, u32[]{:S(2)}) %collective-permute-start.9) | collective-permute-done | bytes 57376 | tf_op jit(solution)/shard_map/ppermute | solution.py:447
  36.8 7.0 %collective-permute-start.13 = (f32[112,128]{1,0:T(8,128)S(1)}, f32[112,128]{1,0:T(8,128)S(1)}, u32[]{:S(2)}, u32[]{:S(2)}) collective-permute-start(f32[112,128]{1,0:T(8,128)S(1)} %get-tuple-element.80.refs_0_), channel_id=1, source_target_pairs={{0,8},{1,9},{2,10},{3,11},{4,12},{5,13},{6,14},{7,15},{8,0},{9,1},... | collective-permute-start | bytes 172040 | tf_op jit(solution)/shard_map/ppermute | solution.py:447
  44.1 0.9 %collective-permute-start.11 = (f32[112,128]{1,0:T(8,128)S(1)}, f32[112,128]{1,0:T(8,128)S(1)}, u32[]{:S(2)}, u32[]{:S(2)}) collective-permute-start(f32[112,128]{1,0:T(8,128)S(1)} %get-tuple-element.80.refs_0_), channel_id=1, source_target_pairs={{0,4},{1,5},{2,6},{3,7},{4,0},{5,1},{6,2},{7,3},{8,12},{9,13},{10,... | collective-permute-start | bytes 172040 | tf_op jit(solution)/shard_map/ppermute | solution.py:447
  45.4 3.6 %collective-permute-done.12.refs_2_ = f32[112,128]{1,0:T(8,128)S(1)} collective-permute-done((f32[112,128]{1,0:T(8,128)S(1)}, f32[112,128]{1,0:T(8,128)S(1)}, u32[]{:S(2)}, u32[]{:S(2)}) %collective-permute-start.12) | collective-permute-done | bytes 57376 | tf_op jit(solution)/shard_map/ppermute | solution.py:447
  49.0 0.9 %shard_map.74 = (f32[256,128]{1,0:T(8,128)S(1)}, f32[256,128]{1,0:T(8,128)S(1)}, f32[256,128]{1,0:T(8,128)S(1)}, f32[32,128]{1,0:T(8,128)S(1)}, f32[32,128]{1,0:T(8,128)S(1)}) custom-call(s32[2]{0:T(128)S(1)} %pad_add_fusion.me, f32[4,112,128]{2,1,0:T(8,128)S(1)} %get-tuple-element.79.got_near, f32[112,128]{1,0:T(8,128)S(1)} %get-tuple-element.80.refs_0_, ...), custom_call_target="tpu_custom_call" | custom-call | flops 1000000 | bytes 1000000 | tf_op jit(solution)/shard_map/pallas_call | solution.py:434
  49.9 6.4 %collective-permute-start.16 = (f32[32,128]{1,0:T(8,128)S(1)}, f32[32,128]{1,0:T(8,128)S(1)}, u32[]{:S(2)}, u32[]{:S(2)}) collective-permute-start(f32[32,128]{1,0:T(8,128)S(1)} %get-tuple-element.84.refs_0_), channel_id=1, source_target_pairs={{0,48},{16,32},{32,16},{48,0},{64,112},{80,96},{96,80},{112,64},{1... | collective-permute-start | bytes 49160 | tf_op jit(solution)/shard_map/ppermute | solution.py:447
  56.3 1.4 %collective-permute-start.15 = (f32[32,128]{1,0:T(8,128)S(1)}, f32[32,128]{1,0:T(8,128)S(1)}, u32[]{:S(2)}, u32[]{:S(2)}) collective-permute-start(f32[32,128]{1,0:T(8,128)S(1)} %get-tuple-element.84.refs_0_), channel_id=1, source_target_pairs={{0,32},{16,48},{32,0},{48,16},{64,96},{80,112},{96,64},{112,80},{1... | collective-permute-start | bytes 49160 | tf_op jit(solution)/shard_map/ppermute | solution.py:447
  59.7 2.2 %collective-permute-start.19 = (f32[32,128]{1,0:T(8,128)S(1)}, f32[32,128]{1,0:T(8,128)S(1)}, u32[]{:S(2)}, u32[]{:S(2)}) collective-permute-start(f32[32,128]{1,0:T(8,128)S(1)} %get-tuple-element.91.refs_0_), channel_id=1, source_target_pairs={{0,192},{16,208},{32,224},{48,240},{64,128},{80,144},{96,160},{112... | collective-permute-start | bytes 49160 | tf_op jit(solution)/shard_map/ppermute | solution.py:447
  62.5 1.6 %collective-permute-start.17 = (f32[32,128]{1,0:T(8,128)S(1)}, f32[32,128]{1,0:T(8,128)S(1)}, u32[]{:S(2)}, u32[]{:S(2)}) collective-permute-start(f32[32,128]{1,0:T(8,128)S(1)} %get-tuple-element.91.refs_0_), channel_id=1, source_target_pairs={{0,128},{16,144},{32,160},{48,176},{64,192},{80,208},{96,224},{112... | collective-permute-start | bytes 49160 | tf_op jit(solution)/shard_map/ppermute | solution.py:447
  64.1 2.5 %shard_map.77 = (f32[3,256,128]{2,1,0:T(8,128)}, f32[3,256,128]{2,1,0:T(8,128)}) custom-call(f32[256,128]{1,0:T(8,128)S(1)} %get-tuple-element.94.part, f32[256,128]{1,0:T(8,128)S(1)} %get-tuple-element.95.rise_y, f32[256,128]{1,0:T(8,128)S(1)} %get-tuple-element.66.w.refs_9_, ...), custom_call_target="tpu_custom_call", output_to_operand_aliasing={{0}: (3, {}), {1}: (4, {})} | custom-call | flops 8000000 | bytes 1000000 | tf_op jit(solution)/shard_map/pallas_call | solution.py:434
  66.7 1.4 %shard_map.78 = (f32[3,256,128]{2,1,0:T(8,128)}, f32[3,256,128]{2,1,0:T(8,128)}) custom-call(s32[2]{0:T(128)S(1)} %pad_add_fusion.me, f32[4,112,128]{2,1,0:T(8,128)S(1)} %get-tuple-element.60.got_near.coefs.coefs_near, f32[4,112,128]{2,1,0:T(8,128)S(1)} %get-tuple-element.77.coefs_far, ...), custom_call_target="tpu_custom_call", output_to_operand_aliasing={{0}: (12, {}), {1}: (13, {})} | custom-call | flops 1000000 | bytes 1000000 | tf_op jit(solution)/shard_map/pallas_call | solution.py:434
  (29 shorter events, 7.2 us)
Async XLA Ops:
  1.5 7.7 %collective-permute-start = (f32[16,128]{1,0:T(8,128)S(1)}, f32[16,128]{1,0:T(8,128)S(1)}, u32[]{:S(2)}, u32[]{:S(2)}) collective-permute-start(f32[16,128]{1,0:T(8,128)S(1)} %bitcast.15), channel_id=1, source_target_pairs={{0,1},{1,2},{2,3},{3,4},{4,5},{5,6},{6,7},{7,8},{8,9},{9,10},{10,1... | collective-permute-start | bytes 24584 | tf_op jit(solution)/shard_map/ppermute | solution.py:473
  9.2 4.8 %collective-permute-start.3 = (f32[112,128]{1,0:T(8,128)S(1)}, f32[112,128]{1,0:T(8,128)S(1)}, u32[]{:S(2)}, u32[]{:S(2)}) collective-permute-start(f32[112,128]{1,0:T(8,128)S(1)} %get-tuple-element.59.refs_0_), channel_id=1, source_target_pairs={{0,48},{16,32},{32,16},{48,0},{64,112},{80,96},{96,80},{112,64},{1... | collective-permute-start | bytes 172040 | tf_op jit(solution)/shard_map/ppermute | solution.py:447
  11.4 3.9 %collective-permute-start.2 = (f32[112,128]{1,0:T(8,128)S(1)}, f32[112,128]{1,0:T(8,128)S(1)}, u32[]{:S(2)}, u32[]{:S(2)}) collective-permute-start(f32[112,128]{1,0:T(8,128)S(1)} %get-tuple-element.59.refs_0_), channel_id=1, source_target_pairs={{0,32},{16,48},{32,0},{48,16},{64,96},{80,112},{96,64},{112,80},{1... | collective-permute-start | bytes 172040 | tf_op jit(solution)/shard_map/ppermute | solution.py:447
  11.6 3.7 %collective-permute-start.1 = (f32[112,128]{1,0:T(8,128)S(1)}, f32[112,128]{1,0:T(8,128)S(1)}, u32[]{:S(2)}, u32[]{:S(2)}) collective-permute-start(f32[112,128]{1,0:T(8,128)S(1)} %get-tuple-element.59.refs_0_), channel_id=1, source_target_pairs={{0,16},{16,0},{32,48},{48,32},{64,80},{80,64},{96,112},{112,96},{1... | collective-permute-start | bytes 172040 | tf_op jit(solution)/shard_map/ppermute | solution.py:447
  11.9 5.9 %collective-permute-start.4 = (f32[16,128]{1,0:T(8,128)S(1)}, f32[16,128]{1,0:T(8,128)S(1)}, u32[]{:S(2)}, u32[]{:S(2)}) collective-permute-start(f32[16,128]{1,0:T(8,128)S(1)} %get-tuple-element.62), channel_id=1, source_target_pairs={{1,0},{2,1},{3,2},{4,3},{5,4},{6,5},{7,6},{8,7},{9,8},{10,9},{11,1... | collective-permute-start | bytes 24584 | tf_op jit(solution)/shard_map/ppermute | solution.py:488
  17.7 6.7 %collective-permute-start.7 = (f32[112,128]{1,0:T(8,128)S(1)}, f32[112,128]{1,0:T(8,128)S(1)}, u32[]{:S(2)}, u32[]{:S(2)}) collective-permute-start(f32[112,128]{1,0:T(8,128)S(1)} %get-tuple-element.63.refs_0_), channel_id=1, source_target_pairs={{0,192},{16,208},{32,224},{48,240},{64,128},{80,144},{96,160},{112... | collective-permute-start | bytes 172040 | tf_op jit(solution)/shard_map/ppermute | solution.py:447
  20.4 4.8 %collective-permute-start.6 = (f32[112,128]{1,0:T(8,128)S(1)}, f32[112,128]{1,0:T(8,128)S(1)}, u32[]{:S(2)}, u32[]{:S(2)}) collective-permute-start(f32[112,128]{1,0:T(8,128)S(1)} %get-tuple-element.63.refs_0_), channel_id=1, source_target_pairs={{0,64},{16,80},{32,96},{48,112},{64,0},{80,16},{96,32},{112,48},{1... | collective-permute-start | bytes 172040 | tf_op jit(solution)/shard_map/ppermute | solution.py:447
  20.8 4.4 %collective-permute-start.5 = (f32[112,128]{1,0:T(8,128)S(1)}, f32[112,128]{1,0:T(8,128)S(1)}, u32[]{:S(2)}, u32[]{:S(2)}) collective-permute-start(f32[112,128]{1,0:T(8,128)S(1)} %get-tuple-element.63.refs_0_), channel_id=1, source_target_pairs={{0,128},{16,144},{32,160},{48,176},{64,192},{80,208},{96,224},{112... | collective-permute-start | bytes 172040 | tf_op jit(solution)/shard_map/ppermute | solution.py:447
  26.6 5.8 %collective-permute-start.10 = (f32[112,128]{1,0:T(8,128)S(1)}, f32[112,128]{1,0:T(8,128)S(1)}, u32[]{:S(2)}, u32[]{:S(2)}) collective-permute-start(f32[112,128]{1,0:T(8,128)S(1)} %get-tuple-element.78.refs_0_), channel_id=1, source_target_pairs={{0,1},{1,0},{2,3},{3,2},{4,5},{5,4},{6,7},{7,6},{8,9},{9,8},{10,11... | collective-permute-start | bytes 172040 | tf_op jit(solution)/shard_map/ppermute | solution.py:447
  30.7 5.4 %collective-permute-start.9 = (f32[112,128]{1,0:T(8,128)S(1)}, f32[112,128]{1,0:T(8,128)S(1)}, u32[]{:S(2)}, u32[]{:S(2)}) collective-permute-start(f32[112,128]{1,0:T(8,128)S(1)} %get-tuple-element.78.refs_0_), channel_id=1, source_target_pairs={{0,3},{1,2},{2,1},{3,0},{4,7},{5,6},{6,5},{7,4},{8,11},{9,10},{10,... | collective-permute-start | bytes 172040 | tf_op jit(solution)/shard_map/ppermute | solution.py:447
  32.4 3.7 %collective-permute-start.8 = (f32[112,128]{1,0:T(8,128)S(1)}, f32[112,128]{1,0:T(8,128)S(1)}, u32[]{:S(2)}, u32[]{:S(2)}) collective-permute-start(f32[112,128]{1,0:T(8,128)S(1)} %get-tuple-element.78.refs_0_), channel_id=1, source_target_pairs={{0,2},{1,3},{2,0},{3,1},{4,6},{5,7},{6,4},{7,5},{8,10},{9,11},{10,... | collective-permute-start | bytes 172040 | tf_op jit(solution)/shard_map/ppermute | solution.py:447
  36.8 8.6 %collective-permute-start.13 = (f32[112,128]{1,0:T(8,128)S(1)}, f32[112,128]{1,0:T(8,128)S(1)}, u32[]{:S(2)}, u32[]{:S(2)}) collective-permute-start(f32[112,128]{1,0:T(8,128)S(1)} %get-tuple-element.80.refs_0_), channel_id=1, source_target_pairs={{0,8},{1,9},{2,10},{3,11},{4,12},{5,13},{6,14},{7,15},{8,0},{9,1},... | collective-permute-start | bytes 172040 | tf_op jit(solution)/shard_map/ppermute | solution.py:447
  43.8 5.2 %collective-permute-start.12 = (f32[112,128]{1,0:T(8,128)S(1)}, f32[112,128]{1,0:T(8,128)S(1)}, u32[]{:S(2)}, u32[]{:S(2)}) collective-permute-start(f32[112,128]{1,0:T(8,128)S(1)} %get-tuple-element.80.refs_0_), channel_id=1, source_target_pairs={{0,12},{1,13},{2,14},{3,15},{4,8},{5,9},{6,10},{7,11},{8,4},{9,5},... | collective-permute-start | bytes 172040 | tf_op jit(solution)/shard_map/ppermute | solution.py:447
  44.1 4.9 %collective-permute-start.11 = (f32[112,128]{1,0:T(8,128)S(1)}, f32[112,128]{1,0:T(8,128)S(1)}, u32[]{:S(2)}, u32[]{:S(2)}) collective-permute-start(f32[112,128]{1,0:T(8,128)S(1)} %get-tuple-element.80.refs_0_), channel_id=1, source_target_pairs={{0,4},{1,5},{2,6},{3,7},{4,0},{5,1},{6,2},{7,3},{8,12},{9,13},{10,... | collective-permute-start | bytes 172040 | tf_op jit(solution)/shard_map/ppermute | solution.py:447
  49.9 8.6 %collective-permute-start.16 = (f32[32,128]{1,0:T(8,128)S(1)}, f32[32,128]{1,0:T(8,128)S(1)}, u32[]{:S(2)}, u32[]{:S(2)}) collective-permute-start(f32[32,128]{1,0:T(8,128)S(1)} %get-tuple-element.84.refs_0_), channel_id=1, source_target_pairs={{0,48},{16,32},{32,16},{48,0},{64,112},{80,96},{96,80},{112,64},{1... | collective-permute-start | bytes 49160 | tf_op jit(solution)/shard_map/ppermute | solution.py:447
  56.3 2.8 %collective-permute-start.15 = (f32[32,128]{1,0:T(8,128)S(1)}, f32[32,128]{1,0:T(8,128)S(1)}, u32[]{:S(2)}, u32[]{:S(2)}) collective-permute-start(f32[32,128]{1,0:T(8,128)S(1)} %get-tuple-element.84.refs_0_), channel_id=1, source_target_pairs={{0,32},{16,48},{32,0},{48,16},{64,96},{80,112},{96,64},{112,80},{1... | collective-permute-start | bytes 49160 | tf_op jit(solution)/shard_map/ppermute | solution.py:447
  57.7 1.4 %collective-permute-start.14 = (f32[32,128]{1,0:T(8,128)S(1)}, f32[32,128]{1,0:T(8,128)S(1)}, u32[]{:S(2)}, u32[]{:S(2)}) collective-permute-start(f32[32,128]{1,0:T(8,128)S(1)} %get-tuple-element.84.refs_0_), channel_id=1, source_target_pairs={{0,16},{16,0},{32,48},{48,32},{64,80},{80,64},{96,112},{112,96},{1... | collective-permute-start | bytes 49160 | tf_op jit(solution)/shard_map/ppermute | solution.py:447
  59.7 7.0 %collective-permute-start.19 = (f32[32,128]{1,0:T(8,128)S(1)}, f32[32,128]{1,0:T(8,128)S(1)}, u32[]{:S(2)}, u32[]{:S(2)}) collective-permute-start(f32[32,128]{1,0:T(8,128)S(1)} %get-tuple-element.91.refs_0_), channel_id=1, source_target_pairs={{0,192},{16,208},{32,224},{48,240},{64,128},{80,144},{96,160},{112... | collective-permute-start | bytes 49160 | tf_op jit(solution)/shard_map/ppermute | solution.py:447
  61.9 4.8 %collective-permute-start.18 = (f32[32,128]{1,0:T(8,128)S(1)}, f32[32,128]{1,0:T(8,128)S(1)}, u32[]{:S(2)}, u32[]{:S(2)}) collective-permute-start(f32[32,128]{1,0:T(8,128)S(1)} %get-tuple-element.91.refs_0_), channel_id=1, source_target_pairs={{0,64},{16,80},{32,96},{48,112},{64,0},{80,16},{96,32},{112,48},{1... | collective-permute-start | bytes 49160 | tf_op jit(solution)/shard_map/ppermute | solution.py:447
  62.5 4.2 %collective-permute-start.17 = (f32[32,128]{1,0:T(8,128)S(1)}, f32[32,128]{1,0:T(8,128)S(1)}, u32[]{:S(2)}, u32[]{:S(2)}) collective-permute-start(f32[32,128]{1,0:T(8,128)S(1)} %get-tuple-element.91.refs_0_), channel_id=1, source_target_pairs={{0,128},{16,144},{32,160},{48,176},{64,192},{80,208},{96,224},{112... | collective-permute-start | bytes 49160 | tf_op jit(solution)/shard_map/ppermute | solution.py:447

commit v6 on v5

--- a/solution.py
+++ b/solution.py
@@ -71,32 +71,29 @@
     return x, end
 
 
-def boundary(me, n, rows_of, coef_of, outer):
+def boundary(me, rows, coefs, here, coef_here, outer):
+    n = len(rows)
     left = [a for a, _ in outer]
     right = [b for _, b in outer]
     beta = delta = jnp.zeros_like(left[0])
     for s in range(n - 1):
-        ff, fl, ll = coef_of(s)
+        ff, fl, ll = coefs[s]
         t = fl / (1.0 - ff * beta)
         on = s < me
-        left = [
-            jnp.where(on, dl + t * (a + beta * gf), a) for a, (gf, dl) in zip(left, rows_of(s))
-        ]
+        left = [jnp.where(on, dl + t * (a + beta * gf), a) for a, (gf, dl) in zip(left, rows[s])]
         beta = jnp.where(on, ll + t * beta * fl, beta)
         m = n - 1 - s
-        ff, fl, ll = coef_of(m)
+        ff, fl, ll = coefs[m]
         t = fl / (1.0 - ll * delta)
         on = m > me
-        right = [
-            jnp.where(on, gf + t * (b + delta * dl), b) for b, (gf, dl) in zip(right, rows_of(m))
-        ]
+        right = [jnp.where(on, gf + t * (b + delta * dl), b) for b, (gf, dl) in zip(right, rows[m])]
         delta = jnp.where(on, ff + t * delta * fl, delta)
-    ff, fl, ll = coef_of(me)
+    ff, fl, ll = coef_here
     after_scale = 1.0 / (1.0 - delta * ll)
     t = fl * after_scale
     before_scale = 1.0 / (1.0 - beta * (ff + t * delta * fl))
     ends = []
-    for a, b, (gf, dl) in zip(left, right, rows_of(me)):
+    for a, b, (gf, dl) in zip(left, right, here):
         before = (a + beta * (gf + t * (b + delta * dl))) * before_scale
         ends.append((before, (b + delta * (dl + fl * before)) * after_scale))
     return ends
@@ -134,17 +131,28 @@
 
 
 def collect(r, order, own, others, got):
-    got[r] = own[...]
-    for s, other in zip(order, others):
-        got[lax.bitwise_xor(r, s)] = other[...]
-
-
-def rows_in(got, sources):
-    return lambda m: [(got[m, plane(2 * k)], got[m, plane(2 * k + 1)]) for k in range(sources)]
-
-
-def coefs_in(got, at):
-    return lambda m: tuple(got[m, plane(at + k)] for k in range(3))
+    refs = [own] + [others[order.index(s)] for s in range(1, len(order) + 1)]
+    count = len(refs)
+    blocks = [[] for _ in refs]
+    for k in range(own.shape[0] // B):
+        values = [ref[plane(k)] for ref in refs]
+        bit = 1
+        while bit < count:
+            swap = lax.bitwise_and(r, bit) != 0
+            values = [jnp.where(swap, values[m ^ bit], values[m]) for m in range(count)]
+            bit *= 2
+        for m, value in enumerate(values):
+            got[m, plane(k)] = value
+            blocks[m].append(value)
+    return blocks
+
+
+def rows_of(block, sources):
+    return [(block[2 * k], block[2 * k + 1]) for k in range(sources)]
+
+
+def stored(got, m, planes):
+    return [got[plane(k)] if m is None else got[m, plane(k)] for k in planes]
 
 
 def tables_kernel(
@@ -182,16 +190,18 @@
         here = magn[0, plane(i)]
         before = jnp.where(row == 0, 0.0, pltpu.roll(here, 1, 0))
         part[plane(i)] = c[plane(i)] * elec[2, plane(i)] + (q - (here - before) * (1.0 / h))
-    ez_first[...] = elec.at[2][strided(0)]
+    for k in range(ez_first.shape[0] // B):
+        ez_first[plane(k)] = elec.at[2][strided(0)]
     for load in loads[7:]:
         load.wait()
 
 
-def first_x_kernel(part, hx_prev, flux, p, u, v, elec, magn, g, msg):
+def first_x_kernel(me, part, hx_prev, flux, p, u, v, elec, magn, g, msg):
     row = lax.broadcasted_iota(jnp.int32, hx_prev.shape, 0)
+    scale = jnp.where(me[1] == 0, 0.0, jnp.where(row == 0, 1.0 / h, 0.0))
 
     def source(i):
-        return part[plane(i)] + jnp.where(row == 0, hx_prev[pl.ds(i, 1)] * (1.0 / h), 0.0)
+        return part[plane(i)] + hx_prev[pl.ds(i, 1)] * scale
 
     first, last = eliminate(source, p, g)
     msg[plane(0)] = first
@@ -203,45 +213,44 @@
     msg[plane(6)] = magn[2, plane(B - 1)]
 
 
+def merged(blocks):
+    while len(blocks) > 1:
+        blocks = [merge(a, b) for a, b in zip(blocks[::2], blocks[1::2])]
+    return blocks[0]
+
+
 def merge_kernel(axis, near, order, sources, halos, me, *refs):
     got, msg = refs[-2:]
-    collect(lax.rem(me[axis], near), order, refs[0], refs[1:near], got)
-    rows_of, coef_of = rows_in(got, sources), coefs_in(got, 2 * sources)
-    blocks = [(coef_of(m), rows_of(m)) for m in range(near)]
-    while len(blocks) > 1:
-        blocks = [merge(a, b) for a, b in zip(blocks[::2], blocks[1::2])]
-    coefs, rows = blocks[0]
+    blocks = collect(lax.rem(me[axis], near), order, refs[0], refs[1:near], got)
+    at = 2 * sources
+    coefs, rows = merged([(b[at : at + 3], rows_of(b, sources)) for b in blocks])
     for k, value in enumerate([v for pair in rows for v in pair] + list(coefs)):
         msg[plane(k)] = value
     if halos:
-        msg[plane(5)] = got[0, plane(5)]
-        msg[plane(6)] = got[near - 1, plane(6)]
+        msg[plane(5)] = blocks[0][5]
+        msg[plane(6)] = blocks[-1][6]
 
 
 def merge_rows_kernel(axis, near, order, me, coefs, *refs):
     got, msg = refs[-2:]
-    collect(lax.rem(me[axis], near), order, refs[0], refs[1:near], got)
-    rows_of, coef_of = rows_in(got, 1), coefs_in(coefs, 2)
-    blocks = [(coef_of(m), rows_of(m)) for m in range(near)]
-    while len(blocks) > 1:
-        blocks = [merge(a, b) for a, b in zip(blocks[::2], blocks[1::2])]
-    msg[plane(0)], msg[plane(1)] = blocks[0][1][0]
-
-
-def solved_ends(here, near, far, sources, got_near, got_far, coefs_near, coefs_far):
-    zero = jnp.zeros_like(got_near[0, plane(0)])
-    outer = boundary(
-        lax.div(here, near), far, rows_in(got_far, sources), coefs_far, [(zero, zero)] * sources
-    )
-    return boundary(lax.rem(here, near), near, rows_in(got_near, sources), coefs_near, outer)
-
-
-def first_z_kernel(me, ef, mf, w, c, p, u, v, r2, src2, curl, flux_y, flux_a, part_a, src, r):
+    blocks = collect(lax.rem(me[axis], near), order, refs[0], refs[1:near], got)
+    _, rows = merged([(stored(coefs, m, (2, 3, 4)), rows_of(b, 1)) for m, b in enumerate(blocks)])
+    msg[plane(0)], msg[plane(1)] = rows[0]
+
+
+def solved_ends(here, near, sources, near_rows, near_coefs, far_rows, far_coefs, own_near, own_far):
+    zero = jnp.zeros_like(far_coefs[0][0])
+    outer = boundary(lax.div(here, near), far_rows, far_coefs, *own_far, [(zero, zero)] * sources)
+    return boundary(lax.rem(here, near), near_rows, near_coefs, *own_near, outer)
+
+
+def first_z_kernel(n, me, ef, mf, ez_next, w, c, p, u, v, r_top, src_top, curl, flux_y, flux_a, part_a, src, r):
     factor(lambda j: w[strided(j)], me[1] == 0, p, u, v)
+    inside = jnp.where(me[1] == n - 1, 0.0, 1.0)
     row = lax.broadcasted_iota(jnp.int32, (B, w.shape[1]), 0)
     for i in range(B):
         ez = ef[2, plane(i)]
-        after = jnp.where(row == B - 1, 0.0, pltpu.roll(ez, B - 1, 0))
+        after = jnp.where(row == B - 1, ez_next[pl.ds(i, 1)] * inside, pltpu.roll(ez, B - 1, 0))
         ri = mf[0, plane(i)] * (1.0 / h) - (after - ez)
         r[plane(i)] = ri
         gain = mf[2, plane(i)]
@@ -253,10 +262,8 @@
             rise = ef[1, plane(i + 1)] - ef[1, plane(i)]
             flux_a[plane(i)] = mf[2, plane(i)] * (1.0 / h) - rise
     flux_a[plane(B - 1)] = mf[2, plane(B - 1)] * (1.0 / h) + ef[1, plane(B - 1)]
-    for two, of in ((r2, r), (src2, src)):
-        two[plane(0)] = of[plane(0)]
-        two[plane(1)] = of[strided(B - 1)]
-
+    r_top[...] = r[plane(0)]
+    src_top[...] = src[plane(0)]
     x = solve_z(src[...], w[...])
     rise = ahead_z(x)
     mx = r[...] + rise
@@ -266,12 +273,13 @@
 
 def both_y_kernel(near, far, order, me, got_near, *refs):
     others, refs = refs[:far], refs[far:]
-    (ez_next, g_b, u_x, v_x, flux_b, w, c, r2, src2, curl_in, flux_y_in, flux_a_in, part_a, p_y, u_y, v_y) = refs[:16]
-    got_far, rise_y, curl, flux_y, flux_a, g_a, g_c, msg, part, fz = refs[16:]
+    (g_b, u_x, v_x, flux_b, w, c, r_top, src_top, curl_in, flux_y_in, flux_a_in, part_a, p_y, u_y, v_y) = refs[:15]
+    got_far, rise_y, curl, flux_y, flux_a, g_a, g_c, msg, part, fz = refs[15:]
     me_x = me[0]
-    top, corner = plane(0), strided(B - 1)
+    top = plane(0)
     q, r = lax.div(me_x, near), lax.rem(me_x, near)
-    collect(q, order, others[0], others[1:], got_far)
+    far_blocks = collect(q, order, others[0], others[1:], got_far)
+    near_blocks = [stored(got_near, m, range(5)) for m in range(near)]
     ey_next = jnp.where(
         r < near - 1,
         got_near[jnp.minimum(r + 1, near - 1), plane(5)],
@@ -286,22 +294,11 @@
     flux_y[...] = flux_y_in[...]
     flux_a[...] = flux_a_in[...]
 
-    last = lax.broadcasted_iota(jnp.int32, ez_next.shape, 0) == B - 1
-    ez = ez_next[...]
-    ez_top = jnp.where(last, ez[0:1], 0.0)
-    rr = jnp.concatenate([r2[plane(0)] - ez_top, r2[plane(1)] - ez])
-    ss = jnp.concatenate(
-        [src2[plane(0)] + (hz_prev * (1.0 / h) - behind_z(ez_top)), src2[plane(1)] - behind_z(ez)]
-    )
-    x = solve_z(ss, jnp.concatenate([w[top], w[corner]]))
+    x = solve_z(src_top[...] + hz_prev * (1.0 / h), w[top])
     rise = ahead_z(x)
-    mx = rr + rise
-    cc = jnp.concatenate([c[top], c[corner]]) * x + behind_z(mx)
-    ff = -(mx + rise)
-    curl[corner] = cc[B:]
-    flux_y[corner] = ff[B:]
-    curl[top] = cc[:B]
-    flux_y[top] = ff[:B]
+    mx = r_top[...] + rise
+    curl[top] = c[top] * x + behind_z(mx)
+    flux_y[top] = -(mx + rise)
 
     flux_a[plane(B - 1)] = flux_a[plane(B - 1)] - ey_next
 
@@ -314,8 +311,17 @@
     first_a, last_a = eliminate(source_a, p_y, g_a)
     last_a = last_a - flux_a[strided(B - 1)]
 
+    own_near, own_far = stored(got_near, r, range(5)), stored(others[0], None, range(5))
     ((before, after),) = solved_ends(
-        me_x, near, far, 1, got_near, got_far, coefs_in(got_near, 2), coefs_in(got_far, 2)
+        me_x,
+        near,
+        1,
+        [rows_of(b, 1) for b in near_blocks],
+        [b[2:5] for b in near_blocks],
+        [rows_of(b, 1) for b in far_blocks],
+        [b[2:5] for b in far_blocks],
+        (rows_of(own_near, 1), own_near[2:5]),
+        (rows_of(own_far, 1), own_far[2:5]),
     )
     for i in range(B):
         fz[plane(i)] = g_b[plane(i)] + (u_x[plane(i)] * before + v_x[plane(i)] * after)
@@ -345,9 +351,19 @@
     others, refs = refs[:far], refs[far:]
     g_a, u, v, flux_a, c, curl, p_x, part, flux2, g2, ends_c, msg, got_far, fx = refs
     my = me[1]
-    collect(lax.div(my, near), order, others[0], others[1:], got_far)
+    far_blocks = collect(lax.div(my, near), order, others[0], others[1:], got_far)
+    near_blocks = [stored(got_near, m, range(7)) for m in range(near)]
+    own_near, own_far = stored(got_near, lax.rem(my, near), range(7)), stored(others[0], None, range(7))
     (before, after), (before_c, after_c) = solved_ends(
-        my, near, far, 2, got_near, got_far, coefs_in(got_near, 4), coefs_in(got_far, 4)
+        my,
+        near,
+        2,
+        [rows_of(b, 2) for b in near_blocks],
+        [b[4:7] for b in near_blocks],
+        [rows_of(b, 2) for b in far_blocks],
+        [b[4:7] for b in far_blocks],
+        (rows_of(own_near, 2), own_near[4:7]),
+        (rows_of(own_far, 2), own_far[4:7]),
     )
     ends_c[plane(0)] = before_c
     ends_c[plane(1)] = after_c
@@ -407,9 +423,18 @@
 def last_kernel(near, far, order, me, coefs_near, coefs_far, got_near, *refs):
     others, refs = refs[:far], refs[far:]
     g, u, v, flux2, _, _, elec, magn, got_far, full_y, new_z, sems = refs
-    collect(lax.div(me[0], near), order, others[0], others[1:], got_far)
+    q, r = lax.div(me[0], near), lax.rem(me[0], near)
+    far_blocks = collect(q, order, others[0], others[1:], got_far)
     ((before, after),) = solved_ends(
-        me[0], near, far, 1, got_near, got_far, coefs_in(coefs_near, 2), coefs_in(coefs_far, 2)
+        me[0],
+        near,
+        1,
+        [rows_of(stored(got_near, m, range(2)), 1) for m in range(near)],
+        [stored(coefs_near, m, (2, 3, 4)) for m in range(near)],
+        [rows_of(b, 1) for b in far_blocks],
+        [stored(coefs_far, m, (2, 3, 4)) for m in range(far)],
+        (rows_of(stored(got_near, r, range(2)), 1), stored(coefs_near, r, (2, 3, 4))),
+        (rows_of(stored(others[0], None, range(2)), 1), stored(coefs_far, q, (2, 3, 4))),
     )
     stores = [(full_y, elec.at[1]), (new_z, magn.at[2])]
     stores = [pltpu.make_async_copy(a, b, sems.at[k]) for k, (a, b) in enumerate(stores)]
@@ -470,37 +495,35 @@
         tuple(s for s in order if s < count) for order, count in zip(orders, counts)
     ]
 
-    hx_prev = lax.ppermute(magnetic[0, :, B - 1], "py", [(i, i + 1) for i in range(ny - 1)])
+    hx_prev = lax.ppermute(magnetic[0, :, B - 1], "py", [(i, (i + 1) % ny) for i in range(ny)])
     w, c, p_x, u_x, v_x, flux_b, part_b, ef, mf, ez_first = call(
         tables_kernel,
         [me, in_hbm(permittivity), in_hbm(conductivity), ids, elec, magn],
-        [cells] * 7 + [(3, *cells)] * 2 + [(B, nz)],
+        [cells] * 7 + [(3, *cells)] * 2 + [(8 * B, nz)],
         specs=[SMEM] + [HBM] * 5,
         scratch=[pltpu.VMEM(cells, jnp.int32)] + [pltpu.SMEM(permittivity.shape, F32)] * 2 + [dma((9,))],
     )
     g_b, msg = call(
         first_x_kernel,
-        [part_b, hx_prev, flux_b, p_x, u_x, v_x, ef, mf],
+        [me, part_b, hx_prev, flux_b, p_x, u_x, v_x, ef, mf],
         [cells, (7 * B, nz)],
-        specs=[VMEM] * 8,
     )
     ins = shared(msg, "px", nx, 1, px_near)
-    ez_next = lax.ppermute(ez_first, "py", [(i + 1, i) for i in range(ny - 1)])
+    ez_next = lax.ppermute(ez_first, "py", [((i + 1) % ny, i) for i in range(ny)])
     near_b, msg = call(
         functools.partial(merge_kernel, 0, near_x, px_near, 1, True),
         [me] + ins,
         [(near_x, 7 * B, nz), (7 * B, nz)],
     )
-    msg, ez_next = lax.optimization_barrier((msg, ez_next))
     ins = shared(msg, "px", nx, near_x, px_far)
-    p_y, u_y, v_y, r2, src2, curl, flux_y, flux_a, part_a = call(
-        first_z_kernel,
-        [me, ef, mf, w, c],
-        [cells] * 3 + [(2 * B, nz)] * 2 + [cells] * 4,
+    p_y, u_y, v_y, r_top, src_top, curl, flux_y, flux_a, part_a = call(
+        functools.partial(first_z_kernel, ny),
+        [me, ef, mf, ez_next, w, c],
+        [cells] * 3 + [(B, nz)] * 2 + [cells] * 4,
         scratch=[cells] * 2,
         flops=8_000_000,
     )
-    ins = [me, near_b] + ins + [ez_next, g_b, u_x, v_x, flux_b, w, c, r2, src2]
+    ins = [me, near_b] + ins + [g_b, u_x, v_x, flux_b, w, c, r_top, src_top]
     far_b, rise_y, curl, flux_y, flux_a, g_a, g_c, msg = call(
         functools.partial(both_y_kernel, near_x, far_x, px_far),
         ins + [curl, flux_y, flux_a, part_a, p_y, u_y, v_y],

time: 68.8 us -> 63.2 us (0.919)
  starting transfers between devices: 40 us -> 34.3 us
    ppermute x18, starting transfers between devices: 33.1 us -> 27.3 us  [shared(): lax.ppermute(value, axis, [(i, i ^ step * s) for i in range(n)])]
    ppermute x18, waiting for transfers between devices: 11.2 us -> 8.47 us  [shared(): lax.ppermute(value, axis, [(i, i ^ step * s) for i in range(n)])]
    ppermute x2, waiting for transfers between devices: 1.84 us -> 4.33 us  [the longest x1 4.33 us: local(): lax.ppermute(magnetic[0, :, B - 1], 'py', [(i, (i + 1) % ny) for i in ran...]
  transfers between devices with their start and end apart: 20 -> 20, of which waited for: 8 -> 10; matrix products, arithmetic and copies ran while one was open for 0% -> 0% of each run, Pallas kernels for 12% -> 13%
where the time goes in v6:
time: 63.2 us; the launch traced here: 62.7 us
  starting transfers between devices  34.3 us (54%)
  Pallas kernels  13.8 us (22%)
  waiting for transfers between devices  12.8 us (20%)
  between operations  0.9 us (1%)
  local copies, waits for them, and re-layouts  0.85 us (1%)
    ppermute x18, starting transfers between devices, shared(): lax.ppermute(value, axis, [(i, i ^ step * s) for i in range(n)])  27.3 us
    pallas_call x11, Pallas kernels, call(): pl.pallas_call(kernel, out_shape=shapes, in_specs=specs or [SMEM] + [VMEM...  13.8 us
    ppermute x18, waiting for transfers between devices, shared(): lax.ppermute(value, axis, [(i, i ^ step * s) for i in range(n)])  8.47 us
    ppermute x1, waiting for transfers between devices, local(): lax.ppermute(magnetic[0, :, B - 1], 'py', [(i, (i + 1) % ny) for i in ran...  4.33 us
    ppermute x1, starting transfers between devices, local(): lax.ppermute(magnetic[0, :, B - 1], 'py', [(i, (i + 1) % ny) for i in ran...  3.74 us
    ppermute x1, starting transfers between devices, local(): lax.ppermute(ez_first, 'py', [((i + 1) % ny, i) for i in range(ny)])  3.25 us
  transfers between devices with their start and end apart: 20, of which 10 were waited for; matrix products, arithmetic and copies ran while one was open for 0% of the time, Pallas kernels for 13%

profile of v6, /device:TPU:1, one launch (start us, length us, event | category | flops | bytes accessed | tf_op | source)
XLA Modules:
  0.0 62.7 jit_solution(10591961146271665333)
XLA Ops:
  0.6 0.9 %slice.3 = f32[1,16,1,128]{3,2,1,0:T(1,128)S(1)} slice(f32[3,16,16,128]{3,2,1,0:T(8,128)} %param.6), slice={[0:1], [0:16], [15:16], [0:128]} | slice | bytes 16384 | tf_op jit(solution)/shard_map/slice | solution.py:498
  1.5 3.7 %collective-permute-start = (f32[16,128]{1,0:T(8,128)S(1)}, f32[16,128]{1,0:T(8,128)S(1)}, u32[]{:S(2)}, u32[]{:S(2)}) collective-permute-start(f32[16,128]{1,0:T(8,128)S(1)} %bitcast.15), channel_id=1, source_target_pairs={{0,1},{1,2},{2,3},{3,4},{4,5},{5,6},{6,7},{7,8},{8,9},{9,10},{10,1... | collective-permute-start | bytes 24584 | tf_op jit(solution)/shard_map/ppermute | solution.py:498
  5.3 1.9 %shard_map.68 = (f32[256,128]{1,0:T(8,128)S(1)}, f32[256,128]{1,0:T(8,128)S(1)}, f32[256,128]{1,0:T(8,128)S(1)}, f32[256,128]{1,0:T(8,128)S(1)}, f32[256,128]{1,...) custom-call(s32[2]{0:T(128)S(1)} %pad_add_fusion.me, ...), custom_call_target="tpu_custom_call" | custom-call | flops 1000000 | bytes 1000000 | tf_op jit(solution)/shard_map/pallas_call | solution.py:459
  7.2 4.3 %collective-permute-done.hx_prev = f32[16,128]{1,0:T(8,128)S(1)} collective-permute-done((f32[16,128]{1,0:T(8,128)S(1)}, f32[16,128]{1,0:T(8,128)S(1)}, u32[]{:S(2)}, u32[]{:S(2)}) %collective-permute-start) | collective-permute-done | bytes 8224 | tf_op jit(solution)/shard_map/ppermute | solution.py:498
  12.2 2.7 %collective-permute-start.3 = (f32[112,128]{1,0:T(8,128)S(1)}, f32[112,128]{1,0:T(8,128)S(1)}, u32[]{:S(2)}, u32[]{:S(2)}) collective-permute-start(f32[112,128]{1,0:T(8,128)S(1)} %get-tuple-element.57.refs_0_), channel_id=1, source_target_pairs={{0,48},{16,32},{32,16},{48,0},{64,112},{80,96},{96,80},{112,64},{1... | collective-permute-start | bytes 172040 | tf_op jit(solution)/shard_map/ppermute | solution.py:472
  15.4 3.2 %collective-permute-start.7 = (f32[128,128]{1,0:T(8,128)S(1)}, f32[128,128]{1,0:T(8,128)S(1)}, u32[]{:S(2)}, u32[]{:S(2)}) collective-permute-start(f32[128,128]{1,0:T(8,128)S(1)} %get-tuple-element.63), channel_id=1, source_target_pairs={{1,0},{2,1},{3,2},{4,3},{5,4},{6,5},{7,6},{8,7},{9,8},{10,9},{11,1... | collective-permute-start | bytes 196616 | tf_op jit(solution)/shard_map/ppermute | solution.py:512
  19.4 2.5 %collective-permute-start.6 = (f32[112,128]{1,0:T(8,128)S(1)}, f32[112,128]{1,0:T(8,128)S(1)}, u32[]{:S(2)}, u32[]{:S(2)}) collective-permute-start(f32[112,128]{1,0:T(8,128)S(1)} %get-tuple-element.59.refs_0_), channel_id=1, source_target_pairs={{0,192},{16,208},{32,224},{48,240},{64,128},{80,144},{96,160},{112... | collective-permute-start | bytes 172040 | tf_op jit(solution)/shard_map/ppermute | solution.py:472
  22.6 1.1 %collective-permute-start.4 = (f32[112,128]{1,0:T(8,128)S(1)}, f32[112,128]{1,0:T(8,128)S(1)}, u32[]{:S(2)}, u32[]{:S(2)}) collective-permute-start(f32[112,128]{1,0:T(8,128)S(1)} %get-tuple-element.59.refs_0_), channel_id=1, source_target_pairs={{0,128},{16,144},{32,160},{48,176},{64,192},{80,208},{96,224},{112... | collective-permute-start | bytes 172040 | tf_op jit(solution)/shard_map/ppermute | solution.py:472
  23.7 2.5 %shard_map.71 = (f32[256,128]{1,0:T(8,128)S(1)}, f32[256,128]{1,0:T(8,128)S(1)}, f32[256,128]{1,0:T(8,128)S(1)}, f32[16,128]{1,0:T(8,128)S(1)}, f32[16,128]{1,0:...) custom-call(s32[2]{0:T(128)S(1)} %pad_add_fusion.me, ...), custom_call_target="tpu_custom_call" | custom-call | flops 8000000 | bytes 1000000 | tf_op jit(solution)/shard_map/pallas_call | solution.py:459
  26.5 1.3 %shard_map.72 = (f32[4,112,128]{2,1,0:T(8,128)S(1)}, f32[256,128]{1,0:T(8,128)S(1)}, f32[256,128]{1,0:T(8,128)S(1)}, f32[256,128]{1,0:T(8,128)S(1)}, f32[256,128...) custom-call(s32[2]{0:T(128)S(1)} %pad_add_fusion.me, ...), custom_call_target="tpu_custom_call" | custom-call | flops 1000000 | bytes 1000000 | tf_op jit(solution)/shard_map/pallas_call | solution.py:459
  29.0 3.1 %collective-permute-start.8 = (f32[112,128]{1,0:T(8,128)S(1)}, f32[112,128]{1,0:T(8,128)S(1)}, u32[]{:S(2)}, u32[]{:S(2)}) collective-permute-start(f32[112,128]{1,0:T(8,128)S(1)} %get-tuple-element.74.refs_0_), channel_id=1, source_target_pairs={{0,2},{1,3},{2,0},{3,1},{4,6},{5,7},{6,4},{7,5},{8,10},{9,11},{10,... | collective-permute-start | bytes 172040 | tf_op jit(solution)/shard_map/ppermute | solution.py:472
  32.5 1.2 %collective-permute-done.9.refs_2_ = f32[112,128]{1,0:T(8,128)S(1)} collective-permute-done((f32[112,128]{1,0:T(8,128)S(1)}, f32[112,128]{1,0:T(8,128)S(1)}, u32[]{:S(2)}, u32[]{:S(2)}) %collective-permute-start.9) | collective-permute-done | bytes 57376 | tf_op jit(solution)/shard_map/ppermute | solution.py:472
  33.7 0.9 %collective-permute-done.8.refs_1_ = f32[112,128]{1,0:T(8,128)S(1)} collective-permute-done((f32[112,128]{1,0:T(8,128)S(1)}, f32[112,128]{1,0:T(8,128)S(1)}, u32[]{:S(2)}, u32[]{:S(2)}) %collective-permute-start.8) | collective-permute-done | bytes 57376 | tf_op jit(solution)/shard_map/ppermute | solution.py:472
  35.1 5.0 %collective-permute-start.13 = (f32[112,128]{1,0:T(8,128)S(1)}, f32[112,128]{1,0:T(8,128)S(1)}, u32[]{:S(2)}, u32[]{:S(2)}) collective-permute-start(f32[112,128]{1,0:T(8,128)S(1)} %get-tuple-element.76.refs_0_), channel_id=1, source_target_pairs={{0,8},{1,9},{2,10},{3,11},{4,12},{5,13},{6,14},{7,15},{8,0},{9,1},... | collective-permute-start | bytes 172040 | tf_op jit(solution)/shard_map/ppermute | solution.py:472
  40.9 1.3 %collective-permute-done.13.refs_3_ = f32[112,128]{1,0:T(8,128)S(1)} collective-permute-done((f32[112,128]{1,0:T(8,128)S(1)}, f32[112,128]{1,0:T(8,128)S(1)}, u32[]{:S(2)}, u32[]{:S(2)}) %collective-permute-start.13) | collective-permute-done | bytes 57376 | tf_op jit(solution)/shard_map/ppermute | solution.py:472
  42.2 3.4 %collective-permute-done.12.refs_2_ = f32[112,128]{1,0:T(8,128)S(1)} collective-permute-done((f32[112,128]{1,0:T(8,128)S(1)}, f32[112,128]{1,0:T(8,128)S(1)}, u32[]{:S(2)}, u32[]{:S(2)}) %collective-permute-start.12) | collective-permute-done | bytes 57376 | tf_op jit(solution)/shard_map/ppermute | solution.py:472
  45.6 0.9 %shard_map.74 = (f32[256,128]{1,0:T(8,128)S(1)}, f32[256,128]{1,0:T(8,128)S(1)}, f32[256,128]{1,0:T(8,128)S(1)}, f32[32,128]{1,0:T(8,128)S(1)}, f32[32,128]{1,0:T(8,128)S(1)}) custom-call(s32[2]{0:T(128)S(1)} %pad_add_fusion.me, f32[4,112,128]{2,1,0:T(8,128)S(1)} %get-tuple-element.75.got_near, f32[112,128]{1,0:T(8,128)S(1)} %get-tuple-element.76.refs_0_, ...), custom_call_target="tpu_custom_call" | custom-call | flops 1000000 | bytes 1000000 | tf_op jit(solution)/shard_map/pallas_call | solution.py:459
  46.5 4.4 %collective-permute-start.16 = (f32[32,128]{1,0:T(8,128)S(1)}, f32[32,128]{1,0:T(8,128)S(1)}, u32[]{:S(2)}, u32[]{:S(2)}) collective-permute-start(f32[32,128]{1,0:T(8,128)S(1)} %get-tuple-element.80.refs_0_), channel_id=1, source_target_pairs={{0,48},{16,32},{32,16},{48,0},{64,112},{80,96},{96,80},{112,64},{1... | collective-permute-start | bytes 49160 | tf_op jit(solution)/shard_map/ppermute | solution.py:472
  50.9 1.3 %collective-permute-start.15 = (f32[32,128]{1,0:T(8,128)S(1)}, f32[32,128]{1,0:T(8,128)S(1)}, u32[]{:S(2)}, u32[]{:S(2)}) collective-permute-start(f32[32,128]{1,0:T(8,128)S(1)} %get-tuple-element.80.refs_0_), channel_id=1, source_target_pairs={{0,32},{16,48},{32,0},{48,16},{64,96},{80,112},{96,64},{112,80},{1... | collective-permute-start | bytes 49160 | tf_op jit(solution)/shard_map/ppermute | solution.py:472
  52.1 0.8 %shard_map.76 = (f32[3,256,128]{2,1,0:T(8,128)}, f32[3,256,128]{2,1,0:T(8,128)}) custom-call(f32[32,128]{1,0:T(8,128)S(1)} %get-tuple-element.83.ends_c, f32[256,128]{1,0:T(8,128)S(1)} %get-tuple-element.84.g_c, f32[256,128]{1,0:T(8,128)S(1)} %get-tuple-element.71.refs_17_.refs_5_.u, f32[256,128]{1,0:T(8,128)S(1)} %get-tuple-element.72.refs_18_.refs_6_.v, ...), custom_call_target="tpu_custom_call" | custom-call | flops 1000000 | bytes 1000000 | tf_op jit(solution)/shard_map/pallas_call | solution.py:459
  54.1 2.7 %collective-permute-start.19 = (f32[32,128]{1,0:T(8,128)S(1)}, f32[32,128]{1,0:T(8,128)S(1)}, u32[]{:S(2)}, u32[]{:S(2)}) collective-permute-start(f32[32,128]{1,0:T(8,128)S(1)} %get-tuple-element.87.refs_0_), channel_id=1, source_target_pairs={{0,192},{16,208},{32,224},{48,240},{64,128},{80,144},{96,160},{112... | collective-permute-start | bytes 49160 | tf_op jit(solution)/shard_map/ppermute | solution.py:472
  57.3 1.1 %collective-permute-start.17 = (f32[32,128]{1,0:T(8,128)S(1)}, f32[32,128]{1,0:T(8,128)S(1)}, u32[]{:S(2)}, u32[]{:S(2)}) collective-permute-start(f32[32,128]{1,0:T(8,128)S(1)} %get-tuple-element.87.refs_0_), channel_id=1, source_target_pairs={{0,128},{16,144},{32,160},{48,176},{64,192},{80,208},{96,224},{112... | collective-permute-start | bytes 49160 | tf_op jit(solution)/shard_map/ppermute | solution.py:472
  58.4 2.5 %shard_map.77 = (f32[3,256,128]{2,1,0:T(8,128)}, f32[3,256,128]{2,1,0:T(8,128)}) custom-call(f32[256,128]{1,0:T(8,128)S(1)} %get-tuple-element.90.part, f32[256,128]{1,0:T(8,128)S(1)} %get-tuple-element.91.rise_y, f32[256,128]{1,0:T(8,128)S(1)} %get-tuple-element.61.w.refs_8_, ...), custom_call_target="tpu_custom_call", output_to_operand_aliasing={{0}: (3, {}), {1}: (4, {})} | custom-call | flops 8000000 | bytes 1000000 | tf_op jit(solution)/shard_map/pallas_call | solution.py:459
  61.2 1.4 %shard_map.78 = (f32[3,256,128]{2,1,0:T(8,128)}, f32[3,256,128]{2,1,0:T(8,128)}) custom-call(s32[2]{0:T(128)S(1)} %pad_add_fusion.me, f32[4,112,128]{2,1,0:T(8,128)S(1)} %get-tuple-element.58.got_near.coefs.coefs_near, f32[4,112,128]{2,1,0:T(8,128)S(1)} %get-tuple-element.73.coefs_far, ...), custom_call_target="tpu_custom_call", output_to_operand_aliasing={{0}: (12, {}), {1}: (13, {})} | custom-call | flops 1000000 | bytes 1000000 | tf_op jit(solution)/shard_map/pallas_call | solution.py:459
  (29 shorter events, 7.8 us)
Async XLA Ops:
  1.5 10.1 %collective-permute-start = (f32[16,128]{1,0:T(8,128)S(1)}, f32[16,128]{1,0:T(8,128)S(1)}, u32[]{:S(2)}, u32[]{:S(2)}) collective-permute-start(f32[16,128]{1,0:T(8,128)S(1)} %bitcast.15), channel_id=1, source_target_pairs={{0,1},{1,2},{2,3},{3,4},{4,5},{5,6},{6,7},{7,8},{8,9},{9,10},{10,1... | collective-permute-start | bytes 24584 | tf_op jit(solution)/shard_map/ppermute | solution.py:498
  12.2 6.5 %collective-permute-start.3 = (f32[112,128]{1,0:T(8,128)S(1)}, f32[112,128]{1,0:T(8,128)S(1)}, u32[]{:S(2)}, u32[]{:S(2)}) collective-permute-start(f32[112,128]{1,0:T(8,128)S(1)} %get-tuple-element.57.refs_0_), channel_id=1, source_target_pairs={{0,48},{16,32},{32,16},{48,0},{64,112},{80,96},{96,80},{112,64},{1... | collective-permute-start | bytes 172040 | tf_op jit(solution)/shard_map/ppermute | solution.py:472
  14.9 3.9 %collective-permute-start.2 = (f32[112,128]{1,0:T(8,128)S(1)}, f32[112,128]{1,0:T(8,128)S(1)}, u32[]{:S(2)}, u32[]{:S(2)}) collective-permute-start(f32[112,128]{1,0:T(8,128)S(1)} %get-tuple-element.57.refs_0_), channel_id=1, source_target_pairs={{0,32},{16,48},{32,0},{48,16},{64,96},{80,112},{96,64},{112,80},{1... | collective-permute-start | bytes 172040 | tf_op jit(solution)/shard_map/ppermute | solution.py:472
  15.2 3.7 %collective-permute-start.1 = (f32[112,128]{1,0:T(8,128)S(1)}, f32[112,128]{1,0:T(8,128)S(1)}, u32[]{:S(2)}, u32[]{:S(2)}) collective-permute-start(f32[112,128]{1,0:T(8,128)S(1)} %get-tuple-element.57.refs_0_), channel_id=1, source_target_pairs={{0,16},{16,0},{32,48},{48,32},{64,80},{80,64},{96,112},{112,96},{1... | collective-permute-start | bytes 172040 | tf_op jit(solution)/shard_map/ppermute | solution.py:472
  15.4 8.3 %collective-permute-start.7 = (f32[128,128]{1,0:T(8,128)S(1)}, f32[128,128]{1,0:T(8,128)S(1)}, u32[]{:S(2)}, u32[]{:S(2)}) collective-permute-start(f32[128,128]{1,0:T(8,128)S(1)} %get-tuple-element.63), channel_id=1, source_target_pairs={{1,0},{2,1},{3,2},{4,3},{5,4},{6,5},{7,6},{8,7},{9,8},{10,9},{11,1... | collective-permute-start | bytes 196616 | tf_op jit(solution)/shard_map/ppermute | solution.py:512
  19.4 6.8 %collective-permute-start.6 = (f32[112,128]{1,0:T(8,128)S(1)}, f32[112,128]{1,0:T(8,128)S(1)}, u32[]{:S(2)}, u32[]{:S(2)}) collective-permute-start(f32[112,128]{1,0:T(8,128)S(1)} %get-tuple-element.59.refs_0_), channel_id=1, source_target_pairs={{0,192},{16,208},{32,224},{48,240},{64,128},{80,144},{96,160},{112... | collective-permute-start | bytes 172040 | tf_op jit(solution)/shard_map/ppermute | solution.py:472
  22.0 4.5 %collective-permute-start.5 = (f32[112,128]{1,0:T(8,128)S(1)}, f32[112,128]{1,0:T(8,128)S(1)}, u32[]{:S(2)}, u32[]{:S(2)}) collective-permute-start(f32[112,128]{1,0:T(8,128)S(1)} %get-tuple-element.59.refs_0_), channel_id=1, source_target_pairs={{0,64},{16,80},{32,96},{48,112},{64,0},{80,16},{96,32},{112,48},{1... | collective-permute-start | bytes 172040 | tf_op jit(solution)/shard_map/ppermute | solution.py:472
  22.6 3.9 %collective-permute-start.4 = (f32[112,128]{1,0:T(8,128)S(1)}, f32[112,128]{1,0:T(8,128)S(1)}, u32[]{:S(2)}, u32[]{:S(2)}) collective-permute-start(f32[112,128]{1,0:T(8,128)S(1)} %get-tuple-element.59.refs_0_), channel_id=1, source_target_pairs={{0,128},{16,144},{32,160},{48,176},{64,192},{80,208},{96,224},{112... | collective-permute-start | bytes 172040 | tf_op jit(solution)/shard_map/ppermute | solution.py:472
  27.8 4.6 %collective-permute-start.10 = (f32[112,128]{1,0:T(8,128)S(1)}, f32[112,128]{1,0:T(8,128)S(1)}, u32[]{:S(2)}, u32[]{:S(2)}) collective-permute-start(f32[112,128]{1,0:T(8,128)S(1)} %get-tuple-element.74.refs_0_), channel_id=1, source_target_pairs={{0,1},{1,0},{2,3},{3,2},{4,5},{5,4},{6,7},{7,6},{8,9},{9,8},{10,11... | collective-permute-start | bytes 172040 | tf_op jit(solution)/shard_map/ppermute | solution.py:472
  28.3 5.4 %collective-permute-start.9 = (f32[112,128]{1,0:T(8,128)S(1)}, f32[112,128]{1,0:T(8,128)S(1)}, u32[]{:S(2)}, u32[]{:S(2)}) collective-permute-start(f32[112,128]{1,0:T(8,128)S(1)} %get-tuple-element.74.refs_0_), channel_id=1, source_target_pairs={{0,3},{1,2},{2,1},{3,0},{4,7},{5,6},{6,5},{7,4},{8,11},{9,10},{10,... | collective-permute-start | bytes 172040 | tf_op jit(solution)/shard_map/ppermute | solution.py:472
  29.0 5.5 %collective-permute-start.8 = (f32[112,128]{1,0:T(8,128)S(1)}, f32[112,128]{1,0:T(8,128)S(1)}, u32[]{:S(2)}, u32[]{:S(2)}) collective-permute-start(f32[112,128]{1,0:T(8,128)S(1)} %get-tuple-element.74.refs_0_), channel_id=1, source_target_pairs={{0,2},{1,3},{2,0},{3,1},{4,6},{5,7},{6,4},{7,5},{8,10},{9,11},{10,... | collective-permute-start | bytes 172040 | tf_op jit(solution)/shard_map/ppermute | solution.py:472
  35.1 7.0 %collective-permute-start.13 = (f32[112,128]{1,0:T(8,128)S(1)}, f32[112,128]{1,0:T(8,128)S(1)}, u32[]{:S(2)}, u32[]{:S(2)}) collective-permute-start(f32[112,128]{1,0:T(8,128)S(1)} %get-tuple-element.76.refs_0_), channel_id=1, source_target_pairs={{0,8},{1,9},{2,10},{3,11},{4,12},{5,13},{6,14},{7,15},{8,0},{9,1},... | collective-permute-start | bytes 172040 | tf_op jit(solution)/shard_map/ppermute | solution.py:472
  40.1 5.4 %collective-permute-start.12 = (f32[112,128]{1,0:T(8,128)S(1)}, f32[112,128]{1,0:T(8,128)S(1)}, u32[]{:S(2)}, u32[]{:S(2)}) collective-permute-start(f32[112,128]{1,0:T(8,128)S(1)} %get-tuple-element.76.refs_0_), channel_id=1, source_target_pairs={{0,12},{1,13},{2,14},{3,15},{4,8},{5,9},{6,10},{7,11},{8,4},{9,5},... | collective-permute-start | bytes 172040 | tf_op jit(solution)/shard_map/ppermute | solution.py:472
  40.1 5.4 %collective-permute-start.11 = (f32[112,128]{1,0:T(8,128)S(1)}, f32[112,128]{1,0:T(8,128)S(1)}, u32[]{:S(2)}, u32[]{:S(2)}) collective-permute-start(f32[112,128]{1,0:T(8,128)S(1)} %get-tuple-element.76.refs_0_), channel_id=1, source_target_pairs={{0,4},{1,5},{2,6},{3,7},{4,0},{5,1},{6,2},{7,3},{8,12},{9,13},{10,... | collective-permute-start | bytes 172040 | tf_op jit(solution)/shard_map/ppermute | solution.py:472
  46.5 6.5 %collective-permute-start.16 = (f32[32,128]{1,0:T(8,128)S(1)}, f32[32,128]{1,0:T(8,128)S(1)}, u32[]{:S(2)}, u32[]{:S(2)}) collective-permute-start(f32[32,128]{1,0:T(8,128)S(1)} %get-tuple-element.80.refs_0_), channel_id=1, source_target_pairs={{0,48},{16,32},{32,16},{48,0},{64,112},{80,96},{96,80},{112,64},{1... | collective-permute-start | bytes 49160 | tf_op jit(solution)/shard_map/ppermute | solution.py:472
  50.9 2.7 %collective-permute-start.15 = (f32[32,128]{1,0:T(8,128)S(1)}, f32[32,128]{1,0:T(8,128)S(1)}, u32[]{:S(2)}, u32[]{:S(2)}) collective-permute-start(f32[32,128]{1,0:T(8,128)S(1)} %get-tuple-element.80.refs_0_), channel_id=1, source_target_pairs={{0,32},{16,48},{32,0},{48,16},{64,96},{80,112},{96,64},{112,80},{1... | collective-permute-start | bytes 49160 | tf_op jit(solution)/shard_map/ppermute | solution.py:472
  52.1 1.4 %collective-permute-start.14 = (f32[32,128]{1,0:T(8,128)S(1)}, f32[32,128]{1,0:T(8,128)S(1)}, u32[]{:S(2)}, u32[]{:S(2)}) collective-permute-start(f32[32,128]{1,0:T(8,128)S(1)} %get-tuple-element.80.refs_0_), channel_id=1, source_target_pairs={{0,16},{16,0},{32,48},{48,32},{64,80},{80,64},{96,112},{112,96},{1... | collective-permute-start | bytes 49160 | tf_op jit(solution)/shard_map/ppermute | solution.py:472
  54.1 6.8 %collective-permute-start.19 = (f32[32,128]{1,0:T(8,128)S(1)}, f32[32,128]{1,0:T(8,128)S(1)}, u32[]{:S(2)}, u32[]{:S(2)}) collective-permute-start(f32[32,128]{1,0:T(8,128)S(1)} %get-tuple-element.87.refs_0_), channel_id=1, source_target_pairs={{0,192},{16,208},{32,224},{48,240},{64,128},{80,144},{96,160},{112... | collective-permute-start | bytes 49160 | tf_op jit(solution)/shard_map/ppermute | solution.py:472
  56.8 4.4 %collective-permute-start.18 = (f32[32,128]{1,0:T(8,128)S(1)}, f32[32,128]{1,0:T(8,128)S(1)}, u32[]{:S(2)}, u32[]{:S(2)}) collective-permute-start(f32[32,128]{1,0:T(8,128)S(1)} %get-tuple-element.87.refs_0_), channel_id=1, source_target_pairs={{0,64},{16,80},{32,96},{48,112},{64,0},{80,16},{96,32},{112,48},{1... | collective-permute-start | bytes 49160 | tf_op jit(solution)/shard_map/ppermute | solution.py:472
  57.3 3.9 %collective-permute-start.17 = (f32[32,128]{1,0:T(8,128)S(1)}, f32[32,128]{1,0:T(8,128)S(1)}, u32[]{:S(2)}, u32[]{:S(2)}) collective-permute-start(f32[32,128]{1,0:T(8,128)S(1)} %get-tuple-element.87.refs_0_), channel_id=1, source_target_pairs={{0,128},{16,144},{32,160},{48,176},{64,192},{80,208},{96,224},{112... | collective-permute-start | bytes 49160 | tf_op jit(solution)/shard_map/ppermute | solution.py:472

commit v7 on v6

--- a/solution.py
+++ b/solution.py
@@ -152,11 +152,27 @@
 
 
 def stored(got, m, planes):
-    return [got[plane(k)] if m is None else got[m, plane(k)] for k in planes]
+    return [got[m, plane(k)] for k in planes]
+
+
+def loaded(msg, planes):
+    return [msg[plane(k)] for k in planes]
+
+
+def pick(values, index):
+    out = values[0]
+    for k in range(1, len(values)):
+        out = jnp.where(index == k, values[k], out)
+    return out
+
+
+def place(pos, axis, near):
+    here = pos[plane(axis)]
+    return lax.shift_right_logical(here, near.bit_length() - 1), lax.bitwise_and(here, near - 1)
 
 
 def tables_kernel(
-    me, eps_in, sig_in, material, elec_in, magn_in, w, c, p, u, v, flux, part, elec, magn, ez_first, ids, eps, sig, sems
+    me, eps_in, sig_in, material, elec_in, magn_in, w, c, p, u, v, flux, part, elec, magn, ez_first, pos, ids, eps, sig, sems
 ):
     loads = [(eps_in, eps), (sig_in, sig), (material, ids)]
     for field, to, k in ((elec_in, elec, 0), (magn_in, magn, 1), (elec_in, elec, 2), (magn_in, magn, 0)):
@@ -165,6 +181,8 @@
     loads = [pltpu.make_async_copy(a, b, sems.at[k]) for k, (a, b) in enumerate(loads)]
     for load in loads:
         load.start()
+    for axis in range(2):
+        pos[plane(axis)] = jnp.full((B, w.shape[1]), me[axis], jnp.int32)
     for load in loads[:3]:
         load.wait()
     ws = [eps[m] * (1.0 / (h * h)) + sig[m] * (0.5 / h) for m in range(eps.shape[0])]
@@ -196,9 +214,9 @@
         load.wait()
 
 
-def first_x_kernel(me, part, hx_prev, flux, p, u, v, elec, magn, g, msg):
+def first_x_kernel(pos, part, hx_prev, flux, p, u, v, elec, magn, g, msg):
     row = lax.broadcasted_iota(jnp.int32, hx_prev.shape, 0)
-    scale = jnp.where(me[1] == 0, 0.0, jnp.where(row == 0, 1.0 / h, 0.0))
+    scale = jnp.where(pos[plane(1)] == 0, 0.0, jnp.where(row == 0, 1.0 / h, 0.0))
 
     def source(i):
         return part[plane(i)] + hx_prev[pl.ds(i, 1)] * scale
@@ -219,9 +237,9 @@
     return blocks[0]
 
 
-def merge_kernel(axis, near, order, sources, halos, me, *refs):
+def merge_kernel(axis, near, order, sources, halos, pos, *refs):
     got, msg = refs[-2:]
-    blocks = collect(lax.rem(me[axis], near), order, refs[0], refs[1:near], got)
+    blocks = collect(place(pos, axis, near)[1], order, refs[0], refs[1:near], got)
     at = 2 * sources
     coefs, rows = merged([(b[at : at + 3], rows_of(b, sources)) for b in blocks])
     for k, value in enumerate([v for pair in rows for v in pair] + list(coefs)):
@@ -231,22 +249,22 @@
         msg[plane(6)] = blocks[-1][6]
 
 
-def merge_rows_kernel(axis, near, order, me, coefs, *refs):
+def merge_rows_kernel(axis, near, order, pos, coefs, *refs):
     got, msg = refs[-2:]
-    blocks = collect(lax.rem(me[axis], near), order, refs[0], refs[1:near], got)
+    blocks = collect(place(pos, axis, near)[1], order, refs[0], refs[1:near], got)
     _, rows = merged([(stored(coefs, m, (2, 3, 4)), rows_of(b, 1)) for m, b in enumerate(blocks)])
     msg[plane(0)], msg[plane(1)] = rows[0]
 
 
-def solved_ends(here, near, sources, near_rows, near_coefs, far_rows, far_coefs, own_near, own_far):
+def solved_ends(q, r, sources, near_rows, near_coefs, far_rows, far_coefs, own_near, own_far):
     zero = jnp.zeros_like(far_coefs[0][0])
-    outer = boundary(lax.div(here, near), far_rows, far_coefs, *own_far, [(zero, zero)] * sources)
-    return boundary(lax.rem(here, near), near_rows, near_coefs, *own_near, outer)
-
-
-def first_z_kernel(n, me, ef, mf, ez_next, w, c, p, u, v, r_top, src_top, curl, flux_y, flux_a, part_a, src, r):
-    factor(lambda j: w[strided(j)], me[1] == 0, p, u, v)
-    inside = jnp.where(me[1] == n - 1, 0.0, 1.0)
+    outer = boundary(q, far_rows, far_coefs, *own_far, [(zero, zero)] * sources)
+    return boundary(r, near_rows, near_coefs, *own_near, outer)
+
+
+def first_z_kernel(n, pos, ef, mf, ez_next, w, c, p, u, v, r_top, src_top, curl, flux_y, flux_a, part_a, src, r):
+    factor(lambda j: w[strided(j)], pos[plane(1)] == 0, p, u, v)
+    inside = jnp.where(pos[pl.ds(B, 1)] == n - 1, 0.0, 1.0)
     row = lax.broadcasted_iota(jnp.int32, (B, w.shape[1]), 0)
     for i in range(B):
         ez = ef[2, plane(i)]
@@ -271,25 +289,18 @@
     flux_y[...] = -(mx + rise)
 
 
-def both_y_kernel(near, far, order, me, got_near, *refs):
+def both_y_kernel(near, far, order, pos, got_near, own_near, *refs):
     others, refs = refs[:far], refs[far:]
     (g_b, u_x, v_x, flux_b, w, c, r_top, src_top, curl_in, flux_y_in, flux_a_in, part_a, p_y, u_y, v_y) = refs[:15]
     got_far, rise_y, curl, flux_y, flux_a, g_a, g_c, msg, part, fz = refs[15:]
-    me_x = me[0]
     top = plane(0)
-    q, r = lax.div(me_x, near), lax.rem(me_x, near)
+    q, r = place(pos, 0, near)
     far_blocks = collect(q, order, others[0], others[1:], got_far)
-    near_blocks = [stored(got_near, m, range(5)) for m in range(near)]
-    ey_next = jnp.where(
-        r < near - 1,
-        got_near[jnp.minimum(r + 1, near - 1), plane(5)],
-        jnp.where(q < far - 1, got_far[jnp.minimum(q + 1, far - 1), plane(5)], 0.0),
-    )
-    hz_prev = jnp.where(
-        r > 0,
-        got_near[jnp.maximum(r - 1, 0), plane(6)],
-        jnp.where(q > 0, got_far[jnp.maximum(q - 1, 0), plane(6)], 0.0),
-    )
+    near_blocks = [stored(got_near, m, range(7)) for m in range(near)]
+    after_group = jnp.where(q < far - 1, pick([b[5] for b in far_blocks], q + 1), 0.0)
+    ey_next = jnp.where(r < near - 1, pick([b[5] for b in near_blocks], r + 1), after_group)
+    before_group = jnp.where(q > 0, pick([b[6] for b in far_blocks], q - 1), 0.0)
+    hz_prev = jnp.where(r > 0, pick([b[6] for b in near_blocks], r - 1), before_group)
     curl[...] = curl_in[...]
     flux_y[...] = flux_y_in[...]
     flux_a[...] = flux_a_in[...]
@@ -311,21 +322,21 @@
     first_a, last_a = eliminate(source_a, p_y, g_a)
     last_a = last_a - flux_a[strided(B - 1)]
 
-    own_near, own_far = stored(got_near, r, range(5)), stored(others[0], None, range(5))
+    own, own_group = loaded(own_near, range(5)), loaded(others[0], range(5))
     ((before, after),) = solved_ends(
-        me_x,
-        near,
+        q,
+        r,
         1,
         [rows_of(b, 1) for b in near_blocks],
         [b[2:5] for b in near_blocks],
         [rows_of(b, 1) for b in far_blocks],
         [b[2:5] for b in far_blocks],
-        (rows_of(own_near, 1), own_near[2:5]),
-        (rows_of(own_far, 1), own_far[2:5]),
+        (rows_of(own, 1), own[2:5]),
+        (rows_of(own_group, 1), own_group[2:5]),
     )
     for i in range(B):
         fz[plane(i)] = g_b[plane(i)] + (u_x[plane(i)] * before + v_x[plane(i)] * after)
-    my_before = jnp.where(me_x == 0, 0.0, fz[top] - before)
+    my_before = jnp.where(pos[plane(0)] == 0, 0.0, fz[top] - before)
     for i in range(B):
         here = fz[plane(i)]
         rise = (fz[plane(i + 1)] if i < B - 1 else after) - here
@@ -347,29 +358,29 @@
         msg[plane(k)] = value
 
 
-def second_x_kernel(near, far, order, me, got_near, *refs):
+def second_x_kernel(near, far, order, pos, got_near, own_near, *refs):
     others, refs = refs[:far], refs[far:]
     g_a, u, v, flux_a, c, curl, p_x, part, flux2, g2, ends_c, msg, got_far, fx = refs
-    my = me[1]
-    far_blocks = collect(lax.div(my, near), order, others[0], others[1:], got_far)
+    q, r = place(pos, 1, near)
+    far_blocks = collect(q, order, others[0], others[1:], got_far)
     near_blocks = [stored(got_near, m, range(7)) for m in range(near)]
-    own_near, own_far = stored(got_near, lax.rem(my, near), range(7)), stored(others[0], None, range(7))
+    own, own_group = loaded(own_near, range(7)), loaded(others[0], range(7))
     (before, after), (before_c, after_c) = solved_ends(
-        my,
-        near,
+        q,
+        r,
         2,
         [rows_of(b, 2) for b in near_blocks],
         [b[4:7] for b in near_blocks],
         [rows_of(b, 2) for b in far_blocks],
         [b[4:7] for b in far_blocks],
-        (rows_of(own_near, 2), own_near[4:7]),
-        (rows_of(own_far, 2), own_far[4:7]),
+        (rows_of(own, 2), own[4:7]),
+        (rows_of(own_group, 2), own_group[4:7]),
     )
     ends_c[plane(0)] = before_c
     ends_c[plane(1)] = after_c
     for j in range(B):
         fx[plane(j)] = g_a[plane(j)] + (u[plane(j)] * before + v[plane(j)] * after)
-    mz_before = jnp.where(my == 0, 0.0, fx[plane(0)] - before)
+    mz_before = jnp.where(pos[plane(1)] == 0, 0.0, fx[plane(0)] - before)
     for j in range(B):
         here = fx[plane(j)]
         rise = (fx[plane(j + 1)] if j < B - 1 else after) - here
@@ -389,7 +400,7 @@
     msg[plane(1)] = last - flux2[plane(B - 1)]
 
 
-def second_y_kernel(ends_c, g_c, u, v, flux_y, elec, magn, full_z, new_x, sems):
+def second_y_kernel(ends_c, g_c, u, v, flux_y, part, rise_y, w, elec, magn, full_x, new_y, full_z, new_x, sems):
     stores = [(full_z, elec.at[2]), (new_x, magn.at[0])]
     stores = [pltpu.make_async_copy(a, b, sems.at[k]) for k, (a, b) in enumerate(stores)]
     before, after = ends_c[plane(0)], ends_c[plane(1)]
@@ -403,38 +414,49 @@
     new_x[strided(B - 1)] = -h * (flux_y[strided(B - 1)] + (after - here))
     for store in stores:
         store.start()
+    rows = pl.ds(0, w.shape[0] // 2)
+    a = rise_y[rows]
+    x = solve_z(part[rows] - behind_z(a), w[rows])
+    full_x[...] = x
+    new_y[...] = h * (a - ahead_z(x))
     for store in stores:
         store.wait()
 
 
-def second_z_kernel(part, rise_y, w, _, __, elec, magn, full_x, new_y, sems):
-    stores = [(full_x, elec.at[0]), (new_y, magn.at[1])]
-    stores = [pltpu.make_async_copy(a, b, sems.at[k]) for k, (a, b) in enumerate(stores)]
-    a = rise_y[...]
-    x = solve_z(part[...] - behind_z(a), w[...])
+def second_z_kernel(part, rise_y, w, x_half, y_half, _, __, elec, magn, full_x, new_y, sems):
+    size = w.shape[0] // 2
+    rows = [pl.ds(0, size), pl.ds(size, size)]
+    stores = [(x_half, 0, elec, 0), (y_half, 0, magn, 1), (full_x, 1, elec, 0), (new_y, 1, magn, 1)]
+    stores = [
+        pltpu.make_async_copy(a, b.at[k, rows[at]], sems.at[i]) for i, (a, at, b, k) in enumerate(stores)
+    ]
+    stores[0].start()
+    stores[1].start()
+    a = rise_y[rows[1]]
+    x = solve_z(part[rows[1]] - behind_z(a), w[rows[1]])
     full_x[...] = x
-    stores[0].start()
+    stores[2].start()
     new_y[...] = h * (a - ahead_z(x))
-    stores[1].start()
+    stores[3].start()
     for store in stores:
         store.wait()
 
 
-def last_kernel(near, far, order, me, coefs_near, coefs_far, got_near, *refs):
+def last_kernel(near, far, order, pos, coefs_near, coefs_far, own_b, group_b, got_near, own_near, *refs):
     others, refs = refs[:far], refs[far:]
     g, u, v, flux2, _, _, elec, magn, got_far, full_y, new_z, sems = refs
-    q, r = lax.div(me[0], near), lax.rem(me[0], near)
+    q, r = place(pos, 0, near)
     far_blocks = collect(q, order, others[0], others[1:], got_far)
     ((before, after),) = solved_ends(
-        me[0],
-        near,
+        q,
+        r,
         1,
         [rows_of(stored(got_near, m, range(2)), 1) for m in range(near)],
         [stored(coefs_near, m, (2, 3, 4)) for m in range(near)],
         [rows_of(b, 1) for b in far_blocks],
         [stored(coefs_far, m, (2, 3, 4)) for m in range(far)],
-        (rows_of(stored(got_near, r, range(2)), 1), stored(coefs_near, r, (2, 3, 4))),
-        (rows_of(stored(others[0], None, range(2)), 1), stored(coefs_far, q, (2, 3, 4))),
+        (rows_of(loaded(own_near, range(2)), 1), loaded(own_b, (2, 3, 4))),
+        (rows_of(loaded(others[0], range(2)), 1), loaded(group_b, (2, 3, 4))),
     )
     stores = [(full_y, elec.at[1]), (new_z, magn.at[2])]
     stores = [pltpu.make_async_copy(a, b, sems.at[k]) for k, (a, b) in enumerate(stores)]
@@ -455,11 +477,11 @@
 
 
 def call(kernel, ins, outs, specs=None, out_specs=None, scratch=(), aliases=None, flops=1_000_000):
-    shapes = [pltpu.HBM(s, F32) if out_specs else jax.ShapeDtypeStruct(s, F32) for s in outs]
+    shapes = [jax.ShapeDtypeStruct(s, F32) if isinstance(s, tuple) else s for s in outs]
     return pl.pallas_call(
         kernel,
         out_shape=shapes,
-        in_specs=specs or [SMEM] + [VMEM] * (len(ins) - 1),
+        in_specs=specs or [VMEM] * len(ins),
         out_specs=out_specs or [VMEM] * len(outs),
         scratch_shapes=[pltpu.VMEM(s, F32) if isinstance(s, tuple) else s for s in scratch],
         input_output_aliases=aliases or {},
@@ -496,84 +518,85 @@
     ]
 
     hx_prev = lax.ppermute(magnetic[0, :, B - 1], "py", [(i, (i + 1) % ny) for i in range(ny)])
-    w, c, p_x, u_x, v_x, flux_b, part_b, ef, mf, ez_first = call(
+    w, c, p_x, u_x, v_x, flux_b, part_b, ef, mf, ez_first, pos = call(
         tables_kernel,
         [me, in_hbm(permittivity), in_hbm(conductivity), ids, elec, magn],
-        [cells] * 7 + [(3, *cells)] * 2 + [(8 * B, nz)],
+        [cells] * 7 + [(3, *cells)] * 2 + [(8 * B, nz), jax.ShapeDtypeStruct((2 * B, nz), jnp.int32)],
         specs=[SMEM] + [HBM] * 5,
         scratch=[pltpu.VMEM(cells, jnp.int32)] + [pltpu.SMEM(permittivity.shape, F32)] * 2 + [dma((9,))],
     )
-    g_b, msg = call(
+    g_b, own_b = call(
         first_x_kernel,
-        [me, part_b, hx_prev, flux_b, p_x, u_x, v_x, ef, mf],
+        [pos, part_b, hx_prev, flux_b, p_x, u_x, v_x, ef, mf],
         [cells, (7 * B, nz)],
     )
-    ins = shared(msg, "px", nx, 1, px_near)
+    ins = shared(own_b, "px", nx, 1, px_near)
     ez_next = lax.ppermute(ez_first, "py", [((i + 1) % ny, i) for i in range(ny)])
-    near_b, msg = call(
+    near_b, group_b = call(
         functools.partial(merge_kernel, 0, near_x, px_near, 1, True),
-        [me] + ins,
+        [pos] + ins,
         [(near_x, 7 * B, nz), (7 * B, nz)],
     )
-    ins = shared(msg, "px", nx, near_x, px_far)
+    ins = shared(group_b, "px", nx, near_x, px_far)
     p_y, u_y, v_y, r_top, src_top, curl, flux_y, flux_a, part_a = call(
         functools.partial(first_z_kernel, ny),
-        [me, ef, mf, ez_next, w, c],
+        [pos, ef, mf, ez_next, w, c],
         [cells] * 3 + [(B, nz)] * 2 + [cells] * 4,
         scratch=[cells] * 2,
         flops=8_000_000,
     )
-    ins = [me, near_b] + ins + [g_b, u_x, v_x, flux_b, w, c, r_top, src_top]
-    far_b, rise_y, curl, flux_y, flux_a, g_a, g_c, msg = call(
+    ins = [pos, near_b, own_b] + ins + [g_b, u_x, v_x, flux_b, w, c, r_top, src_top]
+    far_b, rise_y, curl, flux_y, flux_a, g_a, g_c, own_ac = call(
         functools.partial(both_y_kernel, near_x, far_x, px_far),
         ins + [curl, flux_y, flux_a, part_a, p_y, u_y, v_y],
         [(far_x, 7 * B, nz)] + [cells] * 6 + [(7 * B, nz)],
         scratch=[cells] * 2,
     )
-    ins = shared(msg, "py", ny, 1, py_near)
+    ins = shared(own_ac, "py", ny, 1, py_near)
     near_ac, msg = call(
-        functools.partial(merge_kernel, 1, near_y, py_near, 2, False), [me] + ins, [(near_y, 7 * B, nz), (7 * B, nz)]
+        functools.partial(merge_kernel, 1, near_y, py_near, 2, False), [pos] + ins, [(near_y, 7 * B, nz), (7 * B, nz)]
     )
     ins = shared(msg, "py", ny, near_y, py_far)
-    part_x, flux2, g2, ends_c, msg = call(
+    part_x, flux2, g2, ends_c, own_a = call(
         functools.partial(second_x_kernel, near_y, far_y, py_far),
-        [me, near_ac] + ins + [g_a, u_y, v_y, flux_a, c, curl, p_x],
+        [pos, near_ac, own_ac] + ins + [g_a, u_y, v_y, flux_a, c, curl, p_x],
         [cells] * 3 + [(2 * B, nz)] * 2,
         scratch=[(far_y, 7 * B, nz), cells],
     )
-    ins = shared(msg, "px", nx, 1, px_near)
-    elec, magn = call(
+    ins = shared(own_a, "px", nx, 1, px_near)
+    half, whole = (B * B // 2, nz), pltpu.HBM((3, *cells), F32)
+    elec, magn, x_half, y_half = call(
         second_y_kernel,
-        [ends_c, g_c, u_y, v_y, flux_y],
-        [(3, *cells)] * 2,
-        specs=[VMEM] * 5,
-        out_specs=[HBM] * 2,
+        [ends_c, g_c, u_y, v_y, flux_y, part_x, rise_y, w],
+        [whole, whole, half, half],
+        out_specs=[HBM] * 2 + [VMEM] * 2,
         scratch=[cells] * 2 + [dma((2,))],
+        flops=4_000_000,
     )
     near_a, msg = call(
         functools.partial(merge_rows_kernel, 0, near_x, px_near),
-        [me, near_b] + ins,
+        [pos, near_b] + ins,
         [(near_x, 2 * B, nz), (2 * B, nz)],
     )
     msg, elec = lax.optimization_barrier((msg, elec))
     ins = shared(msg, "px", nx, near_x, px_far)
     elec, magn = call(
         second_z_kernel,
-        [part_x, rise_y, w, elec, magn],
-        [(3, *cells)] * 2,
-        specs=[VMEM] * 3 + [HBM] * 2,
+        [part_x, rise_y, w, x_half, y_half, elec, magn],
+        [whole] * 2,
+        specs=[VMEM] * 5 + [HBM] * 2,
         out_specs=[HBM] * 2,
-        scratch=[cells] * 2 + [dma((2,))],
-        aliases={3: 0, 4: 1},
-        flops=8_000_000,
-    )
-    ins = [me, near_b, far_b, near_a] + ins + [g2, u_x, v_x, flux2]
+        scratch=[half] * 2 + [dma((4,))],
+        aliases={5: 0, 6: 1},
+        flops=4_000_000,
+    )
+    ins = [pos, near_b, far_b, own_b, group_b, near_a, own_a] + ins + [g2, u_x, v_x, flux2]
     at = len(ins)
     out = call(
         functools.partial(last_kernel, near_x, far_x, px_far),
         ins + [elec, magn],
-        [(3, *cells)] * 2,
-        specs=[SMEM] + [VMEM] * (at - 1) + [HBM] * 2,
+        [whole] * 2,
+        specs=[VMEM] * at + [HBM] * 2,
         out_specs=[HBM] * 2,
         scratch=[(far_x, 2 * B, nz), cells, cells, dma((2,))],
         aliases={at: 0, at + 1: 1},

time: 63.2 us -> 59.2 us (0.937)
  Pallas kernels: 13.8 us -> 10 us
    pallas_call x11, Pallas kernels: 13.8 us -> 10 us  [call(): pl.pallas_call(kernel, out_shape=shapes, in_specs=specs or [VMEM] * len(i...]
  transfers between devices with their start and end apart: 20 -> 20, of which waited for: 10 -> 9; matrix products, arithmetic and copies ran while one was open for 0% -> 0% of each run, Pallas kernels for 13% -> 13%
where the time goes in v7:
time: 59.2 us; the launch traced here: 58.9 us
  starting transfers between devices  34.2 us (58%)
  waiting for transfers between devices  12.8 us (22%)
  Pallas kernels  10 us (17%)
  between operations  0.9 us (2%)
  local copies, waits for them, and re-layouts  0.85 us (1%)
    ppermute x18, starting transfers between devices, shared(): lax.ppermute(value, axis, [(i, i ^ step * s) for i in range(n)])  27.2 us
    pallas_call x11, Pallas kernels, call(): pl.pallas_call(kernel, out_shape=shapes, in_specs=specs or [VMEM] * len(i...  10 us
    ppermute x18, waiting for transfers between devices, shared(): lax.ppermute(value, axis, [(i, i ^ step * s) for i in range(n)])  8.47 us
    ppermute x1, waiting for transfers between devices, local(): lax.ppermute(magnetic[0, :, B - 1], 'py', [(i, (i + 1) % ny) for i in ran...  4.33 us
    ppermute x1, starting transfers between devices, local(): lax.ppermute(magnetic[0, :, B - 1], 'py', [(i, (i + 1) % ny) for i in ran...  3.74 us
    ppermute x1, starting transfers between devices, local(): lax.ppermute(ez_first, 'py', [((i + 1) % ny, i) for i in range(ny)])  3.25 us
  transfers between devices with their start and end apart: 20, of which 9 were waited for; matrix products, arithmetic and copies ran while one was open for 0% of the time, Pallas kernels for 13%

profile of v7, /device:TPU:1, one launch (start us, length us, event | category | flops | bytes accessed | tf_op | source)
XLA Modules:
  0.0 58.9 jit_solution(2473710967326653193)
XLA Ops:
  0.6 0.9 %slice.3 = f32[1,16,1,128]{3,2,1,0:T(1,128)S(1)} slice(f32[3,16,16,128]{3,2,1,0:T(8,128)} %param.6), slice={[0:1], [0:16], [15:16], [0:128]} | slice | bytes 16384 | tf_op jit(solution)/shard_map/slice | solution.py:520
  1.5 3.7 %collective-permute-start = (f32[16,128]{1,0:T(8,128)S(1)}, f32[16,128]{1,0:T(8,128)S(1)}, u32[]{:S(2)}, u32[]{:S(2)}) collective-permute-start(f32[16,128]{1,0:T(8,128)S(1)} %bitcast.15), channel_id=1, source_target_pairs={{0,1},{1,2},{2,3},{3,4},{4,5},{5,6},{6,7},{7,8},{8,9},{9,10},{10,1... | collective-permute-start | bytes 24584 | tf_op jit(solution)/shard_map/ppermute | solution.py:520
  5.3 1.9 %shard_map.68 = (f32[256,128]{1,0:T(8,128)S(1)}, f32[256,128]{1,0:T(8,128)S(1)}, f32[256,128]{1,0:T(8,128)S(1)}, f32[256,128]{1,0:T(8,128)S(1)}, f32[256,128]{1,...) custom-call(s32[2]{0:T(128)S(1)} %pad_add_fusion.me, ...), custom_call_target="tpu_custom_call" | custom-call | flops 1000000 | bytes 1000000 | tf_op jit(solution)/shard_map/pallas_call | solution.py:481
  7.2 4.3 %collective-permute-done.hx_prev = f32[16,128]{1,0:T(8,128)S(1)} collective-permute-done((f32[16,128]{1,0:T(8,128)S(1)}, f32[16,128]{1,0:T(8,128)S(1)}, u32[]{:S(2)}, u32[]{:S(2)}) %collective-permute-start) | collective-permute-done | bytes 8224 | tf_op jit(solution)/shard_map/ppermute | solution.py:520
  11.6 2.7 %collective-permute-start.3 = (f32[112,128]{1,0:T(8,128)S(1)}, f32[112,128]{1,0:T(8,128)S(1)}, u32[]{:S(2)}, u32[]{:S(2)}) collective-permute-start(f32[112,128]{1,0:T(8,128)S(1)} %get-tuple-element.61.refs_0_.own_near.own_b), channel_id=1, source_target_pairs={{0,48},{16,32},{32,16},{48,0},{64,112},{80,96},{96,80},{112,64},{1... | collective-permute-start | bytes 172040 | tf_op jit(solution)/shard_map/ppermute | solution.py:494
  14.9 3.2 %collective-permute-start.7 = (f32[128,128]{1,0:T(8,128)S(1)}, f32[128,128]{1,0:T(8,128)S(1)}, u32[]{:S(2)}, u32[]{:S(2)}) collective-permute-start(f32[128,128]{1,0:T(8,128)S(1)} %get-tuple-element.67), channel_id=1, source_target_pairs={{1,0},{2,1},{3,2},{4,3},{5,4},{6,5},{7,6},{8,7},{9,8},{10,9},{11,1... | collective-permute-start | bytes 196616 | tf_op jit(solution)/shard_map/ppermute | solution.py:534
  18.4 2.5 %collective-permute-start.6 = (f32[112,128]{1,0:T(8,128)S(1)}, f32[112,128]{1,0:T(8,128)S(1)}, u32[]{:S(2)}, u32[]{:S(2)}) collective-permute-start(f32[112,128]{1,0:T(8,128)S(1)} %get-tuple-element.63.refs_0_.group_b), channel_id=1, source_target_pairs={{0,192},{16,208},{32,224},{48,240},{64,128},{80,144},{96,160},{112... | collective-permute-start | bytes 172040 | tf_op jit(solution)/shard_map/ppermute | solution.py:494
  21.5 1.1 %collective-permute-start.4 = (f32[112,128]{1,0:T(8,128)S(1)}, f32[112,128]{1,0:T(8,128)S(1)}, u32[]{:S(2)}, u32[]{:S(2)}) collective-permute-start(f32[112,128]{1,0:T(8,128)S(1)} %get-tuple-element.63.refs_0_.group_b), channel_id=1, source_target_pairs={{0,128},{16,144},{32,160},{48,176},{64,192},{80,208},{96,224},{112... | collective-permute-start | bytes 172040 | tf_op jit(solution)/shard_map/ppermute | solution.py:494
  22.6 2.0 %shard_map.71 = (f32[256,128]{1,0:T(8,128)S(1)}, f32[256,128]{1,0:T(8,128)S(1)}, f32[256,128]{1,0:T(8,128)S(1)}, f32[16,128]{1,0:T(8,128)S(1)}, f32[16,128]{1,0:...) custom-call(s32[32,128]{1,0:T(8,128)S(1)} %get-tuple-element.53.pos,, ...), custom_call_target="tpu_custom_call" | custom-call | flops 8000000 | bytes 1000000 | tf_op jit(solution)/shard_map/pallas_call | solution.py:481
  25.4 0.8 %shard_map.72 = (f32[4,112,128]{2,1,0:T(8,128)S(1)}, f32[256,128]{1,0:T(8,128)S(1)}, f32[256,128]{1,0:T(8,128)S(1)}, f32[256,128]{1,0:T(8,128)S(1)}, f32[256,128...) custom-call(s32[32,128]{1,0:T(8,128)S(1)} %get-tuple-element.53.pos, ...), custom_call_target="tpu_custom_call" | custom-call | flops 1000000 | bytes 1000000 | tf_op jit(solution)/shard_map/pallas_call | solution.py:481
  27.4 3.1 %collective-permute-start.8 = (f32[112,128]{1,0:T(8,128)S(1)}, f32[112,128]{1,0:T(8,128)S(1)}, u32[]{:S(2)}, u32[]{:S(2)}) collective-permute-start(f32[112,128]{1,0:T(8,128)S(1)} %get-tuple-element.78.refs_0_.own_near), channel_id=1, source_target_pairs={{0,2},{1,3},{2,0},{3,1},{4,6},{5,7},{6,4},{7,5},{8,10},{9,11},{10,... | collective-permute-start | bytes 172040 | tf_op jit(solution)/shard_map/ppermute | solution.py:494
  30.8 1.2 %collective-permute-done.9.refs_2_ = f32[112,128]{1,0:T(8,128)S(1)} collective-permute-done((f32[112,128]{1,0:T(8,128)S(1)}, f32[112,128]{1,0:T(8,128)S(1)}, u32[]{:S(2)}, u32[]{:S(2)}) %collective-permute-start.9) | collective-permute-done | bytes 57376 | tf_op jit(solution)/shard_map/ppermute | solution.py:494
  32.0 0.9 %collective-permute-done.8.refs_1_ = f32[112,128]{1,0:T(8,128)S(1)} collective-permute-done((f32[112,128]{1,0:T(8,128)S(1)}, f32[112,128]{1,0:T(8,128)S(1)}, u32[]{:S(2)}, u32[]{:S(2)}) %collective-permute-start.8) | collective-permute-done | bytes 57376 | tf_op jit(solution)/shard_map/ppermute | solution.py:494
  33.0 5.0 %collective-permute-start.13 = (f32[112,128]{1,0:T(8,128)S(1)}, f32[112,128]{1,0:T(8,128)S(1)}, u32[]{:S(2)}, u32[]{:S(2)}) collective-permute-start(f32[112,128]{1,0:T(8,128)S(1)} %get-tuple-element.80.refs_0_), channel_id=1, source_target_pairs={{0,8},{1,9},{2,10},{3,11},{4,12},{5,13},{6,14},{7,15},{8,0},{9,1},... | collective-permute-start | bytes 172040 | tf_op jit(solution)/shard_map/ppermute | solution.py:494
  38.7 1.6 %collective-permute-done.13.refs_3_ = f32[112,128]{1,0:T(8,128)S(1)} collective-permute-done((f32[112,128]{1,0:T(8,128)S(1)}, f32[112,128]{1,0:T(8,128)S(1)}, u32[]{:S(2)}, u32[]{:S(2)}) %collective-permute-start.13) | collective-permute-done | bytes 57376 | tf_op jit(solution)/shard_map/ppermute | solution.py:494
  40.4 3.0 %collective-permute-done.12.refs_2_ = f32[112,128]{1,0:T(8,128)S(1)} collective-permute-done((f32[112,128]{1,0:T(8,128)S(1)}, f32[112,128]{1,0:T(8,128)S(1)}, u32[]{:S(2)}, u32[]{:S(2)}) %collective-permute-start.12) | collective-permute-done | bytes 57376 | tf_op jit(solution)/shard_map/ppermute | solution.py:494
  43.8 4.4 %collective-permute-start.16 = (f32[32,128]{1,0:T(8,128)S(1)}, f32[32,128]{1,0:T(8,128)S(1)}, u32[]{:S(2)}, u32[]{:S(2)}) collective-permute-start(f32[32,128]{1,0:T(8,128)S(1)} %get-tuple-element.84.refs_0_.own_near), channel_id=1, source_target_pairs={{0,48},{16,32},{32,16},{48,0},{64,112},{80,96},{96,80},{112,64},{1... | collective-permute-start | bytes 49160 | tf_op jit(solution)/shard_map/ppermute | solution.py:494
  48.1 1.2 %collective-permute-start.15 = (f32[32,128]{1,0:T(8,128)S(1)}, f32[32,128]{1,0:T(8,128)S(1)}, u32[]{:S(2)}, u32[]{:S(2)}) collective-permute-start(f32[32,128]{1,0:T(8,128)S(1)} %get-tuple-element.84.refs_0_.own_near), channel_id=1, source_target_pairs={{0,32},{16,48},{32,0},{48,16},{64,96},{80,112},{96,64},{112,80},{1... | collective-permute-start | bytes 49160 | tf_op jit(solution)/shard_map/ppermute | solution.py:494
  49.3 2.0 %shard_map.76 = (f32[3,256,128]{2,1,0:T(8,128)}, f32[3,256,128]{2,1,0:T(8,128)}, f32[128,128]{1,0:T(8,128)S(1)}, f32[128,128]{1,0:T(8,128)S(1)}) custom-call(f32[32,128]{1,0:T(8,128)S(1)} %get-tuple-element.87.ends_c, f32[256,128]{1,0:T(8,128)S(1)} %get-tuple-element.88.g_c, f32[256,128]{1,0:T(8,128)S(1)} %get-tuple-element.75.refs_17_.refs_5_.u, ...), custom_call_target="tpu_custom_call" | custom-call | flops 4000000 | bytes 1000000 | tf_op jit(solution)/shard_map/pallas_call | solution.py:481
  51.4 2.1 %collective-permute-start.19 = (f32[32,128]{1,0:T(8,128)S(1)}, f32[32,128]{1,0:T(8,128)S(1)}, u32[]{:S(2)}, u32[]{:S(2)}) collective-permute-start(f32[32,128]{1,0:T(8,128)S(1)} %get-tuple-element.93.refs_0_), channel_id=1, source_target_pairs={{0,192},{16,208},{32,224},{48,240},{64,128},{80,144},{96,160},{112... | collective-permute-start | bytes 49160 | tf_op jit(solution)/shard_map/ppermute | solution.py:494
  53.5 0.9 %collective-permute-start.18 = (f32[32,128]{1,0:T(8,128)S(1)}, f32[32,128]{1,0:T(8,128)S(1)}, u32[]{:S(2)}, u32[]{:S(2)}) collective-permute-start(f32[32,128]{1,0:T(8,128)S(1)} %get-tuple-element.93.refs_0_), channel_id=1, source_target_pairs={{0,64},{16,80},{32,96},{48,112},{64,0},{80,16},{96,32},{112,48},{1... | collective-permute-start | bytes 49160 | tf_op jit(solution)/shard_map/ppermute | solution.py:494
  54.4 1.2 %collective-permute-start.17 = (f32[32,128]{1,0:T(8,128)S(1)}, f32[32,128]{1,0:T(8,128)S(1)}, u32[]{:S(2)}, u32[]{:S(2)}) collective-permute-start(f32[32,128]{1,0:T(8,128)S(1)} %get-tuple-element.93.refs_0_), channel_id=1, source_target_pairs={{0,128},{16,144},{32,160},{48,176},{64,192},{80,208},{96,224},{112... | collective-permute-start | bytes 49160 | tf_op jit(solution)/shard_map/ppermute | solution.py:494
  55.6 1.9 %shard_map.77 = (f32[3,256,128]{2,1,0:T(8,128)}, f32[3,256,128]{2,1,0:T(8,128)}) custom-call(f32[256,128]{1,0:T(8,128)S(1)} %get-tuple-element.90.part, f32[256,128]{1,0:T(8,128)S(1)} %get-tuple-element.91.rise_y, f32[256,128]{1,0:T(8,128)S(1)} %get-tuple-element.65.w.refs_8_, ...), custom_call_target="tpu_custom_call", output_to_operand_aliasing={{0}: (5, {}), {1}: (6, {})} | custom-call | flops 4000000 | bytes 1000000 | tf_op jit(solution)/shard_map/pallas_call | solution.py:481
  57.9 0.8 %shard_map.78 = (f32[3,256,128]{2,1,0:T(8,128)}, f32[3,256,128]{2,1,0:T(8,128)}) custom-call(s32[32,128]{1,0:T(8,128)S(1)} %get-tuple-element.53.pos, f32[4,112,128]{2,1,0:T(8,128)S(1)} %get-tuple-element.62.got_near.coefs.coefs_near, f32[4,112,128]{2,1,0:T(8,128)S(1)} %get-tuple-element.77.coefs_far, ...), custom_call_target="tpu_custom_call", output_to_operand_aliasing={{0}: (15, {}), {1}: (16, {})} | custom-call | flops 1000000 | bytes 1000000 | tf_op jit(solution)/shard_map/pallas_call | solution.py:481
  (29 shorter events, 5.5 us)
Async XLA Ops:
  1.5 10.1 %collective-permute-start = (f32[16,128]{1,0:T(8,128)S(1)}, f32[16,128]{1,0:T(8,128)S(1)}, u32[]{:S(2)}, u32[]{:S(2)}) collective-permute-start(f32[16,128]{1,0:T(8,128)S(1)} %bitcast.15), channel_id=1, source_target_pairs={{0,1},{1,2},{2,3},{3,4},{4,5},{5,6},{6,7},{7,8},{8,9},{9,10},{10,1... | collective-permute-start | bytes 24584 | tf_op jit(solution)/shard_map/ppermute | solution.py:520
  11.6 6.5 %collective-permute-start.3 = (f32[112,128]{1,0:T(8,128)S(1)}, f32[112,128]{1,0:T(8,128)S(1)}, u32[]{:S(2)}, u32[]{:S(2)}) collective-permute-start(f32[112,128]{1,0:T(8,128)S(1)} %get-tuple-element.61.refs_0_.own_near.own_b), channel_id=1, source_target_pairs={{0,48},{16,32},{32,16},{48,0},{64,112},{80,96},{96,80},{112,64},{1... | collective-permute-start | bytes 172040 | tf_op jit(solution)/shard_map/ppermute | solution.py:494
  14.4 3.9 %collective-permute-start.2 = (f32[112,128]{1,0:T(8,128)S(1)}, f32[112,128]{1,0:T(8,128)S(1)}, u32[]{:S(2)}, u32[]{:S(2)}) collective-permute-start(f32[112,128]{1,0:T(8,128)S(1)} %get-tuple-element.61.refs_0_.own_near.own_b), channel_id=1, source_target_pairs={{0,32},{16,48},{32,0},{48,16},{64,96},{80,112},{96,64},{112,80},{1... | collective-permute-start | bytes 172040 | tf_op jit(solution)/shard_map/ppermute | solution.py:494
  14.6 3.7 %collective-permute-start.1 = (f32[112,128]{1,0:T(8,128)S(1)}, f32[112,128]{1,0:T(8,128)S(1)}, u32[]{:S(2)}, u32[]{:S(2)}) collective-permute-start(f32[112,128]{1,0:T(8,128)S(1)} %get-tuple-element.61.refs_0_.own_near.own_b), channel_id=1, source_target_pairs={{0,16},{16,0},{32,48},{48,32},{64,80},{80,64},{96,112},{112,96},{1... | collective-permute-start | bytes 172040 | tf_op jit(solution)/shard_map/ppermute | solution.py:494
  14.9 7.7 %collective-permute-start.7 = (f32[128,128]{1,0:T(8,128)S(1)}, f32[128,128]{1,0:T(8,128)S(1)}, u32[]{:S(2)}, u32[]{:S(2)}) collective-permute-start(f32[128,128]{1,0:T(8,128)S(1)} %get-tuple-element.67), channel_id=1, source_target_pairs={{1,0},{2,1},{3,2},{4,3},{5,4},{6,5},{7,6},{8,7},{9,8},{10,9},{11,1... | collective-permute-start | bytes 196616 | tf_op jit(solution)/shard_map/ppermute | solution.py:534
  18.4 6.3 %collective-permute-start.6 = (f32[112,128]{1,0:T(8,128)S(1)}, f32[112,128]{1,0:T(8,128)S(1)}, u32[]{:S(2)}, u32[]{:S(2)}) collective-permute-start(f32[112,128]{1,0:T(8,128)S(1)} %get-tuple-element.63.refs_0_.group_b), channel_id=1, source_target_pairs={{0,192},{16,208},{32,224},{48,240},{64,128},{80,144},{96,160},{112... | collective-permute-start | bytes 172040 | tf_op jit(solution)/shard_map/ppermute | solution.py:494
  20.9 4.5 %collective-permute-start.5 = (f32[112,128]{1,0:T(8,128)S(1)}, f32[112,128]{1,0:T(8,128)S(1)}, u32[]{:S(2)}, u32[]{:S(2)}) collective-permute-start(f32[112,128]{1,0:T(8,128)S(1)} %get-tuple-element.63.refs_0_.group_b), channel_id=1, source_target_pairs={{0,64},{16,80},{32,96},{48,112},{64,0},{80,16},{96,32},{112,48},{1... | collective-permute-start | bytes 172040 | tf_op jit(solution)/shard_map/ppermute | solution.py:494
  21.5 3.9 %collective-permute-start.4 = (f32[112,128]{1,0:T(8,128)S(1)}, f32[112,128]{1,0:T(8,128)S(1)}, u32[]{:S(2)}, u32[]{:S(2)}) collective-permute-start(f32[112,128]{1,0:T(8,128)S(1)} %get-tuple-element.63.refs_0_.group_b), channel_id=1, source_target_pairs={{0,128},{16,144},{32,160},{48,176},{64,192},{80,208},{96,224},{112... | collective-permute-start | bytes 172040 | tf_op jit(solution)/shard_map/ppermute | solution.py:494
  26.2 4.6 %collective-permute-start.10 = (f32[112,128]{1,0:T(8,128)S(1)}, f32[112,128]{1,0:T(8,128)S(1)}, u32[]{:S(2)}, u32[]{:S(2)}) collective-permute-start(f32[112,128]{1,0:T(8,128)S(1)} %get-tuple-element.78.refs_0_.own_near), channel_id=1, source_target_pairs={{0,1},{1,0},{2,3},{3,2},{4,5},{5,4},{6,7},{7,6},{8,9},{9,8},{10,11... | collective-permute-start | bytes 172040 | tf_op jit(solution)/shard_map/ppermute | solution.py:494
  26.6 5.4 %collective-permute-start.9 = (f32[112,128]{1,0:T(8,128)S(1)}, f32[112,128]{1,0:T(8,128)S(1)}, u32[]{:S(2)}, u32[]{:S(2)}) collective-permute-start(f32[112,128]{1,0:T(8,128)S(1)} %get-tuple-element.78.refs_0_.own_near), channel_id=1, source_target_pairs={{0,3},{1,2},{2,1},{3,0},{4,7},{5,6},{6,5},{7,4},{8,11},{9,10},{10,... | collective-permute-start | bytes 172040 | tf_op jit(solution)/shard_map/ppermute | solution.py:494
  27.4 5.5 %collective-permute-start.8 = (f32[112,128]{1,0:T(8,128)S(1)}, f32[112,128]{1,0:T(8,128)S(1)}, u32[]{:S(2)}, u32[]{:S(2)}) collective-permute-start(f32[112,128]{1,0:T(8,128)S(1)} %get-tuple-element.78.refs_0_.own_near), channel_id=1, source_target_pairs={{0,2},{1,3},{2,0},{3,1},{4,6},{5,7},{6,4},{7,5},{8,10},{9,11},{10,... | collective-permute-start | bytes 172040 | tf_op jit(solution)/shard_map/ppermute | solution.py:494
  33.0 7.4 %collective-permute-start.13 = (f32[112,128]{1,0:T(8,128)S(1)}, f32[112,128]{1,0:T(8,128)S(1)}, u32[]{:S(2)}, u32[]{:S(2)}) collective-permute-start(f32[112,128]{1,0:T(8,128)S(1)} %get-tuple-element.80.refs_0_), channel_id=1, source_target_pairs={{0,8},{1,9},{2,10},{3,11},{4,12},{5,13},{6,14},{7,15},{8,0},{9,1},... | collective-permute-start | bytes 172040 | tf_op jit(solution)/shard_map/ppermute | solution.py:494
  38.0 5.4 %collective-permute-start.12 = (f32[112,128]{1,0:T(8,128)S(1)}, f32[112,128]{1,0:T(8,128)S(1)}, u32[]{:S(2)}, u32[]{:S(2)}) collective-permute-start(f32[112,128]{1,0:T(8,128)S(1)} %get-tuple-element.80.refs_0_), channel_id=1, source_target_pairs={{0,12},{1,13},{2,14},{3,15},{4,8},{5,9},{6,10},{7,11},{8,4},{9,5},... | collective-permute-start | bytes 172040 | tf_op jit(solution)/shard_map/ppermute | solution.py:494
  38.0 5.4 %collective-permute-start.11 = (f32[112,128]{1,0:T(8,128)S(1)}, f32[112,128]{1,0:T(8,128)S(1)}, u32[]{:S(2)}, u32[]{:S(2)}) collective-permute-start(f32[112,128]{1,0:T(8,128)S(1)} %get-tuple-element.80.refs_0_), channel_id=1, source_target_pairs={{0,4},{1,5},{2,6},{3,7},{4,0},{5,1},{6,2},{7,3},{8,12},{9,13},{10,... | collective-permute-start | bytes 172040 | tf_op jit(solution)/shard_map/ppermute | solution.py:494
  43.8 7.6 %collective-permute-start.16 = (f32[32,128]{1,0:T(8,128)S(1)}, f32[32,128]{1,0:T(8,128)S(1)}, u32[]{:S(2)}, u32[]{:S(2)}) collective-permute-start(f32[32,128]{1,0:T(8,128)S(1)} %get-tuple-element.84.refs_0_.own_near), channel_id=1, source_target_pairs={{0,48},{16,32},{32,16},{48,0},{64,112},{80,96},{96,80},{112,64},{1... | collective-permute-start | bytes 49160 | tf_op jit(solution)/shard_map/ppermute | solution.py:494
  48.1 3.2 %collective-permute-start.15 = (f32[32,128]{1,0:T(8,128)S(1)}, f32[32,128]{1,0:T(8,128)S(1)}, u32[]{:S(2)}, u32[]{:S(2)}) collective-permute-start(f32[32,128]{1,0:T(8,128)S(1)} %get-tuple-element.84.refs_0_.own_near), channel_id=1, source_target_pairs={{0,32},{16,48},{32,0},{48,16},{64,96},{80,112},{96,64},{112,80},{1... | collective-permute-start | bytes 49160 | tf_op jit(solution)/shard_map/ppermute | solution.py:494
  49.3 2.0 %collective-permute-start.14 = (f32[32,128]{1,0:T(8,128)S(1)}, f32[32,128]{1,0:T(8,128)S(1)}, u32[]{:S(2)}, u32[]{:S(2)}) collective-permute-start(f32[32,128]{1,0:T(8,128)S(1)} %get-tuple-element.84.refs_0_.own_near), channel_id=1, source_target_pairs={{0,16},{16,0},{32,48},{48,32},{64,80},{80,64},{96,112},{112,96},{1... | collective-permute-start | bytes 49160 | tf_op jit(solution)/shard_map/ppermute | solution.py:494
  51.4 6.2 %collective-permute-start.19 = (f32[32,128]{1,0:T(8,128)S(1)}, f32[32,128]{1,0:T(8,128)S(1)}, u32[]{:S(2)}, u32[]{:S(2)}) collective-permute-start(f32[32,128]{1,0:T(8,128)S(1)} %get-tuple-element.93.refs_0_), channel_id=1, source_target_pairs={{0,192},{16,208},{32,224},{48,240},{64,128},{80,144},{96,160},{112... | collective-permute-start | bytes 49160 | tf_op jit(solution)/shard_map/ppermute | solution.py:494
  53.5 4.4 %collective-permute-start.18 = (f32[32,128]{1,0:T(8,128)S(1)}, f32[32,128]{1,0:T(8,128)S(1)}, u32[]{:S(2)}, u32[]{:S(2)}) collective-permute-start(f32[32,128]{1,0:T(8,128)S(1)} %get-tuple-element.93.refs_0_), channel_id=1, source_target_pairs={{0,64},{16,80},{32,96},{48,112},{64,0},{80,16},{96,32},{112,48},{1... | collective-permute-start | bytes 49160 | tf_op jit(solution)/shard_map/ppermute | solution.py:494
  54.4 3.5 %collective-permute-start.17 = (f32[32,128]{1,0:T(8,128)S(1)}, f32[32,128]{1,0:T(8,128)S(1)}, u32[]{:S(2)}, u32[]{:S(2)}) collective-permute-start(f32[32,128]{1,0:T(8,128)S(1)} %get-tuple-element.93.refs_0_), channel_id=1, source_target_pairs={{0,128},{16,144},{32,160},{48,176},{64,192},{80,208},{96,224},{112... | collective-permute-start | bytes 49160 | tf_op jit(solution)/shard_map/ppermute | solution.py:494

commit v8 on v7

--- a/solution.py
+++ b/solution.py
@@ -128,6 +128,33 @@
             e, l = pltpu.roll(g, n - step, 1), pltpu.roll(g, step, 1)
         step *= 2
     return r / s
+
+
+def factors_kernel(w_in, a_out, b_out, scale):
+    w = w_in[...]
+    n = w.shape[1]
+    lane = lanes(w)
+    e = jnp.where(lane == n - 1, 0.0, 1.0)
+    l = jnp.where(lane == 0, 0.0, 1.0)
+    s = w + jnp.where(lane == n - 1, 1.0, 0.0)
+    for k in range(a_out.shape[0]):
+        step = 1 << k
+        inv = 1.0 / (s + (l + e))
+        a, b = e * inv, l * inv
+        a_out[k] = a
+        b_out[k] = b
+        s = s + (pltpu.roll(a * s, step, 1) + pltpu.roll(b * s, n - step, 1))
+        g = a * l
+        e, l = pltpu.roll(g, n - step, 1), pltpu.roll(g, step, 1)
+    scale[...] = 1.0 / s
+
+
+def solve_factored(r, a, b, scale):
+    n = r.shape[1]
+    for k in range(a.shape[0]):
+        step = 1 << k
+        r = r + (pltpu.roll(a[k] * r, step, 1) + pltpu.roll(b[k] * r, n - step, 1))
+    return r * scale[...]
 
 
 def collect(r, order, own, others, got):
@@ -400,7 +427,7 @@
     msg[plane(1)] = last - flux2[plane(B - 1)]
 
 
-def second_y_kernel(ends_c, g_c, u, v, flux_y, part, rise_y, w, elec, magn, full_x, new_y, full_z, new_x, sems):
+def second_y_kernel(ends_c, g_c, u, v, flux_y, elec, magn, full_z, new_x, sems):
     stores = [(full_z, elec.at[2]), (new_x, magn.at[0])]
     stores = [pltpu.make_async_copy(a, b, sems.at[k]) for k, (a, b) in enumerate(stores)]
     before, after = ends_c[plane(0)], ends_c[plane(1)]
@@ -414,30 +441,19 @@
     new_x[strided(B - 1)] = -h * (flux_y[strided(B - 1)] + (after - here))
     for store in stores:
         store.start()
-    rows = pl.ds(0, w.shape[0] // 2)
-    a = rise_y[rows]
-    x = solve_z(part[rows] - behind_z(a), w[rows])
-    full_x[...] = x
-    new_y[...] = h * (a - ahead_z(x))
     for store in stores:
         store.wait()
 
 
-def second_z_kernel(part, rise_y, w, x_half, y_half, _, __, elec, magn, full_x, new_y, sems):
-    size = w.shape[0] // 2
-    rows = [pl.ds(0, size), pl.ds(size, size)]
-    stores = [(x_half, 0, elec, 0), (y_half, 0, magn, 1), (full_x, 1, elec, 0), (new_y, 1, magn, 1)]
-    stores = [
-        pltpu.make_async_copy(a, b.at[k, rows[at]], sems.at[i]) for i, (a, at, b, k) in enumerate(stores)
-    ]
+def second_z_kernel(part, rise_y, z_a, z_b, z_scale, _, __, elec, magn, full_x, new_y, sems):
+    stores = [(full_x, elec.at[0]), (new_y, magn.at[1])]
+    stores = [pltpu.make_async_copy(a, b, sems.at[k]) for k, (a, b) in enumerate(stores)]
+    a = rise_y[...]
+    x = solve_factored(part[...] - behind_z(a), z_a, z_b, z_scale)
+    full_x[...] = x
     stores[0].start()
+    new_y[...] = h * (a - ahead_z(x))
     stores[1].start()
-    a = rise_y[rows[1]]
-    x = solve_z(part[rows[1]] - behind_z(a), w[rows[1]])
-    full_x[...] = x
-    stores[2].start()
-    new_y[...] = h * (a - ahead_z(x))
-    stores[3].start()
     for store in stores:
         store.wait()
 
@@ -490,8 +506,9 @@
     )(*ins)
 
 
-def shared(value, axis, n, step, order):
-    return [value] + [lax.ppermute(value, axis, [(i, i ^ (step * s)) for i in range(n)]) for s in order]
+def shared(value, axis, n, order, near=1, bent=()):
+    masks = [near * s + (near // 2 if s in bent else 0) for s in order]
+    return [value] + [lax.ppermute(value, axis, [(i, i ^ mask) for i in range(n)]) for mask in masks]
 
 
 def split(n):
@@ -530,14 +547,14 @@
         [pos, part_b, hx_prev, flux_b, p_x, u_x, v_x, ef, mf],
         [cells, (7 * B, nz)],
     )
-    ins = shared(own_b, "px", nx, 1, px_near)
+    ins = shared(own_b, "px", nx, px_near)
     ez_next = lax.ppermute(ez_first, "py", [((i + 1) % ny, i) for i in range(ny)])
     near_b, group_b = call(
         functools.partial(merge_kernel, 0, near_x, px_near, 1, True),
         [pos] + ins,
         [(near_x, 7 * B, nz), (7 * B, nz)],
     )
-    ins = shared(group_b, "px", nx, near_x, px_far)
+    ins = shared(group_b, "px", nx, px_far, near_x, (1, 3))
     p_y, u_y, v_y, r_top, src_top, curl, flux_y, flux_a, part_a = call(
         functools.partial(first_z_kernel, ny),
         [pos, ef, mf, ez_next, w, c],
@@ -552,26 +569,29 @@
         [(far_x, 7 * B, nz)] + [cells] * 6 + [(7 * B, nz)],
         scratch=[cells] * 2,
     )
-    ins = shared(own_ac, "py", ny, 1, py_near)
+    ins = shared(own_ac, "py", ny, py_near)
     near_ac, msg = call(
         functools.partial(merge_kernel, 1, near_y, py_near, 2, False), [pos] + ins, [(near_y, 7 * B, nz), (7 * B, nz)]
     )
-    ins = shared(msg, "py", ny, near_y, py_far)
+    msg, w = lax.optimization_barrier((msg, w))
+    ins = shared(msg, "py", ny, py_far, near_y, (2,))
+    steps = (nz - 1).bit_length()
+    z_factors = call(factors_kernel, [w], [(steps, *cells)] * 2 + [cells], flops=8_000_000)
+    ins, z_factors = lax.optimization_barrier((ins, z_factors))
     part_x, flux2, g2, ends_c, own_a = call(
         functools.partial(second_x_kernel, near_y, far_y, py_far),
         [pos, near_ac, own_ac] + ins + [g_a, u_y, v_y, flux_a, c, curl, p_x],
         [cells] * 3 + [(2 * B, nz)] * 2,
         scratch=[(far_y, 7 * B, nz), cells],
     )
-    ins = shared(own_a, "px", nx, 1, px_near)
-    half, whole = (B * B // 2, nz), pltpu.HBM((3, *cells), F32)
-    elec, magn, x_half, y_half = call(
+    ins = shared(own_a, "px", nx, px_near)
+    whole = pltpu.HBM((3, *cells), F32)
+    elec, magn = call(
         second_y_kernel,
-        [ends_c, g_c, u_y, v_y, flux_y, part_x, rise_y, w],
-        [whole, whole, half, half],
-        out_specs=[HBM] * 2 + [VMEM] * 2,
+        [ends_c, g_c, u_y, v_y, flux_y],
+        [whole, whole],
+        out_specs=[HBM] * 2,
         scratch=[cells] * 2 + [dma((2,))],
-        flops=4_000_000,
     )
     near_a, msg = call(
         functools.partial(merge_rows_kernel, 0, near_x, px_near),
@@ -579,14 +599,14 @@
         [(near_x, 2 * B, nz), (2 * B, nz)],
     )
     msg, elec = lax.optimization_barrier((msg, elec))
-    ins = shared(msg, "px", nx, near_x, px_far)
+    ins = shared(msg, "px", nx, px_far, near_x, (1, 3))
     elec, magn = call(
         second_z_kernel,
-        [part_x, rise_y, w, x_half, y_half, elec, magn],
+        [part_x, rise_y, *z_factors, elec, magn],
         [whole] * 2,
         specs=[VMEM] * 5 + [HBM] * 2,
         out_specs=[HBM] * 2,
-        scratch=[half] * 2 + [dma((4,))],
+        scratch=[cells] * 2 + [dma((2,))],
         aliases={5: 0, 6: 1},
         flops=4_000_000,
     )

time: 59.2 us -> 57.7 us (0.975); the launches traced: 58.9 us -> 56.6 us
  waiting for transfers between devices: 12.8 us -> 11.8 us
  starting transfers between devices: 34.2 us -> 33.3 us
    ppermute x18, waiting for transfers between devices: 8.47 us -> 7.42 us  [shared(): lax.ppermute(value, axis, [(i, i ^ mask) for i in range(n)])]
    ppermute x18, starting transfers between devices: 27.2 us -> 26.3 us  [shared(): lax.ppermute(value, axis, [(i, i ^ mask) for i in range(n)])]
    pallas_call x11 -> x12, Pallas kernels: 10 us -> 9.76 us  [call(): pl.pallas_call(kernel, out_shape=shapes, in_specs=specs or [VMEM] * len(i...]
where the time goes in v8:
time: 57.7 us; the launch traced here: 56.6 us
  starting transfers between devices  33.3 us (58%)
  waiting for transfers between devices  11.8 us (20%)
  Pallas kernels  9.76 us (17%)
  between operations  0.9 us (2%)
  local copies, waits for them, and re-layouts  0.85 us (1%)
    ppermute x18, starting transfers between devices, shared(): lax.ppermute(value, axis, [(i, i ^ mask) for i in range(n)])  26.3 us
    pallas_call x12, Pallas kernels, call(): pl.pallas_call(kernel, out_shape=shapes, in_specs=specs or [VMEM] * len(i...  9.76 us
    ppermute x18, waiting for transfers between devices, shared(): lax.ppermute(value, axis, [(i, i ^ mask) for i in range(n)])  7.42 us
    ppermute x1, waiting for transfers between devices, local(): lax.ppermute(magnetic[0, :, B - 1], 'py', [(i, (i + 1) % ny) for i in ran...  4.33 us
    ppermute x1, starting transfers between devices, local(): lax.ppermute(magnetic[0, :, B - 1], 'py', [(i, (i + 1) % ny) for i in ran...  3.74 us
    ppermute x1, starting transfers between devices, local(): lax.ppermute(ez_first, 'py', [((i + 1) % ny, i) for i in range(ny)])  3.25 us
  transfers between devices with their start and end apart: 20, of which 9 were waited for; matrix products, arithmetic and copies ran while one was open for 0% of the time, Pallas kernels for 13%

profile of v8, /device:TPU:1, one launch (start us, length us, event | category | flops | bytes accessed | tf_op | source)
XLA Modules:
  0.0 56.6 jit_solution(4671969831486198946)
XLA Ops:
  0.6 0.9 %slice.3 = f32[1,16,1,128]{3,2,1,0:T(1,128)S(1)} slice(f32[3,16,16,128]{3,2,1,0:T(8,128)} %param.6), slice={[0:1], [0:16], [15:16], [0:128]} | slice | bytes 16384 | tf_op jit(solution)/shard_map/slice | solution.py:537
  1.5 3.7 %collective-permute-start = (f32[16,128]{1,0:T(8,128)S(1)}, f32[16,128]{1,0:T(8,128)S(1)}, u32[]{:S(2)}, u32[]{:S(2)}) collective-permute-start(f32[16,128]{1,0:T(8,128)S(1)} %bitcast.15), channel_id=1, source_target_pairs={{0,1},{1,2},{2,3},{3,4},{4,5},{5,6},{6,7},{7,8},{8,9},{9,10},{10,1... | collective-permute-start | bytes 24584 | tf_op jit(solution)/shard_map/ppermute | solution.py:537
  5.3 1.9 %shard_map.68 = (f32[256,128]{1,0:T(8,128)S(1)}, f32[256,128]{1,0:T(8,128)S(1)}, f32[256,128]{1,0:T(8,128)S(1)}, f32[256,128]{1,0:T(8,128)S(1)}, f32[256,128]{1,...) custom-call(s32[2]{0:T(128)S(1)} %pad_add_fusion.me, ...), custom_call_target="tpu_custom_call" | custom-call | flops 1000000 | bytes 1000000 | tf_op jit(solution)/shard_map/pallas_call | solution.py:497
  7.2 4.3 %collective-permute-done.hx_prev = f32[16,128]{1,0:T(8,128)S(1)} collective-permute-done((f32[16,128]{1,0:T(8,128)S(1)}, f32[16,128]{1,0:T(8,128)S(1)}, u32[]{:S(2)}, u32[]{:S(2)}) %collective-permute-start) | collective-permute-done | bytes 8224 | tf_op jit(solution)/shard_map/ppermute | solution.py:537
  11.6 2.7 %collective-permute-start.3 = (f32[112,128]{1,0:T(8,128)S(1)}, f32[112,128]{1,0:T(8,128)S(1)}, u32[]{:S(2)}, u32[]{:S(2)}) collective-permute-start(f32[112,128]{1,0:T(8,128)S(1)} %get-tuple-element.71.refs_0_.own_near.own_b), channel_id=1, source_target_pairs={{0,48},{16,32},{32,16},{48,0},{64,112},{80,96},{96,80},{112,64},{1... | collective-permute-start | bytes 172040 | tf_op jit(solution)/shard_map/ppermute | solution.py:511
  14.9 3.2 %collective-permute-start.7 = (f32[128,128]{1,0:T(8,128)S(1)}, f32[128,128]{1,0:T(8,128)S(1)}, u32[]{:S(2)}, u32[]{:S(2)}) collective-permute-start(f32[128,128]{1,0:T(8,128)S(1)} %get-tuple-element.77), channel_id=1, source_target_pairs={{1,0},{2,1},{3,2},{4,3},{5,4},{6,5},{7,6},{8,7},{9,8},{10,9},{11,1... | collective-permute-start | bytes 196616 | tf_op jit(solution)/shard_map/ppermute | solution.py:551
  18.4 2.2 %collective-permute-start.6 = (f32[112,128]{1,0:T(8,128)S(1)}, f32[112,128]{1,0:T(8,128)S(1)}, u32[]{:S(2)}, u32[]{:S(2)}) collective-permute-start(f32[112,128]{1,0:T(8,128)S(1)} %get-tuple-element.73.refs_0_.group_b), channel_id=1, source_target_pairs={{0,224},{16,240},{32,192},{48,208},{64,160},{80,176},{96,128},{112... | collective-permute-start | bytes 172040 | tf_op jit(solution)/shard_map/ppermute | solution.py:511
  21.2 1.1 %collective-permute-start.4 = (f32[112,128]{1,0:T(8,128)S(1)}, f32[112,128]{1,0:T(8,128)S(1)}, u32[]{:S(2)}, u32[]{:S(2)}) collective-permute-start(f32[112,128]{1,0:T(8,128)S(1)} %get-tuple-element.73.refs_0_.group_b), channel_id=1, source_target_pairs={{0,128},{16,144},{32,160},{48,176},{64,192},{80,208},{96,224},{112... | collective-permute-start | bytes 172040 | tf_op jit(solution)/shard_map/ppermute | solution.py:511
  22.3 2.0 %shard_map.71 = (f32[256,128]{1,0:T(8,128)S(1)}, f32[256,128]{1,0:T(8,128)S(1)}, f32[256,128]{1,0:T(8,128)S(1)}, f32[16,128]{1,0:T(8,128)S(1)}, f32[16,128]{1,0:...) custom-call(s32[32,128]{1,0:T(8,128)S(1)} %get-tuple-element.63.pos,, ...), custom_call_target="tpu_custom_call" | custom-call | flops 8000000 | bytes 1000000 | tf_op jit(solution)/shard_map/pallas_call | solution.py:497
  24.9 0.8 %shard_map.72 = (f32[4,112,128]{2,1,0:T(8,128)S(1)}, f32[256,128]{1,0:T(8,128)S(1)}, f32[256,128]{1,0:T(8,128)S(1)}, f32[256,128]{1,0:T(8,128)S(1)}, f32[256,128...) custom-call(s32[32,128]{1,0:T(8,128)S(1)} %get-tuple-element.63.pos, ...), custom_call_target="tpu_custom_call" | custom-call | flops 1000000 | bytes 1000000 | tf_op jit(solution)/shard_map/pallas_call | solution.py:497
  26.7 3.2 %collective-permute-start.8 = (f32[112,128]{1,0:T(8,128)S(1)}, f32[112,128]{1,0:T(8,128)S(1)}, u32[]{:S(2)}, u32[]{:S(2)}) collective-permute-start(f32[112,128]{1,0:T(8,128)S(1)} %get-tuple-element.88.refs_0_.own_near), channel_id=1, source_target_pairs={{0,2},{1,3},{2,0},{3,1},{4,6},{5,7},{6,4},{7,5},{8,10},{9,11},{10,... | collective-permute-start | bytes 172040 | tf_op jit(solution)/shard_map/ppermute | solution.py:511
  30.3 1.2 %collective-permute-done.9.refs_2_ = f32[112,128]{1,0:T(8,128)S(1)} collective-permute-done((f32[112,128]{1,0:T(8,128)S(1)}, f32[112,128]{1,0:T(8,128)S(1)}, u32[]{:S(2)}, u32[]{:S(2)}) %collective-permute-start.9) | collective-permute-done | bytes 57376 | tf_op jit(solution)/shard_map/ppermute | solution.py:511
  31.5 0.9 %collective-permute-done.8.refs_1_ = f32[112,128]{1,0:T(8,128)S(1)} collective-permute-done((f32[112,128]{1,0:T(8,128)S(1)}, f32[112,128]{1,0:T(8,128)S(1)}, u32[]{:S(2)}, u32[]{:S(2)}) %collective-permute-start.8) | collective-permute-done | bytes 57376 | tf_op jit(solution)/shard_map/ppermute | solution.py:511
  32.4 4.3 %collective-permute-start.13 = (f32[112,128]{1,0:T(8,128)S(1)}, f32[112,128]{1,0:T(8,128)S(1)}, u32[]{:S(2)}, u32[]{:S(2)}) collective-permute-start(f32[112,128]{1,0:T(8,128)S(1)} %get-tuple-element.96.refs_0_), channel_id=1, source_target_pairs={{0,10},{1,11},{2,8},{3,9},{4,14},{5,15},{6,12},{7,13},{8,2},{9,3},... | collective-permute-start | bytes 172040 | tf_op jit(solution)/shard_map/ppermute | solution.py:511
  37.9 1.3 %shard_map.74 = (f32[7,256,128]{2,1,0:T(8,128)S(1)}, f32[7,256,128]{2,1,0:T(8,128)S(1)}, f32[256,128]{1,0:T(8,128)S(1)}) custom-call(f32[256,128]{1,0:T(8,128)S(1)} %get-tuple-element.92.w.refs_8_.w_in), custom_call_target="tpu_custom_call" | custom-call | flops 8000000 | bytes 1000000 | tf_op jit(solution)/shard_map/pallas_call | solution.py:497
  39.1 3.5 %collective-permute-done.12.refs_2_ = f32[112,128]{1,0:T(8,128)S(1)} collective-permute-done((f32[112,128]{1,0:T(8,128)S(1)}, f32[112,128]{1,0:T(8,128)S(1)}, u32[]{:S(2)}, u32[]{:S(2)}) %collective-permute-start.12) | collective-permute-done | bytes 57376 | tf_op jit(solution)/shard_map/ppermute | solution.py:511
  43.0 3.4 %collective-permute-start.16 = (f32[32,128]{1,0:T(8,128)S(1)}, f32[32,128]{1,0:T(8,128)S(1)}, u32[]{:S(2)}, u32[]{:S(2)}) collective-permute-start(f32[32,128]{1,0:T(8,128)S(1)} %get-tuple-element.103.refs_0_.own_near), channel_id=1, source_target_pairs={{0,48},{16,32},{32,16},{48,0},{64,112},{80,96},{96,80},{112,64},{1... | collective-permute-start | bytes 49160 | tf_op jit(solution)/shard_map/ppermute | solution.py:511
  46.4 2.2 %collective-permute-start.15 = (f32[32,128]{1,0:T(8,128)S(1)}, f32[32,128]{1,0:T(8,128)S(1)}, u32[]{:S(2)}, u32[]{:S(2)}) collective-permute-start(f32[32,128]{1,0:T(8,128)S(1)} %get-tuple-element.103.refs_0_.own_near), channel_id=1, source_target_pairs={{0,32},{16,48},{32,0},{48,16},{64,96},{80,112},{96,64},{112,80},{1... | collective-permute-start | bytes 49160 | tf_op jit(solution)/shard_map/ppermute | solution.py:511
  48.6 0.8 %shard_map.77 = (f32[3,256,128]{2,1,0:T(8,128)}, f32[3,256,128]{2,1,0:T(8,128)}) custom-call(f32[32,128]{1,0:T(8,128)S(1)} %get-tuple-element.106.ends_c, f32[256,128]{1,0:T(8,128)S(1)} %get-tuple-element.107.g_c, f32[256,128]{1,0:T(8,128)S(1)} %get-tuple-element.85.refs_17_.refs_5_.u, f32[256,128]{1,0:T(8,128)S(1)} %get-tuple-element.86.refs_18_.refs_6_.v, ...), custom_call_target="tpu_custom_call" | custom-call | flops 1000000 | bytes 1000000 | tf_op jit(solution)/shard_map/pallas_call | solution.py:497
  50.0 1.8 %collective-permute-start.19 = (f32[32,128]{1,0:T(8,128)S(1)}, f32[32,128]{1,0:T(8,128)S(1)}, u32[]{:S(2)}, u32[]{:S(2)}) collective-permute-start(f32[32,128]{1,0:T(8,128)S(1)} %get-tuple-element.110.refs_0_), channel_id=1, source_target_pairs={{0,224},{16,240},{32,192},{48,208},{64,160},{80,176},{96,128},{112... | collective-permute-start | bytes 49160 | tf_op jit(solution)/shard_map/ppermute | solution.py:511
  51.8 0.8 %collective-permute-start.18 = (f32[32,128]{1,0:T(8,128)S(1)}, f32[32,128]{1,0:T(8,128)S(1)}, u32[]{:S(2)}, u32[]{:S(2)}) collective-permute-start(f32[32,128]{1,0:T(8,128)S(1)} %get-tuple-element.110.refs_0_), channel_id=1, source_target_pairs={{0,96},{16,112},{32,64},{48,80},{64,32},{80,48},{96,0},{112,16},{1... | collective-permute-start | bytes 49160 | tf_op jit(solution)/shard_map/ppermute | solution.py:511
  52.7 1.3 %collective-permute-start.17 = (f32[32,128]{1,0:T(8,128)S(1)}, f32[32,128]{1,0:T(8,128)S(1)}, u32[]{:S(2)}, u32[]{:S(2)}) collective-permute-start(f32[32,128]{1,0:T(8,128)S(1)} %get-tuple-element.110.refs_0_), channel_id=1, source_target_pairs={{0,128},{16,144},{32,160},{48,176},{64,192},{80,208},{96,224},{112... | collective-permute-start | bytes 49160 | tf_op jit(solution)/shard_map/ppermute | solution.py:511
  54.0 1.6 %shard_map.78 = (f32[3,256,128]{2,1,0:T(8,128)}, f32[3,256,128]{2,1,0:T(8,128)}) custom-call(f32[256,128]{1,0:T(8,128)S(1)} %get-tuple-element.113.part, f32[256,128]{1,0:T(8,128)S(1)} %get-tuple-element.114.rise_y, f32[7,256,128]{2,1,0:T(8,128)S(1)} %get-tuple-element.115.z_a, ...), custom_call_target="tpu_custom_call", output_to_operand_aliasing={{0}: (5, {}), {1}: (6, {})} | custom-call | flops 4000000 | bytes 1000000 | tf_op jit(solution)/shard_map/pallas_call | solution.py:497
  55.7 0.8 %shard_map.79 = (f32[3,256,128]{2,1,0:T(8,128)}, f32[3,256,128]{2,1,0:T(8,128)}) custom-call(s32[32,128]{1,0:T(8,128)S(1)} %get-tuple-element.63.pos, f32[4,112,128]{2,1,0:T(8,128)S(1)} %get-tuple-element.72.got_near.coefs.coefs_near, f32[4,112,128]{2,1,0:T(8,128)S(1)} %get-tuple-element.87.coefs_far, ...), custom_call_target="tpu_custom_call", output_to_operand_aliasing={{0}: (15, {}), {1}: (16, {})} | custom-call | flops 1000000 | bytes 1000000 | tf_op jit(solution)/shard_map/pallas_call | solution.py:497
  (30 shorter events, 5.8 us)
Async XLA Ops:
  1.5 10.1 %collective-permute-start = (f32[16,128]{1,0:T(8,128)S(1)}, f32[16,128]{1,0:T(8,128)S(1)}, u32[]{:S(2)}, u32[]{:S(2)}) collective-permute-start(f32[16,128]{1,0:T(8,128)S(1)} %bitcast.15), channel_id=1, source_target_pairs={{0,1},{1,2},{2,3},{3,4},{4,5},{5,6},{6,7},{7,8},{8,9},{9,10},{10,1... | collective-permute-start | bytes 24584 | tf_op jit(solution)/shard_map/ppermute | solution.py:537
  11.6 6.5 %collective-permute-start.3 = (f32[112,128]{1,0:T(8,128)S(1)}, f32[112,128]{1,0:T(8,128)S(1)}, u32[]{:S(2)}, u32[]{:S(2)}) collective-permute-start(f32[112,128]{1,0:T(8,128)S(1)} %get-tuple-element.71.refs_0_.own_near.own_b), channel_id=1, source_target_pairs={{0,48},{16,32},{32,16},{48,0},{64,112},{80,96},{96,80},{112,64},{1... | collective-permute-start | bytes 172040 | tf_op jit(solution)/shard_map/ppermute | solution.py:511
  14.4 3.9 %collective-permute-start.2 = (f32[112,128]{1,0:T(8,128)S(1)}, f32[112,128]{1,0:T(8,128)S(1)}, u32[]{:S(2)}, u32[]{:S(2)}) collective-permute-start(f32[112,128]{1,0:T(8,128)S(1)} %get-tuple-element.71.refs_0_.own_near.own_b), channel_id=1, source_target_pairs={{0,32},{16,48},{32,0},{48,16},{64,96},{80,112},{96,64},{112,80},{1... | collective-permute-start | bytes 172040 | tf_op jit(solution)/shard_map/ppermute | solution.py:511
  14.6 3.7 %collective-permute-start.1 = (f32[112,128]{1,0:T(8,128)S(1)}, f32[112,128]{1,0:T(8,128)S(1)}, u32[]{:S(2)}, u32[]{:S(2)}) collective-permute-start(f32[112,128]{1,0:T(8,128)S(1)} %get-tuple-element.71.refs_0_.own_near.own_b), channel_id=1, source_target_pairs={{0,16},{16,0},{32,48},{48,32},{64,80},{80,64},{96,112},{112,96},{1... | collective-permute-start | bytes 172040 | tf_op jit(solution)/shard_map/ppermute | solution.py:511
  14.9 7.5 %collective-permute-start.7 = (f32[128,128]{1,0:T(8,128)S(1)}, f32[128,128]{1,0:T(8,128)S(1)}, u32[]{:S(2)}, u32[]{:S(2)}) collective-permute-start(f32[128,128]{1,0:T(8,128)S(1)} %get-tuple-element.77), channel_id=1, source_target_pairs={{1,0},{2,1},{3,2},{4,3},{5,4},{6,5},{7,6},{8,7},{9,8},{10,9},{11,1... | collective-permute-start | bytes 196616 | tf_op jit(solution)/shard_map/ppermute | solution.py:551
  18.4 6.0 %collective-permute-start.6 = (f32[112,128]{1,0:T(8,128)S(1)}, f32[112,128]{1,0:T(8,128)S(1)}, u32[]{:S(2)}, u32[]{:S(2)}) collective-permute-start(f32[112,128]{1,0:T(8,128)S(1)} %get-tuple-element.73.refs_0_.group_b), channel_id=1, source_target_pairs={{0,224},{16,240},{32,192},{48,208},{64,160},{80,176},{96,128},{112... | collective-permute-start | bytes 172040 | tf_op jit(solution)/shard_map/ppermute | solution.py:511
  20.6 4.2 %collective-permute-start.5 = (f32[112,128]{1,0:T(8,128)S(1)}, f32[112,128]{1,0:T(8,128)S(1)}, u32[]{:S(2)}, u32[]{:S(2)}) collective-permute-start(f32[112,128]{1,0:T(8,128)S(1)} %get-tuple-element.73.refs_0_.group_b), channel_id=1, source_target_pairs={{0,96},{16,112},{32,64},{48,80},{64,32},{80,48},{96,0},{112,16},{1... | collective-permute-start | bytes 172040 | tf_op jit(solution)/shard_map/ppermute | solution.py:511
  21.2 3.6 %collective-permute-start.4 = (f32[112,128]{1,0:T(8,128)S(1)}, f32[112,128]{1,0:T(8,128)S(1)}, u32[]{:S(2)}, u32[]{:S(2)}) collective-permute-start(f32[112,128]{1,0:T(8,128)S(1)} %get-tuple-element.73.refs_0_.group_b), channel_id=1, source_target_pairs={{0,128},{16,144},{32,160},{48,176},{64,192},{80,208},{96,224},{112... | collective-permute-start | bytes 172040 | tf_op jit(solution)/shard_map/ppermute | solution.py:511
  25.7 4.6 %collective-permute-start.10 = (f32[112,128]{1,0:T(8,128)S(1)}, f32[112,128]{1,0:T(8,128)S(1)}, u32[]{:S(2)}, u32[]{:S(2)}) collective-permute-start(f32[112,128]{1,0:T(8,128)S(1)} %get-tuple-element.88.refs_0_.own_near), channel_id=1, source_target_pairs={{0,1},{1,0},{2,3},{3,2},{4,5},{5,4},{6,7},{7,6},{8,9},{9,8},{10,11... | collective-permute-start | bytes 172040 | tf_op jit(solution)/shard_map/ppermute | solution.py:511
  26.1 5.4 %collective-permute-start.9 = (f32[112,128]{1,0:T(8,128)S(1)}, f32[112,128]{1,0:T(8,128)S(1)}, u32[]{:S(2)}, u32[]{:S(2)}) collective-permute-start(f32[112,128]{1,0:T(8,128)S(1)} %get-tuple-element.88.refs_0_.own_near), channel_id=1, source_target_pairs={{0,3},{1,2},{2,1},{3,0},{4,7},{5,6},{6,5},{7,4},{8,11},{9,10},{10,... | collective-permute-start | bytes 172040 | tf_op jit(solution)/shard_map/ppermute | solution.py:511
  26.7 5.7 %collective-permute-start.8 = (f32[112,128]{1,0:T(8,128)S(1)}, f32[112,128]{1,0:T(8,128)S(1)}, u32[]{:S(2)}, u32[]{:S(2)}) collective-permute-start(f32[112,128]{1,0:T(8,128)S(1)} %get-tuple-element.88.refs_0_.own_near), channel_id=1, source_target_pairs={{0,2},{1,3},{2,0},{3,1},{4,6},{5,7},{6,4},{7,5},{8,10},{9,11},{10,... | collective-permute-start | bytes 172040 | tf_op jit(solution)/shard_map/ppermute | solution.py:511
  32.4 6.7 %collective-permute-start.13 = (f32[112,128]{1,0:T(8,128)S(1)}, f32[112,128]{1,0:T(8,128)S(1)}, u32[]{:S(2)}, u32[]{:S(2)}) collective-permute-start(f32[112,128]{1,0:T(8,128)S(1)} %get-tuple-element.96.refs_0_), channel_id=1, source_target_pairs={{0,10},{1,11},{2,8},{3,9},{4,14},{5,15},{6,12},{7,13},{8,2},{9,3},... | collective-permute-start | bytes 172040 | tf_op jit(solution)/shard_map/ppermute | solution.py:511
  36.7 5.9 %collective-permute-start.12 = (f32[112,128]{1,0:T(8,128)S(1)}, f32[112,128]{1,0:T(8,128)S(1)}, u32[]{:S(2)}, u32[]{:S(2)}) collective-permute-start(f32[112,128]{1,0:T(8,128)S(1)} %get-tuple-element.96.refs_0_), channel_id=1, source_target_pairs={{0,12},{1,13},{2,14},{3,15},{4,8},{5,9},{6,10},{7,11},{8,4},{9,5},... | collective-permute-start | bytes 172040 | tf_op jit(solution)/shard_map/ppermute | solution.py:511
  37.2 5.5 %collective-permute-start.11 = (f32[112,128]{1,0:T(8,128)S(1)}, f32[112,128]{1,0:T(8,128)S(1)}, u32[]{:S(2)}, u32[]{:S(2)}) collective-permute-start(f32[112,128]{1,0:T(8,128)S(1)} %get-tuple-element.96.refs_0_), channel_id=1, source_target_pairs={{0,4},{1,5},{2,6},{3,7},{4,0},{5,1},{6,2},{7,3},{8,12},{9,13},{10,... | collective-permute-start | bytes 172040 | tf_op jit(solution)/shard_map/ppermute | solution.py:511
  43.0 6.4 %collective-permute-start.16 = (f32[32,128]{1,0:T(8,128)S(1)}, f32[32,128]{1,0:T(8,128)S(1)}, u32[]{:S(2)}, u32[]{:S(2)}) collective-permute-start(f32[32,128]{1,0:T(8,128)S(1)} %get-tuple-element.103.refs_0_.own_near), channel_id=1, source_target_pairs={{0,48},{16,32},{32,16},{48,0},{64,112},{80,96},{96,80},{112,64},{1... | collective-permute-start | bytes 49160 | tf_op jit(solution)/shard_map/ppermute | solution.py:511
  46.4 3.6 %collective-permute-start.15 = (f32[32,128]{1,0:T(8,128)S(1)}, f32[32,128]{1,0:T(8,128)S(1)}, u32[]{:S(2)}, u32[]{:S(2)}) collective-permute-start(f32[32,128]{1,0:T(8,128)S(1)} %get-tuple-element.103.refs_0_.own_near), channel_id=1, source_target_pairs={{0,32},{16,48},{32,0},{48,16},{64,96},{80,112},{96,64},{112,80},{1... | collective-permute-start | bytes 49160 | tf_op jit(solution)/shard_map/ppermute | solution.py:511
  48.6 1.4 %collective-permute-start.14 = (f32[32,128]{1,0:T(8,128)S(1)}, f32[32,128]{1,0:T(8,128)S(1)}, u32[]{:S(2)}, u32[]{:S(2)}) collective-permute-start(f32[32,128]{1,0:T(8,128)S(1)} %get-tuple-element.103.refs_0_.own_near), channel_id=1, source_target_pairs={{0,16},{16,0},{32,48},{48,32},{64,80},{80,64},{96,112},{112,96},{1... | collective-permute-start | bytes 49160 | tf_op jit(solution)/shard_map/ppermute | solution.py:511
  50.0 5.5 %collective-permute-start.19 = (f32[32,128]{1,0:T(8,128)S(1)}, f32[32,128]{1,0:T(8,128)S(1)}, u32[]{:S(2)}, u32[]{:S(2)}) collective-permute-start(f32[32,128]{1,0:T(8,128)S(1)} %get-tuple-element.110.refs_0_), channel_id=1, source_target_pairs={{0,224},{16,240},{32,192},{48,208},{64,160},{80,176},{96,128},{112... | collective-permute-start | bytes 49160 | tf_op jit(solution)/shard_map/ppermute | solution.py:511
  51.8 3.8 %collective-permute-start.18 = (f32[32,128]{1,0:T(8,128)S(1)}, f32[32,128]{1,0:T(8,128)S(1)}, u32[]{:S(2)}, u32[]{:S(2)}) collective-permute-start(f32[32,128]{1,0:T(8,128)S(1)} %get-tuple-element.110.refs_0_), channel_id=1, source_target_pairs={{0,96},{16,112},{32,64},{48,80},{64,32},{80,48},{96,0},{112,16},{1... | collective-permute-start | bytes 49160 | tf_op jit(solution)/shard_map/ppermute | solution.py:511
  52.7 3.0 %collective-permute-start.17 = (f32[32,128]{1,0:T(8,128)S(1)}, f32[32,128]{1,0:T(8,128)S(1)}, u32[]{:S(2)}, u32[]{:S(2)}) collective-permute-start(f32[32,128]{1,0:T(8,128)S(1)} %get-tuple-element.110.refs_0_), channel_id=1, source_target_pairs={{0,128},{16,144},{32,160},{48,176},{64,192},{80,208},{96,224},{112... | collective-permute-start | bytes 49160 | tf_op jit(solution)/shard_map/ppermute | solution.py:511

commit v9 on v7

--- a/solution.py
+++ b/solution.py
@@ -169,6 +169,12 @@
 def place(pos, axis, near):
     here = pos[plane(axis)]
     return lax.shift_right_logical(here, near.bit_length() - 1), lax.bitwise_and(here, near - 1)
+
+
+def cut_kernel(magn, hx_last, sem):
+    load = pltpu.make_async_copy(magn.at[0, :, B - 1], hx_last, sem)
+    load.start()
+    load.wait()
 
 
 def tables_kernel(
@@ -249,13 +255,6 @@
         msg[plane(6)] = blocks[-1][6]
 
 
-def merge_rows_kernel(axis, near, order, pos, coefs, *refs):
-    got, msg = refs[-2:]
-    blocks = collect(place(pos, axis, near)[1], order, refs[0], refs[1:near], got)
-    _, rows = merged([(stored(coefs, m, (2, 3, 4)), rows_of(b, 1)) for m, b in enumerate(blocks)])
-    msg[plane(0)], msg[plane(1)] = rows[0]
-
-
 def solved_ends(q, r, sources, near_rows, near_coefs, far_rows, far_coefs, own_near, own_far):
     zero = jnp.zeros_like(far_coefs[0][0])
     outer = boundary(q, far_rows, far_coefs, *own_far, [(zero, zero)] * sources)
@@ -358,9 +357,9 @@
         msg[plane(k)] = value
 
 
-def second_x_kernel(near, far, order, pos, got_near, own_near, *refs):
+def second_x_kernel(near, far, near_x, far_x, order, pos, got_near, own_near, *refs):
     others, refs = refs[:far], refs[far:]
-    g_a, u, v, flux_a, c, curl, p_x, part, flux2, g2, ends_c, msg, got_far, fx = refs
+    g_a, u, v, flux_a, c, curl, p_x, near_b, part, flux2, g2, ends_c, own_a, msg, got_far, fx = refs
     q, r = place(pos, 1, near)
     far_blocks = collect(q, order, others[0], others[1:], got_far)
     near_blocks = [stored(got_near, m, range(7)) for m in range(near)]
@@ -396,12 +395,25 @@
         return curl[plane(i)] + f
 
     first, last = eliminate(source, p_x, g2)
-    msg[plane(0)] = first
-    msg[plane(1)] = last - flux2[plane(B - 1)]
-
-
-def second_y_kernel(ends_c, g_c, u, v, flux_y, part, rise_y, w, elec, magn, full_x, new_y, full_z, new_x, sems):
-    stores = [(full_z, elec.at[2]), (new_x, magn.at[0])]
+    own = [first, last - flux2[plane(B - 1)]]
+    own_a[plane(0)], own_a[plane(1)] = own
+    q, r = place(pos, 0, near_x)
+    alone = [
+        (stored(near_b, m, (2, 3, 4)), [[jnp.where(r == m, value, 0.0) for value in own]])
+        for m in range(near_x)
+    ]
+    share = merged(alone)[1][0]
+    for group in range(far_x):
+        for k in range(2):
+            value = jnp.where(q == group, own[k], share[k])
+            for m in range(near_x):
+                msg[group * near_x + m, plane(k)] = value
+
+
+def second_yz_kernel(
+    ends_c, g_c, u, v, flux_y, part, rise_y, w, elec, magn, full_z, new_x, full_x, new_y, sems
+):
+    stores = [(full_z, elec.at[2]), (new_x, magn.at[0]), (full_x, elec.at[0]), (new_y, magn.at[1])]
     stores = [pltpu.make_async_copy(a, b, sems.at[k]) for k, (a, b) in enumerate(stores)]
     before, after = ends_c[plane(0)], ends_c[plane(1)]
     here = None
@@ -412,28 +424,10 @@
             new_x[strided(j - 1)] = -h * (flux_y[strided(j - 1)] + (ahead - here))
         here = ahead
     new_x[strided(B - 1)] = -h * (flux_y[strided(B - 1)] + (after - here))
-    for store in stores:
-        store.start()
-    rows = pl.ds(0, w.shape[0] // 2)
-    a = rise_y[rows]
-    x = solve_z(part[rows] - behind_z(a), w[rows])
-    full_x[...] = x
-    new_y[...] = h * (a - ahead_z(x))
-    for store in stores:
-        store.wait()
-
-
-def second_z_kernel(part, rise_y, w, x_half, y_half, _, __, elec, magn, full_x, new_y, sems):
-    size = w.shape[0] // 2
-    rows = [pl.ds(0, size), pl.ds(size, size)]
-    stores = [(x_half, 0, elec, 0), (y_half, 0, magn, 1), (full_x, 1, elec, 0), (new_y, 1, magn, 1)]
-    stores = [
-        pltpu.make_async_copy(a, b.at[k, rows[at]], sems.at[i]) for i, (a, at, b, k) in enumerate(stores)
-    ]
     stores[0].start()
     stores[1].start()
-    a = rise_y[rows[1]]
-    x = solve_z(part[rows[1]] - behind_z(a), w[rows[1]])
+    a = rise_y[...]
+    x = solve_z(part[...] - behind_z(a), w[...])
     full_x[...] = x
     stores[2].start()
     new_y[...] = h * (a - ahead_z(x))
@@ -442,21 +436,27 @@
         store.wait()
 
 
-def last_kernel(near, far, order, pos, coefs_near, coefs_far, own_b, group_b, got_near, own_near, *refs):
-    others, refs = refs[:far], refs[far:]
-    g, u, v, flux2, _, _, elec, magn, got_far, full_y, new_z, sems = refs
+def last_kernel(near, far, pos, near_b, far_b, own_b, group_b, got, own_a, *refs):
+    g, u, v, flux2, _, _, elec, magn, full_y, new_z, sems = refs
     q, r = place(pos, 0, near)
-    far_blocks = collect(q, order, others[0], others[1:], got_far)
+    blocks = [[stored(got, group * near + m, range(2)) for m in range(near)] for group in range(far)]
+    near_rows = [
+        rows_of([pick([blocks[group][m][k] for group in range(far)], q) for k in range(2)], 1)
+        for m in range(near)
+    ]
+    near_coefs = [stored(near_b, m, (2, 3, 4)) for m in range(near)]
+    own_rows = merged(list(zip(near_coefs, near_rows)))[1]
+    far_rows = [rows_of([sum(block[k] for block in group) for k in range(2)], 1) for group in blocks]
     ((before, after),) = solved_ends(
         q,
         r,
         1,
-        [rows_of(stored(got_near, m, range(2)), 1) for m in range(near)],
-        [stored(coefs_near, m, (2, 3, 4)) for m in range(near)],
-        [rows_of(b, 1) for b in far_blocks],
-        [stored(coefs_far, m, (2, 3, 4)) for m in range(far)],
-        (rows_of(loaded(own_near, range(2)), 1), loaded(own_b, (2, 3, 4))),
-        (rows_of(loaded(others[0], range(2)), 1), loaded(group_b, (2, 3, 4))),
+        near_rows,
+        near_coefs,
+        far_rows,
+        [stored(far_b, m, (2, 3, 4)) for m in range(far)],
+        (rows_of(loaded(own_a, range(2)), 1), loaded(own_b, (2, 3, 4))),
+        (own_rows, loaded(group_b, (2, 3, 4))),
     )
     stores = [(full_y, elec.at[1]), (new_z, magn.at[2])]
     stores = [pltpu.make_async_copy(a, b, sems.at[k]) for k, (a, b) in enumerate(stores)]
@@ -490,8 +490,9 @@
     )(*ins)
 
 
-def shared(value, axis, n, step, order):
-    return [value] + [lax.ppermute(value, axis, [(i, i ^ (step * s)) for i in range(n)]) for s in order]
+def shared(value, axis, n, order, near=1, bent=()):
+    masks = [near * s + (near // 2 if s in bent else 0) for s in order]
+    return [value] + [lax.ppermute(value, axis, [(i, i ^ mask) for i in range(n)]) for mask in masks]
 
 
 def split(n):
@@ -511,13 +512,16 @@
     magn = in_hbm(magnetic.reshape(3, *cells))
     ids = in_hbm(material.reshape(cells))
     dma = pltpu.SemaphoreType.DMA
-    orders = [(1, 2, 3), (2, 1, 3), (2, 3, 1), (1, 3, 2)]
+    orders = [(1, 2, 3), (2, 1, 3), (2, 1, 3), (1, 3, 2)]
     counts = (near_x, far_x, near_y, far_y)
     px_near, px_far, py_near, py_far = [
         tuple(s for s in order if s < count) for order, count in zip(orders, counts)
     ]
 
-    hx_prev = lax.ppermute(magnetic[0, :, B - 1], "py", [(i, (i + 1) % ny) for i in range(ny)])
+    (hx_last,) = call(
+        cut_kernel, [in_hbm(magnetic)], [(B, nz)], specs=[HBM], scratch=[dma(())], flops=1000
+    )
+    hx_prev = lax.ppermute(hx_last, "py", [(i, (i + 1) % ny) for i in range(ny)])
     w, c, p_x, u_x, v_x, flux_b, part_b, ef, mf, ez_first, pos = call(
         tables_kernel,
         [me, in_hbm(permittivity), in_hbm(conductivity), ids, elec, magn],
@@ -530,14 +534,14 @@
         [pos, part_b, hx_prev, flux_b, p_x, u_x, v_x, ef, mf],
         [cells, (7 * B, nz)],
     )
-    ins = shared(own_b, "px", nx, 1, px_near)
+    ins = shared(own_b, "px", nx, px_near)
     ez_next = lax.ppermute(ez_first, "py", [((i + 1) % ny, i) for i in range(ny)])
     near_b, group_b = call(
         functools.partial(merge_kernel, 0, near_x, px_near, 1, True),
         [pos] + ins,
         [(near_x, 7 * B, nz), (7 * B, nz)],
     )
-    ins = shared(group_b, "px", nx, near_x, px_far)
+    ins = shared(group_b, "px", nx, px_far, near_x, (1, 3))
     p_y, u_y, v_y, r_top, src_top, curl, flux_y, flux_a, part_a = call(
         functools.partial(first_z_kernel, ny),
         [pos, ef, mf, ez_next, w, c],
@@ -552,53 +556,36 @@
         [(far_x, 7 * B, nz)] + [cells] * 6 + [(7 * B, nz)],
         scratch=[cells] * 2,
     )
-    ins = shared(own_ac, "py", ny, 1, py_near)
+    ins = shared(own_ac, "py", ny, py_near)
     near_ac, msg = call(
         functools.partial(merge_kernel, 1, near_y, py_near, 2, False), [pos] + ins, [(near_y, 7 * B, nz), (7 * B, nz)]
     )
-    ins = shared(msg, "py", ny, near_y, py_far)
-    part_x, flux2, g2, ends_c, own_a = call(
-        functools.partial(second_x_kernel, near_y, far_y, py_far),
-        [pos, near_ac, own_ac] + ins + [g_a, u_y, v_y, flux_a, c, curl, p_x],
-        [cells] * 3 + [(2 * B, nz)] * 2,
+    ins = shared(msg, "py", ny, py_far, near_y, (2,))
+    part_x, flux2, g2, ends_c, own_a, msg = call(
+        functools.partial(second_x_kernel, near_y, far_y, near_x, far_x, py_far),
+        [pos, near_ac, own_ac] + ins + [g_a, u_y, v_y, flux_a, c, curl, p_x, near_b],
+        [cells] * 3 + [(2 * B, nz)] * 2 + [(nx, 2 * B, nz)],
         scratch=[(far_y, 7 * B, nz), cells],
     )
-    ins = shared(own_a, "px", nx, 1, px_near)
-    half, whole = (B * B // 2, nz), pltpu.HBM((3, *cells), F32)
-    elec, magn, x_half, y_half = call(
-        second_y_kernel,
+    got = lax.all_to_all(msg, "px", 0, 0, tiled=True)
+    whole = pltpu.HBM((3, *cells), F32)
+    elec, magn = call(
+        second_yz_kernel,
         [ends_c, g_c, u_y, v_y, flux_y, part_x, rise_y, w],
-        [whole, whole, half, half],
-        out_specs=[HBM] * 2 + [VMEM] * 2,
-        scratch=[cells] * 2 + [dma((2,))],
-        flops=4_000_000,
-    )
-    near_a, msg = call(
-        functools.partial(merge_rows_kernel, 0, near_x, px_near),
-        [pos, near_b] + ins,
-        [(near_x, 2 * B, nz), (2 * B, nz)],
-    )
-    msg, elec = lax.optimization_barrier((msg, elec))
-    ins = shared(msg, "px", nx, near_x, px_far)
-    elec, magn = call(
-        second_z_kernel,
-        [part_x, rise_y, w, x_half, y_half, elec, magn],
-        [whole] * 2,
-        specs=[VMEM] * 5 + [HBM] * 2,
+        [whole, whole],
         out_specs=[HBM] * 2,
-        scratch=[half] * 2 + [dma((4,))],
-        aliases={5: 0, 6: 1},
-        flops=4_000_000,
-    )
-    ins = [pos, near_b, far_b, own_b, group_b, near_a, own_a] + ins + [g2, u_x, v_x, flux2]
+        scratch=[cells] * 4 + [dma((4,))],
+        flops=8_000_000,
+    )
+    ins = [pos, near_b, far_b, own_b, group_b, got, own_a, g2, u_x, v_x, flux2]
     at = len(ins)
     out = call(
-        functools.partial(last_kernel, near_x, far_x, px_far),
+        functools.partial(last_kernel, near_x, far_x),
         ins + [elec, magn],
         [whole] * 2,
         specs=[VMEM] * at + [HBM] * 2,
         out_specs=[HBM] * 2,
-        scratch=[(far_x, 2 * B, nz), cells, cells, dma((2,))],
+        scratch=[cells, cells, dma((2,))],
         aliases={at: 0, at + 1: 1},
     )
     return tuple(a.reshape(3, B, B, nz) for a in out)

time: 59.2 us -> 59.5 us (level)
  waiting for transfers between devices: 12.8 us -> 17.8 us
  starting transfers between devices: 34.2 us -> 30.4 us
  local copies, waits for them, and re-layouts: 0.85 us -> 0 us
    ppermute x19 -> x13, starting transfers between devices: 31 us -> 20.3 us  [the longest x12 16.5 us: shared(): lax.ppermute(value, axis, [(i, i ^ mask) for i in range(n)])]
    all_to_all x0 -> x1, starting transfers between devices: none -> 6.84 us  [local(): got = lax.all_to_all(msg, 'px', 0, 0, tiled=True)]
    all_to_all x0 -> x1, waiting for transfers between devices: none -> 4.51 us  [local(): got = lax.all_to_all(msg, 'px', 0, 0, tiled=True)]
    slice x1 -> x0, local copies, waits for them, and re-layouts: 0.85 us -> none  [local(): magnetic[0, :, B - 1]]
    ppermute x19 -> x13, waiting for transfers between devices: 12.8 us -> 13.2 us  [the longest x12 8.9 us: shared(): lax.ppermute(value, axis, [(i, i ^ mask) for i in range(n)])]
    pallas_call x11 -> x10, Pallas kernels: 10 us -> 10.3 us  [call(): pl.pallas_call(kernel, out_shape=shapes, in_specs=specs or [VMEM] * len(i...]
  transfers between devices with their start and end apart: 20 -> 15, of which waited for: 9 -> 8; matrix products, arithmetic and copies ran while one was open for 0% -> 0% of each run, Pallas kernels for 13% -> 11%
where the time goes in v9:
time: 59.5 us; the launch traced here: 59.2 us
  starting transfers between devices  30.4 us (51%)
  waiting for transfers between devices  17.8 us (30%)
  Pallas kernels  10.3 us (17%)
  between operations  0.7 us (1%)
    ppermute x12, starting transfers between devices, shared(): lax.ppermute(value, axis, [(i, i ^ mask) for i in range(n)])  16.5 us
    pallas_call x10, Pallas kernels, call(): pl.pallas_call(kernel, out_shape=shapes, in_specs=specs or [VMEM] * len(i...  10.3 us
    ppermute x12, waiting for transfers between devices, shared(): lax.ppermute(value, axis, [(i, i ^ mask) for i in range(n)])  8.9 us
    all_to_all x1, starting transfers between devices, local(): got = lax.all_to_all(msg, 'px', 0, 0, tiled=True)  6.84 us
    all_to_all x1, waiting for transfers between devices, local(): got = lax.all_to_all(msg, 'px', 0, 0, tiled=True)  4.51 us
    ppermute x1, waiting for transfers between devices, local(): lax.ppermute(hx_last, 'py', [(i, (i + 1) % ny) for i in range(ny)])  4.33 us
    ppermute x1, starting transfers between devices, local(): lax.ppermute(hx_last, 'py', [(i, (i + 1) % ny) for i in range(ny)])  3.82 us
    ppermute x1, starting transfers between devices, local(): lax.ppermute(ez_first, 'py', [((i + 1) % ny, i) for i in range(ny)])  3.24 us
  transfers between devices with their start and end apart: 15, of which 8 were waited for; matrix products, arithmetic and copies ran while one was open for 0% of the time, Pallas kernels for 11%

profile of v9, /device:TPU:1, one launch (start us, length us, event | category | flops | bytes accessed | tf_op | source)
XLA Modules:
  0.0 59.2 jit_solution(17597064322704455884)
XLA Ops:
  0.6 0.7 %shard_map.69 = f32[16,128]{1,0:T(8,128)S(1)} custom-call(f32[3,16,16,128]{3,2,1,0:T(8,128)} %magn.1), custom_call_target="tpu_custom_call" | custom-call | flops 1000 | bytes 1000000 | tf_op jit(solution)/shard_map/pallas_call | solution.py:481
  1.3 3.8 %collective-permute-start = (f32[16,128]{1,0:T(8,128)S(1)}, f32[16,128]{1,0:T(8,128)S(1)}, u32[]{:S(2)}, u32[]{:S(2)}) collective-permute-start(f32[16,128]{1,0:T(8,128)S(1)} %shard_map.69), channel_id=1, source_target_pairs={{0,1},{1,2},{2,3},{3,4},{4,5},{5,6},{6,7},{7,8},{8,9},{9,10},{10,1... | collective-permute-start | bytes 24584 | tf_op jit(solution)/shard_map/ppermute | solution.py:524
  5.2 1.9 %shard_map.68 = (f32[256,128]{1,0:T(8,128)S(1)}, f32[256,128]{1,0:T(8,128)S(1)}, f32[256,128]{1,0:T(8,128)S(1)}, f32[256,128]{1,0:T(8,128)S(1)}, f32[256,128]{1,...) custom-call(s32[2]{0:T(128)S(1)} %pad_add_fusion.me, ...), custom_call_target="tpu_custom_call" | custom-call | flops 1000000 | bytes 1000000 | tf_op jit(solution)/shard_map/pallas_call | solution.py:481
  7.2 4.3 %collective-permute-done.hx_prev = f32[16,128]{1,0:T(8,128)S(1)} collective-permute-done((f32[16,128]{1,0:T(8,128)S(1)}, f32[16,128]{1,0:T(8,128)S(1)}, u32[]{:S(2)}, u32[]{:S(2)}) %collective-permute-start) | collective-permute-done | bytes 8224 | tf_op jit(solution)/shard_map/ppermute | solution.py:524
  11.6 2.7 %collective-permute-start.3 = (f32[112,128]{1,0:T(8,128)S(1)}, f32[112,128]{1,0:T(8,128)S(1)}, u32[]{:S(2)}, u32[]{:S(2)}) collective-permute-start(f32[112,128]{1,0:T(8,128)S(1)} %get-tuple-element.54.refs_0_.own_near.own_b), channel_id=1, source_target_pairs={{0,48},{16,32},{32,16},{48,0},{64,112},{80,96},{96,80},{112,64},{1... | collective-permute-start | bytes 172040 | tf_op jit(solution)/shard_map/ppermute | solution.py:495
  14.8 3.2 %collective-permute-start.7 = (f32[128,128]{1,0:T(8,128)S(1)}, f32[128,128]{1,0:T(8,128)S(1)}, u32[]{:S(2)}, u32[]{:S(2)}) collective-permute-start(f32[128,128]{1,0:T(8,128)S(1)} %get-tuple-element.60), channel_id=1, source_target_pairs={{1,0},{2,1},{3,2},{4,3},{5,4},{6,5},{7,6},{8,7},{9,8},{10,9},{11,1... | collective-permute-start | bytes 196616 | tf_op jit(solution)/shard_map/ppermute | solution.py:538
  18.3 2.2 %collective-permute-start.6 = (f32[112,128]{1,0:T(8,128)S(1)}, f32[112,128]{1,0:T(8,128)S(1)}, u32[]{:S(2)}, u32[]{:S(2)}) collective-permute-start(f32[112,128]{1,0:T(8,128)S(1)} %get-tuple-element.56.refs_0_.group_b), channel_id=1, source_target_pairs={{0,224},{16,240},{32,192},{48,208},{64,160},{80,176},{96,128},{112... | collective-permute-start | bytes 172040 | tf_op jit(solution)/shard_map/ppermute | solution.py:495
  20.5 0.6 %collective-permute-start.5 = (f32[112,128]{1,0:T(8,128)S(1)}, f32[112,128]{1,0:T(8,128)S(1)}, u32[]{:S(2)}, u32[]{:S(2)}) collective-permute-start(f32[112,128]{1,0:T(8,128)S(1)} %get-tuple-element.56.refs_0_.group_b), channel_id=1, source_target_pairs={{0,96},{16,112},{32,64},{48,80},{64,32},{80,48},{96,0},{112,16},{1... | collective-permute-start | bytes 172040 | tf_op jit(solution)/shard_map/ppermute | solution.py:495
  21.2 1.1 %collective-permute-start.4 = (f32[112,128]{1,0:T(8,128)S(1)}, f32[112,128]{1,0:T(8,128)S(1)}, u32[]{:S(2)}, u32[]{:S(2)}) collective-permute-start(f32[112,128]{1,0:T(8,128)S(1)} %get-tuple-element.56.refs_0_.group_b), channel_id=1, source_target_pairs={{0,128},{16,144},{32,160},{48,176},{64,192},{80,208},{96,224},{112... | collective-permute-start | bytes 172040 | tf_op jit(solution)/shard_map/ppermute | solution.py:495
  22.3 2.0 %shard_map.72 = (f32[256,128]{1,0:T(8,128)S(1)}, f32[256,128]{1,0:T(8,128)S(1)}, f32[256,128]{1,0:T(8,128)S(1)}, f32[16,128]{1,0:T(8,128)S(1)}, f32[16,128]{1,0:...) custom-call(s32[32,128]{1,0:T(8,128)S(1)} %get-tuple-element.46.pos,, ...), custom_call_target="tpu_custom_call" | custom-call | flops 8000000 | bytes 1000000 | tf_op jit(solution)/shard_map/pallas_call | solution.py:481
  24.8 0.8 %shard_map.73 = (f32[4,112,128]{2,1,0:T(8,128)S(1)}, f32[256,128]{1,0:T(8,128)S(1)}, f32[256,128]{1,0:T(8,128)S(1)}, f32[256,128]{1,0:T(8,128)S(1)}, f32[256,128...) custom-call(s32[32,128]{1,0:T(8,128)S(1)} %get-tuple-element.46.pos, ...), custom_call_target="tpu_custom_call" | custom-call | flops 1000000 | bytes 1000000 | tf_op jit(solution)/shard_map/pallas_call | solution.py:481
  25.7 0.9 %collective-permute-start.9 = (f32[112,128]{1,0:T(8,128)S(1)}, f32[112,128]{1,0:T(8,128)S(1)}, u32[]{:S(2)}, u32[]{:S(2)}) collective-permute-start(f32[112,128]{1,0:T(8,128)S(1)} %get-tuple-element.71.refs_0_.own_near), channel_id=1, source_target_pairs={{0,1},{1,0},{2,3},{3,2},{4,5},{5,4},{6,7},{7,6},{8,9},{9,8},{10,11... | collective-permute-start | bytes 172040 | tf_op jit(solution)/shard_map/ppermute | solution.py:495
  26.6 3.2 %collective-permute-start.8 = (f32[112,128]{1,0:T(8,128)S(1)}, f32[112,128]{1,0:T(8,128)S(1)}, u32[]{:S(2)}, u32[]{:S(2)}) collective-permute-start(f32[112,128]{1,0:T(8,128)S(1)} %get-tuple-element.71.refs_0_.own_near), channel_id=1, source_target_pairs={{0,2},{1,3},{2,0},{3,1},{4,6},{5,7},{6,4},{7,5},{8,10},{9,11},{10,... | collective-permute-start | bytes 172040 | tf_op jit(solution)/shard_map/ppermute | solution.py:495
  29.9 1.3 %collective-permute-done.10.refs_3_ = f32[112,128]{1,0:T(8,128)S(1)} collective-permute-done((f32[112,128]{1,0:T(8,128)S(1)}, f32[112,128]{1,0:T(8,128)S(1)}, u32[]{:S(2)}, u32[]{:S(2)}) %collective-permute-start.10) | collective-permute-done | bytes 57376 | tf_op jit(solution)/shard_map/ppermute | solution.py:495
  31.1 1.2 %collective-permute-done.8.refs_1_ = f32[112,128]{1,0:T(8,128)S(1)} collective-permute-done((f32[112,128]{1,0:T(8,128)S(1)}, f32[112,128]{1,0:T(8,128)S(1)}, u32[]{:S(2)}, u32[]{:S(2)}) %collective-permute-start.8) | collective-permute-done | bytes 57376 | tf_op jit(solution)/shard_map/ppermute | solution.py:495
  32.4 4.5 %collective-permute-start.13 = (f32[112,128]{1,0:T(8,128)S(1)}, f32[112,128]{1,0:T(8,128)S(1)}, u32[]{:S(2)}, u32[]{:S(2)}) collective-permute-start(f32[112,128]{1,0:T(8,128)S(1)} %get-tuple-element.73.refs_0_), channel_id=1, source_target_pairs={{0,10},{1,11},{2,8},{3,9},{4,14},{5,15},{6,12},{7,13},{8,2},{9,3},... | collective-permute-start | bytes 172040 | tf_op jit(solution)/shard_map/ppermute | solution.py:495
  36.9 0.6 %collective-permute-start.11 = (f32[112,128]{1,0:T(8,128)S(1)}, f32[112,128]{1,0:T(8,128)S(1)}, u32[]{:S(2)}, u32[]{:S(2)}) collective-permute-start(f32[112,128]{1,0:T(8,128)S(1)} %get-tuple-element.73.refs_0_), channel_id=1, source_target_pairs={{0,4},{1,5},{2,6},{3,7},{4,0},{5,1},{6,2},{7,3},{8,12},{9,13},{10,... | collective-permute-start | bytes 172040 | tf_op jit(solution)/shard_map/ppermute | solution.py:495
  37.5 1.7 %collective-permute-done.13.refs_3_ = f32[112,128]{1,0:T(8,128)S(1)} collective-permute-done((f32[112,128]{1,0:T(8,128)S(1)}, f32[112,128]{1,0:T(8,128)S(1)}, u32[]{:S(2)}, u32[]{:S(2)}) %collective-permute-start.13) | collective-permute-done | bytes 57376 | tf_op jit(solution)/shard_map/ppermute | solution.py:495
  39.2 4.0 %collective-permute-done.12.refs_2_ = f32[112,128]{1,0:T(8,128)S(1)} collective-permute-done((f32[112,128]{1,0:T(8,128)S(1)}, f32[112,128]{1,0:T(8,128)S(1)}, u32[]{:S(2)}, u32[]{:S(2)}) %collective-permute-start.12) | collective-permute-done | bytes 57376 | tf_op jit(solution)/shard_map/ppermute | solution.py:495
  43.2 1.1 %shard_map.75 = (f32[256,128]{1,0:T(8,128)S(1)}, f32[256,128]{1,0:T(8,128)S(1)}, f32[256,128]{1,0:T(8,128)S(1)}, f32[32,128]{1,0:T(8,128)S(1)}, f32[32,128]{1,0:T(8,128)S(1)}, /*index=5*/f32[16,32,128]{2,1,0:T(8,128)}) custom-call(s32[32,128]{1,0:T(8,128)S(1)} %get-tuple-element.46.pos, f32[4,112,128]{2,1,0:T(8,128)S(1)} %get-tuple-element.72.got_near, ...), custom_call_target="tpu_custom_call" | custom-call | flops 1000000 | bytes 1000000 | tf_op jit(solution)/shard_map/pallas_call | solution.py:481
  44.3 6.8 %all-to-all-start = ((f32[16,32,128]{2,1,0:T(8,128)}), f32[16,32,128]{2,1,0:T(8,128)S(1)}, u32[]{:S(2)}, u32[]{:S(2)}) async-start(f32[16,32,128]{2,1,0:T(8,128)} %get-tuple-element.77), calls=%async_computation | async-start | bytes 524288 | tf_op jit(solution)/shard_map/all_to_all | solution.py:570
  51.1 2.7 %shard_map.76 = (f32[3,256,128]{2,1,0:T(8,128)}, f32[3,256,128]{2,1,0:T(8,128)}) custom-call(f32[32,128]{1,0:T(8,128)S(1)} %get-tuple-element.81.ends_c, f32[256,128]{1,0:T(8,128)S(1)} %get-tuple-element.82.g_c, f32[256,128]{1,0:T(8,128)S(1)} %get-tuple-element.68.refs_17_.refs_5_.u, f32[256,128]{1,0:T(8,128)S(1)} %get-tuple-element.69.refs_18_.refs_6_.v, ...), custom_call_target="tpu_custom_call" | custom-call | flops 8000000 | bytes 1000000 | tf_op jit(solution)/shard_map/pallas_call | solution.py:481
  53.9 4.5 %all-to-all-done.got = f32[16,32,128]{2,1,0:T(8,128)S(1)} async-done(((f32[16,32,128]{2,1,0:T(8,128)}), f32[16,32,128]{2,1,0:T(8,128)S(1)}, u32[]{:S(2)}, u32[]{:S(2)}) %all-to-all-start) | async-done | bytes 262176 | tf_op jit(solution)/shard_map/all_to_all | solution.py:570
  58.4 0.8 %shard_map.77 = (f32[3,256,128]{2,1,0:T(8,128)}, f32[3,256,128]{2,1,0:T(8,128)}) custom-call(s32[32,128]{1,0:T(8,128)S(1)} %get-tuple-element.46.pos, f32[4,112,128]{2,1,0:T(8,128)S(1)} %get-tuple-element.55.got_near.refs_11_.near_b, f32[4,112,128]{2,1,0:T(8,128)S(1)} %get-tuple-element.70.far_b, ...), custom_call_target="tpu_custom_call", output_to_operand_aliasing={{0}: (11, {}), {1}: (12, {})} | custom-call | flops 1000000 | bytes 1000000 | tf_op jit(solution)/shard_map/pallas_call | solution.py:481
  (17 shorter events, 1.6 us)
Async XLA Ops:
  1.3 10.2 %collective-permute-start = (f32[16,128]{1,0:T(8,128)S(1)}, f32[16,128]{1,0:T(8,128)S(1)}, u32[]{:S(2)}, u32[]{:S(2)}) collective-permute-start(f32[16,128]{1,0:T(8,128)S(1)} %shard_map.69), channel_id=1, source_target_pairs={{0,1},{1,2},{2,3},{3,4},{4,5},{5,6},{6,7},{7,8},{8,9},{9,10},{10,1... | collective-permute-start | bytes 24584 | tf_op jit(solution)/shard_map/ppermute | solution.py:524
  11.6 6.5 %collective-permute-start.3 = (f32[112,128]{1,0:T(8,128)S(1)}, f32[112,128]{1,0:T(8,128)S(1)}, u32[]{:S(2)}, u32[]{:S(2)}) collective-permute-start(f32[112,128]{1,0:T(8,128)S(1)} %get-tuple-element.54.refs_0_.own_near.own_b), channel_id=1, source_target_pairs={{0,48},{16,32},{32,16},{48,0},{64,112},{80,96},{96,80},{112,64},{1... | collective-permute-start | bytes 172040 | tf_op jit(solution)/shard_map/ppermute | solution.py:495
  14.3 3.9 %collective-permute-start.2 = (f32[112,128]{1,0:T(8,128)S(1)}, f32[112,128]{1,0:T(8,128)S(1)}, u32[]{:S(2)}, u32[]{:S(2)}) collective-permute-start(f32[112,128]{1,0:T(8,128)S(1)} %get-tuple-element.54.refs_0_.own_near.own_b), channel_id=1, source_target_pairs={{0,32},{16,48},{32,0},{48,16},{64,96},{80,112},{96,64},{112,80},{1... | collective-permute-start | bytes 172040 | tf_op jit(solution)/shard_map/ppermute | solution.py:495
  14.6 3.7 %collective-permute-start.1 = (f32[112,128]{1,0:T(8,128)S(1)}, f32[112,128]{1,0:T(8,128)S(1)}, u32[]{:S(2)}, u32[]{:S(2)}) collective-permute-start(f32[112,128]{1,0:T(8,128)S(1)} %get-tuple-element.54.refs_0_.own_near.own_b), channel_id=1, source_target_pairs={{0,16},{16,0},{32,48},{48,32},{64,80},{80,64},{96,112},{112,96},{1... | collective-permute-start | bytes 172040 | tf_op jit(solution)/shard_map/ppermute | solution.py:495
  14.8 7.5 %collective-permute-start.7 = (f32[128,128]{1,0:T(8,128)S(1)}, f32[128,128]{1,0:T(8,128)S(1)}, u32[]{:S(2)}, u32[]{:S(2)}) collective-permute-start(f32[128,128]{1,0:T(8,128)S(1)} %get-tuple-element.60), channel_id=1, source_target_pairs={{1,0},{2,1},{3,2},{4,3},{5,4},{6,5},{7,6},{8,7},{9,8},{10,9},{11,1... | collective-permute-start | bytes 196616 | tf_op jit(solution)/shard_map/ppermute | solution.py:538
  18.3 6.0 %collective-permute-start.6 = (f32[112,128]{1,0:T(8,128)S(1)}, f32[112,128]{1,0:T(8,128)S(1)}, u32[]{:S(2)}, u32[]{:S(2)}) collective-permute-start(f32[112,128]{1,0:T(8,128)S(1)} %get-tuple-element.56.refs_0_.group_b), channel_id=1, source_target_pairs={{0,224},{16,240},{32,192},{48,208},{64,160},{80,176},{96,128},{112... | collective-permute-start | bytes 172040 | tf_op jit(solution)/shard_map/ppermute | solution.py:495
  20.5 4.2 %collective-permute-start.5 = (f32[112,128]{1,0:T(8,128)S(1)}, f32[112,128]{1,0:T(8,128)S(1)}, u32[]{:S(2)}, u32[]{:S(2)}) collective-permute-start(f32[112,128]{1,0:T(8,128)S(1)} %get-tuple-element.56.refs_0_.group_b), channel_id=1, source_target_pairs={{0,96},{16,112},{32,64},{48,80},{64,32},{80,48},{96,0},{112,16},{1... | collective-permute-start | bytes 172040 | tf_op jit(solution)/shard_map/ppermute | solution.py:495
  21.2 3.6 %collective-permute-start.4 = (f32[112,128]{1,0:T(8,128)S(1)}, f32[112,128]{1,0:T(8,128)S(1)}, u32[]{:S(2)}, u32[]{:S(2)}) collective-permute-start(f32[112,128]{1,0:T(8,128)S(1)} %get-tuple-element.56.refs_0_.group_b), channel_id=1, source_target_pairs={{0,128},{16,144},{32,160},{48,176},{64,192},{80,208},{96,224},{112... | collective-permute-start | bytes 172040 | tf_op jit(solution)/shard_map/ppermute | solution.py:495
  25.6 5.5 %collective-permute-start.10 = (f32[112,128]{1,0:T(8,128)S(1)}, f32[112,128]{1,0:T(8,128)S(1)}, u32[]{:S(2)}, u32[]{:S(2)}) collective-permute-start(f32[112,128]{1,0:T(8,128)S(1)} %get-tuple-element.71.refs_0_.own_near), channel_id=1, source_target_pairs={{0,3},{1,2},{2,1},{3,0},{4,7},{5,6},{6,5},{7,4},{8,11},{9,10},{10,... | collective-permute-start | bytes 172040 | tf_op jit(solution)/shard_map/ppermute | solution.py:495
  25.7 5.4 %collective-permute-start.9 = (f32[112,128]{1,0:T(8,128)S(1)}, f32[112,128]{1,0:T(8,128)S(1)}, u32[]{:S(2)}, u32[]{:S(2)}) collective-permute-start(f32[112,128]{1,0:T(8,128)S(1)} %get-tuple-element.71.refs_0_.own_near), channel_id=1, source_target_pairs={{0,1},{1,0},{2,3},{3,2},{4,5},{5,4},{6,7},{7,6},{8,9},{9,8},{10,11... | collective-permute-start | bytes 172040 | tf_op jit(solution)/shard_map/ppermute | solution.py:495
  26.6 5.7 %collective-permute-start.8 = (f32[112,128]{1,0:T(8,128)S(1)}, f32[112,128]{1,0:T(8,128)S(1)}, u32[]{:S(2)}, u32[]{:S(2)}) collective-permute-start(f32[112,128]{1,0:T(8,128)S(1)} %get-tuple-element.71.refs_0_.own_near), channel_id=1, source_target_pairs={{0,2},{1,3},{2,0},{3,1},{4,6},{5,7},{6,4},{7,5},{8,10},{9,11},{10,... | collective-permute-start | bytes 172040 | tf_op jit(solution)/shard_map/ppermute | solution.py:495
  32.4 6.8 %collective-permute-start.13 = (f32[112,128]{1,0:T(8,128)S(1)}, f32[112,128]{1,0:T(8,128)S(1)}, u32[]{:S(2)}, u32[]{:S(2)}) collective-permute-start(f32[112,128]{1,0:T(8,128)S(1)} %get-tuple-element.73.refs_0_), channel_id=1, source_target_pairs={{0,10},{1,11},{2,8},{3,9},{4,14},{5,15},{6,12},{7,13},{8,2},{9,3},... | collective-permute-start | bytes 172040 | tf_op jit(solution)/shard_map/ppermute | solution.py:495
  36.9 6.3 %collective-permute-start.12 = (f32[112,128]{1,0:T(8,128)S(1)}, f32[112,128]{1,0:T(8,128)S(1)}, u32[]{:S(2)}, u32[]{:S(2)}) collective-permute-start(f32[112,128]{1,0:T(8,128)S(1)} %get-tuple-element.73.refs_0_), channel_id=1, source_target_pairs={{0,12},{1,13},{2,14},{3,15},{4,8},{5,9},{6,10},{7,11},{8,4},{9,5},... | collective-permute-start | bytes 172040 | tf_op jit(solution)/shard_map/ppermute | solution.py:495
  36.9 6.3 %collective-permute-start.11 = (f32[112,128]{1,0:T(8,128)S(1)}, f32[112,128]{1,0:T(8,128)S(1)}, u32[]{:S(2)}, u32[]{:S(2)}) collective-permute-start(f32[112,128]{1,0:T(8,128)S(1)} %get-tuple-element.73.refs_0_), channel_id=1, source_target_pairs={{0,4},{1,5},{2,6},{3,7},{4,0},{5,1},{6,2},{7,3},{8,12},{9,13},{10,... | collective-permute-start | bytes 172040 | tf_op jit(solution)/shard_map/ppermute | solution.py:495
  44.3 14.1 %all-to-all-start = ((f32[16,32,128]{2,1,0:T(8,128)}), f32[16,32,128]{2,1,0:T(8,128)S(1)}, u32[]{:S(2)}, u32[]{:S(2)}) async-start(f32[16,32,128]{2,1,0:T(8,128)} %get-tuple-element.77), calls=%async_computation | async-start | bytes 524288 | tf_op jit(solution)/shard_map/all_to_all | solution.py:570

commit v10 on v8

--- a/solution.py
+++ b/solution.py
@@ -196,6 +196,12 @@
 def place(pos, axis, near):
     here = pos[plane(axis)]
     return lax.shift_right_logical(here, near.bit_length() - 1), lax.bitwise_and(here, near - 1)
+
+
+def cut_kernel(magn, hx_last, sem):
+    load = pltpu.make_async_copy(magn.at[0, :, B - 1], hx_last, sem)
+    load.start()
+    load.wait()
 
 
 def tables_kernel(
@@ -528,13 +534,16 @@
     magn = in_hbm(magnetic.reshape(3, *cells))
     ids = in_hbm(material.reshape(cells))
     dma = pltpu.SemaphoreType.DMA
-    orders = [(1, 2, 3), (2, 1, 3), (2, 3, 1), (1, 3, 2)]
+    orders = [(1, 2, 3), (2, 1, 3), (2, 1, 3), (1, 3, 2)]
     counts = (near_x, far_x, near_y, far_y)
     px_near, px_far, py_near, py_far = [
         tuple(s for s in order if s < count) for order, count in zip(orders, counts)
     ]
 
-    hx_prev = lax.ppermute(magnetic[0, :, B - 1], "py", [(i, (i + 1) % ny) for i in range(ny)])
+    (hx_last,) = call(
+        cut_kernel, [in_hbm(magnetic)], [(B, nz)], specs=[HBM], scratch=[dma(())], flops=1000
+    )
+    hx_prev = lax.ppermute(hx_last, "py", [(i, (i + 1) % ny) for i in range(ny)])
     w, c, p_x, u_x, v_x, flux_b, part_b, ef, mf, ez_first, pos = call(
         tables_kernel,
         [me, in_hbm(permittivity), in_hbm(conductivity), ids, elec, magn],

time: 57.7 us -> 57.6 us (level)
  waiting for transfers between devices: 11.8 us -> 12.7 us
  local copies, waits for them, and re-layouts: 0.85 us -> 0 us
  starting transfers between devices: 33.3 us -> 32.5 us
  Pallas kernels: 9.76 us -> 10.5 us
    ppermute x18, waiting for transfers between devices: 7.42 us -> 8.32 us  [shared(): lax.ppermute(value, axis, [(i, i ^ mask) for i in range(n)])]
    ppermute x18, starting transfers between devices: 26.3 us -> 25.4 us  [shared(): lax.ppermute(value, axis, [(i, i ^ mask) for i in range(n)])]
    slice x1 -> x0, local copies, waits for them, and re-layouts: 0.85 us -> none  [local(): magnetic[0, :, B - 1]]
    pallas_call x12 -> x13, Pallas kernels: 9.76 us -> 10.5 us  [call(): pl.pallas_call(kernel, out_shape=shapes, in_specs=specs or [VMEM] * len(i...]
where the time goes in v10:
time: 57.6 us; the launch traced here: 56.6 us
  starting transfers between devices  32.5 us (56%)
  waiting for transfers between devices  12.7 us (22%)
  Pallas kernels  10.5 us (18%)
  between operations  0.91 us (2%)
    ppermute x18, starting transfers between devices, shared(): lax.ppermute(value, axis, [(i, i ^ mask) for i in range(n)])  25.4 us
    pallas_call x13, Pallas kernels, call(): pl.pallas_call(kernel, out_shape=shapes, in_specs=specs or [VMEM] * len(i...  10.5 us
    ppermute x18, waiting for transfers between devices, shared(): lax.ppermute(value, axis, [(i, i ^ mask) for i in range(n)])  8.32 us
    ppermute x1, waiting for transfers between devices, local(): lax.ppermute(hx_last, 'py', [(i, (i + 1) % ny) for i in range(ny)])  4.33 us
    ppermute x1, starting transfers between devices, local(): lax.ppermute(hx_last, 'py', [(i, (i + 1) % ny) for i in range(ny)])  3.82 us
    ppermute x1, starting transfers between devices, local(): lax.ppermute(ez_first, 'py', [((i + 1) % ny, i) for i in range(ny)])  3.24 us
  transfers between devices with their start and end apart: 20, of which 9 were waited for; matrix products, arithmetic and copies ran while one was open for 0% of the time, Pallas kernels for 13%

profile of v10, /device:TPU:1, one launch (start us, length us, event | category | flops | bytes accessed | tf_op | source)
XLA Modules:
  0.0 56.6 jit_solution(16047037328587096317)
XLA Ops:
  1.3 3.8 %collective-permute-start = (f32[16,128]{1,0:T(8,128)S(1)}, f32[16,128]{1,0:T(8,128)S(1)}, u32[]{:S(2)}, u32[]{:S(2)}) collective-permute-start(f32[16,128]{1,0:T(8,128)S(1)} %shard_map.69), channel_id=1, source_target_pairs={{0,1},{1,2},{2,3},{3,4},{4,5},{5,6},{6,7},{7,8},{8,9},{9,10},{10,1... | collective-permute-start | bytes 24584 | tf_op jit(solution)/shard_map/ppermute | solution.py:546
  5.2 1.9 %shard_map.68 = (f32[256,128]{1,0:T(8,128)S(1)}, f32[256,128]{1,0:T(8,128)S(1)}, f32[256,128]{1,0:T(8,128)S(1)}, f32[256,128]{1,0:T(8,128)S(1)}, f32[256,128]{1,...) custom-call(s32[2]{0:T(128)S(1)} %pad_add_fusion.me, ...), custom_call_target="tpu_custom_call" | custom-call | flops 1000000 | bytes 1000000 | tf_op jit(solution)/shard_map/pallas_call | solution.py:503
  7.2 4.3 %collective-permute-done.hx_prev = f32[16,128]{1,0:T(8,128)S(1)} collective-permute-done((f32[16,128]{1,0:T(8,128)S(1)}, f32[16,128]{1,0:T(8,128)S(1)}, u32[]{:S(2)}, u32[]{:S(2)}) %collective-permute-start) | collective-permute-done | bytes 8224 | tf_op jit(solution)/shard_map/ppermute | solution.py:546
  11.6 2.7 %collective-permute-start.3 = (f32[112,128]{1,0:T(8,128)S(1)}, f32[112,128]{1,0:T(8,128)S(1)}, u32[]{:S(2)}, u32[]{:S(2)}) collective-permute-start(f32[112,128]{1,0:T(8,128)S(1)} %get-tuple-element.71.refs_0_.own_near.own_b), channel_id=1, source_target_pairs={{0,48},{16,32},{32,16},{48,0},{64,112},{80,96},{96,80},{112,64},{1... | collective-permute-start | bytes 172040 | tf_op jit(solution)/shard_map/ppermute | solution.py:517
  14.8 3.2 %collective-permute-start.7 = (f32[128,128]{1,0:T(8,128)S(1)}, f32[128,128]{1,0:T(8,128)S(1)}, u32[]{:S(2)}, u32[]{:S(2)}) collective-permute-start(f32[128,128]{1,0:T(8,128)S(1)} %get-tuple-element.77), channel_id=1, source_target_pairs={{1,0},{2,1},{3,2},{4,3},{5,4},{6,5},{7,6},{8,7},{9,8},{10,9},{11,1... | collective-permute-start | bytes 196616 | tf_op jit(solution)/shard_map/ppermute | solution.py:560
  18.3 2.2 %collective-permute-start.6 = (f32[112,128]{1,0:T(8,128)S(1)}, f32[112,128]{1,0:T(8,128)S(1)}, u32[]{:S(2)}, u32[]{:S(2)}) collective-permute-start(f32[112,128]{1,0:T(8,128)S(1)} %get-tuple-element.73.refs_0_.group_b), channel_id=1, source_target_pairs={{0,224},{16,240},{32,192},{48,208},{64,160},{80,176},{96,128},{112... | collective-permute-start | bytes 172040 | tf_op jit(solution)/shard_map/ppermute | solution.py:517
  21.2 1.1 %collective-permute-start.4 = (f32[112,128]{1,0:T(8,128)S(1)}, f32[112,128]{1,0:T(8,128)S(1)}, u32[]{:S(2)}, u32[]{:S(2)}) collective-permute-start(f32[112,128]{1,0:T(8,128)S(1)} %get-tuple-element.73.refs_0_.group_b), channel_id=1, source_target_pairs={{0,128},{16,144},{32,160},{48,176},{64,192},{80,208},{96,224},{112... | collective-permute-start | bytes 172040 | tf_op jit(solution)/shard_map/ppermute | solution.py:517
  22.3 2.0 %shard_map.72 = (f32[256,128]{1,0:T(8,128)S(1)}, f32[256,128]{1,0:T(8,128)S(1)}, f32[256,128]{1,0:T(8,128)S(1)}, f32[16,128]{1,0:T(8,128)S(1)}, f32[16,128]{1,0:...) custom-call(s32[32,128]{1,0:T(8,128)S(1)} %get-tuple-element.63.pos,, ...), custom_call_target="tpu_custom_call" | custom-call | flops 8000000 | bytes 1000000 | tf_op jit(solution)/shard_map/pallas_call | solution.py:503
  24.8 0.8 %shard_map.73 = (f32[4,112,128]{2,1,0:T(8,128)S(1)}, f32[256,128]{1,0:T(8,128)S(1)}, f32[256,128]{1,0:T(8,128)S(1)}, f32[256,128]{1,0:T(8,128)S(1)}, f32[256,128...) custom-call(s32[32,128]{1,0:T(8,128)S(1)} %get-tuple-element.63.pos, ...), custom_call_target="tpu_custom_call" | custom-call | flops 1000000 | bytes 1000000 | tf_op jit(solution)/shard_map/pallas_call | solution.py:503
  25.7 0.9 %collective-permute-start.9 = (f32[112,128]{1,0:T(8,128)S(1)}, f32[112,128]{1,0:T(8,128)S(1)}, u32[]{:S(2)}, u32[]{:S(2)}) collective-permute-start(f32[112,128]{1,0:T(8,128)S(1)} %get-tuple-element.88.refs_0_.own_near), channel_id=1, source_target_pairs={{0,1},{1,0},{2,3},{3,2},{4,5},{5,4},{6,7},{7,6},{8,9},{9,8},{10,11... | collective-permute-start | bytes 172040 | tf_op jit(solution)/shard_map/ppermute | solution.py:517
  26.6 3.2 %collective-permute-start.8 = (f32[112,128]{1,0:T(8,128)S(1)}, f32[112,128]{1,0:T(8,128)S(1)}, u32[]{:S(2)}, u32[]{:S(2)}) collective-permute-start(f32[112,128]{1,0:T(8,128)S(1)} %get-tuple-element.88.refs_0_.own_near), channel_id=1, source_target_pairs={{0,2},{1,3},{2,0},{3,1},{4,6},{5,7},{6,4},{7,5},{8,10},{9,11},{10,... | collective-permute-start | bytes 172040 | tf_op jit(solution)/shard_map/ppermute | solution.py:517
  29.9 1.3 %collective-permute-done.10.refs_3_ = f32[112,128]{1,0:T(8,128)S(1)} collective-permute-done((f32[112,128]{1,0:T(8,128)S(1)}, f32[112,128]{1,0:T(8,128)S(1)}, u32[]{:S(2)}, u32[]{:S(2)}) %collective-permute-start.10) | collective-permute-done | bytes 57376 | tf_op jit(solution)/shard_map/ppermute | solution.py:517
  31.1 1.2 %collective-permute-done.8.refs_1_ = f32[112,128]{1,0:T(8,128)S(1)} collective-permute-done((f32[112,128]{1,0:T(8,128)S(1)}, f32[112,128]{1,0:T(8,128)S(1)}, u32[]{:S(2)}, u32[]{:S(2)}) %collective-permute-start.8) | collective-permute-done | bytes 57376 | tf_op jit(solution)/shard_map/ppermute | solution.py:517
  32.4 4.5 %collective-permute-start.13 = (f32[112,128]{1,0:T(8,128)S(1)}, f32[112,128]{1,0:T(8,128)S(1)}, u32[]{:S(2)}, u32[]{:S(2)}) collective-permute-start(f32[112,128]{1,0:T(8,128)S(1)} %get-tuple-element.96.refs_0_), channel_id=1, source_target_pairs={{0,10},{1,11},{2,8},{3,9},{4,14},{5,15},{6,12},{7,13},{8,2},{9,3},... | collective-permute-start | bytes 172040 | tf_op jit(solution)/shard_map/ppermute | solution.py:517
  37.5 1.3 %shard_map.75 = (f32[7,256,128]{2,1,0:T(8,128)S(1)}, f32[7,256,128]{2,1,0:T(8,128)S(1)}, f32[256,128]{1,0:T(8,128)S(1)}) custom-call(f32[256,128]{1,0:T(8,128)S(1)} %get-tuple-element.92.w.refs_8_.w_in), custom_call_target="tpu_custom_call" | custom-call | flops 8000000 | bytes 1000000 | tf_op jit(solution)/shard_map/pallas_call | solution.py:503
  39.2 4.0 %collective-permute-done.12.refs_2_ = f32[112,128]{1,0:T(8,128)S(1)} collective-permute-done((f32[112,128]{1,0:T(8,128)S(1)}, f32[112,128]{1,0:T(8,128)S(1)}, u32[]{:S(2)}, u32[]{:S(2)}) %collective-permute-start.12) | collective-permute-done | bytes 57376 | tf_op jit(solution)/shard_map/ppermute | solution.py:517
  43.6 2.8 %collective-permute-start.16 = (f32[32,128]{1,0:T(8,128)S(1)}, f32[32,128]{1,0:T(8,128)S(1)}, u32[]{:S(2)}, u32[]{:S(2)}) collective-permute-start(f32[32,128]{1,0:T(8,128)S(1)} %get-tuple-element.103.refs_0_.own_near), channel_id=1, source_target_pairs={{0,48},{16,32},{32,16},{48,0},{64,112},{80,96},{96,80},{112,64},{1... | collective-permute-start | bytes 49160 | tf_op jit(solution)/shard_map/ppermute | solution.py:517
  46.3 2.2 %collective-permute-start.15 = (f32[32,128]{1,0:T(8,128)S(1)}, f32[32,128]{1,0:T(8,128)S(1)}, u32[]{:S(2)}, u32[]{:S(2)}) collective-permute-start(f32[32,128]{1,0:T(8,128)S(1)} %get-tuple-element.103.refs_0_.own_near), channel_id=1, source_target_pairs={{0,32},{16,48},{32,0},{48,16},{64,96},{80,112},{96,64},{112,80},{1... | collective-permute-start | bytes 49160 | tf_op jit(solution)/shard_map/ppermute | solution.py:517
  48.5 0.8 %shard_map.78 = (f32[3,256,128]{2,1,0:T(8,128)}, f32[3,256,128]{2,1,0:T(8,128)}) custom-call(f32[32,128]{1,0:T(8,128)S(1)} %get-tuple-element.106.ends_c, f32[256,128]{1,0:T(8,128)S(1)} %get-tuple-element.107.g_c, f32[256,128]{1,0:T(8,128)S(1)} %get-tuple-element.85.refs_17_.refs_5_.u, f32[256,128]{1,0:T(8,128)S(1)} %get-tuple-element.86.refs_18_.refs_6_.v, ...), custom_call_target="tpu_custom_call" | custom-call | flops 1000000 | bytes 1000000 | tf_op jit(solution)/shard_map/pallas_call | solution.py:503
  50.0 1.8 %collective-permute-start.19 = (f32[32,128]{1,0:T(8,128)S(1)}, f32[32,128]{1,0:T(8,128)S(1)}, u32[]{:S(2)}, u32[]{:S(2)}) collective-permute-start(f32[32,128]{1,0:T(8,128)S(1)} %get-tuple-element.110.refs_0_), channel_id=1, source_target_pairs={{0,224},{16,240},{32,192},{48,208},{64,160},{80,176},{96,128},{112... | collective-permute-start | bytes 49160 | tf_op jit(solution)/shard_map/ppermute | solution.py:517
  51.8 0.8 %collective-permute-start.18 = (f32[32,128]{1,0:T(8,128)S(1)}, f32[32,128]{1,0:T(8,128)S(1)}, u32[]{:S(2)}, u32[]{:S(2)}) collective-permute-start(f32[32,128]{1,0:T(8,128)S(1)} %get-tuple-element.110.refs_0_), channel_id=1, source_target_pairs={{0,96},{16,112},{32,64},{48,80},{64,32},{80,48},{96,0},{112,16},{1... | collective-permute-start | bytes 49160 | tf_op jit(solution)/shard_map/ppermute | solution.py:517
  52.6 1.3 %collective-permute-start.17 = (f32[32,128]{1,0:T(8,128)S(1)}, f32[32,128]{1,0:T(8,128)S(1)}, u32[]{:S(2)}, u32[]{:S(2)}) collective-permute-start(f32[32,128]{1,0:T(8,128)S(1)} %get-tuple-element.110.refs_0_), channel_id=1, source_target_pairs={{0,128},{16,144},{32,160},{48,176},{64,192},{80,208},{96,224},{112... | collective-permute-start | bytes 49160 | tf_op jit(solution)/shard_map/ppermute | solution.py:517
  53.9 1.6 %shard_map.79 = (f32[3,256,128]{2,1,0:T(8,128)}, f32[3,256,128]{2,1,0:T(8,128)}) custom-call(f32[256,128]{1,0:T(8,128)S(1)} %get-tuple-element.113.part, f32[256,128]{1,0:T(8,128)S(1)} %get-tuple-element.114.rise_y, f32[7,256,128]{2,1,0:T(8,128)S(1)} %get-tuple-element.115.z_a, ...), custom_call_target="tpu_custom_call", output_to_operand_aliasing={{0}: (5, {}), {1}: (6, {})} | custom-call | flops 4000000 | bytes 1000000 | tf_op jit(solution)/shard_map/pallas_call | solution.py:503
  55.6 0.8 %shard_map.80 = (f32[3,256,128]{2,1,0:T(8,128)}, f32[3,256,128]{2,1,0:T(8,128)}) custom-call(s32[32,128]{1,0:T(8,128)S(1)} %get-tuple-element.63.pos, f32[4,112,128]{2,1,0:T(8,128)S(1)} %get-tuple-element.72.got_near.coefs.coefs_near, f32[4,112,128]{2,1,0:T(8,128)S(1)} %get-tuple-element.87.coefs_far, ...), custom_call_target="tpu_custom_call", output_to_operand_aliasing={{0}: (15, {}), {1}: (16, {})} | custom-call | flops 1000000 | bytes 1000000 | tf_op jit(solution)/shard_map/pallas_call | solution.py:503
  (30 shorter events, 5.1 us)
Async XLA Ops:
  1.3 10.2 %collective-permute-start = (f32[16,128]{1,0:T(8,128)S(1)}, f32[16,128]{1,0:T(8,128)S(1)}, u32[]{:S(2)}, u32[]{:S(2)}) collective-permute-start(f32[16,128]{1,0:T(8,128)S(1)} %shard_map.69), channel_id=1, source_target_pairs={{0,1},{1,2},{2,3},{3,4},{4,5},{5,6},{6,7},{7,8},{8,9},{9,10},{10,1... | collective-permute-start | bytes 24584 | tf_op jit(solution)/shard_map/ppermute | solution.py:546
  11.6 6.5 %collective-permute-start.3 = (f32[112,128]{1,0:T(8,128)S(1)}, f32[112,128]{1,0:T(8,128)S(1)}, u32[]{:S(2)}, u32[]{:S(2)}) collective-permute-start(f32[112,128]{1,0:T(8,128)S(1)} %get-tuple-element.71.refs_0_.own_near.own_b), channel_id=1, source_target_pairs={{0,48},{16,32},{32,16},{48,0},{64,112},{80,96},{96,80},{112,64},{1... | collective-permute-start | bytes 172040 | tf_op jit(solution)/shard_map/ppermute | solution.py:517
  14.3 3.9 %collective-permute-start.2 = (f32[112,128]{1,0:T(8,128)S(1)}, f32[112,128]{1,0:T(8,128)S(1)}, u32[]{:S(2)}, u32[]{:S(2)}) collective-permute-start(f32[112,128]{1,0:T(8,128)S(1)} %get-tuple-element.71.refs_0_.own_near.own_b), channel_id=1, source_target_pairs={{0,32},{16,48},{32,0},{48,16},{64,96},{80,112},{96,64},{112,80},{1... | collective-permute-start | bytes 172040 | tf_op jit(solution)/shard_map/ppermute | solution.py:517
  14.6 3.7 %collective-permute-start.1 = (f32[112,128]{1,0:T(8,128)S(1)}, f32[112,128]{1,0:T(8,128)S(1)}, u32[]{:S(2)}, u32[]{:S(2)}) collective-permute-start(f32[112,128]{1,0:T(8,128)S(1)} %get-tuple-element.71.refs_0_.own_near.own_b), channel_id=1, source_target_pairs={{0,16},{16,0},{32,48},{48,32},{64,80},{80,64},{96,112},{112,96},{1... | collective-permute-start | bytes 172040 | tf_op jit(solution)/shard_map/ppermute | solution.py:517
  14.8 7.5 %collective-permute-start.7 = (f32[128,128]{1,0:T(8,128)S(1)}, f32[128,128]{1,0:T(8,128)S(1)}, u32[]{:S(2)}, u32[]{:S(2)}) collective-permute-start(f32[128,128]{1,0:T(8,128)S(1)} %get-tuple-element.77), channel_id=1, source_target_pairs={{1,0},{2,1},{3,2},{4,3},{5,4},{6,5},{7,6},{8,7},{9,8},{10,9},{11,1... | collective-permute-start | bytes 196616 | tf_op jit(solution)/shard_map/ppermute | solution.py:560
  18.3 6.0 %collective-permute-start.6 = (f32[112,128]{1,0:T(8,128)S(1)}, f32[112,128]{1,0:T(8,128)S(1)}, u32[]{:S(2)}, u32[]{:S(2)}) collective-permute-start(f32[112,128]{1,0:T(8,128)S(1)} %get-tuple-element.73.refs_0_.group_b), channel_id=1, source_target_pairs={{0,224},{16,240},{32,192},{48,208},{64,160},{80,176},{96,128},{112... | collective-permute-start | bytes 172040 | tf_op jit(solution)/shard_map/ppermute | solution.py:517
  20.5 4.2 %collective-permute-start.5 = (f32[112,128]{1,0:T(8,128)S(1)}, f32[112,128]{1,0:T(8,128)S(1)}, u32[]{:S(2)}, u32[]{:S(2)}) collective-permute-start(f32[112,128]{1,0:T(8,128)S(1)} %get-tuple-element.73.refs_0_.group_b), channel_id=1, source_target_pairs={{0,96},{16,112},{32,64},{48,80},{64,32},{80,48},{96,0},{112,16},{1... | collective-permute-start | bytes 172040 | tf_op jit(solution)/shard_map/ppermute | solution.py:517
  21.2 3.6 %collective-permute-start.4 = (f32[112,128]{1,0:T(8,128)S(1)}, f32[112,128]{1,0:T(8,128)S(1)}, u32[]{:S(2)}, u32[]{:S(2)}) collective-permute-start(f32[112,128]{1,0:T(8,128)S(1)} %get-tuple-element.73.refs_0_.group_b), channel_id=1, source_target_pairs={{0,128},{16,144},{32,160},{48,176},{64,192},{80,208},{96,224},{112... | collective-permute-start | bytes 172040 | tf_op jit(solution)/shard_map/ppermute | solution.py:517
  25.6 5.5 %collective-permute-start.10 = (f32[112,128]{1,0:T(8,128)S(1)}, f32[112,128]{1,0:T(8,128)S(1)}, u32[]{:S(2)}, u32[]{:S(2)}) collective-permute-start(f32[112,128]{1,0:T(8,128)S(1)} %get-tuple-element.88.refs_0_.own_near), channel_id=1, source_target_pairs={{0,3},{1,2},{2,1},{3,0},{4,7},{5,6},{6,5},{7,4},{8,11},{9,10},{10,... | collective-permute-start | bytes 172040 | tf_op jit(solution)/shard_map/ppermute | solution.py:517
  25.7 5.4 %collective-permute-start.9 = (f32[112,128]{1,0:T(8,128)S(1)}, f32[112,128]{1,0:T(8,128)S(1)}, u32[]{:S(2)}, u32[]{:S(2)}) collective-permute-start(f32[112,128]{1,0:T(8,128)S(1)} %get-tuple-element.88.refs_0_.own_near), channel_id=1, source_target_pairs={{0,1},{1,0},{2,3},{3,2},{4,5},{5,4},{6,7},{7,6},{8,9},{9,8},{10,11... | collective-permute-start | bytes 172040 | tf_op jit(solution)/shard_map/ppermute | solution.py:517
  26.6 5.7 %collective-permute-start.8 = (f32[112,128]{1,0:T(8,128)S(1)}, f32[112,128]{1,0:T(8,128)S(1)}, u32[]{:S(2)}, u32[]{:S(2)}) collective-permute-start(f32[112,128]{1,0:T(8,128)S(1)} %get-tuple-element.88.refs_0_.own_near), channel_id=1, source_target_pairs={{0,2},{1,3},{2,0},{3,1},{4,6},{5,7},{6,4},{7,5},{8,10},{9,11},{10,... | collective-permute-start | bytes 172040 | tf_op jit(solution)/shard_map/ppermute | solution.py:517
  32.4 6.8 %collective-permute-start.13 = (f32[112,128]{1,0:T(8,128)S(1)}, f32[112,128]{1,0:T(8,128)S(1)}, u32[]{:S(2)}, u32[]{:S(2)}) collective-permute-start(f32[112,128]{1,0:T(8,128)S(1)} %get-tuple-element.96.refs_0_), channel_id=1, source_target_pairs={{0,10},{1,11},{2,8},{3,9},{4,14},{5,15},{6,12},{7,13},{8,2},{9,3},... | collective-permute-start | bytes 172040 | tf_op jit(solution)/shard_map/ppermute | solution.py:517
  36.9 6.3 %collective-permute-start.12 = (f32[112,128]{1,0:T(8,128)S(1)}, f32[112,128]{1,0:T(8,128)S(1)}, u32[]{:S(2)}, u32[]{:S(2)}) collective-permute-start(f32[112,128]{1,0:T(8,128)S(1)} %get-tuple-element.96.refs_0_), channel_id=1, source_target_pairs={{0,12},{1,13},{2,14},{3,15},{4,8},{5,9},{6,10},{7,11},{8,4},{9,5},... | collective-permute-start | bytes 172040 | tf_op jit(solution)/shard_map/ppermute | solution.py:517
  36.9 6.3 %collective-permute-start.11 = (f32[112,128]{1,0:T(8,128)S(1)}, f32[112,128]{1,0:T(8,128)S(1)}, u32[]{:S(2)}, u32[]{:S(2)}) collective-permute-start(f32[112,128]{1,0:T(8,128)S(1)} %get-tuple-element.96.refs_0_), channel_id=1, source_target_pairs={{0,4},{1,5},{2,6},{3,7},{4,0},{5,1},{6,2},{7,3},{8,12},{9,13},{10,... | collective-permute-start | bytes 172040 | tf_op jit(solution)/shard_map/ppermute | solution.py:517
  43.6 5.8 %collective-permute-start.16 = (f32[32,128]{1,0:T(8,128)S(1)}, f32[32,128]{1,0:T(8,128)S(1)}, u32[]{:S(2)}, u32[]{:S(2)}) collective-permute-start(f32[32,128]{1,0:T(8,128)S(1)} %get-tuple-element.103.refs_0_.own_near), channel_id=1, source_target_pairs={{0,48},{16,32},{32,16},{48,0},{64,112},{80,96},{96,80},{112,64},{1... | collective-permute-start | bytes 49160 | tf_op jit(solution)/shard_map/ppermute | solution.py:517
  46.3 3.6 %collective-permute-start.15 = (f32[32,128]{1,0:T(8,128)S(1)}, f32[32,128]{1,0:T(8,128)S(1)}, u32[]{:S(2)}, u32[]{:S(2)}) collective-permute-start(f32[32,128]{1,0:T(8,128)S(1)} %get-tuple-element.103.refs_0_.own_near), channel_id=1, source_target_pairs={{0,32},{16,48},{32,0},{48,16},{64,96},{80,112},{96,64},{112,80},{1... | collective-permute-start | bytes 49160 | tf_op jit(solution)/shard_map/ppermute | solution.py:517
  48.5 1.4 %collective-permute-start.14 = (f32[32,128]{1,0:T(8,128)S(1)}, f32[32,128]{1,0:T(8,128)S(1)}, u32[]{:S(2)}, u32[]{:S(2)}) collective-permute-start(f32[32,128]{1,0:T(8,128)S(1)} %get-tuple-element.103.refs_0_.own_near), channel_id=1, source_target_pairs={{0,16},{16,0},{32,48},{48,32},{64,80},{80,64},{96,112},{112,96},{1... | collective-permute-start | bytes 49160 | tf_op jit(solution)/shard_map/ppermute | solution.py:517
  50.0 5.5 %collective-permute-start.19 = (f32[32,128]{1,0:T(8,128)S(1)}, f32[32,128]{1,0:T(8,128)S(1)}, u32[]{:S(2)}, u32[]{:S(2)}) collective-permute-start(f32[32,128]{1,0:T(8,128)S(1)} %get-tuple-element.110.refs_0_), channel_id=1, source_target_pairs={{0,224},{16,240},{32,192},{48,208},{64,160},{80,176},{96,128},{112... | collective-permute-start | bytes 49160 | tf_op jit(solution)/shard_map/ppermute | solution.py:517
  51.8 3.8 %collective-permute-start.18 = (f32[32,128]{1,0:T(8,128)S(1)}, f32[32,128]{1,0:T(8,128)S(1)}, u32[]{:S(2)}, u32[]{:S(2)}) collective-permute-start(f32[32,128]{1,0:T(8,128)S(1)} %get-tuple-element.110.refs_0_), channel_id=1, source_target_pairs={{0,96},{16,112},{32,64},{48,80},{64,32},{80,48},{96,0},{112,16},{1... | collective-permute-start | bytes 49160 | tf_op jit(solution)/shard_map/ppermute | solution.py:517
  52.6 3.0 %collective-permute-start.17 = (f32[32,128]{1,0:T(8,128)S(1)}, f32[32,128]{1,0:T(8,128)S(1)}, u32[]{:S(2)}, u32[]{:S(2)}) collective-permute-start(f32[32,128]{1,0:T(8,128)S(1)} %get-tuple-element.110.refs_0_), channel_id=1, source_target_pairs={{0,128},{16,144},{32,160},{48,176},{64,192},{80,208},{96,224},{112... | collective-permute-start | bytes 49160 | tf_op jit(solution)/shard_map/ppermute | solution.py:517

commit v11 on v8

--- a/solution.py
+++ b/solution.py
@@ -159,10 +159,14 @@
 
 def collect(r, order, own, others, got):
     refs = [own] + [others[order.index(s)] for s in range(1, len(order) + 1)]
-    count = len(refs)
-    blocks = [[] for _ in refs]
-    for k in range(own.shape[0] // B):
-        values = [ref[plane(k)] for ref in refs]
+    return ordered(r, [loaded(ref, range(ref.shape[0] // B)) for ref in refs], got)
+
+
+def ordered(r, found, got):
+    count = len(found)
+    blocks = [[] for _ in found]
+    for k in range(len(found[0])):
+        values = [planes[k] for planes in found]
         bit = 1
         while bit < count:
             swap = lax.bitwise_and(r, bit) != 0
@@ -198,8 +202,17 @@
     return lax.shift_right_logical(here, near.bit_length() - 1), lax.bitwise_and(here, near - 1)
 
 
+def cut_kernel(elec, magn, hx_last, ez_first, sems):
+    loads = [(magn.at[0, :, B - 1], hx_last), (elec.at[2, :, 0], ez_first)]
+    loads = [pltpu.make_async_copy(a, b, sems.at[k]) for k, (a, b) in enumerate(loads)]
+    for load in loads:
+        load.start()
+    for load in loads:
+        load.wait()
+
+
 def tables_kernel(
-    me, eps_in, sig_in, material, elec_in, magn_in, w, c, p, u, v, flux, part, elec, magn, ez_first, pos, ids, eps, sig, sems
+    me, eps_in, sig_in, material, elec_in, magn_in, w, c, p, u, v, flux, part, elec, magn, pos, early, ids, eps, sig, sems
 ):
     loads = [(eps_in, eps), (sig_in, sig), (material, ids)]
     for field, to, k in ((elec_in, elec, 0), (magn_in, magn, 1), (elec_in, elec, 2), (magn_in, magn, 0)):
@@ -235,13 +248,14 @@
         here = magn[0, plane(i)]
         before = jnp.where(row == 0, 0.0, pltpu.roll(here, 1, 0))
         part[plane(i)] = c[plane(i)] * elec[2, plane(i)] + (q - (here - before) * (1.0 / h))
-    for k in range(ez_first.shape[0] // B):
-        ez_first[plane(k)] = elec.at[2][strided(0)]
     for load in loads[7:]:
         load.wait()
-
-
-def first_x_kernel(pos, part, hx_prev, flux, p, u, v, elec, magn, g, msg):
+    sent = [u[plane(0)], v[plane(0)], v[plane(B - 1)], elec[1, plane(0)], magn[2, plane(B - 1)]]
+    for k in range(early.shape[0] // B):
+        early[plane(k)] = sent[min(k, 4)]
+
+
+def first_x_kernel(pos, part, hx_prev, flux, p, early, g, own, ends):
     row = lax.broadcasted_iota(jnp.int32, hx_prev.shape, 0)
     scale = jnp.where(pos[plane(1)] == 0, 0.0, jnp.where(row == 0, 1.0 / h, 0.0))
 
@@ -249,13 +263,10 @@
         return part[plane(i)] + hx_prev[pl.ds(i, 1)] * scale
 
     first, last = eliminate(source, p, g)
-    msg[plane(0)] = first
-    msg[plane(1)] = last - flux[plane(B - 1)]
-    msg[plane(2)] = u[plane(0)]
-    msg[plane(3)] = v[plane(0)]
-    msg[plane(4)] = v[plane(B - 1)]
-    msg[plane(5)] = elec[1, plane(0)]
-    msg[plane(6)] = magn[2, plane(B - 1)]
+    ends[plane(0)] = first
+    ends[plane(1)] = last - flux[plane(B - 1)]
+    own[pl.ds(0, 2 * B)] = ends[...]
+    own[pl.ds(2 * B, 5 * B)] = early[pl.ds(0, 5 * B)]
 
 
 def merged(blocks):
@@ -264,16 +275,24 @@
     return blocks[0]
 
 
-def merge_kernel(axis, near, order, sources, halos, pos, *refs):
+def merge_kernel(axis, near, order, sources, pos, *refs):
     got, msg = refs[-2:]
     blocks = collect(place(pos, axis, near)[1], order, refs[0], refs[1:near], got)
     at = 2 * sources
     coefs, rows = merged([(b[at : at + 3], rows_of(b, sources)) for b in blocks])
     for k, value in enumerate([v for pair in rows for v in pair] + list(coefs)):
         msg[plane(k)] = value
-    if halos:
-        msg[plane(5)] = blocks[0][5]
-        msg[plane(6)] = blocks[-1][6]
+
+
+def merge_first_kernel(near, pos, own, *refs):
+    got, msg = refs[-2:]
+    early, nearest, ends = refs[: near - 2], refs[near - 2], refs[near - 1 : -2]
+    found = [loaded(own, range(7)), loaded(nearest, range(7))]
+    found += [loaded(a, range(2)) + loaded(b, range(5)) for a, b in zip(ends, early)]
+    blocks = ordered(place(pos, 0, near)[1], found, got)
+    coefs, rows = merged([(b[2:5], rows_of(b, 1)) for b in blocks])
+    for k, value in enumerate([*rows[0], *coefs, blocks[0][5], blocks[-1][6]]):
+        msg[plane(k)] = value
 
 
 def merge_rows_kernel(axis, near, order, pos, coefs, *refs):
@@ -528,29 +547,40 @@
     magn = in_hbm(magnetic.reshape(3, *cells))
     ids = in_hbm(material.reshape(cells))
     dma = pltpu.SemaphoreType.DMA
-    orders = [(1, 2, 3), (2, 1, 3), (2, 3, 1), (1, 3, 2)]
+    orders = [(1, 2, 3), (2, 1, 3), (2, 1, 3), (1, 3, 2)]
     counts = (near_x, far_x, near_y, far_y)
     px_near, px_far, py_near, py_far = [
         tuple(s for s in order if s < count) for order, count in zip(orders, counts)
     ]
 
-    hx_prev = lax.ppermute(magnetic[0, :, B - 1], "py", [(i, (i + 1) % ny) for i in range(ny)])
-    w, c, p_x, u_x, v_x, flux_b, part_b, ef, mf, ez_first, pos = call(
+    hx_last, ez_first = call(
+        cut_kernel,
+        [in_hbm(electric), in_hbm(magnetic)],
+        [(B, nz)] * 2,
+        specs=[HBM] * 2,
+        scratch=[dma((2,))],
+        flops=1000,
+    )
+    hx_prev = lax.ppermute(hx_last, "py", [(i, (i + 1) % ny) for i in range(ny)])
+    ez_next = lax.ppermute(ez_first, "py", [((i + 1) % ny, i) for i in range(ny)])
+    w, c, p_x, u_x, v_x, flux_b, part_b, ef, mf, pos, early = call(
         tables_kernel,
         [me, in_hbm(permittivity), in_hbm(conductivity), ids, elec, magn],
-        [cells] * 7 + [(3, *cells)] * 2 + [(8 * B, nz), jax.ShapeDtypeStruct((2 * B, nz), jnp.int32)],
+        [cells] * 7 + [(3, *cells)] * 2 + [jax.ShapeDtypeStruct((2 * B, nz), jnp.int32), (7 * B, nz)],
         specs=[SMEM] + [HBM] * 5,
         scratch=[pltpu.VMEM(cells, jnp.int32)] + [pltpu.SMEM(permittivity.shape, F32)] * 2 + [dma((9,))],
     )
-    g_b, own_b = call(
+    beyond = tuple(range(2, near_x))
+    sent = shared(early, "px", nx, beyond)
+    hx_prev, ez_next = lax.optimization_barrier((hx_prev, ez_next))
+    g_b, own_b, ends = call(
         first_x_kernel,
-        [pos, part_b, hx_prev, flux_b, p_x, u_x, v_x, ef, mf],
-        [cells, (7 * B, nz)],
-    )
-    ins = shared(own_b, "px", nx, px_near)
-    ez_next = lax.ppermute(ez_first, "py", [((i + 1) % ny, i) for i in range(ny)])
+        [pos, part_b, hx_prev, flux_b, p_x, early],
+        [cells, (7 * B, nz), (2 * B, nz)],
+    )
+    ins = [own_b] + sent[1:] + shared(own_b, "px", nx, (1,))[1:] + shared(ends, "px", nx, beyond)[1:]
     near_b, group_b = call(
-        functools.partial(merge_kernel, 0, near_x, px_near, 1, True),
+        functools.partial(merge_first_kernel, near_x),
         [pos] + ins,
         [(near_x, 7 * B, nz), (7 * B, nz)],
     )
@@ -571,7 +601,7 @@
     )
     ins = shared(own_ac, "py", ny, py_near)
     near_ac, msg = call(
-        functools.partial(merge_kernel, 1, near_y, py_near, 2, False), [pos] + ins, [(near_y, 7 * B, nz), (7 * B, nz)]
+        functools.partial(merge_kernel, 1, near_y, py_near, 2), [pos] + ins, [(near_y, 7 * B, nz), (7 * B, nz)]
     )
     msg, w = lax.optimization_barrier((msg, w))
     ins = shared(msg, "py", ny, py_far, near_y, (2,))

time: 57.7 us -> 61.2 us (1.061)
  the two profiles are of different devices: /device:TPU:1 before, /device:TPU:40 now
where the time goes in v11:
time: 61.2 us; the launch traced here: 61 us
  starting transfers between devices  33.6 us (55%)
  waiting for transfers between devices  15.9 us (26%)
  Pallas kernels  10.5 us (17%)
  between operations  0.91 us (1%)
    ppermute x20, starting transfers between devices, shared(): lax.ppermute(value, axis, [(i, i ^ mask) for i in range(n)])  29.1 us
    ppermute x20, waiting for transfers between devices, shared(): lax.ppermute(value, axis, [(i, i ^ mask) for i in range(n)])  15.9 us
    pallas_call x13, Pallas kernels, call(): pl.pallas_call(kernel, out_shape=shapes, in_specs=specs or [VMEM] * len(i...  10.5 us
    ppermute x1, starting transfers between devices, local(): lax.ppermute(hx_last, 'py', [(i, (i + 1) % ny) for i in range(ny)])  2.37 us
    ppermute x1, starting transfers between devices, local(): lax.ppermute(ez_first, 'py', [((i + 1) % ny, i) for i in range(ny)])  2.13 us
  transfers between devices with their start and end apart: 22, of which 12 were waited for; matrix products, arithmetic and copies ran while one was open for 0% of the time, Pallas kernels for 13%

profile of v11, /device:TPU:40, one launch (start us, length us, event | category | flops | bytes accessed | tf_op | source)
XLA Modules:
  0.0 61.0 jit_solution(4287760204832420976)
XLA Ops:
  1.4 2.4 %collective-permute-start = (f32[16,128]{1,0:T(8,128)S(1)}, f32[16,128]{1,0:T(8,128)S(1)}, u32[]{:S(2)}, u32[]{:S(2)}) collective-permute-start(f32[16,128]{1,0:T(8,128)S(1)} %get-tuple-element.70), channel_id=1, source_target_pairs={{0,1},{1,2},{2,3},{3,4},{4,5},{5,6},{6,7},{7,8},{8,9},{9,10},{10,1... | collective-permute-start | bytes 24584 | tf_op jit(solution)/shard_map/ppermute | solution.py:564
  3.7 2.1 %collective-permute-start.1 = (f32[16,128]{1,0:T(8,128)S(1)}, f32[16,128]{1,0:T(8,128)S(1)}, u32[]{:S(2)}, u32[]{:S(2)}) collective-permute-start(f32[16,128]{1,0:T(8,128)S(1)} %get-tuple-element.71), channel_id=1, source_target_pairs={{1,0},{2,1},{3,2},{4,3},{5,4},{6,5},{7,6},{8,7},{9,8},{10,9},{11,1... | collective-permute-start | bytes 24584 | tf_op jit(solution)/shard_map/ppermute | solution.py:565
  6.0 1.9 %shard_map.68 = (f32[256,128]{1,0:T(8,128)S(1)}, f32[256,128]{1,0:T(8,128)S(1)}, f32[256,128]{1,0:T(8,128)S(1)}, f32[256,128]{1,0:T(8,128)S(1)}, f32[256,128]{1,...) custom-call(s32[2]{0:T(128)S(1)} %pad_add_fusion.me, ...), custom_call_target="tpu_custom_call" | custom-call | flops 1000000 | bytes 1000000 | tf_op jit(solution)/shard_map/pallas_call | solution.py:516
  8.3 1.2 %collective-permute-start.2 = (f32[112,128]{1,0:T(8,128)S(1)}, f32[112,128]{1,0:T(8,128)S(1)}, u32[]{:S(2)}, u32[]{:S(2)}) collective-permute-start(f32[112,128]{1,0:T(8,128)S(1)} %get-tuple-element.75.early), channel_id=1, source_target_pairs={{0,32},{16,48},{32,0},{48,16},{64,96},{80,112},{96,64},{112,80},{1... | collective-permute-start | bytes 172040 | tf_op jit(solution)/shard_map/ppermute | solution.py:530
  10.0 1.2 %collective-permute-start.6 = (f32[32,128]{1,0:T(8,128)S(1)}, f32[32,128]{1,0:T(8,128)S(1)}, u32[]{:S(2)}, u32[]{:S(2)}) collective-permute-start(f32[32,128]{1,0:T(8,128)S(1)} %get-tuple-element.77), channel_id=1, source_target_pairs={{0,48},{16,32},{32,16},{48,0},{64,112},{80,96},{96,80},{112,64},{1... | collective-permute-start | bytes 49160 | tf_op jit(solution)/shard_map/ppermute | solution.py:530
  11.9 1.9 %collective-permute-done.6.refs_4_ = f32[32,128]{1,0:T(8,128)S(1)} collective-permute-done((f32[32,128]{1,0:T(8,128)S(1)}, f32[32,128]{1,0:T(8,128)S(1)}, u32[]{:S(2)}, u32[]{:S(2)}) %collective-permute-start.6) | collective-permute-done | bytes 16416 | tf_op jit(solution)/shard_map/ppermute | solution.py:530
  13.7 1.2 %collective-permute-done.5.refs_3_ = f32[32,128]{1,0:T(8,128)S(1)} collective-permute-done((f32[32,128]{1,0:T(8,128)S(1)}, f32[32,128]{1,0:T(8,128)S(1)}, u32[]{:S(2)}, u32[]{:S(2)}) %collective-permute-start.5) | collective-permute-done | bytes 16416 | tf_op jit(solution)/shard_map/ppermute | solution.py:530
  15.0 2.5 %collective-permute-start.9 = (f32[112,128]{1,0:T(8,128)S(1)}, f32[112,128]{1,0:T(8,128)S(1)}, u32[]{:S(2)}, u32[]{:S(2)}) collective-permute-start(f32[112,128]{1,0:T(8,128)S(1)} %get-tuple-element.79.refs_0_.group_b), channel_id=1, source_target_pairs={{0,224},{16,240},{32,192},{48,208},{64,160},{80,176},{96,128},{112... | collective-permute-start | bytes 172040 | tf_op jit(solution)/shard_map/ppermute | solution.py:530
  17.5 1.1 %collective-permute-start.8 = (f32[112,128]{1,0:T(8,128)S(1)}, f32[112,128]{1,0:T(8,128)S(1)}, u32[]{:S(2)}, u32[]{:S(2)}) collective-permute-start(f32[112,128]{1,0:T(8,128)S(1)} %get-tuple-element.79.refs_0_.group_b), channel_id=1, source_target_pairs={{0,96},{16,112},{32,64},{48,80},{64,32},{80,48},{96,0},{112,16},{1... | collective-permute-start | bytes 172040 | tf_op jit(solution)/shard_map/ppermute | solution.py:530
  18.6 1.2 %collective-permute-start.7 = (f32[112,128]{1,0:T(8,128)S(1)}, f32[112,128]{1,0:T(8,128)S(1)}, u32[]{:S(2)}, u32[]{:S(2)}) collective-permute-start(f32[112,128]{1,0:T(8,128)S(1)} %get-tuple-element.79.refs_0_.group_b), channel_id=1, source_target_pairs={{0,128},{16,144},{32,160},{48,176},{64,192},{80,208},{96,224},{112... | collective-permute-start | bytes 172040 | tf_op jit(solution)/shard_map/ppermute | solution.py:530
  19.8 2.0 %shard_map.72 = (f32[256,128]{1,0:T(8,128)S(1)}, f32[256,128]{1,0:T(8,128)S(1)}, f32[256,128]{1,0:T(8,128)S(1)}, f32[16,128]{1,0:T(8,128)S(1)}, f32[16,128]{1,0:...) custom-call(s32[32,128]{1,0:T(8,128)S(1)} %get-tuple-element.68.pos,, ...), custom_call_target="tpu_custom_call" | custom-call | flops 8000000 | bytes 1000000 | tf_op jit(solution)/shard_map/pallas_call | solution.py:516
  23.6 2.0 %collective-permute-start.12 = (f32[112,128]{1,0:T(8,128)S(1)}, f32[112,128]{1,0:T(8,128)S(1)}, u32[]{:S(2)}, u32[]{:S(2)}) collective-permute-start(f32[112,128]{1,0:T(8,128)S(1)} %get-tuple-element.98.refs_0_.own_near), channel_id=1, source_target_pairs={{0,3},{1,2},{2,1},{3,0},{4,7},{5,6},{6,5},{7,4},{8,11},{9,10},{10,... | collective-permute-start | bytes 172040 | tf_op jit(solution)/shard_map/ppermute | solution.py:530
  25.7 4.9 %collective-permute-start.11 = (f32[112,128]{1,0:T(8,128)S(1)}, f32[112,128]{1,0:T(8,128)S(1)}, u32[]{:S(2)}, u32[]{:S(2)}) collective-permute-start(f32[112,128]{1,0:T(8,128)S(1)} %get-tuple-element.98.refs_0_.own_near), channel_id=1, source_target_pairs={{0,1},{1,0},{2,3},{3,2},{4,5},{5,4},{6,7},{7,6},{8,9},{9,8},{10,11... | collective-permute-start | bytes 172040 | tf_op jit(solution)/shard_map/ppermute | solution.py:530
  30.6 2.1 %collective-permute-done.11.refs_2_ = f32[112,128]{1,0:T(8,128)S(1)} collective-permute-done((f32[112,128]{1,0:T(8,128)S(1)}, f32[112,128]{1,0:T(8,128)S(1)}, u32[]{:S(2)}, u32[]{:S(2)}) %collective-permute-start.11) | collective-permute-done | bytes 57376 | tf_op jit(solution)/shard_map/ppermute | solution.py:530
  32.7 2.0 %collective-permute-done.10.refs_1_ = f32[112,128]{1,0:T(8,128)S(1)} collective-permute-done((f32[112,128]{1,0:T(8,128)S(1)}, f32[112,128]{1,0:T(8,128)S(1)}, u32[]{:S(2)}, u32[]{:S(2)}) %collective-permute-start.10) | collective-permute-done | bytes 57376 | tf_op jit(solution)/shard_map/ppermute | solution.py:530
  34.8 3.1 %collective-permute-start.15 = (f32[112,128]{1,0:T(8,128)S(1)}, f32[112,128]{1,0:T(8,128)S(1)}, u32[]{:S(2)}, u32[]{:S(2)}) collective-permute-start(f32[112,128]{1,0:T(8,128)S(1)} %get-tuple-element.106.refs_0_), channel_id=1, source_target_pairs={{0,10},{1,11},{2,8},{3,9},{4,14},{5,15},{6,12},{7,13},{8,2},{9,3},... | collective-permute-start | bytes 172040 | tf_op jit(solution)/shard_map/ppermute | solution.py:530
  37.9 3.3 %collective-permute-start.14 = (f32[112,128]{1,0:T(8,128)S(1)}, f32[112,128]{1,0:T(8,128)S(1)}, u32[]{:S(2)}, u32[]{:S(2)}) collective-permute-start(f32[112,128]{1,0:T(8,128)S(1)} %get-tuple-element.106.refs_0_), channel_id=1, source_target_pairs={{0,12},{1,13},{2,14},{3,15},{4,8},{5,9},{6,10},{7,11},{8,4},{9,5},... | collective-permute-start | bytes 172040 | tf_op jit(solution)/shard_map/ppermute | solution.py:530
  41.2 1.3 %shard_map.75 = (f32[7,256,128]{2,1,0:T(8,128)S(1)}, f32[7,256,128]{2,1,0:T(8,128)S(1)}, f32[256,128]{1,0:T(8,128)S(1)}) custom-call(f32[256,128]{1,0:T(8,128)S(1)} %get-tuple-element.102.w.refs_8_.w_in), custom_call_target="tpu_custom_call" | custom-call | flops 8000000 | bytes 1000000 | tf_op jit(solution)/shard_map/pallas_call | solution.py:516
  42.8 1.5 %collective-permute-done.14.refs_2_ = f32[112,128]{1,0:T(8,128)S(1)} collective-permute-done((f32[112,128]{1,0:T(8,128)S(1)}, f32[112,128]{1,0:T(8,128)S(1)}, u32[]{:S(2)}, u32[]{:S(2)}) %collective-permute-start.14) | collective-permute-done | bytes 57376 | tf_op jit(solution)/shard_map/ppermute | solution.py:530
  44.3 2.0 %collective-permute-done.13.refs_1_ = f32[112,128]{1,0:T(8,128)S(1)} collective-permute-done((f32[112,128]{1,0:T(8,128)S(1)}, f32[112,128]{1,0:T(8,128)S(1)}, u32[]{:S(2)}, u32[]{:S(2)}) %collective-permute-start.13) | collective-permute-done | bytes 57376 | tf_op jit(solution)/shard_map/ppermute | solution.py:530
  46.9 1.7 %collective-permute-start.16 = (f32[32,128]{1,0:T(8,128)S(1)}, f32[32,128]{1,0:T(8,128)S(1)}, u32[]{:S(2)}, u32[]{:S(2)}) collective-permute-start(f32[32,128]{1,0:T(8,128)S(1)} %get-tuple-element.113.refs_0_.own_near), channel_id=1, source_target_pairs={{0,16},{16,0},{32,48},{48,32},{64,80},{80,64},{96,112},{112,96},{1... | collective-permute-start | bytes 49160 | tf_op jit(solution)/shard_map/ppermute | solution.py:530
  50.6 4.4 %collective-permute-start.21 = (f32[32,128]{1,0:T(8,128)S(1)}, f32[32,128]{1,0:T(8,128)S(1)}, u32[]{:S(2)}, u32[]{:S(2)}) collective-permute-start(f32[32,128]{1,0:T(8,128)S(1)} %get-tuple-element.120.refs_0_), channel_id=1, source_target_pairs={{0,224},{16,240},{32,192},{48,208},{64,160},{80,176},{96,128},{112... | collective-permute-start | bytes 49160 | tf_op jit(solution)/shard_map/ppermute | solution.py:530
  55.8 1.6 %shard_map.79 = (f32[3,256,128]{2,1,0:T(8,128)}, f32[3,256,128]{2,1,0:T(8,128)}) custom-call(f32[256,128]{1,0:T(8,128)S(1)} %get-tuple-element.123.part, f32[256,128]{1,0:T(8,128)S(1)} %get-tuple-element.124.rise_y, f32[7,256,128]{2,1,0:T(8,128)S(1)} %get-tuple-element.125.z_a, ...), custom_call_target="tpu_custom_call", output_to_operand_aliasing={{0}: (5, {}), {1}: (6, {})} | custom-call | flops 4000000 | bytes 1000000 | tf_op jit(solution)/shard_map/pallas_call | solution.py:516
  57.4 2.6 %collective-permute-done.20.refs_2_ = f32[32,128]{1,0:T(8,128)S(1)} collective-permute-done((f32[32,128]{1,0:T(8,128)S(1)}, f32[32,128]{1,0:T(8,128)S(1)}, u32[]{:S(2)}, u32[]{:S(2)}) %collective-permute-start.20) | collective-permute-done | bytes 16416 | tf_op jit(solution)/shard_map/ppermute | solution.py:530
  (34 shorter events, 8.7 us)
Async XLA Ops:
  1.4 8.2 %collective-permute-start = (f32[16,128]{1,0:T(8,128)S(1)}, f32[16,128]{1,0:T(8,128)S(1)}, u32[]{:S(2)}, u32[]{:S(2)}) collective-permute-start(f32[16,128]{1,0:T(8,128)S(1)} %get-tuple-element.70), channel_id=1, source_target_pairs={{0,1},{1,2},{2,3},{3,4},{4,5},{5,6},{6,7},{7,8},{8,9},{9,10},{10,1... | collective-permute-start | bytes 24584 | tf_op jit(solution)/shard_map/ppermute | solution.py:564
  3.7 5.8 %collective-permute-start.1 = (f32[16,128]{1,0:T(8,128)S(1)}, f32[16,128]{1,0:T(8,128)S(1)}, u32[]{:S(2)}, u32[]{:S(2)}) collective-permute-start(f32[16,128]{1,0:T(8,128)S(1)} %get-tuple-element.71), channel_id=1, source_target_pairs={{1,0},{2,1},{3,2},{4,3},{5,4},{6,5},{7,6},{8,7},{9,8},{10,9},{11,1... | collective-permute-start | bytes 24584 | tf_op jit(solution)/shard_map/ppermute | solution.py:565
  7.9 7.1 %collective-permute-start.3 = (f32[112,128]{1,0:T(8,128)S(1)}, f32[112,128]{1,0:T(8,128)S(1)}, u32[]{:S(2)}, u32[]{:S(2)}) collective-permute-start(f32[112,128]{1,0:T(8,128)S(1)} %get-tuple-element.75.early), channel_id=1, source_target_pairs={{0,48},{16,32},{32,16},{48,0},{64,112},{80,96},{96,80},{112,64},{1... | collective-permute-start | bytes 172040 | tf_op jit(solution)/shard_map/ppermute | solution.py:530
  8.3 6.6 %collective-permute-start.2 = (f32[112,128]{1,0:T(8,128)S(1)}, f32[112,128]{1,0:T(8,128)S(1)}, u32[]{:S(2)}, u32[]{:S(2)}) collective-permute-start(f32[112,128]{1,0:T(8,128)S(1)} %get-tuple-element.75.early), channel_id=1, source_target_pairs={{0,32},{16,48},{32,0},{48,16},{64,96},{80,112},{96,64},{112,80},{1... | collective-permute-start | bytes 172040 | tf_op jit(solution)/shard_map/ppermute | solution.py:530
  9.6 5.3 %collective-permute-start.4 = (f32[112,128]{1,0:T(8,128)S(1)}, f32[112,128]{1,0:T(8,128)S(1)}, u32[]{:S(2)}, u32[]{:S(2)}) collective-permute-start(f32[112,128]{1,0:T(8,128)S(1)} %get-tuple-element.76.own.own_near.own_b), channel_id=1, source_target_pairs={{0,16},{16,0},{32,48},{48,32},{64,80},{80,64},{96,112},{112,96},{1... | collective-permute-start | bytes 172040 | tf_op jit(solution)/shard_map/ppermute | solution.py:530
  10.0 3.7 %collective-permute-start.6 = (f32[32,128]{1,0:T(8,128)S(1)}, f32[32,128]{1,0:T(8,128)S(1)}, u32[]{:S(2)}, u32[]{:S(2)}) collective-permute-start(f32[32,128]{1,0:T(8,128)S(1)} %get-tuple-element.77), channel_id=1, source_target_pairs={{0,48},{16,32},{32,16},{48,0},{64,112},{80,96},{96,80},{112,64},{1... | collective-permute-start | bytes 49160 | tf_op jit(solution)/shard_map/ppermute | solution.py:530
  11.2 3.7 %collective-permute-start.5 = (f32[32,128]{1,0:T(8,128)S(1)}, f32[32,128]{1,0:T(8,128)S(1)}, u32[]{:S(2)}, u32[]{:S(2)}) collective-permute-start(f32[32,128]{1,0:T(8,128)S(1)} %get-tuple-element.77), channel_id=1, source_target_pairs={{0,32},{16,48},{32,0},{48,16},{64,96},{80,112},{96,64},{112,80},{1... | collective-permute-start | bytes 49160 | tf_op jit(solution)/shard_map/ppermute | solution.py:530
  15.0 6.9 %collective-permute-start.9 = (f32[112,128]{1,0:T(8,128)S(1)}, f32[112,128]{1,0:T(8,128)S(1)}, u32[]{:S(2)}, u32[]{:S(2)}) collective-permute-start(f32[112,128]{1,0:T(8,128)S(1)} %get-tuple-element.79.refs_0_.group_b), channel_id=1, source_target_pairs={{0,224},{16,240},{32,192},{48,208},{64,160},{80,176},{96,128},{112... | collective-permute-start | bytes 172040 | tf_op jit(solution)/shard_map/ppermute | solution.py:530
  17.5 5.4 %collective-permute-start.8 = (f32[112,128]{1,0:T(8,128)S(1)}, f32[112,128]{1,0:T(8,128)S(1)}, u32[]{:S(2)}, u32[]{:S(2)}) collective-permute-start(f32[112,128]{1,0:T(8,128)S(1)} %get-tuple-element.79.refs_0_.group_b), channel_id=1, source_target_pairs={{0,96},{16,112},{32,64},{48,80},{64,32},{80,48},{96,0},{112,16},{1... | collective-permute-start | bytes 172040 | tf_op jit(solution)/shard_map/ppermute | solution.py:530
  18.6 4.2 %collective-permute-start.7 = (f32[112,128]{1,0:T(8,128)S(1)}, f32[112,128]{1,0:T(8,128)S(1)}, u32[]{:S(2)}, u32[]{:S(2)}) collective-permute-start(f32[112,128]{1,0:T(8,128)S(1)} %get-tuple-element.79.refs_0_.group_b), channel_id=1, source_target_pairs={{0,128},{16,144},{32,160},{48,176},{64,192},{80,208},{96,224},{112... | collective-permute-start | bytes 172040 | tf_op jit(solution)/shard_map/ppermute | solution.py:530
  23.6 6.9 %collective-permute-start.12 = (f32[112,128]{1,0:T(8,128)S(1)}, f32[112,128]{1,0:T(8,128)S(1)}, u32[]{:S(2)}, u32[]{:S(2)}) collective-permute-start(f32[112,128]{1,0:T(8,128)S(1)} %get-tuple-element.98.refs_0_.own_near), channel_id=1, source_target_pairs={{0,3},{1,2},{2,1},{3,0},{4,7},{5,6},{6,5},{7,4},{8,11},{9,10},{10,... | collective-permute-start | bytes 172040 | tf_op jit(solution)/shard_map/ppermute | solution.py:530
  25.7 7.0 %collective-permute-start.11 = (f32[112,128]{1,0:T(8,128)S(1)}, f32[112,128]{1,0:T(8,128)S(1)}, u32[]{:S(2)}, u32[]{:S(2)}) collective-permute-start(f32[112,128]{1,0:T(8,128)S(1)} %get-tuple-element.98.refs_0_.own_near), channel_id=1, source_target_pairs={{0,1},{1,0},{2,3},{3,2},{4,5},{5,4},{6,7},{7,6},{8,9},{9,8},{10,11... | collective-permute-start | bytes 172040 | tf_op jit(solution)/shard_map/ppermute | solution.py:530
  30.6 4.2 %collective-permute-start.10 = (f32[112,128]{1,0:T(8,128)S(1)}, f32[112,128]{1,0:T(8,128)S(1)}, u32[]{:S(2)}, u32[]{:S(2)}) collective-permute-start(f32[112,128]{1,0:T(8,128)S(1)} %get-tuple-element.98.refs_0_.own_near), channel_id=1, source_target_pairs={{0,2},{1,3},{2,0},{3,1},{4,6},{5,7},{6,4},{7,5},{8,10},{9,11},{10,... | collective-permute-start | bytes 172040 | tf_op jit(solution)/shard_map/ppermute | solution.py:530
  34.8 8.0 %collective-permute-start.15 = (f32[112,128]{1,0:T(8,128)S(1)}, f32[112,128]{1,0:T(8,128)S(1)}, u32[]{:S(2)}, u32[]{:S(2)}) collective-permute-start(f32[112,128]{1,0:T(8,128)S(1)} %get-tuple-element.106.refs_0_), channel_id=1, source_target_pairs={{0,10},{1,11},{2,8},{3,9},{4,14},{5,15},{6,12},{7,13},{8,2},{9,3},... | collective-permute-start | bytes 172040 | tf_op jit(solution)/shard_map/ppermute | solution.py:530
  37.9 6.4 %collective-permute-start.14 = (f32[112,128]{1,0:T(8,128)S(1)}, f32[112,128]{1,0:T(8,128)S(1)}, u32[]{:S(2)}, u32[]{:S(2)}) collective-permute-start(f32[112,128]{1,0:T(8,128)S(1)} %get-tuple-element.106.refs_0_), channel_id=1, source_target_pairs={{0,12},{1,13},{2,14},{3,15},{4,8},{5,9},{6,10},{7,11},{8,4},{9,5},... | collective-permute-start | bytes 172040 | tf_op jit(solution)/shard_map/ppermute | solution.py:530
  41.2 5.1 %collective-permute-start.13 = (f32[112,128]{1,0:T(8,128)S(1)}, f32[112,128]{1,0:T(8,128)S(1)}, u32[]{:S(2)}, u32[]{:S(2)}) collective-permute-start(f32[112,128]{1,0:T(8,128)S(1)} %get-tuple-element.106.refs_0_), channel_id=1, source_target_pairs={{0,4},{1,5},{2,6},{3,7},{4,0},{5,1},{6,2},{7,3},{8,12},{9,13},{10,... | collective-permute-start | bytes 172040 | tf_op jit(solution)/shard_map/ppermute | solution.py:530
  46.7 3.2 %collective-permute-start.18 = (f32[32,128]{1,0:T(8,128)S(1)}, f32[32,128]{1,0:T(8,128)S(1)}, u32[]{:S(2)}, u32[]{:S(2)}) collective-permute-start(f32[32,128]{1,0:T(8,128)S(1)} %get-tuple-element.113.refs_0_.own_near), channel_id=1, source_target_pairs={{0,48},{16,32},{32,16},{48,0},{64,112},{80,96},{96,80},{112,64},{1... | collective-permute-start | bytes 49160 | tf_op jit(solution)/shard_map/ppermute | solution.py:530
  46.8 3.8 %collective-permute-start.17 = (f32[32,128]{1,0:T(8,128)S(1)}, f32[32,128]{1,0:T(8,128)S(1)}, u32[]{:S(2)}, u32[]{:S(2)}) collective-permute-start(f32[32,128]{1,0:T(8,128)S(1)} %get-tuple-element.113.refs_0_.own_near), channel_id=1, source_target_pairs={{0,32},{16,48},{32,0},{48,16},{64,96},{80,112},{96,64},{112,80},{1... | collective-permute-start | bytes 49160 | tf_op jit(solution)/shard_map/ppermute | solution.py:530
  46.9 3.7 %collective-permute-start.16 = (f32[32,128]{1,0:T(8,128)S(1)}, f32[32,128]{1,0:T(8,128)S(1)}, u32[]{:S(2)}, u32[]{:S(2)}) collective-permute-start(f32[32,128]{1,0:T(8,128)S(1)} %get-tuple-element.113.refs_0_.own_near), channel_id=1, source_target_pairs={{0,16},{16,0},{32,48},{48,32},{64,80},{80,64},{96,112},{112,96},{1... | collective-permute-start | bytes 49160 | tf_op jit(solution)/shard_map/ppermute | solution.py:530
  50.6 6.7 %collective-permute-start.21 = (f32[32,128]{1,0:T(8,128)S(1)}, f32[32,128]{1,0:T(8,128)S(1)}, u32[]{:S(2)}, u32[]{:S(2)}) collective-permute-start(f32[32,128]{1,0:T(8,128)S(1)} %get-tuple-element.120.refs_0_), channel_id=1, source_target_pairs={{0,224},{16,240},{32,192},{48,208},{64,160},{80,176},{96,128},{112... | collective-permute-start | bytes 49160 | tf_op jit(solution)/shard_map/ppermute | solution.py:530
  55.1 4.9 %collective-permute-start.20 = (f32[32,128]{1,0:T(8,128)S(1)}, f32[32,128]{1,0:T(8,128)S(1)}, u32[]{:S(2)}, u32[]{:S(2)}) collective-permute-start(f32[32,128]{1,0:T(8,128)S(1)} %get-tuple-element.120.refs_0_), channel_id=1, source_target_pairs={{0,96},{16,112},{32,64},{48,80},{64,32},{80,48},{96,0},{112,16},{1... | collective-permute-start | bytes 49160 | tf_op jit(solution)/shard_map/ppermute | solution.py:530
  55.8 4.3 %collective-permute-start.19 = (f32[32,128]{1,0:T(8,128)S(1)}, f32[32,128]{1,0:T(8,128)S(1)}, u32[]{:S(2)}, u32[]{:S(2)}) collective-permute-start(f32[32,128]{1,0:T(8,128)S(1)} %get-tuple-element.120.refs_0_), channel_id=1, source_target_pairs={{0,128},{16,144},{32,160},{48,176},{64,192},{80,208},{96,224},{112... | collective-permute-start | bytes 49160 | tf_op jit(solution)/shard_map/ppermute | solution.py:530

commit v12 on v10

--- a/solution.py
+++ b/solution.py
@@ -159,10 +159,14 @@
 
 def collect(r, order, own, others, got):
     refs = [own] + [others[order.index(s)] for s in range(1, len(order) + 1)]
-    count = len(refs)
-    blocks = [[] for _ in refs]
-    for k in range(own.shape[0] // B):
-        values = [ref[plane(k)] for ref in refs]
+    return ordered(r, [loaded(ref, range(got.shape[1] // B)) for ref in refs], got)
+
+
+def ordered(r, found, got):
+    count = len(found)
+    blocks = [[] for _ in found]
+    for k in range(got.shape[1] // B):
+        values = [planes[k] for planes in found]
         bit = 1
         while bit < count:
             swap = lax.bitwise_and(r, bit) != 0
@@ -247,7 +251,7 @@
         load.wait()
 
 
-def first_x_kernel(pos, part, hx_prev, flux, p, u, v, elec, magn, g, msg):
+def first_x_kernel(pos, part, hx_prev, flux, p, u, v, elec, magn, g, msg, inner, outer):
     row = lax.broadcasted_iota(jnp.int32, hx_prev.shape, 0)
     scale = jnp.where(pos[plane(1)] == 0, 0.0, jnp.where(row == 0, 1.0 / h, 0.0))
 
@@ -262,6 +266,10 @@
     msg[plane(4)] = v[plane(B - 1)]
     msg[plane(5)] = elec[1, plane(0)]
     msg[plane(6)] = magn[2, plane(B - 1)]
+    even = lax.bitwise_and(pos[plane(0)], 1) == 0
+    for sent, halo in ((inner, (6, 5)), (outer, (5, 6))):
+        sent[pl.ds(0, 5 * B)] = msg[pl.ds(0, 5 * B)]
+        sent[plane(5)] = jnp.where(even, msg[plane(halo[0])], msg[plane(halo[1])])
 
 
 def merged(blocks):
@@ -270,16 +278,26 @@
     return blocks[0]
 
 
-def merge_kernel(axis, near, order, sources, halos, pos, *refs):
+def merge_kernel(axis, near, order, sources, pos, *refs):
     got, msg = refs[-2:]
     blocks = collect(place(pos, axis, near)[1], order, refs[0], refs[1:near], got)
     at = 2 * sources
     coefs, rows = merged([(b[at : at + 3], rows_of(b, sources)) for b in blocks])
     for k, value in enumerate([v for pair in rows for v in pair] + list(coefs)):
         msg[plane(k)] = value
-    if halos:
-        msg[plane(5)] = blocks[0][5]
-        msg[plane(6)] = blocks[-1][6]
+
+
+def merge_first_kernel(near, pos, own, *refs):
+    got, msg, halos = refs[-3:]
+    r = place(pos, 0, near)[1]
+    blocks = ordered(r, [loaded(ref, range(5)) for ref in (own, *refs[: near - 1])], got)
+    coefs, rows = merged([(b[2:5], rows_of(b, 1)) for b in blocks])
+    for k, value in enumerate([*rows[0], *coefs, jnp.where(r == 0, own[plane(5)], own[plane(6)])]):
+        msg[plane(k)] = value
+    inner, outer = refs[0][plane(5)], refs[near - 2][plane(5)]
+    odd = lax.bitwise_and(r, 1) == 1
+    halos[plane(0)] = jnp.where(odd, outer, inner)
+    halos[plane(1)] = jnp.where(odd, inner, outer)
 
 
 def merge_rows_kernel(axis, near, order, pos, coefs, *refs):
@@ -324,16 +342,17 @@
 
 def both_y_kernel(near, far, order, pos, got_near, own_near, *refs):
     others, refs = refs[:far], refs[far:]
-    (g_b, u_x, v_x, flux_b, w, c, r_top, src_top, curl_in, flux_y_in, flux_a_in, part_a, p_y, u_y, v_y) = refs[:15]
-    got_far, rise_y, curl, flux_y, flux_a, g_a, g_c, msg, part, fz = refs[15:]
+    (halos, g_b, u_x, v_x, flux_b, w, c, r_top, src_top, curl_in, flux_y_in, flux_a_in, part_a, p_y, u_y, v_y) = refs[:16]
+    got_far, rise_y, curl, flux_y, flux_a, g_a, g_c, msg, part, fz = refs[16:]
     top = plane(0)
     q, r = place(pos, 0, near)
     far_blocks = collect(q, order, others[0], others[1:], got_far)
-    near_blocks = [stored(got_near, m, range(7)) for m in range(near)]
-    after_group = jnp.where(q < far - 1, pick([b[5] for b in far_blocks], q + 1), 0.0)
-    ey_next = jnp.where(r < near - 1, pick([b[5] for b in near_blocks], r + 1), after_group)
-    before_group = jnp.where(q > 0, pick([b[6] for b in far_blocks], q - 1), 0.0)
-    hz_prev = jnp.where(r > 0, pick([b[6] for b in near_blocks], r - 1), before_group)
+    near_blocks = [stored(got_near, m, range(5)) for m in range(near)]
+    ends = [b[5] for b in far_blocks]
+    after_group = jnp.where(q < far - 1, pick(ends, q + 1), 0.0)
+    ey_next = jnp.where(r < near - 1, halos[plane(0)], after_group)
+    before_group = jnp.where(q > 0, pick(ends, q - 1), 0.0)
+    hz_prev = jnp.where(r > 0, halos[plane(1)], before_group)
     curl[...] = curl_in[...]
     flux_y[...] = flux_y_in[...]
     flux_a[...] = flux_a_in[...]
@@ -512,8 +531,8 @@
     )(*ins)
 
 
-def shared(value, axis, n, order, near=1, bent=()):
-    masks = [near * s + (near // 2 if s in bent else 0) for s in order]
+def shared(value, axis, n, order, near=1, bent=(), by=0):
+    masks = [near * s + (by if s in bent else 0) for s in order]
     return [value] + [lax.ppermute(value, axis, [(i, i ^ mask) for i in range(n)]) for mask in masks]
 
 
@@ -551,19 +570,19 @@
         specs=[SMEM] + [HBM] * 5,
         scratch=[pltpu.VMEM(cells, jnp.int32)] + [pltpu.SMEM(permittivity.shape, F32)] * 2 + [dma((9,))],
     )
-    g_b, own_b = call(
+    g_b, own_b, inner, outer = call(
         first_x_kernel,
         [pos, part_b, hx_prev, flux_b, p_x, u_x, v_x, ef, mf],
-        [cells, (7 * B, nz)],
-    )
-    ins = shared(own_b, "px", nx, px_near)
+        [cells, (7 * B, nz), (6 * B, nz), (6 * B, nz)],
+    )
+    ins = [own_b] + [shared(outer if k == 3 else inner, "px", nx, (k,))[1] for k in px_near]
     ez_next = lax.ppermute(ez_first, "py", [((i + 1) % ny, i) for i in range(ny)])
-    near_b, group_b = call(
-        functools.partial(merge_kernel, 0, near_x, px_near, 1, True),
+    near_b, group_b, halos = call(
+        functools.partial(merge_first_kernel, near_x),
         [pos] + ins,
-        [(near_x, 7 * B, nz), (7 * B, nz)],
-    )
-    ins = shared(group_b, "px", nx, px_far, near_x, (1, 3))
+        [(near_x, 5 * B, nz), (6 * B, nz), (2 * B, nz)],
+    )
+    ins = shared(group_b, "px", nx, px_far, near_x, (1, 3), near_x - 1)
     p_y, u_y, v_y, r_top, src_top, curl, flux_y, flux_a, part_a = call(
         functools.partial(first_z_kernel, ny),
         [pos, ef, mf, ez_next, w, c],
@@ -571,19 +590,19 @@
         scratch=[cells] * 2,
         flops=8_000_000,
     )
-    ins = [pos, near_b, own_b] + ins + [g_b, u_x, v_x, flux_b, w, c, r_top, src_top]
+    ins = [pos, near_b, own_b] + ins + [halos, g_b, u_x, v_x, flux_b, w, c, r_top, src_top]
     far_b, rise_y, curl, flux_y, flux_a, g_a, g_c, own_ac = call(
         functools.partial(both_y_kernel, near_x, far_x, px_far),
         ins + [curl, flux_y, flux_a, part_a, p_y, u_y, v_y],
-        [(far_x, 7 * B, nz)] + [cells] * 6 + [(7 * B, nz)],
+        [(far_x, 6 * B, nz)] + [cells] * 6 + [(7 * B, nz)],
         scratch=[cells] * 2,
     )
     ins = shared(own_ac, "py", ny, py_near)
     near_ac, msg = call(
-        functools.partial(merge_kernel, 1, near_y, py_near, 2, False), [pos] + ins, [(near_y, 7 * B, nz), (7 * B, nz)]
+        functools.partial(merge_kernel, 1, near_y, py_near, 2), [pos] + ins, [(near_y, 7 * B, nz), (7 * B, nz)]
     )
     msg, w = lax.optimization_barrier((msg, w))
-    ins = shared(msg, "py", ny, py_far, near_y, (2,))
+    ins = shared(msg, "py", ny, py_far, near_y, (2,), near_y // 2)
     steps = (nz - 1).bit_length()
     z_factors = call(factors_kernel, [w], [(steps, *cells)] * 2 + [cells], flops=8_000_000)
     ins, z_factors = lax.optimization_barrier((ins, z_factors))
@@ -608,7 +627,7 @@
         [(near_x, 2 * B, nz), (2 * B, nz)],
     )
     msg, elec = lax.optimization_barrier((msg, elec))
-    ins = shared(msg, "px", nx, px_far, near_x, (1, 3))
+    ins = shared(msg, "px", nx, px_far, near_x, (1, 3), near_x // 2)
     elec, magn = call(
         second_z_kernel,
         [part_x, rise_y, *z_factors, elec, magn],

time: 57.6 us -> 57 us (0.990)
  waiting for transfers between devices: 12.7 us -> 12 us
    ppermute x18, waiting for transfers between devices: 8.32 us -> 7.7 us  [shared(): lax.ppermute(value, axis, [(i, i ^ mask) for i in range(n)])]
  transfers between devices with their start and end apart: 20 -> 20, of which waited for: 9 -> 8; matrix products, arithmetic and copies ran while one was open for 0% -> 0% of each run, Pallas kernels for 13% -> 14%
where the time goes in v12:
time: 57 us; the launch traced here: 56.4 us
  starting transfers between devices  32.9 us (58%)
  waiting for transfers between devices  12 us (21%)
  Pallas kernels  10.5 us (18%)
  between operations  0.92 us (2%)
    ppermute x18, starting transfers between devices, shared(): lax.ppermute(value, axis, [(i, i ^ mask) for i in range(n)])  25.9 us
    pallas_call x13, Pallas kernels, call(): pl.pallas_call(kernel, out_shape=shapes, in_specs=specs or [VMEM] * len(i...  10.5 us
    ppermute x18, waiting for transfers between devices, shared(): lax.ppermute(value, axis, [(i, i ^ mask) for i in range(n)])  7.7 us
    ppermute x1, waiting for transfers between devices, local(): lax.ppermute(hx_last, 'py', [(i, (i + 1) % ny) for i in range(ny)])  4.33 us
    ppermute x1, starting transfers between devices, local(): lax.ppermute(hx_last, 'py', [(i, (i + 1) % ny) for i in range(ny)])  3.82 us
    ppermute x1, starting transfers between devices, local(): lax.ppermute(ez_first, 'py', [((i + 1) % ny, i) for i in range(ny)])  3.24 us
  transfers between devices with their start and end apart: 20, of which 8 were waited for; matrix products, arithmetic and copies ran while one was open for 0% of the time, Pallas kernels for 14%

profile of v12, /device:TPU:1, one launch (start us, length us, event | category | flops | bytes accessed | tf_op | source)
XLA Modules:
  0.0 56.4 jit_solution(6801190432632812805)
XLA Ops:
  1.3 3.8 %collective-permute-start = (f32[16,128]{1,0:T(8,128)S(1)}, f32[16,128]{1,0:T(8,128)S(1)}, u32[]{:S(2)}, u32[]{:S(2)}) collective-permute-start(f32[16,128]{1,0:T(8,128)S(1)} %shard_map.69), channel_id=1, source_target_pairs={{0,1},{1,2},{2,3},{3,4},{4,5},{5,6},{6,7},{7,8},{8,9},{9,10},{10,1... | collective-permute-start | bytes 24584 | tf_op jit(solution)/shard_map/ppermute | solution.py:565
  5.2 1.9 %shard_map.68 = (f32[256,128]{1,0:T(8,128)S(1)}, f32[256,128]{1,0:T(8,128)S(1)}, f32[256,128]{1,0:T(8,128)S(1)}, f32[256,128]{1,0:T(8,128)S(1)}, f32[256,128]{1,...) custom-call(s32[2]{0:T(128)S(1)} %pad_add_fusion.me, ...), custom_call_target="tpu_custom_call" | custom-call | flops 1000000 | bytes 1000000 | tf_op jit(solution)/shard_map/pallas_call | solution.py:522
  7.2 4.3 %collective-permute-done.hx_prev = f32[16,128]{1,0:T(8,128)S(1)} collective-permute-done((f32[16,128]{1,0:T(8,128)S(1)}, f32[16,128]{1,0:T(8,128)S(1)}, u32[]{:S(2)}, u32[]{:S(2)}) %collective-permute-start) | collective-permute-done | bytes 8224 | tf_op jit(solution)/shard_map/ppermute | solution.py:565
  11.6 2.7 %collective-permute-start.3 = (f32[96,128]{1,0:T(8,128)S(1)}, f32[96,128]{1,0:T(8,128)S(1)}, u32[]{:S(2)}, u32[]{:S(2)}) collective-permute-start(f32[96,128]{1,0:T(8,128)S(1)} %get-tuple-element.76), channel_id=1, source_target_pairs={{0,48},{16,32},{32,16},{48,0},{64,112},{80,96},{96,80},{112,64},{1... | collective-permute-start | bytes 147464 | tf_op jit(solution)/shard_map/ppermute | solution.py:536
  14.8 3.2 %collective-permute-start.7 = (f32[128,128]{1,0:T(8,128)S(1)}, f32[128,128]{1,0:T(8,128)S(1)}, u32[]{:S(2)}, u32[]{:S(2)}) collective-permute-start(f32[128,128]{1,0:T(8,128)S(1)} %get-tuple-element.83), channel_id=1, source_target_pairs={{1,0},{2,1},{3,2},{4,3},{5,4},{6,5},{7,6},{8,7},{9,8},{10,9},{11,1... | collective-permute-start | bytes 196616 | tf_op jit(solution)/shard_map/ppermute | solution.py:579
  18.1 3.1 %collective-permute-start.6 = (f32[96,128]{1,0:T(8,128)S(1)}, f32[96,128]{1,0:T(8,128)S(1)}, u32[]{:S(2)}, u32[]{:S(2)}) collective-permute-start(f32[96,128]{1,0:T(8,128)S(1)} %get-tuple-element.78.refs_0_.group_b), channel_id=1, source_target_pairs={{0,240},{16,224},{32,208},{48,192},{64,176},{80,160},{96,144},{112... | collective-permute-start | bytes 147464 | tf_op jit(solution)/shard_map/ppermute | solution.py:536
  21.3 1.1 %collective-permute-start.4 = (f32[96,128]{1,0:T(8,128)S(1)}, f32[96,128]{1,0:T(8,128)S(1)}, u32[]{:S(2)}, u32[]{:S(2)}) collective-permute-start(f32[96,128]{1,0:T(8,128)S(1)} %get-tuple-element.78.refs_0_.group_b), channel_id=1, source_target_pairs={{0,128},{16,144},{32,160},{48,176},{64,192},{80,208},{96,224},{112... | collective-permute-start | bytes 147464 | tf_op jit(solution)/shard_map/ppermute | solution.py:536
  22.3 2.0 %shard_map.72 = (f32[256,128]{1,0:T(8,128)S(1)}, f32[256,128]{1,0:T(8,128)S(1)}, f32[256,128]{1,0:T(8,128)S(1)}, f32[16,128]{1,0:T(8,128)S(1)}, f32[16,128]{1,0:...) custom-call(s32[32,128]{1,0:T(8,128)S(1)} %get-tuple-element.66.pos,, ...), custom_call_target="tpu_custom_call" | custom-call | flops 8000000 | bytes 1000000 | tf_op jit(solution)/shard_map/pallas_call | solution.py:522
  24.4 1.6 %collective-permute-done.5.refs_2_ = f32[96,128]{1,0:T(8,128)S(1)} collective-permute-done((f32[96,128]{1,0:T(8,128)S(1)}, f32[96,128]{1,0:T(8,128)S(1)}, u32[]{:S(2)}, u32[]{:S(2)}) %collective-permute-start.5) | collective-permute-done | bytes 49184 | tf_op jit(solution)/shard_map/ppermute | solution.py:536
  26.0 0.8 %shard_map.73 = (f32[4,96,128]{2,1,0:T(8,128)S(1)}, f32[256,128]{1,0:T(8,128)S(1)}, f32[256,128]{1,0:T(8,128)S(1)}, f32[256,128]{1,0:T(8,128)S(1)}, f32[256,128]...) custom-call(s32[32,128]{1,0:T(8,128)S(1)} %get-tuple-element.66.pos, ...), custom_call_target="tpu_custom_call" | custom-call | flops 1000000 | bytes 1000000 | tf_op jit(solution)/shard_map/pallas_call | solution.py:522
  27.3 3.7 %collective-permute-start.8 = (f32[112,128]{1,0:T(8,128)S(1)}, f32[112,128]{1,0:T(8,128)S(1)}, u32[]{:S(2)}, u32[]{:S(2)}) collective-permute-start(f32[112,128]{1,0:T(8,128)S(1)} %get-tuple-element.94.refs_0_.own_near), channel_id=1, source_target_pairs={{0,2},{1,3},{2,0},{3,1},{4,6},{5,7},{6,4},{7,5},{8,10},{9,11},{10,... | collective-permute-start | bytes 172040 | tf_op jit(solution)/shard_map/ppermute | solution.py:536
  31.0 1.8 %collective-permute-done.10.refs_3_ = f32[112,128]{1,0:T(8,128)S(1)} collective-permute-done((f32[112,128]{1,0:T(8,128)S(1)}, f32[112,128]{1,0:T(8,128)S(1)}, u32[]{:S(2)}, u32[]{:S(2)}) %collective-permute-start.10) | collective-permute-done | bytes 57376 | tf_op jit(solution)/shard_map/ppermute | solution.py:536
  32.9 4.5 %collective-permute-start.13 = (f32[112,128]{1,0:T(8,128)S(1)}, f32[112,128]{1,0:T(8,128)S(1)}, u32[]{:S(2)}, u32[]{:S(2)}) collective-permute-start(f32[112,128]{1,0:T(8,128)S(1)} %get-tuple-element.102.refs_0_), channel_id=1, source_target_pairs={{0,10},{1,11},{2,8},{3,9},{4,14},{5,15},{6,12},{7,13},{8,2},{9,3},... | collective-permute-start | bytes 172040 | tf_op jit(solution)/shard_map/ppermute | solution.py:536
  37.4 1.5 %collective-permute-start.11 = (f32[112,128]{1,0:T(8,128)S(1)}, f32[112,128]{1,0:T(8,128)S(1)}, u32[]{:S(2)}, u32[]{:S(2)}) collective-permute-start(f32[112,128]{1,0:T(8,128)S(1)} %get-tuple-element.102.refs_0_), channel_id=1, source_target_pairs={{0,4},{1,5},{2,6},{3,7},{4,0},{5,1},{6,2},{7,3},{8,12},{9,13},{10,... | collective-permute-start | bytes 172040 | tf_op jit(solution)/shard_map/ppermute | solution.py:536
  38.9 1.3 %shard_map.75 = (f32[7,256,128]{2,1,0:T(8,128)S(1)}, f32[7,256,128]{2,1,0:T(8,128)S(1)}, f32[256,128]{1,0:T(8,128)S(1)}) custom-call(f32[256,128]{1,0:T(8,128)S(1)} %get-tuple-element.98.w.refs_9_.w_in), custom_call_target="tpu_custom_call" | custom-call | flops 8000000 | bytes 1000000 | tf_op jit(solution)/shard_map/pallas_call | solution.py:522
  40.2 2.3 %collective-permute-done.12.refs_2_ = f32[112,128]{1,0:T(8,128)S(1)} collective-permute-done((f32[112,128]{1,0:T(8,128)S(1)}, f32[112,128]{1,0:T(8,128)S(1)}, u32[]{:S(2)}, u32[]{:S(2)}) %collective-permute-start.12) | collective-permute-done | bytes 57376 | tf_op jit(solution)/shard_map/ppermute | solution.py:536
  43.5 2.2 %collective-permute-start.16 = (f32[32,128]{1,0:T(8,128)S(1)}, f32[32,128]{1,0:T(8,128)S(1)}, u32[]{:S(2)}, u32[]{:S(2)}) collective-permute-start(f32[32,128]{1,0:T(8,128)S(1)} %get-tuple-element.109.refs_0_.own_near), channel_id=1, source_target_pairs={{0,48},{16,32},{32,16},{48,0},{64,112},{80,96},{96,80},{112,64},{1... | collective-permute-start | bytes 49160 | tf_op jit(solution)/shard_map/ppermute | solution.py:536
  45.7 2.0 %collective-permute-start.15 = (f32[32,128]{1,0:T(8,128)S(1)}, f32[32,128]{1,0:T(8,128)S(1)}, u32[]{:S(2)}, u32[]{:S(2)}) collective-permute-start(f32[32,128]{1,0:T(8,128)S(1)} %get-tuple-element.109.refs_0_.own_near), channel_id=1, source_target_pairs={{0,32},{16,48},{32,0},{48,16},{64,96},{80,112},{96,64},{112,80},{1... | collective-permute-start | bytes 49160 | tf_op jit(solution)/shard_map/ppermute | solution.py:536
  47.7 0.8 %shard_map.78 = (f32[3,256,128]{2,1,0:T(8,128)}, f32[3,256,128]{2,1,0:T(8,128)}) custom-call(f32[32,128]{1,0:T(8,128)S(1)} %get-tuple-element.112.ends_c, f32[256,128]{1,0:T(8,128)S(1)} %get-tuple-element.113.g_c, f32[256,128]{1,0:T(8,128)S(1)} %get-tuple-element.91.refs_18_.refs_5_.u, f32[256,128]{1,0:T(8,128)S(1)} %get-tuple-element.92.refs_19_.refs_6_.v, ...), custom_call_target="tpu_custom_call" | custom-call | flops 1000000 | bytes 1000000 | tf_op jit(solution)/shard_map/pallas_call | solution.py:522
  49.1 2.2 %collective-permute-start.19 = (f32[32,128]{1,0:T(8,128)S(1)}, f32[32,128]{1,0:T(8,128)S(1)}, u32[]{:S(2)}, u32[]{:S(2)}) collective-permute-start(f32[32,128]{1,0:T(8,128)S(1)} %get-tuple-element.116.refs_0_), channel_id=1, source_target_pairs={{0,224},{16,240},{32,192},{48,208},{64,160},{80,176},{96,128},{112... | collective-permute-start | bytes 49160 | tf_op jit(solution)/shard_map/ppermute | solution.py:536
  51.9 1.2 %collective-permute-start.17 = (f32[32,128]{1,0:T(8,128)S(1)}, f32[32,128]{1,0:T(8,128)S(1)}, u32[]{:S(2)}, u32[]{:S(2)}) collective-permute-start(f32[32,128]{1,0:T(8,128)S(1)} %get-tuple-element.116.refs_0_), channel_id=1, source_target_pairs={{0,128},{16,144},{32,160},{48,176},{64,192},{80,208},{96,224},{112... | collective-permute-start | bytes 49160 | tf_op jit(solution)/shard_map/ppermute | solution.py:536
  53.1 1.6 %shard_map.79 = (f32[3,256,128]{2,1,0:T(8,128)}, f32[3,256,128]{2,1,0:T(8,128)}) custom-call(f32[256,128]{1,0:T(8,128)S(1)} %get-tuple-element.119.part, f32[256,128]{1,0:T(8,128)S(1)} %get-tuple-element.120.rise_y, f32[7,256,128]{2,1,0:T(8,128)S(1)} %get-tuple-element.121.z_a, ...), custom_call_target="tpu_custom_call", output_to_operand_aliasing={{0}: (5, {}), {1}: (6, {})} | custom-call | flops 4000000 | bytes 1000000 | tf_op jit(solution)/shard_map/pallas_call | solution.py:522
  54.7 0.8 %collective-permute-done.18.refs_2_ = f32[32,128]{1,0:T(8,128)S(1)} collective-permute-done((f32[32,128]{1,0:T(8,128)S(1)}, f32[32,128]{1,0:T(8,128)S(1)}, u32[]{:S(2)}, u32[]{:S(2)}) %collective-permute-start.18) | collective-permute-done | bytes 16416 | tf_op jit(solution)/shard_map/ppermute | solution.py:536
  55.5 0.8 %shard_map.80 = (f32[3,256,128]{2,1,0:T(8,128)}, f32[3,256,128]{2,1,0:T(8,128)}) custom-call(s32[32,128]{1,0:T(8,128)S(1)} %get-tuple-element.66.pos, f32[4,80,128]{2,1,0:T(8,128)S(1)} %get-tuple-element.77.got_near.coefs.coefs_near, f32[4,96,128]{2,1,0:T(8,128)S(1)} %get-tuple-element.93.coefs_far, ...), custom_call_target="tpu_custom_call", output_to_operand_aliasing={{0}: (15, {}), {1}: (16, {})} | custom-call | flops 1000000 | bytes 1000000 | tf_op jit(solution)/shard_map/pallas_call | solution.py:522
  (30 shorter events, 4.1 us)
Async XLA Ops:
  1.3 10.2 %collective-permute-start = (f32[16,128]{1,0:T(8,128)S(1)}, f32[16,128]{1,0:T(8,128)S(1)}, u32[]{:S(2)}, u32[]{:S(2)}) collective-permute-start(f32[16,128]{1,0:T(8,128)S(1)} %shard_map.69), channel_id=1, source_target_pairs={{0,1},{1,2},{2,3},{3,4},{4,5},{5,6},{6,7},{7,8},{8,9},{9,10},{10,1... | collective-permute-start | bytes 24584 | tf_op jit(solution)/shard_map/ppermute | solution.py:565
  11.6 6.5 %collective-permute-start.3 = (f32[96,128]{1,0:T(8,128)S(1)}, f32[96,128]{1,0:T(8,128)S(1)}, u32[]{:S(2)}, u32[]{:S(2)}) collective-permute-start(f32[96,128]{1,0:T(8,128)S(1)} %get-tuple-element.76), channel_id=1, source_target_pairs={{0,48},{16,32},{32,16},{48,0},{64,112},{80,96},{96,80},{112,64},{1... | collective-permute-start | bytes 147464 | tf_op jit(solution)/shard_map/ppermute | solution.py:536
  14.3 3.7 %collective-permute-start.2 = (f32[96,128]{1,0:T(8,128)S(1)}, f32[96,128]{1,0:T(8,128)S(1)}, u32[]{:S(2)}, u32[]{:S(2)}) collective-permute-start(f32[96,128]{1,0:T(8,128)S(1)} %get-tuple-element.75), channel_id=1, source_target_pairs={{0,32},{16,48},{32,0},{48,16},{64,96},{80,112},{96,64},{112,80},{1... | collective-permute-start | bytes 147464 | tf_op jit(solution)/shard_map/ppermute | solution.py:536
  14.6 3.5 %collective-permute-start.1 = (f32[96,128]{1,0:T(8,128)S(1)}, f32[96,128]{1,0:T(8,128)S(1)}, u32[]{:S(2)}, u32[]{:S(2)}) collective-permute-start(f32[96,128]{1,0:T(8,128)S(1)} %get-tuple-element.75), channel_id=1, source_target_pairs={{0,16},{16,0},{32,48},{48,32},{64,80},{80,64},{96,112},{112,96},{1... | collective-permute-start | bytes 147464 | tf_op jit(solution)/shard_map/ppermute | solution.py:536
  14.8 7.5 %collective-permute-start.7 = (f32[128,128]{1,0:T(8,128)S(1)}, f32[128,128]{1,0:T(8,128)S(1)}, u32[]{:S(2)}, u32[]{:S(2)}) collective-permute-start(f32[128,128]{1,0:T(8,128)S(1)} %get-tuple-element.83), channel_id=1, source_target_pairs={{1,0},{2,1},{3,2},{4,3},{5,4},{6,5},{7,6},{8,7},{9,8},{10,9},{11,1... | collective-permute-start | bytes 196616 | tf_op jit(solution)/shard_map/ppermute | solution.py:579
  18.1 6.3 %collective-permute-start.6 = (f32[96,128]{1,0:T(8,128)S(1)}, f32[96,128]{1,0:T(8,128)S(1)}, u32[]{:S(2)}, u32[]{:S(2)}) collective-permute-start(f32[96,128]{1,0:T(8,128)S(1)} %get-tuple-element.78.refs_0_.group_b), channel_id=1, source_target_pairs={{0,240},{16,224},{32,208},{48,192},{64,176},{80,160},{96,144},{112... | collective-permute-start | bytes 147464 | tf_op jit(solution)/shard_map/ppermute | solution.py:536
  21.2 4.7 %collective-permute-start.5 = (f32[96,128]{1,0:T(8,128)S(1)}, f32[96,128]{1,0:T(8,128)S(1)}, u32[]{:S(2)}, u32[]{:S(2)}) collective-permute-start(f32[96,128]{1,0:T(8,128)S(1)} %get-tuple-element.78.refs_0_.group_b), channel_id=1, source_target_pairs={{0,112},{16,96},{32,80},{48,64},{64,48},{80,32},{96,16},{112,0},{1... | collective-permute-start | bytes 147464 | tf_op jit(solution)/shard_map/ppermute | solution.py:536
  21.3 4.7 %collective-permute-start.4 = (f32[96,128]{1,0:T(8,128)S(1)}, f32[96,128]{1,0:T(8,128)S(1)}, u32[]{:S(2)}, u32[]{:S(2)}) collective-permute-start(f32[96,128]{1,0:T(8,128)S(1)} %get-tuple-element.78.refs_0_.group_b), channel_id=1, source_target_pairs={{0,128},{16,144},{32,160},{48,176},{64,192},{80,208},{96,224},{112... | collective-permute-start | bytes 147464 | tf_op jit(solution)/shard_map/ppermute | solution.py:536
  26.8 6.0 %collective-permute-start.10 = (f32[112,128]{1,0:T(8,128)S(1)}, f32[112,128]{1,0:T(8,128)S(1)}, u32[]{:S(2)}, u32[]{:S(2)}) collective-permute-start(f32[112,128]{1,0:T(8,128)S(1)} %get-tuple-element.94.refs_0_.own_near), channel_id=1, source_target_pairs={{0,3},{1,2},{2,1},{3,0},{4,7},{5,6},{6,5},{7,4},{8,11},{9,10},{10,... | collective-permute-start | bytes 172040 | tf_op jit(solution)/shard_map/ppermute | solution.py:536
  26.8 5.9 %collective-permute-start.9 = (f32[112,128]{1,0:T(8,128)S(1)}, f32[112,128]{1,0:T(8,128)S(1)}, u32[]{:S(2)}, u32[]{:S(2)}) collective-permute-start(f32[112,128]{1,0:T(8,128)S(1)} %get-tuple-element.94.refs_0_.own_near), channel_id=1, source_target_pairs={{0,1},{1,0},{2,3},{3,2},{4,5},{5,4},{6,7},{7,6},{8,9},{9,8},{10,11... | collective-permute-start | bytes 172040 | tf_op jit(solution)/shard_map/ppermute | solution.py:536
  27.3 5.6 %collective-permute-start.8 = (f32[112,128]{1,0:T(8,128)S(1)}, f32[112,128]{1,0:T(8,128)S(1)}, u32[]{:S(2)}, u32[]{:S(2)}) collective-permute-start(f32[112,128]{1,0:T(8,128)S(1)} %get-tuple-element.94.refs_0_.own_near), channel_id=1, source_target_pairs={{0,2},{1,3},{2,0},{3,1},{4,6},{5,7},{6,4},{7,5},{8,10},{9,11},{10,... | collective-permute-start | bytes 172040 | tf_op jit(solution)/shard_map/ppermute | solution.py:536
  32.9 7.3 %collective-permute-start.13 = (f32[112,128]{1,0:T(8,128)S(1)}, f32[112,128]{1,0:T(8,128)S(1)}, u32[]{:S(2)}, u32[]{:S(2)}) collective-permute-start(f32[112,128]{1,0:T(8,128)S(1)} %get-tuple-element.102.refs_0_), channel_id=1, source_target_pairs={{0,10},{1,11},{2,8},{3,9},{4,14},{5,15},{6,12},{7,13},{8,2},{9,3},... | collective-permute-start | bytes 172040 | tf_op jit(solution)/shard_map/ppermute | solution.py:536
  37.4 5.1 %collective-permute-start.12 = (f32[112,128]{1,0:T(8,128)S(1)}, f32[112,128]{1,0:T(8,128)S(1)}, u32[]{:S(2)}, u32[]{:S(2)}) collective-permute-start(f32[112,128]{1,0:T(8,128)S(1)} %get-tuple-element.102.refs_0_), channel_id=1, source_target_pairs={{0,12},{1,13},{2,14},{3,15},{4,8},{5,9},{6,10},{7,11},{8,4},{9,5},... | collective-permute-start | bytes 172040 | tf_op jit(solution)/shard_map/ppermute | solution.py:536
  37.4 5.7 %collective-permute-start.11 = (f32[112,128]{1,0:T(8,128)S(1)}, f32[112,128]{1,0:T(8,128)S(1)}, u32[]{:S(2)}, u32[]{:S(2)}) collective-permute-start(f32[112,128]{1,0:T(8,128)S(1)} %get-tuple-element.102.refs_0_), channel_id=1, source_target_pairs={{0,4},{1,5},{2,6},{3,7},{4,0},{5,1},{6,2},{7,3},{8,12},{9,13},{10,... | collective-permute-start | bytes 172040 | tf_op jit(solution)/shard_map/ppermute | solution.py:536
  43.5 5.0 %collective-permute-start.16 = (f32[32,128]{1,0:T(8,128)S(1)}, f32[32,128]{1,0:T(8,128)S(1)}, u32[]{:S(2)}, u32[]{:S(2)}) collective-permute-start(f32[32,128]{1,0:T(8,128)S(1)} %get-tuple-element.109.refs_0_.own_near), channel_id=1, source_target_pairs={{0,48},{16,32},{32,16},{48,0},{64,112},{80,96},{96,80},{112,64},{1... | collective-permute-start | bytes 49160 | tf_op jit(solution)/shard_map/ppermute | solution.py:536
  45.7 3.4 %collective-permute-start.15 = (f32[32,128]{1,0:T(8,128)S(1)}, f32[32,128]{1,0:T(8,128)S(1)}, u32[]{:S(2)}, u32[]{:S(2)}) collective-permute-start(f32[32,128]{1,0:T(8,128)S(1)} %get-tuple-element.109.refs_0_.own_near), channel_id=1, source_target_pairs={{0,32},{16,48},{32,0},{48,16},{64,96},{80,112},{96,64},{112,80},{1... | collective-permute-start | bytes 49160 | tf_op jit(solution)/shard_map/ppermute | solution.py:536
  47.7 1.4 %collective-permute-start.14 = (f32[32,128]{1,0:T(8,128)S(1)}, f32[32,128]{1,0:T(8,128)S(1)}, u32[]{:S(2)}, u32[]{:S(2)}) collective-permute-start(f32[32,128]{1,0:T(8,128)S(1)} %get-tuple-element.109.refs_0_.own_near), channel_id=1, source_target_pairs={{0,16},{16,0},{32,48},{48,32},{64,80},{80,64},{96,112},{112,96},{1... | collective-permute-start | bytes 49160 | tf_op jit(solution)/shard_map/ppermute | solution.py:536
  49.1 5.5 %collective-permute-start.19 = (f32[32,128]{1,0:T(8,128)S(1)}, f32[32,128]{1,0:T(8,128)S(1)}, u32[]{:S(2)}, u32[]{:S(2)}) collective-permute-start(f32[32,128]{1,0:T(8,128)S(1)} %get-tuple-element.116.refs_0_), channel_id=1, source_target_pairs={{0,224},{16,240},{32,192},{48,208},{64,160},{80,176},{96,128},{112... | collective-permute-start | bytes 49160 | tf_op jit(solution)/shard_map/ppermute | solution.py:536
  51.4 4.1 %collective-permute-start.18 = (f32[32,128]{1,0:T(8,128)S(1)}, f32[32,128]{1,0:T(8,128)S(1)}, u32[]{:S(2)}, u32[]{:S(2)}) collective-permute-start(f32[32,128]{1,0:T(8,128)S(1)} %get-tuple-element.116.refs_0_), channel_id=1, source_target_pairs={{0,96},{16,112},{32,64},{48,80},{64,32},{80,48},{96,0},{112,16},{1... | collective-permute-start | bytes 49160 | tf_op jit(solution)/shard_map/ppermute | solution.py:536
  51.9 3.6 %collective-permute-start.17 = (f32[32,128]{1,0:T(8,128)S(1)}, f32[32,128]{1,0:T(8,128)S(1)}, u32[]{:S(2)}, u32[]{:S(2)}) collective-permute-start(f32[32,128]{1,0:T(8,128)S(1)} %get-tuple-element.116.refs_0_), channel_id=1, source_target_pairs={{0,128},{16,144},{32,160},{48,176},{64,192},{80,208},{96,224},{112... | collective-permute-start | bytes 49160 | tf_op jit(solution)/shard_map/ppermute | solution.py:536

commit v13 on v12

--- a/solution.py
+++ b/solution.py
@@ -553,7 +553,7 @@
     magn = in_hbm(magnetic.reshape(3, *cells))
     ids = in_hbm(material.reshape(cells))
     dma = pltpu.SemaphoreType.DMA
-    orders = [(1, 2, 3), (2, 1, 3), (2, 1, 3), (1, 3, 2)]
+    orders = [(1, 2, 3), (2, 1, 3), (2, 1, 3), (1, 2, 3)]
     counts = (near_x, far_x, near_y, far_y)
     px_near, px_far, py_near, py_far = [
         tuple(s for s in order if s < count) for order, count in zip(orders, counts)

time: 57 us -> 57.3 us (level)
  starting transfers between devices: 32.9 us -> 34.5 us
  waiting for transfers between devices: 12 us -> 10.6 us
    ppermute x18, starting transfers between devices: 25.9 us -> 27.4 us  [shared(): lax.ppermute(value, axis, [(i, i ^ mask) for i in range(n)])]
    ppermute x18, waiting for transfers between devices: 7.7 us -> 6.23 us  [shared(): lax.ppermute(value, axis, [(i, i ^ mask) for i in range(n)])]
  transfers between devices with their start and end apart: 20 -> 20, of which waited for: 8 -> 7; matrix products, arithmetic and copies ran while one was open for 0% -> 0% of each run, Pallas kernels for 14% -> 13%
where the time goes in v13:
time: 57.3 us; the launch traced here: 56.5 us
  starting transfers between devices  34.5 us (60%)
  waiting for transfers between devices  10.6 us (18%)
  Pallas kernels  10.5 us (18%)
  between operations  0.92 us (2%)
    ppermute x18, starting transfers between devices, shared(): lax.ppermute(value, axis, [(i, i ^ mask) for i in range(n)])  27.4 us
    pallas_call x13, Pallas kernels, call(): pl.pallas_call(kernel, out_shape=shapes, in_specs=specs or [VMEM] * len(i...  10.5 us
    ppermute x18, waiting for transfers between devices, shared(): lax.ppermute(value, axis, [(i, i ^ mask) for i in range(n)])  6.23 us
    ppermute x1, waiting for transfers between devices, local(): lax.ppermute(hx_last, 'py', [(i, (i + 1) % ny) for i in range(ny)])  4.33 us
    ppermute x1, starting transfers between devices, local(): lax.ppermute(hx_last, 'py', [(i, (i + 1) % ny) for i in range(ny)])  3.82 us
    ppermute x1, starting transfers between devices, local(): lax.ppermute(ez_first, 'py', [((i + 1) % ny, i) for i in range(ny)])  3.24 us
  transfers between devices with their start and end apart: 20, of which 7 were waited for; matrix products, arithmetic and copies ran while one was open for 0% of the time, Pallas kernels for 13%

profile of v13, /device:TPU:1, one launch (start us, length us, event | category | flops | bytes accessed | tf_op | source)
XLA Modules:
  0.0 56.5 jit_solution(8218188555966934847)
XLA Ops:
  1.3 3.8 %collective-permute-start = (f32[16,128]{1,0:T(8,128)S(1)}, f32[16,128]{1,0:T(8,128)S(1)}, u32[]{:S(2)}, u32[]{:S(2)}) collective-permute-start(f32[16,128]{1,0:T(8,128)S(1)} %shard_map.69), channel_id=1, source_target_pairs={{0,1},{1,2},{2,3},{3,4},{4,5},{5,6},{6,7},{7,8},{8,9},{9,10},{10,1... | collective-permute-start | bytes 24584 | tf_op jit(solution)/shard_map/ppermute | solution.py:565
  5.2 1.9 %shard_map.68 = (f32[256,128]{1,0:T(8,128)S(1)}, f32[256,128]{1,0:T(8,128)S(1)}, f32[256,128]{1,0:T(8,128)S(1)}, f32[256,128]{1,0:T(8,128)S(1)}, f32[256,128]{1,...) custom-call(s32[2]{0:T(128)S(1)} %pad_add_fusion.me, ...), custom_call_target="tpu_custom_call" | custom-call | flops 1000000 | bytes 1000000 | tf_op jit(solution)/shard_map/pallas_call | solution.py:522
  7.2 4.3 %collective-permute-done.hx_prev = f32[16,128]{1,0:T(8,128)S(1)} collective-permute-done((f32[16,128]{1,0:T(8,128)S(1)}, f32[16,128]{1,0:T(8,128)S(1)}, u32[]{:S(2)}, u32[]{:S(2)}) %collective-permute-start) | collective-permute-done | bytes 8224 | tf_op jit(solution)/shard_map/ppermute | solution.py:565
  11.6 2.7 %collective-permute-start.3 = (f32[96,128]{1,0:T(8,128)S(1)}, f32[96,128]{1,0:T(8,128)S(1)}, u32[]{:S(2)}, u32[]{:S(2)}) collective-permute-start(f32[96,128]{1,0:T(8,128)S(1)} %get-tuple-element.76), channel_id=1, source_target_pairs={{0,48},{16,32},{32,16},{48,0},{64,112},{80,96},{96,80},{112,64},{1... | collective-permute-start | bytes 147464 | tf_op jit(solution)/shard_map/ppermute | solution.py:536
  14.8 3.2 %collective-permute-start.7 = (f32[128,128]{1,0:T(8,128)S(1)}, f32[128,128]{1,0:T(8,128)S(1)}, u32[]{:S(2)}, u32[]{:S(2)}) collective-permute-start(f32[128,128]{1,0:T(8,128)S(1)} %get-tuple-element.83), channel_id=1, source_target_pairs={{1,0},{2,1},{3,2},{4,3},{5,4},{6,5},{7,6},{8,7},{9,8},{10,9},{11,1... | collective-permute-start | bytes 196616 | tf_op jit(solution)/shard_map/ppermute | solution.py:579
  18.1 3.1 %collective-permute-start.6 = (f32[96,128]{1,0:T(8,128)S(1)}, f32[96,128]{1,0:T(8,128)S(1)}, u32[]{:S(2)}, u32[]{:S(2)}) collective-permute-start(f32[96,128]{1,0:T(8,128)S(1)} %get-tuple-element.78.refs_0_.group_b), channel_id=1, source_target_pairs={{0,240},{16,224},{32,208},{48,192},{64,176},{80,160},{96,144},{112... | collective-permute-start | bytes 147464 | tf_op jit(solution)/shard_map/ppermute | solution.py:536
  21.3 1.1 %collective-permute-start.4 = (f32[96,128]{1,0:T(8,128)S(1)}, f32[96,128]{1,0:T(8,128)S(1)}, u32[]{:S(2)}, u32[]{:S(2)}) collective-permute-start(f32[96,128]{1,0:T(8,128)S(1)} %get-tuple-element.78.refs_0_.group_b), channel_id=1, source_target_pairs={{0,128},{16,144},{32,160},{48,176},{64,192},{80,208},{96,224},{112... | collective-permute-start | bytes 147464 | tf_op jit(solution)/shard_map/ppermute | solution.py:536
  22.3 2.0 %shard_map.72 = (f32[256,128]{1,0:T(8,128)S(1)}, f32[256,128]{1,0:T(8,128)S(1)}, f32[256,128]{1,0:T(8,128)S(1)}, f32[16,128]{1,0:T(8,128)S(1)}, f32[16,128]{1,0:...) custom-call(s32[32,128]{1,0:T(8,128)S(1)} %get-tuple-element.66.pos,, ...), custom_call_target="tpu_custom_call" | custom-call | flops 8000000 | bytes 1000000 | tf_op jit(solution)/shard_map/pallas_call | solution.py:522
  24.4 1.6 %collective-permute-done.5.refs_2_ = f32[96,128]{1,0:T(8,128)S(1)} collective-permute-done((f32[96,128]{1,0:T(8,128)S(1)}, f32[96,128]{1,0:T(8,128)S(1)}, u32[]{:S(2)}, u32[]{:S(2)}) %collective-permute-start.5) | collective-permute-done | bytes 49184 | tf_op jit(solution)/shard_map/ppermute | solution.py:536
  27.3 3.7 %collective-permute-start.8 = (f32[112,128]{1,0:T(8,128)S(1)}, f32[112,128]{1,0:T(8,128)S(1)}, u32[]{:S(2)}, u32[]{:S(2)}) collective-permute-start(f32[112,128]{1,0:T(8,128)S(1)} %get-tuple-element.94.refs_0_.own_near), channel_id=1, source_target_pairs={{0,2},{1,3},{2,0},{3,1},{4,6},{5,7},{6,4},{7,5},{8,10},{9,11},{10,... | collective-permute-start | bytes 172040 | tf_op jit(solution)/shard_map/ppermute | solution.py:536
  31.0 1.8 %collective-permute-done.10.refs_3_ = f32[112,128]{1,0:T(8,128)S(1)} collective-permute-done((f32[112,128]{1,0:T(8,128)S(1)}, f32[112,128]{1,0:T(8,128)S(1)}, u32[]{:S(2)}, u32[]{:S(2)}) %collective-permute-start.10) | collective-permute-done | bytes 57376 | tf_op jit(solution)/shard_map/ppermute | solution.py:536
  32.9 2.9 %collective-permute-start.13 = (f32[112,128]{1,0:T(8,128)S(1)}, f32[112,128]{1,0:T(8,128)S(1)}, u32[]{:S(2)}, u32[]{:S(2)}) collective-permute-start(f32[112,128]{1,0:T(8,128)S(1)} %get-tuple-element.102.refs_0_), channel_id=1, source_target_pairs={{0,12},{1,13},{2,14},{3,15},{4,8},{5,9},{6,10},{7,11},{8,4},{9,5},... | collective-permute-start | bytes 172040 | tf_op jit(solution)/shard_map/ppermute | solution.py:536
  35.9 1.7 %collective-permute-start.12 = (f32[112,128]{1,0:T(8,128)S(1)}, f32[112,128]{1,0:T(8,128)S(1)}, u32[]{:S(2)}, u32[]{:S(2)}) collective-permute-start(f32[112,128]{1,0:T(8,128)S(1)} %get-tuple-element.102.refs_0_), channel_id=1, source_target_pairs={{0,10},{1,11},{2,8},{3,9},{4,14},{5,15},{6,12},{7,13},{8,2},{9,3},... | collective-permute-start | bytes 172040 | tf_op jit(solution)/shard_map/ppermute | solution.py:536
  37.5 1.3 %collective-permute-start.11 = (f32[112,128]{1,0:T(8,128)S(1)}, f32[112,128]{1,0:T(8,128)S(1)}, u32[]{:S(2)}, u32[]{:S(2)}) collective-permute-start(f32[112,128]{1,0:T(8,128)S(1)} %get-tuple-element.102.refs_0_), channel_id=1, source_target_pairs={{0,4},{1,5},{2,6},{3,7},{4,0},{5,1},{6,2},{7,3},{8,12},{9,13},{10,... | collective-permute-start | bytes 172040 | tf_op jit(solution)/shard_map/ppermute | solution.py:536
  38.8 1.3 %shard_map.75 = (f32[7,256,128]{2,1,0:T(8,128)S(1)}, f32[7,256,128]{2,1,0:T(8,128)S(1)}, f32[256,128]{1,0:T(8,128)S(1)}) custom-call(f32[256,128]{1,0:T(8,128)S(1)} %get-tuple-element.98.w.refs_9_.w_in), custom_call_target="tpu_custom_call" | custom-call | flops 8000000 | bytes 1000000 | tf_op jit(solution)/shard_map/pallas_call | solution.py:522
  40.1 1.8 %collective-permute-done.12.refs_2_ = f32[112,128]{1,0:T(8,128)S(1)} collective-permute-done((f32[112,128]{1,0:T(8,128)S(1)}, f32[112,128]{1,0:T(8,128)S(1)}, u32[]{:S(2)}, u32[]{:S(2)}) %collective-permute-start.12) | collective-permute-done | bytes 57376 | tf_op jit(solution)/shard_map/ppermute | solution.py:536
  42.3 4.2 %collective-permute-start.16 = (f32[32,128]{1,0:T(8,128)S(1)}, f32[32,128]{1,0:T(8,128)S(1)}, u32[]{:S(2)}, u32[]{:S(2)}) collective-permute-start(f32[32,128]{1,0:T(8,128)S(1)} %get-tuple-element.109.refs_0_.own_near), channel_id=1, source_target_pairs={{0,48},{16,32},{32,16},{48,0},{64,112},{80,96},{96,80},{112,64},{1... | collective-permute-start | bytes 49160 | tf_op jit(solution)/shard_map/ppermute | solution.py:536
  46.4 1.7 %collective-permute-start.15 = (f32[32,128]{1,0:T(8,128)S(1)}, f32[32,128]{1,0:T(8,128)S(1)}, u32[]{:S(2)}, u32[]{:S(2)}) collective-permute-start(f32[32,128]{1,0:T(8,128)S(1)} %get-tuple-element.109.refs_0_.own_near), channel_id=1, source_target_pairs={{0,32},{16,48},{32,0},{48,16},{64,96},{80,112},{96,64},{112,80},{1... | collective-permute-start | bytes 49160 | tf_op jit(solution)/shard_map/ppermute | solution.py:536
  48.2 0.8 %shard_map.78 = (f32[3,256,128]{2,1,0:T(8,128)}, f32[3,256,128]{2,1,0:T(8,128)}) custom-call(f32[32,128]{1,0:T(8,128)S(1)} %get-tuple-element.112.ends_c, f32[256,128]{1,0:T(8,128)S(1)} %get-tuple-element.113.g_c, f32[256,128]{1,0:T(8,128)S(1)} %get-tuple-element.91.refs_18_.refs_5_.u, f32[256,128]{1,0:T(8,128)S(1)} %get-tuple-element.92.refs_19_.refs_6_.v, ...), custom_call_target="tpu_custom_call" | custom-call | flops 1000000 | bytes 1000000 | tf_op jit(solution)/shard_map/pallas_call | solution.py:522
  49.6 2.1 %collective-permute-start.19 = (f32[32,128]{1,0:T(8,128)S(1)}, f32[32,128]{1,0:T(8,128)S(1)}, u32[]{:S(2)}, u32[]{:S(2)}) collective-permute-start(f32[32,128]{1,0:T(8,128)S(1)} %get-tuple-element.116.refs_0_), channel_id=1, source_target_pairs={{0,224},{16,240},{32,192},{48,208},{64,160},{80,176},{96,128},{112... | collective-permute-start | bytes 49160 | tf_op jit(solution)/shard_map/ppermute | solution.py:536
  51.8 0.9 %collective-permute-start.18 = (f32[32,128]{1,0:T(8,128)S(1)}, f32[32,128]{1,0:T(8,128)S(1)}, u32[]{:S(2)}, u32[]{:S(2)}) collective-permute-start(f32[32,128]{1,0:T(8,128)S(1)} %get-tuple-element.116.refs_0_), channel_id=1, source_target_pairs={{0,96},{16,112},{32,64},{48,80},{64,32},{80,48},{96,0},{112,16},{1... | collective-permute-start | bytes 49160 | tf_op jit(solution)/shard_map/ppermute | solution.py:536
  52.6 0.9 %collective-permute-start.17 = (f32[32,128]{1,0:T(8,128)S(1)}, f32[32,128]{1,0:T(8,128)S(1)}, u32[]{:S(2)}, u32[]{:S(2)}) collective-permute-start(f32[32,128]{1,0:T(8,128)S(1)} %get-tuple-element.116.refs_0_), channel_id=1, source_target_pairs={{0,128},{16,144},{32,160},{48,176},{64,192},{80,208},{96,224},{112... | collective-permute-start | bytes 49160 | tf_op jit(solution)/shard_map/ppermute | solution.py:536
  53.5 1.6 %shard_map.79 = (f32[3,256,128]{2,1,0:T(8,128)}, f32[3,256,128]{2,1,0:T(8,128)}) custom-call(f32[256,128]{1,0:T(8,128)S(1)} %get-tuple-element.119.part, f32[256,128]{1,0:T(8,128)S(1)} %get-tuple-element.120.rise_y, f32[7,256,128]{2,1,0:T(8,128)S(1)} %get-tuple-element.121.z_a, ...), custom_call_target="tpu_custom_call", output_to_operand_aliasing={{0}: (5, {}), {1}: (6, {})} | custom-call | flops 4000000 | bytes 1000000 | tf_op jit(solution)/shard_map/pallas_call | solution.py:522
  55.6 0.8 %shard_map.80 = (f32[3,256,128]{2,1,0:T(8,128)}, f32[3,256,128]{2,1,0:T(8,128)}) custom-call(s32[32,128]{1,0:T(8,128)S(1)} %get-tuple-element.66.pos, f32[4,80,128]{2,1,0:T(8,128)S(1)} %get-tuple-element.77.got_near.coefs.coefs_near, f32[4,96,128]{2,1,0:T(8,128)S(1)} %get-tuple-element.93.coefs_far, ...), custom_call_target="tpu_custom_call", output_to_operand_aliasing={{0}: (15, {}), {1}: (16, {})} | custom-call | flops 1000000 | bytes 1000000 | tf_op jit(solution)/shard_map/pallas_call | solution.py:522
  (30 shorter events, 4.3 us)
Async XLA Ops:
  1.3 10.2 %collective-permute-start = (f32[16,128]{1,0:T(8,128)S(1)}, f32[16,128]{1,0:T(8,128)S(1)}, u32[]{:S(2)}, u32[]{:S(2)}) collective-permute-start(f32[16,128]{1,0:T(8,128)S(1)} %shard_map.69), channel_id=1, source_target_pairs={{0,1},{1,2},{2,3},{3,4},{4,5},{5,6},{6,7},{7,8},{8,9},{9,10},{10,1... | collective-permute-start | bytes 24584 | tf_op jit(solution)/shard_map/ppermute | solution.py:565
  11.6 6.5 %collective-permute-start.3 = (f32[96,128]{1,0:T(8,128)S(1)}, f32[96,128]{1,0:T(8,128)S(1)}, u32[]{:S(2)}, u32[]{:S(2)}) collective-permute-start(f32[96,128]{1,0:T(8,128)S(1)} %get-tuple-element.76), channel_id=1, source_target_pairs={{0,48},{16,32},{32,16},{48,0},{64,112},{80,96},{96,80},{112,64},{1... | collective-permute-start | bytes 147464 | tf_op jit(solution)/shard_map/ppermute | solution.py:536
  14.3 3.7 %collective-permute-start.2 = (f32[96,128]{1,0:T(8,128)S(1)}, f32[96,128]{1,0:T(8,128)S(1)}, u32[]{:S(2)}, u32[]{:S(2)}) collective-permute-start(f32[96,128]{1,0:T(8,128)S(1)} %get-tuple-element.75), channel_id=1, source_target_pairs={{0,32},{16,48},{32,0},{48,16},{64,96},{80,112},{96,64},{112,80},{1... | collective-permute-start | bytes 147464 | tf_op jit(solution)/shard_map/ppermute | solution.py:536
  14.6 3.5 %collective-permute-start.1 = (f32[96,128]{1,0:T(8,128)S(1)}, f32[96,128]{1,0:T(8,128)S(1)}, u32[]{:S(2)}, u32[]{:S(2)}) collective-permute-start(f32[96,128]{1,0:T(8,128)S(1)} %get-tuple-element.75), channel_id=1, source_target_pairs={{0,16},{16,0},{32,48},{48,32},{64,80},{80,64},{96,112},{112,96},{1... | collective-permute-start | bytes 147464 | tf_op jit(solution)/shard_map/ppermute | solution.py:536
  14.8 7.5 %collective-permute-start.7 = (f32[128,128]{1,0:T(8,128)S(1)}, f32[128,128]{1,0:T(8,128)S(1)}, u32[]{:S(2)}, u32[]{:S(2)}) collective-permute-start(f32[128,128]{1,0:T(8,128)S(1)} %get-tuple-element.83), channel_id=1, source_target_pairs={{1,0},{2,1},{3,2},{4,3},{5,4},{6,5},{7,6},{8,7},{9,8},{10,9},{11,1... | collective-permute-start | bytes 196616 | tf_op jit(solution)/shard_map/ppermute | solution.py:579
  18.1 6.3 %collective-permute-start.6 = (f32[96,128]{1,0:T(8,128)S(1)}, f32[96,128]{1,0:T(8,128)S(1)}, u32[]{:S(2)}, u32[]{:S(2)}) collective-permute-start(f32[96,128]{1,0:T(8,128)S(1)} %get-tuple-element.78.refs_0_.group_b), channel_id=1, source_target_pairs={{0,240},{16,224},{32,208},{48,192},{64,176},{80,160},{96,144},{112... | collective-permute-start | bytes 147464 | tf_op jit(solution)/shard_map/ppermute | solution.py:536
  21.2 4.7 %collective-permute-start.5 = (f32[96,128]{1,0:T(8,128)S(1)}, f32[96,128]{1,0:T(8,128)S(1)}, u32[]{:S(2)}, u32[]{:S(2)}) collective-permute-start(f32[96,128]{1,0:T(8,128)S(1)} %get-tuple-element.78.refs_0_.group_b), channel_id=1, source_target_pairs={{0,112},{16,96},{32,80},{48,64},{64,48},{80,32},{96,16},{112,0},{1... | collective-permute-start | bytes 147464 | tf_op jit(solution)/shard_map/ppermute | solution.py:536
  21.3 4.7 %collective-permute-start.4 = (f32[96,128]{1,0:T(8,128)S(1)}, f32[96,128]{1,0:T(8,128)S(1)}, u32[]{:S(2)}, u32[]{:S(2)}) collective-permute-start(f32[96,128]{1,0:T(8,128)S(1)} %get-tuple-element.78.refs_0_.group_b), channel_id=1, source_target_pairs={{0,128},{16,144},{32,160},{48,176},{64,192},{80,208},{96,224},{112... | collective-permute-start | bytes 147464 | tf_op jit(solution)/shard_map/ppermute | solution.py:536
  26.8 6.0 %collective-permute-start.10 = (f32[112,128]{1,0:T(8,128)S(1)}, f32[112,128]{1,0:T(8,128)S(1)}, u32[]{:S(2)}, u32[]{:S(2)}) collective-permute-start(f32[112,128]{1,0:T(8,128)S(1)} %get-tuple-element.94.refs_0_.own_near), channel_id=1, source_target_pairs={{0,3},{1,2},{2,1},{3,0},{4,7},{5,6},{6,5},{7,4},{8,11},{9,10},{10,... | collective-permute-start | bytes 172040 | tf_op jit(solution)/shard_map/ppermute | solution.py:536
  26.8 5.9 %collective-permute-start.9 = (f32[112,128]{1,0:T(8,128)S(1)}, f32[112,128]{1,0:T(8,128)S(1)}, u32[]{:S(2)}, u32[]{:S(2)}) collective-permute-start(f32[112,128]{1,0:T(8,128)S(1)} %get-tuple-element.94.refs_0_.own_near), channel_id=1, source_target_pairs={{0,1},{1,0},{2,3},{3,2},{4,5},{5,4},{6,7},{7,6},{8,9},{9,8},{10,11... | collective-permute-start | bytes 172040 | tf_op jit(solution)/shard_map/ppermute | solution.py:536
  27.3 5.6 %collective-permute-start.8 = (f32[112,128]{1,0:T(8,128)S(1)}, f32[112,128]{1,0:T(8,128)S(1)}, u32[]{:S(2)}, u32[]{:S(2)}) collective-permute-start(f32[112,128]{1,0:T(8,128)S(1)} %get-tuple-element.94.refs_0_.own_near), channel_id=1, source_target_pairs={{0,2},{1,3},{2,0},{3,1},{4,6},{5,7},{6,4},{7,5},{8,10},{9,11},{10,... | collective-permute-start | bytes 172040 | tf_op jit(solution)/shard_map/ppermute | solution.py:536
  32.9 7.2 %collective-permute-start.13 = (f32[112,128]{1,0:T(8,128)S(1)}, f32[112,128]{1,0:T(8,128)S(1)}, u32[]{:S(2)}, u32[]{:S(2)}) collective-permute-start(f32[112,128]{1,0:T(8,128)S(1)} %get-tuple-element.102.refs_0_), channel_id=1, source_target_pairs={{0,12},{1,13},{2,14},{3,15},{4,8},{5,9},{6,10},{7,11},{8,4},{9,5},... | collective-permute-start | bytes 172040 | tf_op jit(solution)/shard_map/ppermute | solution.py:536
  35.9 6.0 %collective-permute-start.12 = (f32[112,128]{1,0:T(8,128)S(1)}, f32[112,128]{1,0:T(8,128)S(1)}, u32[]{:S(2)}, u32[]{:S(2)}) collective-permute-start(f32[112,128]{1,0:T(8,128)S(1)} %get-tuple-element.102.refs_0_), channel_id=1, source_target_pairs={{0,10},{1,11},{2,8},{3,9},{4,14},{5,15},{6,12},{7,13},{8,2},{9,3},... | collective-permute-start | bytes 172040 | tf_op jit(solution)/shard_map/ppermute | solution.py:536
  37.5 4.4 %collective-permute-start.11 = (f32[112,128]{1,0:T(8,128)S(1)}, f32[112,128]{1,0:T(8,128)S(1)}, u32[]{:S(2)}, u32[]{:S(2)}) collective-permute-start(f32[112,128]{1,0:T(8,128)S(1)} %get-tuple-element.102.refs_0_), channel_id=1, source_target_pairs={{0,4},{1,5},{2,6},{3,7},{4,0},{5,1},{6,2},{7,3},{8,12},{9,13},{10,... | collective-permute-start | bytes 172040 | tf_op jit(solution)/shard_map/ppermute | solution.py:536
  42.3 6.7 %collective-permute-start.16 = (f32[32,128]{1,0:T(8,128)S(1)}, f32[32,128]{1,0:T(8,128)S(1)}, u32[]{:S(2)}, u32[]{:S(2)}) collective-permute-start(f32[32,128]{1,0:T(8,128)S(1)} %get-tuple-element.109.refs_0_.own_near), channel_id=1, source_target_pairs={{0,48},{16,32},{32,16},{48,0},{64,112},{80,96},{96,80},{112,64},{1... | collective-permute-start | bytes 49160 | tf_op jit(solution)/shard_map/ppermute | solution.py:536
  46.4 3.1 %collective-permute-start.15 = (f32[32,128]{1,0:T(8,128)S(1)}, f32[32,128]{1,0:T(8,128)S(1)}, u32[]{:S(2)}, u32[]{:S(2)}) collective-permute-start(f32[32,128]{1,0:T(8,128)S(1)} %get-tuple-element.109.refs_0_.own_near), channel_id=1, source_target_pairs={{0,32},{16,48},{32,0},{48,16},{64,96},{80,112},{96,64},{112,80},{1... | collective-permute-start | bytes 49160 | tf_op jit(solution)/shard_map/ppermute | solution.py:536
  48.1 1.4 %collective-permute-start.14 = (f32[32,128]{1,0:T(8,128)S(1)}, f32[32,128]{1,0:T(8,128)S(1)}, u32[]{:S(2)}, u32[]{:S(2)}) collective-permute-start(f32[32,128]{1,0:T(8,128)S(1)} %get-tuple-element.109.refs_0_.own_near), channel_id=1, source_target_pairs={{0,16},{16,0},{32,48},{48,32},{64,80},{80,64},{96,112},{112,96},{1... | collective-permute-start | bytes 49160 | tf_op jit(solution)/shard_map/ppermute | solution.py:536
  49.6 5.5 %collective-permute-start.19 = (f32[32,128]{1,0:T(8,128)S(1)}, f32[32,128]{1,0:T(8,128)S(1)}, u32[]{:S(2)}, u32[]{:S(2)}) collective-permute-start(f32[32,128]{1,0:T(8,128)S(1)} %get-tuple-element.116.refs_0_), channel_id=1, source_target_pairs={{0,224},{16,240},{32,192},{48,208},{64,160},{80,176},{96,128},{112... | collective-permute-start | bytes 49160 | tf_op jit(solution)/shard_map/ppermute | solution.py:536
  51.8 3.8 %collective-permute-start.18 = (f32[32,128]{1,0:T(8,128)S(1)}, f32[32,128]{1,0:T(8,128)S(1)}, u32[]{:S(2)}, u32[]{:S(2)}) collective-permute-start(f32[32,128]{1,0:T(8,128)S(1)} %get-tuple-element.116.refs_0_), channel_id=1, source_target_pairs={{0,96},{16,112},{32,64},{48,80},{64,32},{80,48},{96,0},{112,16},{1... | collective-permute-start | bytes 49160 | tf_op jit(solution)/shard_map/ppermute | solution.py:536
  52.6 2.9 %collective-permute-start.17 = (f32[32,128]{1,0:T(8,128)S(1)}, f32[32,128]{1,0:T(8,128)S(1)}, u32[]{:S(2)}, u32[]{:S(2)}) collective-permute-start(f32[32,128]{1,0:T(8,128)S(1)} %get-tuple-element.116.refs_0_), channel_id=1, source_target_pairs={{0,128},{16,144},{32,160},{48,176},{64,192},{80,208},{96,224},{112... | collective-permute-start | bytes 49160 | tf_op jit(solution)/shard_map/ppermute | solution.py:536

commit v14 on v13

--- a/solution.py
+++ b/solution.py
@@ -499,17 +499,24 @@
         (rows_of(loaded(own_near, range(2)), 1), loaded(own_b, (2, 3, 4))),
         (rows_of(loaded(others[0], range(2)), 1), loaded(group_b, (2, 3, 4))),
     )
-    stores = [(full_y, elec.at[1]), (new_z, magn.at[2])]
-    stores = [pltpu.make_async_copy(a, b, sems.at[k]) for k, (a, b) in enumerate(stores)]
+    def store(value, field, k, part, sem):
+        rows = pl.ds(part * 4 * B, 4 * B)
+        copy = pltpu.make_async_copy(value.at[rows], field.at[k, rows], sems.at[sem])
+        copy.start()
+        return copy
+
+    stores = []
     for i in range(B):
         full_y[plane(i)] = g[plane(i)] + (u[plane(i)] * before + v[plane(i)] * after)
-    stores[0].start()
+        if i % 4 == 3:
+            stores.append(store(full_y, elec, 1, i // 4, i // 4))
     for i in range(B):
         rise = (full_y[plane(i + 1)] if i < B - 1 else after) - full_y[plane(i)]
         new_z[plane(i)] = -h * (flux2[plane(i)] + rise)
-    stores[1].start()
-    for store in stores:
-        store.wait()
+        if i % 4 == 3:
+            stores.append(store(new_z, magn, 2, i // 4, 4 + i // 4))
+    for copy in stores:
+        copy.wait()
 
 
 VMEM = pl.BlockSpec(memory_space=pltpu.VMEM)
@@ -646,7 +653,7 @@
         [whole] * 2,
         specs=[VMEM] * at + [HBM] * 2,
         out_specs=[HBM] * 2,
-        scratch=[(far_x, 2 * B, nz), cells, cells, dma((2,))],
+        scratch=[(far_x, 2 * B, nz), cells, cells, dma((8,))],
         aliases={at: 0, at + 1: 1},
     )
     return tuple(a.reshape(3, B, B, nz) for a in out)

time: 57.3 us -> 57.3 us (level)
  no operation moved by 1% of the time
where the time goes in v14:
time: 57.3 us; the launch traced here: 56.6 us
  starting transfers between devices  34.5 us (60%)
  waiting for transfers between devices  10.6 us (18%)
  Pallas kernels  10.5 us (18%)
  between operations  0.92 us (2%)
    ppermute x18, starting transfers between devices, shared(): lax.ppermute(value, axis, [(i, i ^ mask) for i in range(n)])  27.4 us
    pallas_call x13, Pallas kernels, call(): pl.pallas_call(kernel, out_shape=shapes, in_specs=specs or [VMEM] * len(i...  10.5 us
    ppermute x18, waiting for transfers between devices, shared(): lax.ppermute(value, axis, [(i, i ^ mask) for i in range(n)])  6.23 us
    ppermute x1, waiting for transfers between devices, local(): lax.ppermute(hx_last, 'py', [(i, (i + 1) % ny) for i in range(ny)])  4.33 us
    ppermute x1, starting transfers between devices, local(): lax.ppermute(hx_last, 'py', [(i, (i + 1) % ny) for i in range(ny)])  3.82 us
    ppermute x1, starting transfers between devices, local(): lax.ppermute(ez_first, 'py', [((i + 1) % ny, i) for i in range(ny)])  3.24 us
  transfers between devices with their start and end apart: 20, of which 7 were waited for; matrix products, arithmetic and copies ran while one was open for 0% of the time, Pallas kernels for 13%

profile of v14, /device:TPU:1, one launch (start us, length us, event | category | flops | bytes accessed | tf_op | source)
XLA Modules:
  0.0 56.6 jit_solution(18054485311397801858)
XLA Ops:
  1.3 3.8 %collective-permute-start = (f32[16,128]{1,0:T(8,128)S(1)}, f32[16,128]{1,0:T(8,128)S(1)}, u32[]{:S(2)}, u32[]{:S(2)}) collective-permute-start(f32[16,128]{1,0:T(8,128)S(1)} %shard_map.69), channel_id=1, source_target_pairs={{0,1},{1,2},{2,3},{3,4},{4,5},{5,6},{6,7},{7,8},{8,9},{9,10},{10,1... | collective-permute-start | bytes 24584 | tf_op jit(solution)/shard_map/ppermute | solution.py:572
  5.2 1.9 %shard_map.68 = (f32[256,128]{1,0:T(8,128)S(1)}, f32[256,128]{1,0:T(8,128)S(1)}, f32[256,128]{1,0:T(8,128)S(1)}, f32[256,128]{1,0:T(8,128)S(1)}, f32[256,128]{1,...) custom-call(s32[2]{0:T(128)S(1)} %pad_add_fusion.me, ...), custom_call_target="tpu_custom_call" | custom-call | flops 1000000 | bytes 1000000 | tf_op jit(solution)/shard_map/pallas_call | solution.py:529
  7.2 4.3 %collective-permute-done.hx_prev = f32[16,128]{1,0:T(8,128)S(1)} collective-permute-done((f32[16,128]{1,0:T(8,128)S(1)}, f32[16,128]{1,0:T(8,128)S(1)}, u32[]{:S(2)}, u32[]{:S(2)}) %collective-permute-start) | collective-permute-done | bytes 8224 | tf_op jit(solution)/shard_map/ppermute | solution.py:572
  11.6 2.7 %collective-permute-start.3 = (f32[96,128]{1,0:T(8,128)S(1)}, f32[96,128]{1,0:T(8,128)S(1)}, u32[]{:S(2)}, u32[]{:S(2)}) collective-permute-start(f32[96,128]{1,0:T(8,128)S(1)} %get-tuple-element.76), channel_id=1, source_target_pairs={{0,48},{16,32},{32,16},{48,0},{64,112},{80,96},{96,80},{112,64},{1... | collective-permute-start | bytes 147464 | tf_op jit(solution)/shard_map/ppermute | solution.py:543
  14.8 3.2 %collective-permute-start.7 = (f32[128,128]{1,0:T(8,128)S(1)}, f32[128,128]{1,0:T(8,128)S(1)}, u32[]{:S(2)}, u32[]{:S(2)}) collective-permute-start(f32[128,128]{1,0:T(8,128)S(1)} %get-tuple-element.83), channel_id=1, source_target_pairs={{1,0},{2,1},{3,2},{4,3},{5,4},{6,5},{7,6},{8,7},{9,8},{10,9},{11,1... | collective-permute-start | bytes 196616 | tf_op jit(solution)/shard_map/ppermute | solution.py:586
  18.1 3.1 %collective-permute-start.6 = (f32[96,128]{1,0:T(8,128)S(1)}, f32[96,128]{1,0:T(8,128)S(1)}, u32[]{:S(2)}, u32[]{:S(2)}) collective-permute-start(f32[96,128]{1,0:T(8,128)S(1)} %get-tuple-element.78.refs_0_.group_b), channel_id=1, source_target_pairs={{0,240},{16,224},{32,208},{48,192},{64,176},{80,160},{96,144},{112... | collective-permute-start | bytes 147464 | tf_op jit(solution)/shard_map/ppermute | solution.py:543
  21.3 1.1 %collective-permute-start.4 = (f32[96,128]{1,0:T(8,128)S(1)}, f32[96,128]{1,0:T(8,128)S(1)}, u32[]{:S(2)}, u32[]{:S(2)}) collective-permute-start(f32[96,128]{1,0:T(8,128)S(1)} %get-tuple-element.78.refs_0_.group_b), channel_id=1, source_target_pairs={{0,128},{16,144},{32,160},{48,176},{64,192},{80,208},{96,224},{112... | collective-permute-start | bytes 147464 | tf_op jit(solution)/shard_map/ppermute | solution.py:543
  22.3 2.0 %shard_map.72 = (f32[256,128]{1,0:T(8,128)S(1)}, f32[256,128]{1,0:T(8,128)S(1)}, f32[256,128]{1,0:T(8,128)S(1)}, f32[16,128]{1,0:T(8,128)S(1)}, f32[16,128]{1,0:...) custom-call(s32[32,128]{1,0:T(8,128)S(1)} %get-tuple-element.66.pos,, ...), custom_call_target="tpu_custom_call" | custom-call | flops 8000000 | bytes 1000000 | tf_op jit(solution)/shard_map/pallas_call | solution.py:529
  24.4 1.6 %collective-permute-done.5.refs_2_ = f32[96,128]{1,0:T(8,128)S(1)} collective-permute-done((f32[96,128]{1,0:T(8,128)S(1)}, f32[96,128]{1,0:T(8,128)S(1)}, u32[]{:S(2)}, u32[]{:S(2)}) %collective-permute-start.5) | collective-permute-done | bytes 49184 | tf_op jit(solution)/shard_map/ppermute | solution.py:543
  27.3 3.7 %collective-permute-start.8 = (f32[112,128]{1,0:T(8,128)S(1)}, f32[112,128]{1,0:T(8,128)S(1)}, u32[]{:S(2)}, u32[]{:S(2)}) collective-permute-start(f32[112,128]{1,0:T(8,128)S(1)} %get-tuple-element.94.refs_0_.own_near), channel_id=1, source_target_pairs={{0,2},{1,3},{2,0},{3,1},{4,6},{5,7},{6,4},{7,5},{8,10},{9,11},{10,... | collective-permute-start | bytes 172040 | tf_op jit(solution)/shard_map/ppermute | solution.py:543
  31.0 1.8 %collective-permute-done.10.refs_3_ = f32[112,128]{1,0:T(8,128)S(1)} collective-permute-done((f32[112,128]{1,0:T(8,128)S(1)}, f32[112,128]{1,0:T(8,128)S(1)}, u32[]{:S(2)}, u32[]{:S(2)}) %collective-permute-start.10) | collective-permute-done | bytes 57376 | tf_op jit(solution)/shard_map/ppermute | solution.py:543
  32.9 2.9 %collective-permute-start.13 = (f32[112,128]{1,0:T(8,128)S(1)}, f32[112,128]{1,0:T(8,128)S(1)}, u32[]{:S(2)}, u32[]{:S(2)}) collective-permute-start(f32[112,128]{1,0:T(8,128)S(1)} %get-tuple-element.102.refs_0_), channel_id=1, source_target_pairs={{0,12},{1,13},{2,14},{3,15},{4,8},{5,9},{6,10},{7,11},{8,4},{9,5},... | collective-permute-start | bytes 172040 | tf_op jit(solution)/shard_map/ppermute | solution.py:543
  35.9 1.7 %collective-permute-start.12 = (f32[112,128]{1,0:T(8,128)S(1)}, f32[112,128]{1,0:T(8,128)S(1)}, u32[]{:S(2)}, u32[]{:S(2)}) collective-permute-start(f32[112,128]{1,0:T(8,128)S(1)} %get-tuple-element.102.refs_0_), channel_id=1, source_target_pairs={{0,10},{1,11},{2,8},{3,9},{4,14},{5,15},{6,12},{7,13},{8,2},{9,3},... | collective-permute-start | bytes 172040 | tf_op jit(solution)/shard_map/ppermute | solution.py:543
  37.5 1.3 %collective-permute-start.11 = (f32[112,128]{1,0:T(8,128)S(1)}, f32[112,128]{1,0:T(8,128)S(1)}, u32[]{:S(2)}, u32[]{:S(2)}) collective-permute-start(f32[112,128]{1,0:T(8,128)S(1)} %get-tuple-element.102.refs_0_), channel_id=1, source_target_pairs={{0,4},{1,5},{2,6},{3,7},{4,0},{5,1},{6,2},{7,3},{8,12},{9,13},{10,... | collective-permute-start | bytes 172040 | tf_op jit(solution)/shard_map/ppermute | solution.py:543
  38.8 1.3 %shard_map.75 = (f32[7,256,128]{2,1,0:T(8,128)S(1)}, f32[7,256,128]{2,1,0:T(8,128)S(1)}, f32[256,128]{1,0:T(8,128)S(1)}) custom-call(f32[256,128]{1,0:T(8,128)S(1)} %get-tuple-element.98.w.refs_9_.w_in), custom_call_target="tpu_custom_call" | custom-call | flops 8000000 | bytes 1000000 | tf_op jit(solution)/shard_map/pallas_call | solution.py:529
  40.1 1.8 %collective-permute-done.12.refs_2_ = f32[112,128]{1,0:T(8,128)S(1)} collective-permute-done((f32[112,128]{1,0:T(8,128)S(1)}, f32[112,128]{1,0:T(8,128)S(1)}, u32[]{:S(2)}, u32[]{:S(2)}) %collective-permute-start.12) | collective-permute-done | bytes 57376 | tf_op jit(solution)/shard_map/ppermute | solution.py:543
  42.3 4.2 %collective-permute-start.16 = (f32[32,128]{1,0:T(8,128)S(1)}, f32[32,128]{1,0:T(8,128)S(1)}, u32[]{:S(2)}, u32[]{:S(2)}) collective-permute-start(f32[32,128]{1,0:T(8,128)S(1)} %get-tuple-element.109.refs_0_.own_near), channel_id=1, source_target_pairs={{0,48},{16,32},{32,16},{48,0},{64,112},{80,96},{96,80},{112,64},{1... | collective-permute-start | bytes 49160 | tf_op jit(solution)/shard_map/ppermute | solution.py:543
  46.4 1.7 %collective-permute-start.15 = (f32[32,128]{1,0:T(8,128)S(1)}, f32[32,128]{1,0:T(8,128)S(1)}, u32[]{:S(2)}, u32[]{:S(2)}) collective-permute-start(f32[32,128]{1,0:T(8,128)S(1)} %get-tuple-element.109.refs_0_.own_near), channel_id=1, source_target_pairs={{0,32},{16,48},{32,0},{48,16},{64,96},{80,112},{96,64},{112,80},{1... | collective-permute-start | bytes 49160 | tf_op jit(solution)/shard_map/ppermute | solution.py:543
  48.2 0.8 %shard_map.78 = (f32[3,256,128]{2,1,0:T(8,128)}, f32[3,256,128]{2,1,0:T(8,128)}) custom-call(f32[32,128]{1,0:T(8,128)S(1)} %get-tuple-element.112.ends_c, f32[256,128]{1,0:T(8,128)S(1)} %get-tuple-element.113.g_c, f32[256,128]{1,0:T(8,128)S(1)} %get-tuple-element.91.refs_18_.refs_5_.u, f32[256,128]{1,0:T(8,128)S(1)} %get-tuple-element.92.refs_19_.refs_6_.v, ...), custom_call_target="tpu_custom_call" | custom-call | flops 1000000 | bytes 1000000 | tf_op jit(solution)/shard_map/pallas_call | solution.py:529
  49.6 2.1 %collective-permute-start.19 = (f32[32,128]{1,0:T(8,128)S(1)}, f32[32,128]{1,0:T(8,128)S(1)}, u32[]{:S(2)}, u32[]{:S(2)}) collective-permute-start(f32[32,128]{1,0:T(8,128)S(1)} %get-tuple-element.116.refs_0_), channel_id=1, source_target_pairs={{0,224},{16,240},{32,192},{48,208},{64,160},{80,176},{96,128},{112... | collective-permute-start | bytes 49160 | tf_op jit(solution)/shard_map/ppermute | solution.py:543
  51.8 0.9 %collective-permute-start.18 = (f32[32,128]{1,0:T(8,128)S(1)}, f32[32,128]{1,0:T(8,128)S(1)}, u32[]{:S(2)}, u32[]{:S(2)}) collective-permute-start(f32[32,128]{1,0:T(8,128)S(1)} %get-tuple-element.116.refs_0_), channel_id=1, source_target_pairs={{0,96},{16,112},{32,64},{48,80},{64,32},{80,48},{96,0},{112,16},{1... | collective-permute-start | bytes 49160 | tf_op jit(solution)/shard_map/ppermute | solution.py:543
  52.6 0.9 %collective-permute-start.17 = (f32[32,128]{1,0:T(8,128)S(1)}, f32[32,128]{1,0:T(8,128)S(1)}, u32[]{:S(2)}, u32[]{:S(2)}) collective-permute-start(f32[32,128]{1,0:T(8,128)S(1)} %get-tuple-element.116.refs_0_), channel_id=1, source_target_pairs={{0,128},{16,144},{32,160},{48,176},{64,192},{80,208},{96,224},{112... | collective-permute-start | bytes 49160 | tf_op jit(solution)/shard_map/ppermute | solution.py:543
  53.5 1.6 %shard_map.79 = (f32[3,256,128]{2,1,0:T(8,128)}, f32[3,256,128]{2,1,0:T(8,128)}) custom-call(f32[256,128]{1,0:T(8,128)S(1)} %get-tuple-element.119.part, f32[256,128]{1,0:T(8,128)S(1)} %get-tuple-element.120.rise_y, f32[7,256,128]{2,1,0:T(8,128)S(1)} %get-tuple-element.121.z_a, ...), custom_call_target="tpu_custom_call", output_to_operand_aliasing={{0}: (5, {}), {1}: (6, {})} | custom-call | flops 4000000 | bytes 1000000 | tf_op jit(solution)/shard_map/pallas_call | solution.py:529
  55.6 0.9 %shard_map.80 = (f32[3,256,128]{2,1,0:T(8,128)}, f32[3,256,128]{2,1,0:T(8,128)}) custom-call(s32[32,128]{1,0:T(8,128)S(1)} %get-tuple-element.66.pos, f32[4,80,128]{2,1,0:T(8,128)S(1)} %get-tuple-element.77.got_near.coefs.coefs_near, f32[4,96,128]{2,1,0:T(8,128)S(1)} %get-tuple-element.93.coefs_far, ...), custom_call_target="tpu_custom_call", output_to_operand_aliasing={{0}: (15, {}), {1}: (16, {})} | custom-call | flops 1000000 | bytes 1000000 | tf_op jit(solution)/shard_map/pallas_call | solution.py:529
  (30 shorter events, 4.3 us)
Async XLA Ops:
  1.3 10.2 %collective-permute-start = (f32[16,128]{1,0:T(8,128)S(1)}, f32[16,128]{1,0:T(8,128)S(1)}, u32[]{:S(2)}, u32[]{:S(2)}) collective-permute-start(f32[16,128]{1,0:T(8,128)S(1)} %shard_map.69), channel_id=1, source_target_pairs={{0,1},{1,2},{2,3},{3,4},{4,5},{5,6},{6,7},{7,8},{8,9},{9,10},{10,1... | collective-permute-start | bytes 24584 | tf_op jit(solution)/shard_map/ppermute | solution.py:572
  11.6 6.5 %collective-permute-start.3 = (f32[96,128]{1,0:T(8,128)S(1)}, f32[96,128]{1,0:T(8,128)S(1)}, u32[]{:S(2)}, u32[]{:S(2)}) collective-permute-start(f32[96,128]{1,0:T(8,128)S(1)} %get-tuple-element.76), channel_id=1, source_target_pairs={{0,48},{16,32},{32,16},{48,0},{64,112},{80,96},{96,80},{112,64},{1... | collective-permute-start | bytes 147464 | tf_op jit(solution)/shard_map/ppermute | solution.py:543
  14.3 3.7 %collective-permute-start.2 = (f32[96,128]{1,0:T(8,128)S(1)}, f32[96,128]{1,0:T(8,128)S(1)}, u32[]{:S(2)}, u32[]{:S(2)}) collective-permute-start(f32[96,128]{1,0:T(8,128)S(1)} %get-tuple-element.75), channel_id=1, source_target_pairs={{0,32},{16,48},{32,0},{48,16},{64,96},{80,112},{96,64},{112,80},{1... | collective-permute-start | bytes 147464 | tf_op jit(solution)/shard_map/ppermute | solution.py:543
  14.6 3.5 %collective-permute-start.1 = (f32[96,128]{1,0:T(8,128)S(1)}, f32[96,128]{1,0:T(8,128)S(1)}, u32[]{:S(2)}, u32[]{:S(2)}) collective-permute-start(f32[96,128]{1,0:T(8,128)S(1)} %get-tuple-element.75), channel_id=1, source_target_pairs={{0,16},{16,0},{32,48},{48,32},{64,80},{80,64},{96,112},{112,96},{1... | collective-permute-start | bytes 147464 | tf_op jit(solution)/shard_map/ppermute | solution.py:543
  14.8 7.5 %collective-permute-start.7 = (f32[128,128]{1,0:T(8,128)S(1)}, f32[128,128]{1,0:T(8,128)S(1)}, u32[]{:S(2)}, u32[]{:S(2)}) collective-permute-start(f32[128,128]{1,0:T(8,128)S(1)} %get-tuple-element.83), channel_id=1, source_target_pairs={{1,0},{2,1},{3,2},{4,3},{5,4},{6,5},{7,6},{8,7},{9,8},{10,9},{11,1... | collective-permute-start | bytes 196616 | tf_op jit(solution)/shard_map/ppermute | solution.py:586
  18.1 6.3 %collective-permute-start.6 = (f32[96,128]{1,0:T(8,128)S(1)}, f32[96,128]{1,0:T(8,128)S(1)}, u32[]{:S(2)}, u32[]{:S(2)}) collective-permute-start(f32[96,128]{1,0:T(8,128)S(1)} %get-tuple-element.78.refs_0_.group_b), channel_id=1, source_target_pairs={{0,240},{16,224},{32,208},{48,192},{64,176},{80,160},{96,144},{112... | collective-permute-start | bytes 147464 | tf_op jit(solution)/shard_map/ppermute | solution.py:543
  21.2 4.7 %collective-permute-start.5 = (f32[96,128]{1,0:T(8,128)S(1)}, f32[96,128]{1,0:T(8,128)S(1)}, u32[]{:S(2)}, u32[]{:S(2)}) collective-permute-start(f32[96,128]{1,0:T(8,128)S(1)} %get-tuple-element.78.refs_0_.group_b), channel_id=1, source_target_pairs={{0,112},{16,96},{32,80},{48,64},{64,48},{80,32},{96,16},{112,0},{1... | collective-permute-start | bytes 147464 | tf_op jit(solution)/shard_map/ppermute | solution.py:543
  21.3 4.7 %collective-permute-start.4 = (f32[96,128]{1,0:T(8,128)S(1)}, f32[96,128]{1,0:T(8,128)S(1)}, u32[]{:S(2)}, u32[]{:S(2)}) collective-permute-start(f32[96,128]{1,0:T(8,128)S(1)} %get-tuple-element.78.refs_0_.group_b), channel_id=1, source_target_pairs={{0,128},{16,144},{32,160},{48,176},{64,192},{80,208},{96,224},{112... | collective-permute-start | bytes 147464 | tf_op jit(solution)/shard_map/ppermute | solution.py:543
  26.8 6.0 %collective-permute-start.10 = (f32[112,128]{1,0:T(8,128)S(1)}, f32[112,128]{1,0:T(8,128)S(1)}, u32[]{:S(2)}, u32[]{:S(2)}) collective-permute-start(f32[112,128]{1,0:T(8,128)S(1)} %get-tuple-element.94.refs_0_.own_near), channel_id=1, source_target_pairs={{0,3},{1,2},{2,1},{3,0},{4,7},{5,6},{6,5},{7,4},{8,11},{9,10},{10,... | collective-permute-start | bytes 172040 | tf_op jit(solution)/shard_map/ppermute | solution.py:543
  26.8 5.9 %collective-permute-start.9 = (f32[112,128]{1,0:T(8,128)S(1)}, f32[112,128]{1,0:T(8,128)S(1)}, u32[]{:S(2)}, u32[]{:S(2)}) collective-permute-start(f32[112,128]{1,0:T(8,128)S(1)} %get-tuple-element.94.refs_0_.own_near), channel_id=1, source_target_pairs={{0,1},{1,0},{2,3},{3,2},{4,5},{5,4},{6,7},{7,6},{8,9},{9,8},{10,11... | collective-permute-start | bytes 172040 | tf_op jit(solution)/shard_map/ppermute | solution.py:543
  27.3 5.6 %collective-permute-start.8 = (f32[112,128]{1,0:T(8,128)S(1)}, f32[112,128]{1,0:T(8,128)S(1)}, u32[]{:S(2)}, u32[]{:S(2)}) collective-permute-start(f32[112,128]{1,0:T(8,128)S(1)} %get-tuple-element.94.refs_0_.own_near), channel_id=1, source_target_pairs={{0,2},{1,3},{2,0},{3,1},{4,6},{5,7},{6,4},{7,5},{8,10},{9,11},{10,... | collective-permute-start | bytes 172040 | tf_op jit(solution)/shard_map/ppermute | solution.py:543
  32.9 7.2 %collective-permute-start.13 = (f32[112,128]{1,0:T(8,128)S(1)}, f32[112,128]{1,0:T(8,128)S(1)}, u32[]{:S(2)}, u32[]{:S(2)}) collective-permute-start(f32[112,128]{1,0:T(8,128)S(1)} %get-tuple-element.102.refs_0_), channel_id=1, source_target_pairs={{0,12},{1,13},{2,14},{3,15},{4,8},{5,9},{6,10},{7,11},{8,4},{9,5},... | collective-permute-start | bytes 172040 | tf_op jit(solution)/shard_map/ppermute | solution.py:543
  35.9 6.0 %collective-permute-start.12 = (f32[112,128]{1,0:T(8,128)S(1)}, f32[112,128]{1,0:T(8,128)S(1)}, u32[]{:S(2)}, u32[]{:S(2)}) collective-permute-start(f32[112,128]{1,0:T(8,128)S(1)} %get-tuple-element.102.refs_0_), channel_id=1, source_target_pairs={{0,10},{1,11},{2,8},{3,9},{4,14},{5,15},{6,12},{7,13},{8,2},{9,3},... | collective-permute-start | bytes 172040 | tf_op jit(solution)/shard_map/ppermute | solution.py:543
  37.5 4.4 %collective-permute-start.11 = (f32[112,128]{1,0:T(8,128)S(1)}, f32[112,128]{1,0:T(8,128)S(1)}, u32[]{:S(2)}, u32[]{:S(2)}) collective-permute-start(f32[112,128]{1,0:T(8,128)S(1)} %get-tuple-element.102.refs_0_), channel_id=1, source_target_pairs={{0,4},{1,5},{2,6},{3,7},{4,0},{5,1},{6,2},{7,3},{8,12},{9,13},{10,... | collective-permute-start | bytes 172040 | tf_op jit(solution)/shard_map/ppermute | solution.py:543
  42.3 6.7 %collective-permute-start.16 = (f32[32,128]{1,0:T(8,128)S(1)}, f32[32,128]{1,0:T(8,128)S(1)}, u32[]{:S(2)}, u32[]{:S(2)}) collective-permute-start(f32[32,128]{1,0:T(8,128)S(1)} %get-tuple-element.109.refs_0_.own_near), channel_id=1, source_target_pairs={{0,48},{16,32},{32,16},{48,0},{64,112},{80,96},{96,80},{112,64},{1... | collective-permute-start | bytes 49160 | tf_op jit(solution)/shard_map/ppermute | solution.py:543
  46.4 3.1 %collective-permute-start.15 = (f32[32,128]{1,0:T(8,128)S(1)}, f32[32,128]{1,0:T(8,128)S(1)}, u32[]{:S(2)}, u32[]{:S(2)}) collective-permute-start(f32[32,128]{1,0:T(8,128)S(1)} %get-tuple-element.109.refs_0_.own_near), channel_id=1, source_target_pairs={{0,32},{16,48},{32,0},{48,16},{64,96},{80,112},{96,64},{112,80},{1... | collective-permute-start | bytes 49160 | tf_op jit(solution)/shard_map/ppermute | solution.py:543
  48.1 1.4 %collective-permute-start.14 = (f32[32,128]{1,0:T(8,128)S(1)}, f32[32,128]{1,0:T(8,128)S(1)}, u32[]{:S(2)}, u32[]{:S(2)}) collective-permute-start(f32[32,128]{1,0:T(8,128)S(1)} %get-tuple-element.109.refs_0_.own_near), channel_id=1, source_target_pairs={{0,16},{16,0},{32,48},{48,32},{64,80},{80,64},{96,112},{112,96},{1... | collective-permute-start | bytes 49160 | tf_op jit(solution)/shard_map/ppermute | solution.py:543
  49.6 5.5 %collective-permute-start.19 = (f32[32,128]{1,0:T(8,128)S(1)}, f32[32,128]{1,0:T(8,128)S(1)}, u32[]{:S(2)}, u32[]{:S(2)}) collective-permute-start(f32[32,128]{1,0:T(8,128)S(1)} %get-tuple-element.116.refs_0_), channel_id=1, source_target_pairs={{0,224},{16,240},{32,192},{48,208},{64,160},{80,176},{96,128},{112... | collective-permute-start | bytes 49160 | tf_op jit(solution)/shard_map/ppermute | solution.py:543
  51.8 3.8 %collective-permute-start.18 = (f32[32,128]{1,0:T(8,128)S(1)}, f32[32,128]{1,0:T(8,128)S(1)}, u32[]{:S(2)}, u32[]{:S(2)}) collective-permute-start(f32[32,128]{1,0:T(8,128)S(1)} %get-tuple-element.116.refs_0_), channel_id=1, source_target_pairs={{0,96},{16,112},{32,64},{48,80},{64,32},{80,48},{96,0},{112,16},{1... | collective-permute-start | bytes 49160 | tf_op jit(solution)/shard_map/ppermute | solution.py:543
  52.6 2.9 %collective-permute-start.17 = (f32[32,128]{1,0:T(8,128)S(1)}, f32[32,128]{1,0:T(8,128)S(1)}, u32[]{:S(2)}, u32[]{:S(2)}) collective-permute-start(f32[32,128]{1,0:T(8,128)S(1)} %get-tuple-element.116.refs_0_), channel_id=1, source_target_pairs={{0,128},{16,144},{32,160},{48,176},{64,192},{80,208},{96,224},{112... | collective-permute-start | bytes 49160 | tf_op jit(solution)/shard_map/ppermute | solution.py:543

commit v15 on v13

--- a/solution.py
+++ b/solution.py
@@ -566,7 +566,7 @@
     w, c, p_x, u_x, v_x, flux_b, part_b, ef, mf, ez_first, pos = call(
         tables_kernel,
         [me, in_hbm(permittivity), in_hbm(conductivity), ids, elec, magn],
-        [cells] * 7 + [(3, *cells)] * 2 + [(8 * B, nz), jax.ShapeDtypeStruct((2 * B, nz), jnp.int32)],
+        [cells] * 7 + [(3, *cells)] * 2 + [(6 * B, nz), jax.ShapeDtypeStruct((2 * B, nz), jnp.int32)],
         specs=[SMEM] + [HBM] * 5,
         scratch=[pltpu.VMEM(cells, jnp.int32)] + [pltpu.SMEM(permittivity.shape, F32)] * 2 + [dma((9,))],
     )

time: 57.3 us -> 57.3 us (level)
  no operation moved by 1% of the time
where the time goes in v15:
time: 57.3 us; the launch traced here: 56.5 us
  starting transfers between devices  34.5 us (60%)
  waiting for transfers between devices  10.6 us (18%)
  Pallas kernels  10.5 us (18%)
  between operations  0.91 us (2%)
    ppermute x18, starting transfers between devices, shared(): lax.ppermute(value, axis, [(i, i ^ mask) for i in range(n)])  27.4 us
    pallas_call x13, Pallas kernels, call(): pl.pallas_call(kernel, out_shape=shapes, in_specs=specs or [VMEM] * len(i...  10.5 us
    ppermute x18, waiting for transfers between devices, shared(): lax.ppermute(value, axis, [(i, i ^ mask) for i in range(n)])  6.23 us
    ppermute x1, waiting for transfers between devices, local(): lax.ppermute(hx_last, 'py', [(i, (i + 1) % ny) for i in range(ny)])  4.33 us
    ppermute x1, starting transfers between devices, local(): lax.ppermute(hx_last, 'py', [(i, (i + 1) % ny) for i in range(ny)])  3.82 us
    ppermute x1, starting transfers between devices, local(): lax.ppermute(ez_first, 'py', [((i + 1) % ny, i) for i in range(ny)])  3.24 us
  transfers between devices with their start and end apart: 20, of which 7 were waited for; matrix products, arithmetic and copies ran while one was open for 0% of the time, Pallas kernels for 13%

profile of v15, /device:TPU:1, one launch (start us, length us, event | category | flops | bytes accessed | tf_op | source)
XLA Modules:
  0.0 56.5 jit_solution(2614402455837342609)
XLA Ops:
  1.3 3.8 %collective-permute-start = (f32[16,128]{1,0:T(8,128)S(1)}, f32[16,128]{1,0:T(8,128)S(1)}, u32[]{:S(2)}, u32[]{:S(2)}) collective-permute-start(f32[16,128]{1,0:T(8,128)S(1)} %shard_map.69), channel_id=1, source_target_pairs={{0,1},{1,2},{2,3},{3,4},{4,5},{5,6},{6,7},{7,8},{8,9},{9,10},{10,1... | collective-permute-start | bytes 24584 | tf_op jit(solution)/shard_map/ppermute | solution.py:565
  5.2 1.9 %shard_map.68 = (f32[256,128]{1,0:T(8,128)S(1)}, f32[256,128]{1,0:T(8,128)S(1)}, f32[256,128]{1,0:T(8,128)S(1)}, f32[256,128]{1,0:T(8,128)S(1)}, f32[256,128]{1,...) custom-call(s32[2]{0:T(128)S(1)} %pad_add_fusion.me, ...), custom_call_target="tpu_custom_call" | custom-call | flops 1000000 | bytes 1000000 | tf_op jit(solution)/shard_map/pallas_call | solution.py:522
  7.2 4.3 %collective-permute-done.hx_prev = f32[16,128]{1,0:T(8,128)S(1)} collective-permute-done((f32[16,128]{1,0:T(8,128)S(1)}, f32[16,128]{1,0:T(8,128)S(1)}, u32[]{:S(2)}, u32[]{:S(2)}) %collective-permute-start) | collective-permute-done | bytes 8224 | tf_op jit(solution)/shard_map/ppermute | solution.py:565
  11.6 2.7 %collective-permute-start.3 = (f32[96,128]{1,0:T(8,128)S(1)}, f32[96,128]{1,0:T(8,128)S(1)}, u32[]{:S(2)}, u32[]{:S(2)}) collective-permute-start(f32[96,128]{1,0:T(8,128)S(1)} %get-tuple-element.76), channel_id=1, source_target_pairs={{0,48},{16,32},{32,16},{48,0},{64,112},{80,96},{96,80},{112,64},{1... | collective-permute-start | bytes 147464 | tf_op jit(solution)/shard_map/ppermute | solution.py:536
  14.8 3.2 %collective-permute-start.7 = (f32[96,128]{1,0:T(8,128)S(1)}, f32[96,128]{1,0:T(8,128)S(1)}, u32[]{:S(2)}, u32[]{:S(2)}) collective-permute-start(f32[96,128]{1,0:T(8,128)S(1)} %get-tuple-element.83), channel_id=1, source_target_pairs={{1,0},{2,1},{3,2},{4,3},{5,4},{6,5},{7,6},{8,7},{9,8},{10,9},{11,1... | collective-permute-start | bytes 147464 | tf_op jit(solution)/shard_map/ppermute | solution.py:579
  18.1 3.1 %collective-permute-start.6 = (f32[96,128]{1,0:T(8,128)S(1)}, f32[96,128]{1,0:T(8,128)S(1)}, u32[]{:S(2)}, u32[]{:S(2)}) collective-permute-start(f32[96,128]{1,0:T(8,128)S(1)} %get-tuple-element.78.refs_0_.group_b), channel_id=1, source_target_pairs={{0,240},{16,224},{32,208},{48,192},{64,176},{80,160},{96,144},{112... | collective-permute-start | bytes 147464 | tf_op jit(solution)/shard_map/ppermute | solution.py:536
  21.3 1.1 %collective-permute-start.4 = (f32[96,128]{1,0:T(8,128)S(1)}, f32[96,128]{1,0:T(8,128)S(1)}, u32[]{:S(2)}, u32[]{:S(2)}) collective-permute-start(f32[96,128]{1,0:T(8,128)S(1)} %get-tuple-element.78.refs_0_.group_b), channel_id=1, source_target_pairs={{0,128},{16,144},{32,160},{48,176},{64,192},{80,208},{96,224},{112... | collective-permute-start | bytes 147464 | tf_op jit(solution)/shard_map/ppermute | solution.py:536
  22.3 2.0 %shard_map.72 = (f32[256,128]{1,0:T(8,128)S(1)}, f32[256,128]{1,0:T(8,128)S(1)}, f32[256,128]{1,0:T(8,128)S(1)}, f32[16,128]{1,0:T(8,128)S(1)}, f32[16,128]{1,0:...) custom-call(s32[32,128]{1,0:T(8,128)S(1)} %get-tuple-element.66.pos,, ...), custom_call_target="tpu_custom_call" | custom-call | flops 8000000 | bytes 1000000 | tf_op jit(solution)/shard_map/pallas_call | solution.py:522
  24.4 1.6 %collective-permute-done.5.refs_2_ = f32[96,128]{1,0:T(8,128)S(1)} collective-permute-done((f32[96,128]{1,0:T(8,128)S(1)}, f32[96,128]{1,0:T(8,128)S(1)}, u32[]{:S(2)}, u32[]{:S(2)}) %collective-permute-start.5) | collective-permute-done | bytes 49184 | tf_op jit(solution)/shard_map/ppermute | solution.py:536
  27.3 3.7 %collective-permute-start.8 = (f32[112,128]{1,0:T(8,128)S(1)}, f32[112,128]{1,0:T(8,128)S(1)}, u32[]{:S(2)}, u32[]{:S(2)}) collective-permute-start(f32[112,128]{1,0:T(8,128)S(1)} %get-tuple-element.94.refs_0_.own_near), channel_id=1, source_target_pairs={{0,2},{1,3},{2,0},{3,1},{4,6},{5,7},{6,4},{7,5},{8,10},{9,11},{10,... | collective-permute-start | bytes 172040 | tf_op jit(solution)/shard_map/ppermute | solution.py:536
  31.0 1.8 %collective-permute-done.10.refs_3_ = f32[112,128]{1,0:T(8,128)S(1)} collective-permute-done((f32[112,128]{1,0:T(8,128)S(1)}, f32[112,128]{1,0:T(8,128)S(1)}, u32[]{:S(2)}, u32[]{:S(2)}) %collective-permute-start.10) | collective-permute-done | bytes 57376 | tf_op jit(solution)/shard_map/ppermute | solution.py:536
  32.9 2.9 %collective-permute-start.13 = (f32[112,128]{1,0:T(8,128)S(1)}, f32[112,128]{1,0:T(8,128)S(1)}, u32[]{:S(2)}, u32[]{:S(2)}) collective-permute-start(f32[112,128]{1,0:T(8,128)S(1)} %get-tuple-element.102.refs_0_), channel_id=1, source_target_pairs={{0,12},{1,13},{2,14},{3,15},{4,8},{5,9},{6,10},{7,11},{8,4},{9,5},... | collective-permute-start | bytes 172040 | tf_op jit(solution)/shard_map/ppermute | solution.py:536
  35.9 1.7 %collective-permute-start.12 = (f32[112,128]{1,0:T(8,128)S(1)}, f32[112,128]{1,0:T(8,128)S(1)}, u32[]{:S(2)}, u32[]{:S(2)}) collective-permute-start(f32[112,128]{1,0:T(8,128)S(1)} %get-tuple-element.102.refs_0_), channel_id=1, source_target_pairs={{0,10},{1,11},{2,8},{3,9},{4,14},{5,15},{6,12},{7,13},{8,2},{9,3},... | collective-permute-start | bytes 172040 | tf_op jit(solution)/shard_map/ppermute | solution.py:536
  37.5 1.3 %collective-permute-start.11 = (f32[112,128]{1,0:T(8,128)S(1)}, f32[112,128]{1,0:T(8,128)S(1)}, u32[]{:S(2)}, u32[]{:S(2)}) collective-permute-start(f32[112,128]{1,0:T(8,128)S(1)} %get-tuple-element.102.refs_0_), channel_id=1, source_target_pairs={{0,4},{1,5},{2,6},{3,7},{4,0},{5,1},{6,2},{7,3},{8,12},{9,13},{10,... | collective-permute-start | bytes 172040 | tf_op jit(solution)/shard_map/ppermute | solution.py:536
  38.8 1.3 %shard_map.75 = (f32[7,256,128]{2,1,0:T(8,128)S(1)}, f32[7,256,128]{2,1,0:T(8,128)S(1)}, f32[256,128]{1,0:T(8,128)S(1)}) custom-call(f32[256,128]{1,0:T(8,128)S(1)} %get-tuple-element.98.w.refs_9_.w_in), custom_call_target="tpu_custom_call" | custom-call | flops 8000000 | bytes 1000000 | tf_op jit(solution)/shard_map/pallas_call | solution.py:522
  40.1 1.8 %collective-permute-done.12.refs_2_ = f32[112,128]{1,0:T(8,128)S(1)} collective-permute-done((f32[112,128]{1,0:T(8,128)S(1)}, f32[112,128]{1,0:T(8,128)S(1)}, u32[]{:S(2)}, u32[]{:S(2)}) %collective-permute-start.12) | collective-permute-done | bytes 57376 | tf_op jit(solution)/shard_map/ppermute | solution.py:536
  42.3 3.5 %collective-permute-start.16 = (f32[32,128]{1,0:T(8,128)S(1)}, f32[32,128]{1,0:T(8,128)S(1)}, u32[]{:S(2)}, u32[]{:S(2)}) collective-permute-start(f32[32,128]{1,0:T(8,128)S(1)} %get-tuple-element.109.refs_0_.own_near), channel_id=1, source_target_pairs={{0,48},{16,32},{32,16},{48,0},{64,112},{80,96},{96,80},{112,64},{1... | collective-permute-start | bytes 49160 | tf_op jit(solution)/shard_map/ppermute | solution.py:536
  45.8 2.3 %collective-permute-start.15 = (f32[32,128]{1,0:T(8,128)S(1)}, f32[32,128]{1,0:T(8,128)S(1)}, u32[]{:S(2)}, u32[]{:S(2)}) collective-permute-start(f32[32,128]{1,0:T(8,128)S(1)} %get-tuple-element.109.refs_0_.own_near), channel_id=1, source_target_pairs={{0,32},{16,48},{32,0},{48,16},{64,96},{80,112},{96,64},{112,80},{1... | collective-permute-start | bytes 49160 | tf_op jit(solution)/shard_map/ppermute | solution.py:536
  48.2 0.8 %shard_map.78 = (f32[3,256,128]{2,1,0:T(8,128)}, f32[3,256,128]{2,1,0:T(8,128)}) custom-call(f32[32,128]{1,0:T(8,128)S(1)} %get-tuple-element.112.ends_c, f32[256,128]{1,0:T(8,128)S(1)} %get-tuple-element.113.g_c, f32[256,128]{1,0:T(8,128)S(1)} %get-tuple-element.91.refs_18_.refs_5_.u, f32[256,128]{1,0:T(8,128)S(1)} %get-tuple-element.92.refs_19_.refs_6_.v, ...), custom_call_target="tpu_custom_call" | custom-call | flops 1000000 | bytes 1000000 | tf_op jit(solution)/shard_map/pallas_call | solution.py:522
  49.6 2.1 %collective-permute-start.19 = (f32[32,128]{1,0:T(8,128)S(1)}, f32[32,128]{1,0:T(8,128)S(1)}, u32[]{:S(2)}, u32[]{:S(2)}) collective-permute-start(f32[32,128]{1,0:T(8,128)S(1)} %get-tuple-element.116.refs_0_), channel_id=1, source_target_pairs={{0,224},{16,240},{32,192},{48,208},{64,160},{80,176},{96,128},{112... | collective-permute-start | bytes 49160 | tf_op jit(solution)/shard_map/ppermute | solution.py:536
  51.8 0.9 %collective-permute-start.18 = (f32[32,128]{1,0:T(8,128)S(1)}, f32[32,128]{1,0:T(8,128)S(1)}, u32[]{:S(2)}, u32[]{:S(2)}) collective-permute-start(f32[32,128]{1,0:T(8,128)S(1)} %get-tuple-element.116.refs_0_), channel_id=1, source_target_pairs={{0,96},{16,112},{32,64},{48,80},{64,32},{80,48},{96,0},{112,16},{1... | collective-permute-start | bytes 49160 | tf_op jit(solution)/shard_map/ppermute | solution.py:536
  52.6 0.9 %collective-permute-start.17 = (f32[32,128]{1,0:T(8,128)S(1)}, f32[32,128]{1,0:T(8,128)S(1)}, u32[]{:S(2)}, u32[]{:S(2)}) collective-permute-start(f32[32,128]{1,0:T(8,128)S(1)} %get-tuple-element.116.refs_0_), channel_id=1, source_target_pairs={{0,128},{16,144},{32,160},{48,176},{64,192},{80,208},{96,224},{112... | collective-permute-start | bytes 49160 | tf_op jit(solution)/shard_map/ppermute | solution.py:536
  53.6 1.6 %shard_map.79 = (f32[3,256,128]{2,1,0:T(8,128)}, f32[3,256,128]{2,1,0:T(8,128)}) custom-call(f32[256,128]{1,0:T(8,128)S(1)} %get-tuple-element.119.part, f32[256,128]{1,0:T(8,128)S(1)} %get-tuple-element.120.rise_y, f32[7,256,128]{2,1,0:T(8,128)S(1)} %get-tuple-element.121.z_a, ...), custom_call_target="tpu_custom_call", output_to_operand_aliasing={{0}: (5, {}), {1}: (6, {})} | custom-call | flops 4000000 | bytes 1000000 | tf_op jit(solution)/shard_map/pallas_call | solution.py:522
  55.6 0.8 %shard_map.80 = (f32[3,256,128]{2,1,0:T(8,128)}, f32[3,256,128]{2,1,0:T(8,128)}) custom-call(s32[32,128]{1,0:T(8,128)S(1)} %get-tuple-element.66.pos, f32[4,80,128]{2,1,0:T(8,128)S(1)} %get-tuple-element.77.got_near.coefs.coefs_near, f32[4,96,128]{2,1,0:T(8,128)S(1)} %get-tuple-element.93.coefs_far, ...), custom_call_target="tpu_custom_call", output_to_operand_aliasing={{0}: (15, {}), {1}: (16, {})} | custom-call | flops 1000000 | bytes 1000000 | tf_op jit(solution)/shard_map/pallas_call | solution.py:522
  (30 shorter events, 4.3 us)
Async XLA Ops:
  1.3 10.2 %collective-permute-start = (f32[16,128]{1,0:T(8,128)S(1)}, f32[16,128]{1,0:T(8,128)S(1)}, u32[]{:S(2)}, u32[]{:S(2)}) collective-permute-start(f32[16,128]{1,0:T(8,128)S(1)} %shard_map.69), channel_id=1, source_target_pairs={{0,1},{1,2},{2,3},{3,4},{4,5},{5,6},{6,7},{7,8},{8,9},{9,10},{10,1... | collective-permute-start | bytes 24584 | tf_op jit(solution)/shard_map/ppermute | solution.py:565
  11.6 6.5 %collective-permute-start.3 = (f32[96,128]{1,0:T(8,128)S(1)}, f32[96,128]{1,0:T(8,128)S(1)}, u32[]{:S(2)}, u32[]{:S(2)}) collective-permute-start(f32[96,128]{1,0:T(8,128)S(1)} %get-tuple-element.76), channel_id=1, source_target_pairs={{0,48},{16,32},{32,16},{48,0},{64,112},{80,96},{96,80},{112,64},{1... | collective-permute-start | bytes 147464 | tf_op jit(solution)/shard_map/ppermute | solution.py:536
  14.3 3.7 %collective-permute-start.2 = (f32[96,128]{1,0:T(8,128)S(1)}, f32[96,128]{1,0:T(8,128)S(1)}, u32[]{:S(2)}, u32[]{:S(2)}) collective-permute-start(f32[96,128]{1,0:T(8,128)S(1)} %get-tuple-element.75), channel_id=1, source_target_pairs={{0,32},{16,48},{32,0},{48,16},{64,96},{80,112},{96,64},{112,80},{1... | collective-permute-start | bytes 147464 | tf_op jit(solution)/shard_map/ppermute | solution.py:536
  14.6 3.5 %collective-permute-start.1 = (f32[96,128]{1,0:T(8,128)S(1)}, f32[96,128]{1,0:T(8,128)S(1)}, u32[]{:S(2)}, u32[]{:S(2)}) collective-permute-start(f32[96,128]{1,0:T(8,128)S(1)} %get-tuple-element.75), channel_id=1, source_target_pairs={{0,16},{16,0},{32,48},{48,32},{64,80},{80,64},{96,112},{112,96},{1... | collective-permute-start | bytes 147464 | tf_op jit(solution)/shard_map/ppermute | solution.py:536
  14.8 7.5 %collective-permute-start.7 = (f32[96,128]{1,0:T(8,128)S(1)}, f32[96,128]{1,0:T(8,128)S(1)}, u32[]{:S(2)}, u32[]{:S(2)}) collective-permute-start(f32[96,128]{1,0:T(8,128)S(1)} %get-tuple-element.83), channel_id=1, source_target_pairs={{1,0},{2,1},{3,2},{4,3},{5,4},{6,5},{7,6},{8,7},{9,8},{10,9},{11,1... | collective-permute-start | bytes 147464 | tf_op jit(solution)/shard_map/ppermute | solution.py:579
  18.1 6.3 %collective-permute-start.6 = (f32[96,128]{1,0:T(8,128)S(1)}, f32[96,128]{1,0:T(8,128)S(1)}, u32[]{:S(2)}, u32[]{:S(2)}) collective-permute-start(f32[96,128]{1,0:T(8,128)S(1)} %get-tuple-element.78.refs_0_.group_b), channel_id=1, source_target_pairs={{0,240},{16,224},{32,208},{48,192},{64,176},{80,160},{96,144},{112... | collective-permute-start | bytes 147464 | tf_op jit(solution)/shard_map/ppermute | solution.py:536
  21.2 4.7 %collective-permute-start.5 = (f32[96,128]{1,0:T(8,128)S(1)}, f32[96,128]{1,0:T(8,128)S(1)}, u32[]{:S(2)}, u32[]{:S(2)}) collective-permute-start(f32[96,128]{1,0:T(8,128)S(1)} %get-tuple-element.78.refs_0_.group_b), channel_id=1, source_target_pairs={{0,112},{16,96},{32,80},{48,64},{64,48},{80,32},{96,16},{112,0},{1... | collective-permute-start | bytes 147464 | tf_op jit(solution)/shard_map/ppermute | solution.py:536
  21.3 4.7 %collective-permute-start.4 = (f32[96,128]{1,0:T(8,128)S(1)}, f32[96,128]{1,0:T(8,128)S(1)}, u32[]{:S(2)}, u32[]{:S(2)}) collective-permute-start(f32[96,128]{1,0:T(8,128)S(1)} %get-tuple-element.78.refs_0_.group_b), channel_id=1, source_target_pairs={{0,128},{16,144},{32,160},{48,176},{64,192},{80,208},{96,224},{112... | collective-permute-start | bytes 147464 | tf_op jit(solution)/shard_map/ppermute | solution.py:536
  26.8 6.0 %collective-permute-start.10 = (f32[112,128]{1,0:T(8,128)S(1)}, f32[112,128]{1,0:T(8,128)S(1)}, u32[]{:S(2)}, u32[]{:S(2)}) collective-permute-start(f32[112,128]{1,0:T(8,128)S(1)} %get-tuple-element.94.refs_0_.own_near), channel_id=1, source_target_pairs={{0,3},{1,2},{2,1},{3,0},{4,7},{5,6},{6,5},{7,4},{8,11},{9,10},{10,... | collective-permute-start | bytes 172040 | tf_op jit(solution)/shard_map/ppermute | solution.py:536
  26.8 5.9 %collective-permute-start.9 = (f32[112,128]{1,0:T(8,128)S(1)}, f32[112,128]{1,0:T(8,128)S(1)}, u32[]{:S(2)}, u32[]{:S(2)}) collective-permute-start(f32[112,128]{1,0:T(8,128)S(1)} %get-tuple-element.94.refs_0_.own_near), channel_id=1, source_target_pairs={{0,1},{1,0},{2,3},{3,2},{4,5},{5,4},{6,7},{7,6},{8,9},{9,8},{10,11... | collective-permute-start | bytes 172040 | tf_op jit(solution)/shard_map/ppermute | solution.py:536
  27.3 5.6 %collective-permute-start.8 = (f32[112,128]{1,0:T(8,128)S(1)}, f32[112,128]{1,0:T(8,128)S(1)}, u32[]{:S(2)}, u32[]{:S(2)}) collective-permute-start(f32[112,128]{1,0:T(8,128)S(1)} %get-tuple-element.94.refs_0_.own_near), channel_id=1, source_target_pairs={{0,2},{1,3},{2,0},{3,1},{4,6},{5,7},{6,4},{7,5},{8,10},{9,11},{10,... | collective-permute-start | bytes 172040 | tf_op jit(solution)/shard_map/ppermute | solution.py:536
  32.9 7.2 %collective-permute-start.13 = (f32[112,128]{1,0:T(8,128)S(1)}, f32[112,128]{1,0:T(8,128)S(1)}, u32[]{:S(2)}, u32[]{:S(2)}) collective-permute-start(f32[112,128]{1,0:T(8,128)S(1)} %get-tuple-element.102.refs_0_), channel_id=1, source_target_pairs={{0,12},{1,13},{2,14},{3,15},{4,8},{5,9},{6,10},{7,11},{8,4},{9,5},... | collective-permute-start | bytes 172040 | tf_op jit(solution)/shard_map/ppermute | solution.py:536
  35.9 6.0 %collective-permute-start.12 = (f32[112,128]{1,0:T(8,128)S(1)}, f32[112,128]{1,0:T(8,128)S(1)}, u32[]{:S(2)}, u32[]{:S(2)}) collective-permute-start(f32[112,128]{1,0:T(8,128)S(1)} %get-tuple-element.102.refs_0_), channel_id=1, source_target_pairs={{0,10},{1,11},{2,8},{3,9},{4,14},{5,15},{6,12},{7,13},{8,2},{9,3},... | collective-permute-start | bytes 172040 | tf_op jit(solution)/shard_map/ppermute | solution.py:536
  37.5 4.4 %collective-permute-start.11 = (f32[112,128]{1,0:T(8,128)S(1)}, f32[112,128]{1,0:T(8,128)S(1)}, u32[]{:S(2)}, u32[]{:S(2)}) collective-permute-start(f32[112,128]{1,0:T(8,128)S(1)} %get-tuple-element.102.refs_0_), channel_id=1, source_target_pairs={{0,4},{1,5},{2,6},{3,7},{4,0},{5,1},{6,2},{7,3},{8,12},{9,13},{10,... | collective-permute-start | bytes 172040 | tf_op jit(solution)/shard_map/ppermute | solution.py:536
  42.3 6.7 %collective-permute-start.16 = (f32[32,128]{1,0:T(8,128)S(1)}, f32[32,128]{1,0:T(8,128)S(1)}, u32[]{:S(2)}, u32[]{:S(2)}) collective-permute-start(f32[32,128]{1,0:T(8,128)S(1)} %get-tuple-element.109.refs_0_.own_near), channel_id=1, source_target_pairs={{0,48},{16,32},{32,16},{48,0},{64,112},{80,96},{96,80},{112,64},{1... | collective-permute-start | bytes 49160 | tf_op jit(solution)/shard_map/ppermute | solution.py:536
  45.8 3.8 %collective-permute-start.15 = (f32[32,128]{1,0:T(8,128)S(1)}, f32[32,128]{1,0:T(8,128)S(1)}, u32[]{:S(2)}, u32[]{:S(2)}) collective-permute-start(f32[32,128]{1,0:T(8,128)S(1)} %get-tuple-element.109.refs_0_.own_near), channel_id=1, source_target_pairs={{0,32},{16,48},{32,0},{48,16},{64,96},{80,112},{96,64},{112,80},{1... | collective-permute-start | bytes 49160 | tf_op jit(solution)/shard_map/ppermute | solution.py:536
  48.1 1.4 %collective-permute-start.14 = (f32[32,128]{1,0:T(8,128)S(1)}, f32[32,128]{1,0:T(8,128)S(1)}, u32[]{:S(2)}, u32[]{:S(2)}) collective-permute-start(f32[32,128]{1,0:T(8,128)S(1)} %get-tuple-element.109.refs_0_.own_near), channel_id=1, source_target_pairs={{0,16},{16,0},{32,48},{48,32},{64,80},{80,64},{96,112},{112,96},{1... | collective-permute-start | bytes 49160 | tf_op jit(solution)/shard_map/ppermute | solution.py:536
  49.6 5.5 %collective-permute-start.19 = (f32[32,128]{1,0:T(8,128)S(1)}, f32[32,128]{1,0:T(8,128)S(1)}, u32[]{:S(2)}, u32[]{:S(2)}) collective-permute-start(f32[32,128]{1,0:T(8,128)S(1)} %get-tuple-element.116.refs_0_), channel_id=1, source_target_pairs={{0,224},{16,240},{32,192},{48,208},{64,160},{80,176},{96,128},{112... | collective-permute-start | bytes 49160 | tf_op jit(solution)/shard_map/ppermute | solution.py:536
  51.8 3.8 %collective-permute-start.18 = (f32[32,128]{1,0:T(8,128)S(1)}, f32[32,128]{1,0:T(8,128)S(1)}, u32[]{:S(2)}, u32[]{:S(2)}) collective-permute-start(f32[32,128]{1,0:T(8,128)S(1)} %get-tuple-element.116.refs_0_), channel_id=1, source_target_pairs={{0,96},{16,112},{32,64},{48,80},{64,32},{80,48},{96,0},{112,16},{1... | collective-permute-start | bytes 49160 | tf_op jit(solution)/shard_map/ppermute | solution.py:536
  52.6 2.9 %collective-permute-start.17 = (f32[32,128]{1,0:T(8,128)S(1)}, f32[32,128]{1,0:T(8,128)S(1)}, u32[]{:S(2)}, u32[]{:S(2)}) collective-permute-start(f32[32,128]{1,0:T(8,128)S(1)} %get-tuple-element.116.refs_0_), channel_id=1, source_target_pairs={{0,128},{16,144},{32,160},{48,176},{64,192},{80,208},{96,224},{112... | collective-permute-start | bytes 49160 | tf_op jit(solution)/shard_map/ppermute | solution.py:536

commit v16 on v13

--- a/solution.py
+++ b/solution.py
@@ -553,7 +553,7 @@
     magn = in_hbm(magnetic.reshape(3, *cells))
     ids = in_hbm(material.reshape(cells))
     dma = pltpu.SemaphoreType.DMA
-    orders = [(1, 2, 3), (2, 1, 3), (2, 1, 3), (1, 2, 3)]
+    orders = [(1, 2, 3), (1, 2, 3), (2, 1, 3), (1, 2, 3)]
     counts = (near_x, far_x, near_y, far_y)
     px_near, px_far, py_near, py_far = [
         tuple(s for s in order if s < count) for order, count in zip(orders, counts)

time: 57.3 us -> 57.8 us (level)
  waiting for transfers between devices: 10.6 us -> 11.4 us
    ppermute x18, waiting for transfers between devices: 6.23 us -> 7.11 us  [shared(): lax.ppermute(value, axis, [(i, i ^ mask) for i in range(n)])]
  transfers between devices with their start and end apart: 20 -> 20, of which waited for: 7 -> 8; matrix products, arithmetic and copies ran while one was open for 0% -> 0% of each run, Pallas kernels for 13% -> 13%
where the time goes in v16:
time: 57.8 us; the launch traced here: 57.3 us
  starting transfers between devices  34.4 us (60%)
  waiting for transfers between devices  11.4 us (20%)
  Pallas kernels  10.5 us (18%)
  between operations  0.93 us (2%)
    ppermute x18, starting transfers between devices, shared(): lax.ppermute(value, axis, [(i, i ^ mask) for i in range(n)])  27.3 us
    pallas_call x13, Pallas kernels, call(): pl.pallas_call(kernel, out_shape=shapes, in_specs=specs or [VMEM] * len(i...  10.5 us
    ppermute x18, waiting for transfers between devices, shared(): lax.ppermute(value, axis, [(i, i ^ mask) for i in range(n)])  7.11 us
    ppermute x1, waiting for transfers between devices, local(): lax.ppermute(hx_last, 'py', [(i, (i + 1) % ny) for i in range(ny)])  4.33 us
    ppermute x1, starting transfers between devices, local(): lax.ppermute(hx_last, 'py', [(i, (i + 1) % ny) for i in range(ny)])  3.82 us
    ppermute x1, starting transfers between devices, local(): lax.ppermute(ez_first, 'py', [((i + 1) % ny, i) for i in range(ny)])  3.24 us
  transfers between devices with their start and end apart: 20, of which 8 were waited for; matrix products, arithmetic and copies ran while one was open for 0% of the time, Pallas kernels for 13%

profile of v16, /device:TPU:1, one launch (start us, length us, event | category | flops | bytes accessed | tf_op | source)
XLA Modules:
  0.0 57.3 jit_solution(18445597603619718839)
XLA Ops:
  1.3 3.8 %collective-permute-start = (f32[16,128]{1,0:T(8,128)S(1)}, f32[16,128]{1,0:T(8,128)S(1)}, u32[]{:S(2)}, u32[]{:S(2)}) collective-permute-start(f32[16,128]{1,0:T(8,128)S(1)} %shard_map.69), channel_id=1, source_target_pairs={{0,1},{1,2},{2,3},{3,4},{4,5},{5,6},{6,7},{7,8},{8,9},{9,10},{10,1... | collective-permute-start | bytes 24584 | tf_op jit(solution)/shard_map/ppermute | solution.py:565
  5.2 1.9 %shard_map.68 = (f32[256,128]{1,0:T(8,128)S(1)}, f32[256,128]{1,0:T(8,128)S(1)}, f32[256,128]{1,0:T(8,128)S(1)}, f32[256,128]{1,0:T(8,128)S(1)}, f32[256,128]{1,...) custom-call(s32[2]{0:T(128)S(1)} %pad_add_fusion.me, ...), custom_call_target="tpu_custom_call" | custom-call | flops 1000000 | bytes 1000000 | tf_op jit(solution)/shard_map/pallas_call | solution.py:522
  7.2 4.3 %collective-permute-done.hx_prev = f32[16,128]{1,0:T(8,128)S(1)} collective-permute-done((f32[16,128]{1,0:T(8,128)S(1)}, f32[16,128]{1,0:T(8,128)S(1)}, u32[]{:S(2)}, u32[]{:S(2)}) %collective-permute-start) | collective-permute-done | bytes 8224 | tf_op jit(solution)/shard_map/ppermute | solution.py:565
  11.6 2.7 %collective-permute-start.3 = (f32[96,128]{1,0:T(8,128)S(1)}, f32[96,128]{1,0:T(8,128)S(1)}, u32[]{:S(2)}, u32[]{:S(2)}) collective-permute-start(f32[96,128]{1,0:T(8,128)S(1)} %get-tuple-element.76), channel_id=1, source_target_pairs={{0,48},{16,32},{32,16},{48,0},{64,112},{80,96},{96,80},{112,64},{1... | collective-permute-start | bytes 147464 | tf_op jit(solution)/shard_map/ppermute | solution.py:536
  14.8 3.2 %collective-permute-start.7 = (f32[128,128]{1,0:T(8,128)S(1)}, f32[128,128]{1,0:T(8,128)S(1)}, u32[]{:S(2)}, u32[]{:S(2)}) collective-permute-start(f32[128,128]{1,0:T(8,128)S(1)} %get-tuple-element.83), channel_id=1, source_target_pairs={{1,0},{2,1},{3,2},{4,3},{5,4},{6,5},{7,6},{8,7},{9,8},{10,9},{11,1... | collective-permute-start | bytes 196616 | tf_op jit(solution)/shard_map/ppermute | solution.py:579
  18.1 3.1 %collective-permute-start.6 = (f32[96,128]{1,0:T(8,128)S(1)}, f32[96,128]{1,0:T(8,128)S(1)}, u32[]{:S(2)}, u32[]{:S(2)}) collective-permute-start(f32[96,128]{1,0:T(8,128)S(1)} %get-tuple-element.78.refs_0_.group_b), channel_id=1, source_target_pairs={{0,240},{16,224},{32,208},{48,192},{64,176},{80,160},{96,144},{112... | collective-permute-start | bytes 147464 | tf_op jit(solution)/shard_map/ppermute | solution.py:536
  21.2 1.1 %collective-permute-start.5 = (f32[96,128]{1,0:T(8,128)S(1)}, f32[96,128]{1,0:T(8,128)S(1)}, u32[]{:S(2)}, u32[]{:S(2)}) collective-permute-start(f32[96,128]{1,0:T(8,128)S(1)} %get-tuple-element.78.refs_0_.group_b), channel_id=1, source_target_pairs={{0,128},{16,144},{32,160},{48,176},{64,192},{80,208},{96,224},{112... | collective-permute-start | bytes 147464 | tf_op jit(solution)/shard_map/ppermute | solution.py:536
  22.6 2.0 %shard_map.72 = (f32[256,128]{1,0:T(8,128)S(1)}, f32[256,128]{1,0:T(8,128)S(1)}, f32[256,128]{1,0:T(8,128)S(1)}, f32[16,128]{1,0:T(8,128)S(1)}, f32[16,128]{1,0:...) custom-call(s32[32,128]{1,0:T(8,128)S(1)} %get-tuple-element.66.pos,, ...), custom_call_target="tpu_custom_call" | custom-call | flops 8000000 | bytes 1000000 | tf_op jit(solution)/shard_map/pallas_call | solution.py:522
  24.6 0.9 %collective-permute-done.5.refs_2_ = f32[96,128]{1,0:T(8,128)S(1)} collective-permute-done((f32[96,128]{1,0:T(8,128)S(1)}, f32[96,128]{1,0:T(8,128)S(1)}, u32[]{:S(2)}, u32[]{:S(2)}) %collective-permute-start.5) | collective-permute-done | bytes 49184 | tf_op jit(solution)/shard_map/ppermute | solution.py:536
  25.5 1.5 %collective-permute-done.4.refs_1_ = f32[96,128]{1,0:T(8,128)S(1)} collective-permute-done((f32[96,128]{1,0:T(8,128)S(1)}, f32[96,128]{1,0:T(8,128)S(1)}, u32[]{:S(2)}, u32[]{:S(2)}) %collective-permute-start.4) | collective-permute-done | bytes 49184 | tf_op jit(solution)/shard_map/ppermute | solution.py:536
  28.0 4.0 %collective-permute-start.8 = (f32[112,128]{1,0:T(8,128)S(1)}, f32[112,128]{1,0:T(8,128)S(1)}, u32[]{:S(2)}, u32[]{:S(2)}) collective-permute-start(f32[112,128]{1,0:T(8,128)S(1)} %get-tuple-element.94.refs_0_.own_near), channel_id=1, source_target_pairs={{0,2},{1,3},{2,0},{3,1},{4,6},{5,7},{6,4},{7,5},{8,10},{9,11},{10,... | collective-permute-start | bytes 172040 | tf_op jit(solution)/shard_map/ppermute | solution.py:536
  32.1 1.8 %collective-permute-done.10.refs_3_ = f32[112,128]{1,0:T(8,128)S(1)} collective-permute-done((f32[112,128]{1,0:T(8,128)S(1)}, f32[112,128]{1,0:T(8,128)S(1)}, u32[]{:S(2)}, u32[]{:S(2)}) %collective-permute-start.10) | collective-permute-done | bytes 57376 | tf_op jit(solution)/shard_map/ppermute | solution.py:536
  34.0 2.3 %collective-permute-start.13 = (f32[112,128]{1,0:T(8,128)S(1)}, f32[112,128]{1,0:T(8,128)S(1)}, u32[]{:S(2)}, u32[]{:S(2)}) collective-permute-start(f32[112,128]{1,0:T(8,128)S(1)} %get-tuple-element.102.refs_0_), channel_id=1, source_target_pairs={{0,12},{1,13},{2,14},{3,15},{4,8},{5,9},{6,10},{7,11},{8,4},{9,5},... | collective-permute-start | bytes 172040 | tf_op jit(solution)/shard_map/ppermute | solution.py:536
  36.3 1.5 %collective-permute-start.12 = (f32[112,128]{1,0:T(8,128)S(1)}, f32[112,128]{1,0:T(8,128)S(1)}, u32[]{:S(2)}, u32[]{:S(2)}) collective-permute-start(f32[112,128]{1,0:T(8,128)S(1)} %get-tuple-element.102.refs_0_), channel_id=1, source_target_pairs={{0,10},{1,11},{2,8},{3,9},{4,14},{5,15},{6,12},{7,13},{8,2},{9,3},... | collective-permute-start | bytes 172040 | tf_op jit(solution)/shard_map/ppermute | solution.py:536
  37.8 1.9 %collective-permute-start.11 = (f32[112,128]{1,0:T(8,128)S(1)}, f32[112,128]{1,0:T(8,128)S(1)}, u32[]{:S(2)}, u32[]{:S(2)}) collective-permute-start(f32[112,128]{1,0:T(8,128)S(1)} %get-tuple-element.102.refs_0_), channel_id=1, source_target_pairs={{0,4},{1,5},{2,6},{3,7},{4,0},{5,1},{6,2},{7,3},{8,12},{9,13},{10,... | collective-permute-start | bytes 172040 | tf_op jit(solution)/shard_map/ppermute | solution.py:536
  39.7 1.3 %shard_map.75 = (f32[7,256,128]{2,1,0:T(8,128)S(1)}, f32[7,256,128]{2,1,0:T(8,128)S(1)}, f32[256,128]{1,0:T(8,128)S(1)}) custom-call(f32[256,128]{1,0:T(8,128)S(1)} %get-tuple-element.98.w.refs_9_.w_in), custom_call_target="tpu_custom_call" | custom-call | flops 8000000 | bytes 1000000 | tf_op jit(solution)/shard_map/pallas_call | solution.py:522
  41.0 1.4 %collective-permute-done.12.refs_2_ = f32[112,128]{1,0:T(8,128)S(1)} collective-permute-done((f32[112,128]{1,0:T(8,128)S(1)}, f32[112,128]{1,0:T(8,128)S(1)}, u32[]{:S(2)}, u32[]{:S(2)}) %collective-permute-start.12) | collective-permute-done | bytes 57376 | tf_op jit(solution)/shard_map/ppermute | solution.py:536
  42.7 3.7 %collective-permute-start.16 = (f32[32,128]{1,0:T(8,128)S(1)}, f32[32,128]{1,0:T(8,128)S(1)}, u32[]{:S(2)}, u32[]{:S(2)}) collective-permute-start(f32[32,128]{1,0:T(8,128)S(1)} %get-tuple-element.109.refs_0_.own_near), channel_id=1, source_target_pairs={{0,48},{16,32},{32,16},{48,0},{64,112},{80,96},{96,80},{112,64},{1... | collective-permute-start | bytes 49160 | tf_op jit(solution)/shard_map/ppermute | solution.py:536
  46.5 2.0 %collective-permute-start.15 = (f32[32,128]{1,0:T(8,128)S(1)}, f32[32,128]{1,0:T(8,128)S(1)}, u32[]{:S(2)}, u32[]{:S(2)}) collective-permute-start(f32[32,128]{1,0:T(8,128)S(1)} %get-tuple-element.109.refs_0_.own_near), channel_id=1, source_target_pairs={{0,32},{16,48},{32,0},{48,16},{64,96},{80,112},{96,64},{112,80},{1... | collective-permute-start | bytes 49160 | tf_op jit(solution)/shard_map/ppermute | solution.py:536
  49.9 1.5 %collective-permute-start.19 = (f32[32,128]{1,0:T(8,128)S(1)}, f32[32,128]{1,0:T(8,128)S(1)}, u32[]{:S(2)}, u32[]{:S(2)}) collective-permute-start(f32[32,128]{1,0:T(8,128)S(1)} %get-tuple-element.116.refs_0_), channel_id=1, source_target_pairs={{0,224},{16,240},{32,192},{48,208},{64,160},{80,176},{96,128},{112... | collective-permute-start | bytes 49160 | tf_op jit(solution)/shard_map/ppermute | solution.py:536
  52.1 1.7 %collective-permute-start.17 = (f32[32,128]{1,0:T(8,128)S(1)}, f32[32,128]{1,0:T(8,128)S(1)}, u32[]{:S(2)}, u32[]{:S(2)}) collective-permute-start(f32[32,128]{1,0:T(8,128)S(1)} %get-tuple-element.116.refs_0_), channel_id=1, source_target_pairs={{0,96},{16,112},{32,64},{48,80},{64,32},{80,48},{96,0},{112,16},{1... | collective-permute-start | bytes 49160 | tf_op jit(solution)/shard_map/ppermute | solution.py:536
  53.8 1.6 %shard_map.79 = (f32[3,256,128]{2,1,0:T(8,128)}, f32[3,256,128]{2,1,0:T(8,128)}) custom-call(f32[256,128]{1,0:T(8,128)S(1)} %get-tuple-element.119.part, f32[256,128]{1,0:T(8,128)S(1)} %get-tuple-element.120.rise_y, f32[7,256,128]{2,1,0:T(8,128)S(1)} %get-tuple-element.121.z_a, ...), custom_call_target="tpu_custom_call", output_to_operand_aliasing={{0}: (5, {}), {1}: (6, {})} | custom-call | flops 4000000 | bytes 1000000 | tf_op jit(solution)/shard_map/pallas_call | solution.py:522
  55.5 0.9 %collective-permute-done.17.refs_1_ = f32[32,128]{1,0:T(8,128)S(1)} collective-permute-done((f32[32,128]{1,0:T(8,128)S(1)}, f32[32,128]{1,0:T(8,128)S(1)}, u32[]{:S(2)}, u32[]{:S(2)}) %collective-permute-start.17) | collective-permute-done | bytes 16416 | tf_op jit(solution)/shard_map/ppermute | solution.py:536
  56.4 0.8 %shard_map.80 = (f32[3,256,128]{2,1,0:T(8,128)}, f32[3,256,128]{2,1,0:T(8,128)}) custom-call(s32[32,128]{1,0:T(8,128)S(1)} %get-tuple-element.66.pos, f32[4,80,128]{2,1,0:T(8,128)S(1)} %get-tuple-element.77.got_near.coefs.coefs_near, f32[4,96,128]{2,1,0:T(8,128)S(1)} %get-tuple-element.93.coefs_far, ...), custom_call_target="tpu_custom_call", output_to_operand_aliasing={{0}: (15, {}), {1}: (16, {})} | custom-call | flops 1000000 | bytes 1000000 | tf_op jit(solution)/shard_map/pallas_call | solution.py:522
  (30 shorter events, 5.4 us)
Async XLA Ops:
  1.3 10.2 %collective-permute-start = (f32[16,128]{1,0:T(8,128)S(1)}, f32[16,128]{1,0:T(8,128)S(1)}, u32[]{:S(2)}, u32[]{:S(2)}) collective-permute-start(f32[16,128]{1,0:T(8,128)S(1)} %shard_map.69), channel_id=1, source_target_pairs={{0,1},{1,2},{2,3},{3,4},{4,5},{5,6},{6,7},{7,8},{8,9},{9,10},{10,1... | collective-permute-start | bytes 24584 | tf_op jit(solution)/shard_map/ppermute | solution.py:565
  11.6 6.5 %collective-permute-start.3 = (f32[96,128]{1,0:T(8,128)S(1)}, f32[96,128]{1,0:T(8,128)S(1)}, u32[]{:S(2)}, u32[]{:S(2)}) collective-permute-start(f32[96,128]{1,0:T(8,128)S(1)} %get-tuple-element.76), channel_id=1, source_target_pairs={{0,48},{16,32},{32,16},{48,0},{64,112},{80,96},{96,80},{112,64},{1... | collective-permute-start | bytes 147464 | tf_op jit(solution)/shard_map/ppermute | solution.py:536
  14.3 3.7 %collective-permute-start.2 = (f32[96,128]{1,0:T(8,128)S(1)}, f32[96,128]{1,0:T(8,128)S(1)}, u32[]{:S(2)}, u32[]{:S(2)}) collective-permute-start(f32[96,128]{1,0:T(8,128)S(1)} %get-tuple-element.75), channel_id=1, source_target_pairs={{0,32},{16,48},{32,0},{48,16},{64,96},{80,112},{96,64},{112,80},{1... | collective-permute-start | bytes 147464 | tf_op jit(solution)/shard_map/ppermute | solution.py:536
  14.6 3.5 %collective-permute-start.1 = (f32[96,128]{1,0:T(8,128)S(1)}, f32[96,128]{1,0:T(8,128)S(1)}, u32[]{:S(2)}, u32[]{:S(2)}) collective-permute-start(f32[96,128]{1,0:T(8,128)S(1)} %get-tuple-element.75), channel_id=1, source_target_pairs={{0,16},{16,0},{32,48},{48,32},{64,80},{80,64},{96,112},{112,96},{1... | collective-permute-start | bytes 147464 | tf_op jit(solution)/shard_map/ppermute | solution.py:536
  14.8 7.8 %collective-permute-start.7 = (f32[128,128]{1,0:T(8,128)S(1)}, f32[128,128]{1,0:T(8,128)S(1)}, u32[]{:S(2)}, u32[]{:S(2)}) collective-permute-start(f32[128,128]{1,0:T(8,128)S(1)} %get-tuple-element.83), channel_id=1, source_target_pairs={{1,0},{2,1},{3,2},{4,3},{5,4},{6,5},{7,6},{8,7},{9,8},{10,9},{11,1... | collective-permute-start | bytes 196616 | tf_op jit(solution)/shard_map/ppermute | solution.py:579
  18.1 6.5 %collective-permute-start.6 = (f32[96,128]{1,0:T(8,128)S(1)}, f32[96,128]{1,0:T(8,128)S(1)}, u32[]{:S(2)}, u32[]{:S(2)}) collective-permute-start(f32[96,128]{1,0:T(8,128)S(1)} %get-tuple-element.78.refs_0_.group_b), channel_id=1, source_target_pairs={{0,240},{16,224},{32,208},{48,192},{64,176},{80,160},{96,144},{112... | collective-permute-start | bytes 147464 | tf_op jit(solution)/shard_map/ppermute | solution.py:536
  21.2 4.3 %collective-permute-start.5 = (f32[96,128]{1,0:T(8,128)S(1)}, f32[96,128]{1,0:T(8,128)S(1)}, u32[]{:S(2)}, u32[]{:S(2)}) collective-permute-start(f32[96,128]{1,0:T(8,128)S(1)} %get-tuple-element.78.refs_0_.group_b), channel_id=1, source_target_pairs={{0,128},{16,144},{32,160},{48,176},{64,192},{80,208},{96,224},{112... | collective-permute-start | bytes 147464 | tf_op jit(solution)/shard_map/ppermute | solution.py:536
  22.3 4.7 %collective-permute-start.4 = (f32[96,128]{1,0:T(8,128)S(1)}, f32[96,128]{1,0:T(8,128)S(1)}, u32[]{:S(2)}, u32[]{:S(2)}) collective-permute-start(f32[96,128]{1,0:T(8,128)S(1)} %get-tuple-element.78.refs_0_.group_b), channel_id=1, source_target_pairs={{0,112},{16,96},{32,80},{48,64},{64,48},{80,32},{96,16},{112,0},{1... | collective-permute-start | bytes 147464 | tf_op jit(solution)/shard_map/ppermute | solution.py:536
  27.8 6.0 %collective-permute-start.10 = (f32[112,128]{1,0:T(8,128)S(1)}, f32[112,128]{1,0:T(8,128)S(1)}, u32[]{:S(2)}, u32[]{:S(2)}) collective-permute-start(f32[112,128]{1,0:T(8,128)S(1)} %get-tuple-element.94.refs_0_.own_near), channel_id=1, source_target_pairs={{0,3},{1,2},{2,1},{3,0},{4,7},{5,6},{6,5},{7,4},{8,11},{9,10},{10,... | collective-permute-start | bytes 172040 | tf_op jit(solution)/shard_map/ppermute | solution.py:536
  27.9 5.9 %collective-permute-start.9 = (f32[112,128]{1,0:T(8,128)S(1)}, f32[112,128]{1,0:T(8,128)S(1)}, u32[]{:S(2)}, u32[]{:S(2)}) collective-permute-start(f32[112,128]{1,0:T(8,128)S(1)} %get-tuple-element.94.refs_0_.own_near), channel_id=1, source_target_pairs={{0,1},{1,0},{2,3},{3,2},{4,5},{5,4},{6,7},{7,6},{8,9},{9,8},{10,11... | collective-permute-start | bytes 172040 | tf_op jit(solution)/shard_map/ppermute | solution.py:536
  28.0 5.9 %collective-permute-start.8 = (f32[112,128]{1,0:T(8,128)S(1)}, f32[112,128]{1,0:T(8,128)S(1)}, u32[]{:S(2)}, u32[]{:S(2)}) collective-permute-start(f32[112,128]{1,0:T(8,128)S(1)} %get-tuple-element.94.refs_0_.own_near), channel_id=1, source_target_pairs={{0,2},{1,3},{2,0},{3,1},{4,6},{5,7},{6,4},{7,5},{8,10},{9,11},{10,... | collective-permute-start | bytes 172040 | tf_op jit(solution)/shard_map/ppermute | solution.py:536
  34.0 7.0 %collective-permute-start.13 = (f32[112,128]{1,0:T(8,128)S(1)}, f32[112,128]{1,0:T(8,128)S(1)}, u32[]{:S(2)}, u32[]{:S(2)}) collective-permute-start(f32[112,128]{1,0:T(8,128)S(1)} %get-tuple-element.102.refs_0_), channel_id=1, source_target_pairs={{0,12},{1,13},{2,14},{3,15},{4,8},{5,9},{6,10},{7,11},{8,4},{9,5},... | collective-permute-start | bytes 172040 | tf_op jit(solution)/shard_map/ppermute | solution.py:536
  36.3 6.0 %collective-permute-start.12 = (f32[112,128]{1,0:T(8,128)S(1)}, f32[112,128]{1,0:T(8,128)S(1)}, u32[]{:S(2)}, u32[]{:S(2)}) collective-permute-start(f32[112,128]{1,0:T(8,128)S(1)} %get-tuple-element.102.refs_0_), channel_id=1, source_target_pairs={{0,10},{1,11},{2,8},{3,9},{4,14},{5,15},{6,12},{7,13},{8,2},{9,3},... | collective-permute-start | bytes 172040 | tf_op jit(solution)/shard_map/ppermute | solution.py:536
  37.8 4.6 %collective-permute-start.11 = (f32[112,128]{1,0:T(8,128)S(1)}, f32[112,128]{1,0:T(8,128)S(1)}, u32[]{:S(2)}, u32[]{:S(2)}) collective-permute-start(f32[112,128]{1,0:T(8,128)S(1)} %get-tuple-element.102.refs_0_), channel_id=1, source_target_pairs={{0,4},{1,5},{2,6},{3,7},{4,0},{5,1},{6,2},{7,3},{8,12},{9,13},{10,... | collective-permute-start | bytes 172040 | tf_op jit(solution)/shard_map/ppermute | solution.py:536
  42.7 6.5 %collective-permute-start.16 = (f32[32,128]{1,0:T(8,128)S(1)}, f32[32,128]{1,0:T(8,128)S(1)}, u32[]{:S(2)}, u32[]{:S(2)}) collective-permute-start(f32[32,128]{1,0:T(8,128)S(1)} %get-tuple-element.109.refs_0_.own_near), channel_id=1, source_target_pairs={{0,48},{16,32},{32,16},{48,0},{64,112},{80,96},{96,80},{112,64},{1... | collective-permute-start | bytes 49160 | tf_op jit(solution)/shard_map/ppermute | solution.py:536
  46.5 3.4 %collective-permute-start.15 = (f32[32,128]{1,0:T(8,128)S(1)}, f32[32,128]{1,0:T(8,128)S(1)}, u32[]{:S(2)}, u32[]{:S(2)}) collective-permute-start(f32[32,128]{1,0:T(8,128)S(1)} %get-tuple-element.109.refs_0_.own_near), channel_id=1, source_target_pairs={{0,32},{16,48},{32,0},{48,16},{64,96},{80,112},{96,64},{112,80},{1... | collective-permute-start | bytes 49160 | tf_op jit(solution)/shard_map/ppermute | solution.py:536
  48.4 1.4 %collective-permute-start.14 = (f32[32,128]{1,0:T(8,128)S(1)}, f32[32,128]{1,0:T(8,128)S(1)}, u32[]{:S(2)}, u32[]{:S(2)}) collective-permute-start(f32[32,128]{1,0:T(8,128)S(1)} %get-tuple-element.109.refs_0_.own_near), channel_id=1, source_target_pairs={{0,16},{16,0},{32,48},{48,32},{64,80},{80,64},{96,112},{112,96},{1... | collective-permute-start | bytes 49160 | tf_op jit(solution)/shard_map/ppermute | solution.py:536
  49.9 5.5 %collective-permute-start.19 = (f32[32,128]{1,0:T(8,128)S(1)}, f32[32,128]{1,0:T(8,128)S(1)}, u32[]{:S(2)}, u32[]{:S(2)}) collective-permute-start(f32[32,128]{1,0:T(8,128)S(1)} %get-tuple-element.116.refs_0_), channel_id=1, source_target_pairs={{0,224},{16,240},{32,192},{48,208},{64,160},{80,176},{96,128},{112... | collective-permute-start | bytes 49160 | tf_op jit(solution)/shard_map/ppermute | solution.py:536
  51.4 4.0 %collective-permute-start.18 = (f32[32,128]{1,0:T(8,128)S(1)}, f32[32,128]{1,0:T(8,128)S(1)}, u32[]{:S(2)}, u32[]{:S(2)}) collective-permute-start(f32[32,128]{1,0:T(8,128)S(1)} %get-tuple-element.116.refs_0_), channel_id=1, source_target_pairs={{0,128},{16,144},{32,160},{48,176},{64,192},{80,208},{96,224},{112... | collective-permute-start | bytes 49160 | tf_op jit(solution)/shard_map/ppermute | solution.py:536
  52.1 4.2 %collective-permute-start.17 = (f32[32,128]{1,0:T(8,128)S(1)}, f32[32,128]{1,0:T(8,128)S(1)}, u32[]{:S(2)}, u32[]{:S(2)}) collective-permute-start(f32[32,128]{1,0:T(8,128)S(1)} %get-tuple-element.116.refs_0_), channel_id=1, source_target_pairs={{0,96},{16,112},{32,64},{48,80},{64,32},{80,48},{96,0},{112,16},{1... | collective-permute-start | bytes 49160 | tf_op jit(solution)/shard_map/ppermute | solution.py:536
